TPU v7x, 32 devices: a whole 2x2x4 slice. The times are simulated.
32 devices in a mesh: wide: 8 (over z, core), narrow: 4 (over y, x).
Axes of the slice: x: 2, y: 2, z: 4, core: 2. Of those that a mesh axis runs over, the one named last changes fastest.
Arguments:
- right_sides: float32 [4, 512, 128], P(None, ('wide', 'narrow')), may hold values from -6 to 6
- brinkman: float32 [512, 128], P(('wide', 'narrow')), may hold values from 0.1 to 1
- east_faces: float32 [512, 128], P(('wide', 'narrow')), may hold values from 0.1 to 10
- north_faces: float32 [512, 128], P(('wide', 'narrow')), may hold values from 0.1 to 10
- support: int32 [1024, 4], P(('wide', 'narrow')), may hold values from 0 to 31
- basis: float32 [1024, 64, 256], P(('wide', 'narrow')), may hold values from -0.75 to 0.75
- links: int32 [32, 4], P('wide'), may hold values from 0 to 31
- coarse_block_inverses: float32 [32, 64, 64], P('wide')
- coarse_coupling: float32 [32, 64, 256], P('wide')
Outputs:
- solution: float32 [4, 512, 128], P(None, ('wide', 'narrow'))
- coarse_solution: float32 [32, 256], P('wide')
All inputs are finite; a program needn't handle non-finite values.
Results may differ from a plain program's by a relative error of at most 0.0001.
Values sent between devices are 32-bit elements; how exact they have to be, the bound alone decides.
No kernel may reach another device: no remote copies, remote signals or barrier semaphores. Data moves between devices by JAX's collectives and lax.ppermute only.
A program may use at most 64 MiB of HBM per device.

v0:
```python
import jax
import jax.numpy as jnp
from jax import lax
from jax.sharding import PartitionSpec as P

SWEEPS = 2
COARSE_SWEEPS = 3


relax_weight = 0.7


def shifted(value, axis, steps):
    count = lax.axis_size(axis)
    first, last = (max(0, -steps), min(count, count - steps))
    return lax.ppermute(value, axis, [(source, source + steps) for source in range(first, last)])


def with_halo(block, sides, width):
    for axis, dim in sides:
        count = lax.axis_size(axis)
        forward = [(i, i + 1) for i in range(count - 1)]
        backward = [(target, source) for source, target in forward]
        low = lax.ppermute(
            lax.slice_in_dim(block, block.shape[dim] - width, None, axis=dim), axis, forward
        )
        high = lax.ppermute(lax.slice_in_dim(block, 0, width, axis=dim), axis, backward)
        block = jnp.concatenate([low, block, high], axis=dim)
    return block


def body(
    right_sides,
    brinkman,
    east_faces,
    north_faces,
    support,
    basis,
    links,
    coarse_block_inverses,
    coarse_coupling,
):
    top_precision = lax.Precision.HIGHEST
    adjoints, grid_rows, cells_per_row = right_sides.shape
    block_size = basis.shape[1]
    blocks_here = basis.shape[0]
    support_count = support.shape[1]
    owned = coarse_block_inverses.shape[0]
    link_count = links.shape[1]
    coarse_count = owned * lax.axis_size("wide")
    lower_row = shifted(north_faces[-1:], ("wide", "narrow"), 1)
    south = jnp.concatenate([lower_row, north_faces[:-1]], 0)
    west = jnp.roll(east_faces, 1, axis=1)
    diagonal = brinkman + east_faces + west + north_faces + south

    def operate(field):
        padded = with_halo(field, ((("wide", "narrow"), 1),), 1)
        above = padded[:, :-2]
        below = padded[:, 2:]
        return (
            diagonal * field
            - north_faces * below
            - south * above
            - east_faces * jnp.roll(field, -1, axis=2)
            - west * jnp.roll(field, 1, axis=2)
        )

    def sweep(field):
        return field + relax_weight * (right_sides - operate(field)) / diagonal

    field = jnp.zeros_like(right_sides)
    for step in range(SWEEPS):
        field = sweep(field)
    resid = (right_sides - operate(field)).reshape(adjoints, blocks_here, block_size)
    contrib = jnp.einsum("bfm,abf->bam", basis, resid, precision=top_precision)
    contrib = contrib.reshape(blocks_here, adjoints, support_count, block_size).transpose(
        0, 2, 1, 3
    )
    contrib = contrib.reshape(blocks_here * support_count, adjoints * block_size)
    columns = jnp.arange(coarse_count, dtype=jnp.int32)
    support_hot = (support.reshape(-1)[:, None] == columns[None, :]).astype(jnp.float32)
    coarse_level_terms = jnp.einsum(
        "pn,pv->nv", support_hot, contrib, precision=top_precision
    ).reshape(-1)
    portion = lax.psum_scatter(
        coarse_level_terms, ("wide", "narrow"), scatter_dimension=0, tiled=True
    )
    owned_rhs = lax.all_gather(portion, "narrow", axis=0, tiled=True)
    coarse_rhs = owned_rhs.reshape(owned, adjoints, block_size)

    def apply_inverse(adjoint_vector):
        return jnp.einsum(
            "lzo,lso->lsz", coarse_block_inverses, adjoint_vector, precision=top_precision
        )

    def spread(adjoint_vector):
        return lax.all_gather(
            adjoint_vector.reshape(owned, adjoints * block_size), "wide", axis=0, tiled=True
        )

    link_hot = (links.reshape(-1)[:, None] == columns[None, :]).astype(jnp.float32)
    coarse = apply_inverse(coarse_rhs)
    for step in range(COARSE_SWEEPS):
        everything = spread(coarse)
        nearby = jnp.dot(link_hot, everything, precision=top_precision)
        nearby = nearby.reshape(owned, link_count, adjoints, block_size).transpose(0, 2, 1, 3)
        nearby = nearby.reshape(owned, adjoints, link_count * block_size)
        pulled = jnp.einsum("icm,iam->iac", coarse_coupling, nearby, precision=top_precision)
        coarse = apply_inverse(coarse_rhs + pulled)
    everything = spread(coarse)
    chosen = jnp.dot(support_hot, everything, precision=top_precision)
    chosen = chosen.reshape(blocks_here, support_count, adjoints, block_size).transpose(0, 2, 1, 3)
    chosen = chosen.reshape(blocks_here, adjoints, support_count * block_size)
    coarse_update = jnp.einsum("bfm,bam->abf", basis, chosen, precision=top_precision)
    field = field + coarse_update.reshape(adjoints, grid_rows, cells_per_row)
    for step in range(SWEEPS):
        field = sweep(field)
    return (field, coarse.reshape(owned, adjoints * block_size))


def solution(mesh):
    return jax.shard_map(
        body,
        mesh=mesh,
        in_specs=(
            P(None, ("wide", "narrow"), None),
            P(("wide", "narrow"), None),
            P(("wide", "narrow"), None),
            P(("wide", "narrow"), None),
            P(("wide", "narrow"), None),
            P(("wide", "narrow"), None, None),
            P("wide", None),
            P("wide", None, None),
            P("wide", None, None),
        ),
        out_specs=(P(None, ("wide", "narrow"), None), P("wide", None)),
        check_vma=False,
    )
```

profile of v0, /device:TPU:0, one launch (start us, length us, event | category | flops | bytes accessed | tf_op | source)
XLA Modules:
  0.0 167.8 jit_solution(10737839963191231058)
XLA Ops:
  0.7 5.0 %collective-permute-start.2 = (f32[4,1,128]{2,1,0:T(1,128)S(1)}, f32[4,1,128]{2,1,0:T(1,128)S(1)}, u32[]{:S(2)}, u32[]{:S(2)}) collective-permute-start(f32[4,1,128]{2,1,0:T(1,128)S(1)} %broadcast.28), channel_id=1, source_target_pairs={{0,1},{1,2},{2,3},{3,4},{4,5},{5,6},{6,7},{7,8},{8,9},{9,10},{10,1... | collective-permute-start | bytes 6152 | tf_op jit(solution)/shard_map/ppermute | solution.py:24
  5.6 1.3 collective-permute-start.1
  6.9 0.7 slice.138
  7.6 4.5 %collective-permute-start = (f32[1,128]{1,0:T(1,128)S(1)}, f32[1,128]{1,0:T(1,128)S(1)}, u32[]{:S(2)}, u32[]{:S(2)}) collective-permute-start(f32[1,128]{1,0:T(1,128)S(1)} %slice.138), channel_id=1, source_target_pairs={{0,1},{1,2},{2,3},{3,4},{4,5},{5,6},{6,7},{7,8},{8,9},{9,10},{10,1... | collective-permute-start | bytes 1544 | tf_op jit(solution)/shard_map/ppermute | solution.py:16
  12.2 0.8 eq.34
  13.0 0.8 slice.136
  13.7 0.8 copy.22
  14.6 0.9 broadcast_multiply_fusion.1
  15.5 0.8 fusion.10
  16.4 1.3 collective-permute-start.3
  17.7 4.9 %collective-permute-start.4 = (f32[4,1,128]{2,1,0:T(1,128)S(1)}, f32[4,1,128]{2,1,0:T(1,128)S(1)}, u32[]{:S(2)}, u32[]{:S(2)}) collective-permute-start(f32[4,1,128]{2,1,0:T(1,128)S(1)} %get-tuple-element.29), channel_id=1, source_target_pairs={{0,1},{1,2},{2,3},{3,4},{4,5},{5,6},{6,7},{7,8},{8,9},{9,10},{10,1... | collective-permute-start | bytes 6152 | tf_op jit(solution)/shard_map/ppermute | solution.py:24
  22.7 1.2 collective-permute-done.4
  23.9 0.9 fusion.46
  24.9 1.3 collective-permute-start.5
  26.2 5.4 %collective-permute-start.6 = (f32[4,1,128]{2,1,0:T(1,128)S(1)}, f32[4,1,128]{2,1,0:T(1,128)S(1)}, u32[]{:S(2)}, u32[]{:S(2)}) collective-permute-start(f32[4,1,128]{2,1,0:T(1,128)S(1)} %get-tuple-element.23), channel_id=1, source_target_pairs={{0,1},{1,2},{2,3},{3,4},{4,5},{5,6},{6,7},{7,8},{8,9},{9,10},{10,1... | collective-permute-start | bytes 6152 | tf_op jit(solution)/shard_map/ppermute | solution.py:24
  31.7 1.2 collective-permute-done.6
  32.9 0.9 fusion.36
  33.9 1.1 fusion
  35.0 0.2 reshape.68
  35.3 0.2 reshape.69
  35.5 0.3 convolution_bitcast_fusion.1
  35.8 45.0 %all-reduce.3 = f32[8192]{0:T(1024)S(1)} all-reduce(f32[8192]{0:T(1024)S(1)} %bitcast.47), channel_id=2, replica_groups=mesh['wide'=8,'narrow'=4] {'wide','narrow'}, use_global_device_ids=true, to_apply=%region_0.1.clone | all-reduce | flops 8192 | bytes 65536
  80.9 8.8 %all-gather = f32[4,1,256]{2,1,0:T(1,128)S(1)} all-gather(f32[1,1,256]{2,1,0:T(1,128)S(1)} %bitcast.51), channel_id=1, replica_groups=mesh['wide'=8,'narrow'=4] {'narrow'}, dimensions={0}, use_global_device_ids=true | all-gather | bytes 5120 | tf_op jit(solution)/shard_map/all_gather | solution.py:88
  89.8 0.3 fusion.69
  90.2 14.0 %all-gather.1 = f32[8,4,256]{2,1,0:T(4,128)S(1)} all-gather(f32[1,4,256]{2,1,0:T(4,128)S(1)} %reshape.87), channel_id=1, replica_groups=mesh['wide'=8,'narrow'=4] {'wide'}, dimensions={0}, use_global_device_ids=true | all-gather | bytes 36864 | tf_op jit(solution)/shard_map/all_gather | solution.py:97
  104.2 0.2 fusion.53
  104.6 0.3 convolution_add_fusion.2
  104.9 0.3 fusion.70
  105.3 14.0 %all-gather.2 = f32[8,4,256]{2,1,0:T(4,128)S(1)} all-gather(f32[1,4,256]{2,1,0:T(4,128)S(1)} %reshape.89), channel_id=1, replica_groups=mesh['wide'=8,'narrow'=4] {'wide'}, dimensions={0}, use_global_device_ids=true | all-gather | bytes 36864 | tf_op jit(solution)/shard_map/all_gather | solution.py:97
  119.4 0.2 fusion.52
  119.8 0.3 convolution_add_fusion.1
  120.1 0.3 fusion.71
  120.5 14.0 %all-gather.3 = f32[8,4,256]{2,1,0:T(4,128)S(1)} all-gather(f32[1,4,256]{2,1,0:T(4,128)S(1)} %reshape.91), channel_id=1, replica_groups=mesh['wide'=8,'narrow'=4] {'wide'}, dimensions={0}, use_global_device_ids=true | all-gather | bytes 36864 | tf_op jit(solution)/shard_map/all_gather | solution.py:97
  134.5 0.2 fusion.51
  134.9 0.3 convolution_add_fusion
  135.2 0.3 fusion.72
  135.6 14.0 %all-gather.4 = f32[8,4,256]{2,1,0:T(4,128)S(1)} all-gather(f32[1,4,256]{2,1,0:T(4,128)S(1)} %reshape.93), channel_id=1, replica_groups=mesh['wide'=8,'narrow'=4] {'wide'}, dimensions={0}, use_global_device_ids=true | all-gather | bytes 36864 | tf_op jit(solution)/shard_map/all_gather | solution.py:97
  149.6 0.3 fusion.2
  150.2 0.2 reshape.83
  150.4 1.8 %convolution_bitcast_fusion = f32[4,32,64]{2,0,1:T(4,128)S(1)} fusion(f32[32,4,256]{2,1,0:T(4,128)S(1)} %reshape.83, f32[32,64,256]{2,1,0:T(8,128)S(1)} %copy-done), kind=kOutput, calls=%fused_computation | convolution fusion | flops 25165824 | bytes 2260992 | tf_op jit(solution)/shard_map/bfm,bam->abf/dot_general | solution.py:114
  152.4 1.3 collective-permute-start.7
  153.7 4.5 %collective-permute-start.8 = (f32[4,1,128]{2,1,0:T(1,128)S(1)}, f32[4,1,128]{2,1,0:T(1,128)S(1)}, u32[]{:S(2)}, u32[]{:S(2)}) collective-permute-start(f32[4,1,128]{2,1,0:T(1,128)S(1)} %get-tuple-element.17), channel_id=1, source_target_pairs={{0,1},{1,2},{2,3},{3,4},{4,5},{5,6},{6,7},{7,8},{8,9},{9,10},{10,1... | collective-permute-start | bytes 6152 | tf_op jit(solution)/shard_map/ppermute | solution.py:24
  158.3 0.7 reshape.81
  159.0 0.5 collective-permute-done.8
  159.7 1.3 collective-permute-start.9
  161.0 4.8 %collective-permute-start.10 = (f32[4,1,128]{2,1,0:T(1,128)S(1)}, f32[4,1,128]{2,1,0:T(1,128)S(1)}, u32[]{:S(2)}, u32[]{:S(2)}) collective-permute-start(f32[4,1,128]{2,1,0:T(1,128)S(1)} %get-tuple-element.11), channel_id=1, source_target_pairs={{0,1},{1,2},{2,3},{3,4},{4,5},{5,6},{6,7},{7,8},{8,9},{9,10},{10,1... | collective-permute-start | bytes 6152 | tf_op jit(solution)/shard_map/ppermute | solution.py:24
  165.9 1.2 collective-permute-done.10
  167.1 0.7 fusion.19
  (65 shorter events, 2.5 us)
Async XLA Ops:
  0.6 33.3 %copy-start = (f32[32,64,256]{2,1,0:T(8,128)S(1)}, f32[32,64,256]{2,1,0:T(8,128)}, u32[]{:S(2)}) copy-start(f32[32,64,256]{2,1,0:T(8,128)} %param.14) | copy-start | bytes 6291460
  0.7 14.8 %collective-permute-start.2 = (f32[4,1,128]{2,1,0:T(1,128)S(1)}, f32[4,1,128]{2,1,0:T(1,128)S(1)}, u32[]{:S(2)}, u32[]{:S(2)}) collective-permute-start(f32[4,1,128]{2,1,0:T(1,128)S(1)} %broadcast.28), channel_id=1, source_target_pairs={{0,1},{1,2},{2,3},{3,4},{4,5},{5,6},{6,7},{7,8},{8,9},{9,10},{10,1... | collective-permute-start | bytes 6152 | tf_op jit(solution)/shard_map/ppermute | solution.py:24
  5.6 9.8 %collective-permute-start.1 = (f32[4,1,128]{2,1,0:T(1,128)S(1)}, f32[4,1,128]{2,1,0:T(1,128)S(1)}, u32[]{:S(2)}, u32[]{:S(2)}) collective-permute-start(f32[4,1,128]{2,1,0:T(1,128)S(1)} %broadcast.28), channel_id=1, source_target_pairs={{1,0},{2,1},{3,2},{4,3},{5,4},{6,5},{7,6},{8,7},{9,8},{10,9},{11,1... | collective-permute-start | bytes 6152 | tf_op jit(solution)/shard_map/ppermute | solution.py:27
  7.6 7.0 %collective-permute-start = (f32[1,128]{1,0:T(1,128)S(1)}, f32[1,128]{1,0:T(1,128)S(1)}, u32[]{:S(2)}, u32[]{:S(2)}) collective-permute-start(f32[1,128]{1,0:T(1,128)S(1)} %slice.138), channel_id=1, source_target_pairs={{0,1},{1,2},{2,3},{3,4},{4,5},{5,6},{6,7},{7,8},{8,9},{9,10},{10,1... | collective-permute-start | bytes 1544 | tf_op jit(solution)/shard_map/ppermute | solution.py:16
  16.4 6.3 %collective-permute-start.3 = (f32[4,1,128]{2,1,0:T(1,128)S(1)}, f32[4,1,128]{2,1,0:T(1,128)S(1)}, u32[]{:S(2)}, u32[]{:S(2)}) collective-permute-start(f32[4,1,128]{2,1,0:T(1,128)S(1)} %get-tuple-element.28), channel_id=1, source_target_pairs={{1,0},{2,1},{3,2},{4,3},{5,4},{6,5},{7,6},{8,7},{9,8},{10,9},{11,1... | collective-permute-start | bytes 6152 | tf_op jit(solution)/shard_map/ppermute | solution.py:27
  17.7 6.2 %collective-permute-start.4 = (f32[4,1,128]{2,1,0:T(1,128)S(1)}, f32[4,1,128]{2,1,0:T(1,128)S(1)}, u32[]{:S(2)}, u32[]{:S(2)}) collective-permute-start(f32[4,1,128]{2,1,0:T(1,128)S(1)} %get-tuple-element.29), channel_id=1, source_target_pairs={{0,1},{1,2},{2,3},{3,4},{4,5},{5,6},{6,7},{7,8},{8,9},{9,10},{10,1... | collective-permute-start | bytes 6152 | tf_op jit(solution)/shard_map/ppermute | solution.py:24
  24.9 6.8 %collective-permute-start.5 = (f32[4,1,128]{2,1,0:T(1,128)S(1)}, f32[4,1,128]{2,1,0:T(1,128)S(1)}, u32[]{:S(2)}, u32[]{:S(2)}) collective-permute-start(f32[4,1,128]{2,1,0:T(1,128)S(1)} %get-tuple-element.22), channel_id=1, source_target_pairs={{1,0},{2,1},{3,2},{4,3},{5,4},{6,5},{7,6},{8,7},{9,8},{10,9},{11,1... | collective-permute-start | bytes 6152 | tf_op jit(solution)/shard_map/ppermute | solution.py:27
  26.2 6.7 %collective-permute-start.6 = (f32[4,1,128]{2,1,0:T(1,128)S(1)}, f32[4,1,128]{2,1,0:T(1,128)S(1)}, u32[]{:S(2)}, u32[]{:S(2)}) collective-permute-start(f32[4,1,128]{2,1,0:T(1,128)S(1)} %get-tuple-element.23), channel_id=1, source_target_pairs={{0,1},{1,2},{2,3},{3,4},{4,5},{5,6},{6,7},{7,8},{8,9},{9,10},{10,1... | collective-permute-start | bytes 6152 | tf_op jit(solution)/shard_map/ppermute | solution.py:24
  32.9 56.9 %copy-start.2 = (f32[4,64,64]{2,1,0:T(8,128)S(1)}, f32[4,64,64]{2,1,0:T(8,128)}, u32[]{:S(2)}) copy-start(f32[4,64,64]{2,1,0:T(8,128)} %param.16) | copy-start | bytes 196612
  33.9 70.7 %copy-start.1 = (f32[4,64,256]{2,1,0:T(8,128)S(1)}, f32[4,64,256]{2,1,0:T(8,128)}, u32[]{:S(2)}) copy-start(f32[4,64,256]{2,1,0:T(8,128)} %param.17) | copy-start | bytes 786436
  149.9 9.6 %copy-start.3 = (f32[4,16,128]{2,1,0:T(8,128)S(1)}, f32[4,16,128]{2,1,0:T(8,128)}, u32[]{:S(2)}) copy-start(f32[4,16,128]{2,1,0:T(8,128)} %param.9) | copy-start | bytes 98308
  149.9 9.6 %copy-start.4 = (f32[16,128]{1,0:T(8,128)S(1)}, f32[16,128]{1,0:T(8,128)}, u32[]{:S(2)}) copy-start(f32[16,128]{1,0:T(8,128)} %param.11) | copy-start | bytes 24580
  149.9 9.6 %copy-start.5 = (f32[16,128]{1,0:T(8,128)S(1)}, f32[16,128]{1,0:T(8,128)}, u32[]{:S(2)}) copy-start(f32[16,128]{1,0:T(8,128)} %param.12) | copy-start | bytes 24580
  152.4 6.6 %collective-permute-start.7 = (f32[4,1,128]{2,1,0:T(1,128)S(1)}, f32[4,1,128]{2,1,0:T(1,128)S(1)}, u32[]{:S(2)}, u32[]{:S(2)}) collective-permute-start(f32[4,1,128]{2,1,0:T(1,128)S(1)} %get-tuple-element.16), channel_id=1, source_target_pairs={{1,0},{2,1},{3,2},{4,3},{5,4},{6,5},{7,6},{8,7},{9,8},{10,9},{11,1... | collective-permute-start | bytes 6152 | tf_op jit(solution)/shard_map/ppermute | solution.py:27
  153.7 5.8 %collective-permute-start.8 = (f32[4,1,128]{2,1,0:T(1,128)S(1)}, f32[4,1,128]{2,1,0:T(1,128)S(1)}, u32[]{:S(2)}, u32[]{:S(2)}) collective-permute-start(f32[4,1,128]{2,1,0:T(1,128)S(1)} %get-tuple-element.17), channel_id=1, source_target_pairs={{0,1},{1,2},{2,3},{3,4},{4,5},{5,6},{6,7},{7,8},{8,9},{9,10},{10,1... | collective-permute-start | bytes 6152 | tf_op jit(solution)/shard_map/ppermute | solution.py:24
  159.7 6.2 %collective-permute-start.9 = (f32[4,1,128]{2,1,0:T(1,128)S(1)}, f32[4,1,128]{2,1,0:T(1,128)S(1)}, u32[]{:S(2)}, u32[]{:S(2)}) collective-permute-start(f32[4,1,128]{2,1,0:T(1,128)S(1)} %get-tuple-element.10), channel_id=1, source_target_pairs={{1,0},{2,1},{3,2},{4,3},{5,4},{6,5},{7,6},{8,7},{9,8},{10,9},{11,1... | collective-permute-start | bytes 6152 | tf_op jit(solution)/shard_map/ppermute | solution.py:27
  161.0 6.1 %collective-permute-start.10 = (f32[4,1,128]{2,1,0:T(1,128)S(1)}, f32[4,1,128]{2,1,0:T(1,128)S(1)}, u32[]{:S(2)}, u32[]{:S(2)}) collective-permute-start(f32[4,1,128]{2,1,0:T(1,128)S(1)} %get-tuple-element.11), channel_id=1, source_target_pairs={{0,1},{1,2},{2,3},{3,4},{4,5},{5,6},{6,7},{7,8},{8,9},{9,10},{10,1... | collective-permute-start | bytes 6152 | tf_op jit(solution)/shard_map/ppermute | solution.py:24
where the time goes:
time: 171 us; the launch traced here: 168 us
  blocking collectives  110 us (64%)
  starting transfers between devices  35.7 us (21%)
  local copies, waits for them, and re-layouts  6.62 us (4%)
  matrix products  6.21 us (4%)
  other arithmetic  4.28 us (3%)
  waiting for transfers between devices  4.19 us (2%)
    all_gather x4, blocking collectives, spread(): lax.all_gather(adjoint_vector.reshape(owned, adjoints * block_size), 'wid...  56.1 us
    unnamed x1, blocking collectives  45 us
    ppermute x5, starting transfers between devices, with_halo(): lax.ppermute(lax.slice_in_dim(block, block.shape[dim] - width, None, axis...  24.7 us
    all_gather x1, blocking collectives, body(): owned_rhs = lax.all_gather(portion, 'narrow', axis=0, tiled=True)  8.82 us
    ppermute x5, starting transfers between devices, with_halo(): lax.ppermute(lax.slice_in_dim(block, 0, width, axis=dim), axis, backward)  6.43 us
    ppermute x1, starting transfers between devices, shifted(): lax.ppermute(value, axis, [(source, source + steps) for source in range(f...  4.53 us
    ppermute x5, waiting for transfers between devices, with_halo(): lax.ppermute(lax.slice_in_dim(block, block.shape[dim] - width, None, axis...  4.18 us
  transfers between devices with their start and end apart: 11, of which 4 were waited for; matrix products, arithmetic and copies ran while one was open for 3% of the time, Pallas kernels for 0%

commit v1 on v0

v1 whole, which is shorter than its diff:
```python
import functools

import jax
import jax.numpy as jnp
from jax import lax
from jax.experimental import pallas as pl
from jax.experimental.pallas import tpu as pltpu
from jax.sharding import PartitionSpec as P

SWEEPS = 2
COARSE_SWEEPS = 3
relax_weight = 0.7

BOTH = ("wide", "narrow")
HALO = 3
FIELD = 24
PIECE = 88
F32 = jnp.float32
BF16 = jnp.bfloat16


def swap(value, axis, bits):
    size = lax.axis_size(axis)
    return lax.ppermute(value, axis, [(i, i ^ bits) for i in range(size)])


def pair_swaps(to_first, to_second):
    count = lax.axis_size(BOTH)
    first = lax.ppermute(to_first, BOTH, [(i, i ^ 1) for i in range(count)])
    odd = [(i, i + 1) for i in range(1, count - 1, 2)] + [(count - 1, 0)]
    second = lax.ppermute(to_second, BOTH, odd + [(target, source) for source, target in odd])
    return first, second


def groups_of(size):
    rounds, base = [], 1
    while base < size:
        span = 4 if base * 4 <= size else 2
        rounds.append([base * k for k in range(1, span)])
        base *= span
    return rounds


def sum_all(value):
    value = value + swap(value, "wide", 1)
    for masks in groups_of(lax.axis_size("narrow")):
        value = sum([swap(value, "narrow", k) for k in masks], value)
    for masks in groups_of(lax.axis_size("wide") // 2):
        value = sum([swap(value, "wide", 2 * k) for k in masks], value)
    return value


def place():
    wide, narrow = lax.axis_index("wide"), lax.axis_index("narrow")
    line = wide * lax.axis_size("narrow") + narrow
    count = lax.axis_size("wide") * lax.axis_size("narrow")
    return line, count


def lanes(shape):
    return lax.broadcasted_iota(jnp.int32, shape, len(shape) - 1)


def rows(shape):
    return lax.broadcasted_iota(jnp.int32, shape, len(shape) - 2)


def split(value):
    high = value.astype(BF16)
    return high, (value - high.astype(F32)).astype(BF16)


def dot(left, right):
    return lax.dot_general(left, right, (((1,), (0,)), ((), ())), preferred_element_type=F32)


def dot_t(left, right):
    return lax.dot_general(left, right, (((1,), (1,)), ((), ())), preferred_element_type=F32)


def half_turn(value):
    return pltpu.roll(value, 64, 1)


def edges_kernel(r, b, e, n, first, second):
    grid_rows = b.shape[0]
    line, _ = place()
    even = lax.rem(line, 2) == 0

    def message(start, north_start):
        parts = [r[a, start:start + HALO, :] for a in range(r.shape[0])]
        parts += [b[start:start + HALO, :], e[start:start + HALO, :]]
        parts += [n[north_start:north_start + HALO + 1, :], jnp.zeros((2, b.shape[1]), F32)]
        return parts

    top = message(0, 0)
    bottom = message(grid_rows - HALO, grid_rows - HALO - 1)
    at = 0
    for low, high in zip(top, bottom):
        size = low.shape[0]
        first[at:at + size, :] = jnp.where(even, high, low)
        second[at:at + size, :] = jnp.where(even, low, high)
        at += size


def pack_kernel(owned, links, coupling, inverses, block, own):
    q = lax.rem(lax.axis_index("narrow"), owned)
    lane = lanes((8, 256))
    for j_rel in range(owned):
        j = jnp.bitwise_xor(q, j_rel)
        base = j_rel * PIECE
        matrix = coupling[j]
        inverse = inverses[j]
        packed = jnp.concatenate([inverse[16 * t:16 * t + 16, :] for t in range(4)], axis=1)
        tail = jnp.zeros((8, 256), F32)
        for l in range(links.shape[1]):
            tail = jnp.where(lane == l, links[j, l].astype(F32), tail)
        block[base:base + 64, :] = matrix
        block[base + 64:base + 80, :] = packed
        block[base + 80:base + 88, :] = tail
        if j_rel == 0:
            own[0:64, :] = matrix
            own[64:80, :] = packed
            own[80:88, :] = tail


class Fine:
    def __init__(self, r, b, e, n, from_first, from_second, rx, bx, ex, nx, field):
        line, count = place()
        even = lax.rem(line, 2) == 0
        low_ok, high_ok = line > 0, line < count - 1
        one, two = from_first[...], from_second[...]
        low = jnp.where(low_ok, jnp.where(even, two, one), 0.0)
        high = jnp.where(high_ok, jnp.where(even, one, two), 0.0)
        self.even, self.low_ok, self.high_ok = even, low_ok, high_ok
        self.adjoints, self.grid_rows, width = r.shape
        top = HALO + self.grid_rows
        zeros = jnp.zeros((8, width), F32)
        for a in range(self.adjoints):
            rx[a, 16:24, :] = zeros
            rx[a, 0:HALO, :] = low[3 * a:3 * a + 3]
            rx[a, HALO:top, :] = r[a]
            rx[a, top:top + HALO, :] = high[3 * a:3 * a + 3]
            field[a, 0:8, :] = zeros
            field[a, 32:40, :] = zeros
        bx[16:24, :] = zeros
        bx[0:HALO, :] = low[12:15]
        bx[HALO:top, :] = b[...]
        bx[top:top + HALO, :] = high[12:15]
        ex[16:24, :] = zeros
        ex[0:HALO, :] = low[15:18]
        ex[HALO:top, :] = e[...]
        ex[top:top + HALO, :] = high[15:18]
        nx[16:24, :] = zeros
        nx[24:32, :] = zeros
        nx[0:HALO + 1, :] = low[18:22]
        nx[HALO + 1:top + 1, :] = n[...]
        nx[top + 1:top + 1 + HALO, :] = high[18:21]
        self.r = rx[...]
        self.east = ex[...]
        self.north = nx[1:1 + FIELD, :]
        self.south = nx[0:FIELD, :]
        self.west = pltpu.roll(self.east, 1, 1)
        self.diagonal = bx[...] + self.east + self.west + self.north + self.south
        t = rows((FIELD, width))
        valid = ((t >= HALO) | low_ok) & ((t < top) | high_ok) & (t < top + HALO)
        self.scale = jnp.where(valid, relax_weight / jnp.where(valid, self.diagonal, 1.0), 0.0)
        self.field = field
        self.width = width

    def apply(self, x):
        self.field[:, 8:32, :] = x
        above = self.field[:, 7:31, :]
        below = self.field[:, 9:33, :]
        east = pltpu.roll(x, self.width - 1, 2)
        west = pltpu.roll(x, 1, 2)
        return self.diagonal * x - self.north * below - self.south * above - self.east * east - self.west * west

    def sweep(self, x):
        return x + self.scale * (self.r - self.apply(x))


def fine_scratch(adjoints, width):
    return [
        pltpu.VMEM((adjoints, FIELD, width), F32),
        pltpu.VMEM((FIELD, width), F32),
        pltpu.VMEM((FIELD, width), F32),
        pltpu.VMEM((32, width), F32),
        pltpu.VMEM((adjoints, 40, width), F32),
    ]


def restrict_kernel(coarse_rows, r, b, e, n, from_first, from_second, basis, sup, out, x_out,
                    rx, bx, ex, nx, field, by_row, contrib):
    fine = Fine(r, b, e, n, from_first, from_second, rx, bx, ex, nx, field)
    x = fine.scale * fine.r
    for step in range(SWEEPS - 1):
        x = fine.sweep(x)
    resid = fine.r - fine.apply(x)
    for a in range(fine.adjoints):
        x_out[a] = field[a, 8 + HALO:8 + HALO + fine.grid_rows, :]
    field[:, 8:32, :] = resid
    for a in range(fine.adjoints):
        by_row[pl.ds(a, fine.grid_rows, stride=4), :] = field[a, 8 + HALO:8 + HALO + fine.grid_rows, :]
    left = lanes((8, 128)) < 64
    upper = rows((8, 128)) < 4
    for g in range(fine.grid_rows // 2):
        z = by_row[8 * g:8 * g + 8, :]
        parts = []
        for here in (left, ~left):
            held = jnp.where(here, z, 0.0)
            parts.append(jnp.concatenate([jnp.where(upper, held, 0.0), jnp.where(upper, 0.0, held)], axis=1))
        high, low = split(jnp.concatenate(parts, axis=0))
        w_high, w_low = split(basis[256 * g:256 * g + 256, :])
        both = dot(jnp.concatenate([high, low], axis=0), w_high)
        contrib[16 * g:16 * g + 16, :] = both[0:16] + both[16:32] + dot(high, w_low)
    c_high, c_low = split(contrib[...])
    weights = jnp.concatenate([
        jnp.concatenate([c_high[:, 0:128], c_low[:, 0:128]], axis=1),
        jnp.concatenate([c_high[:, 128:256], c_low[:, 128:256]], axis=1)], axis=0)
    size = 4 * coarse_rows
    at = rows((size, 128))
    hot = [jnp.where(at == sup[k:k + 1, :], 1.0, 0.0).astype(BF16) for k in range(4)]
    hots = jnp.concatenate([
        jnp.concatenate([hot[0], hot[2]], axis=1), jnp.concatenate([hot[1], hot[3]], axis=1)], axis=0)
    total = dot(hots, weights)
    total = total[:, 0:128] + total[:, 128:256]
    here = lanes((size, 128)) < 64
    even = jnp.where(here, total[0:size], 0.0)
    odd = jnp.where(here, 0.0, total[size:2 * size])
    mid = size // 2
    out[...] = even[0:mid] + half_turn(odd[0:mid]) + half_turn(even[mid:size]) + odd[mid:size]


def coarse_kernel(owned, coarse_rows, zs, refs):
    refs = list(refs)

    def take(count):
        got = refs[:count]
        del refs[:count]
        return got

    (rhs_ref,) = take(1)
    pieces = take(2 * (1 + owned))
    basis, sup, x_ref = take(3)
    y_ref, coarse_ref, first, second = take(4)
    w_high, w_low, w_inv, link_rows, hots, product, u_ref, by_row = refs
    size = 4 * coarse_rows
    wide, narrow = lax.axis_index("wide"), lax.axis_index("narrow")
    q = lax.rem(narrow, owned)
    mine = wide * owned + q

    lane16 = lanes((16, 128)) < 64
    for z_rel in range(zs):
        for c_rel in range(2):
            for j_rel in range(owned):
                i = (z_rel * 2 + c_rel) * owned + j_rel
                if z_rel == 0:
                    piece, base = pieces[c_rel * (1 + owned)], j_rel * PIECE
                else:
                    piece, base = pieces[c_rel * (1 + owned) + 1 + j_rel], (z_rel - 1) * PIECE
                high, low = split(piece[base:base + 64, :])
                w_high[64 * i:64 * i + 64, :] = high
                w_low[64 * i:64 * i + 64, :] = low
                quarters = []
                for half in range(2):
                    packed = piece[base + 64:base + 80, 128 * half:128 * half + 128]
                    turned = half_turn(packed)
                    quarters += [jnp.where(lane16, packed, turned), jnp.where(lane16, turned, packed)]
                high, low = split(jnp.concatenate(quarters, axis=0))
                w_inv[64 * i:64 * i + 64, 0:128] = high
                w_inv[64 * i:64 * i + 64, 128:256] = low
                link_rows[4 * i:4 * i + 4, :] = piece[base + 80:base + 84, 0:128]

    lane = lanes((size, size))
    a_col = jnp.bitwise_and(rows((size, 1)), 3)
    for l in range(4):
        target = jnp.bitwise_xor(link_rows[:, l:l + 1].astype(jnp.int32), mine) * 4 + a_col
        hots[size * l:size * l + size, :] = jnp.where(lane == target, 1.0, 0.0).astype(BF16)

    here = lanes((size, 128)) < 64
    packed = rhs_ref[...]
    turned = half_turn(packed)
    here_mid = here[0:size // 2]
    rhs = jnp.concatenate([jnp.where(here_mid, packed, turned), jnp.where(here_mid, turned, packed)], axis=0)

    def hi_lo(value):
        high, low = split(value)
        return jnp.concatenate([high, low], axis=1)

    source = jnp.bitwise_xor(rows((size, 1)), mine * 4)
    order = jnp.where(lane == source, 1.0, 0.0).astype(BF16)
    rhs = dot(order, hi_lo(rhs))
    rhs = rhs[:, 0:128] + rhs[:, 128:256]

    own_block = jnp.bitwise_and(lax.shift_right_logical(rows((size, 256)), 2), 3) == lax.shift_right_logical(
        lanes((size, 256)), 6)

    def fold():
        value = jnp.where(own_block, product[...], 0.0)
        value = value[:, 0:128] + value[:, 128:256]
        return value + half_turn(value)

    def apply_inverse(value):
        high, low = split(value)
        mixed = jnp.where(here, high.astype(F32), low.astype(F32)).astype(BF16)
        mixed = jnp.concatenate([mixed, mixed], axis=1)
        for g in range(coarse_rows // 4):
            product[16 * g:16 * g + 16, :] = dot_t(mixed[16 * g:16 * g + 16], w_inv[256 * g:256 * g + 256, :])
        return fold()

    def pick(got, step):
        sel = lanes((step, 128)) < 64
        high = [jnp.where(sel, got[step * k:step * k + step, 0:128], got[step * k + step:step * k + 2 * step, 0:128])
                for k in (0, 2)]
        low = [jnp.where(sel, got[step * k:step * k + step, 128:256],
                         got[step * k + step:step * k + 2 * step, 128:256]) for k in (0, 2)]
        return jnp.concatenate(high, axis=1).astype(BF16), jnp.concatenate(low, axis=1).astype(BF16)

    u = apply_inverse(rhs)
    for step in range(COARSE_SWEEPS):
        high, low = pick(dot(hots[...], hi_lo(u)), size)
        for g in range(coarse_rows // 4):
            near = slice(16 * g, 16 * g + 16)
            block = slice(256 * g, 256 * g + 256)
            both = dot_t(jnp.concatenate([high[near], low[near]], axis=0), w_high[block, :])
            product[near, :] = both[0:16] + both[16:32] + dot_t(high[near], w_low[block, :])
        u = apply_inverse(rhs + fold())

    u_ref[...] = u[0:4 * owned]
    here1 = lanes((1, 128)) < 64
    for j in range(owned):
        got = u_ref[pl.ds(jnp.bitwise_xor(q, j) * 4, 4), :]
        coarse_ref[j:j + 1, 0:128] = jnp.where(here1, got[0:1], got[1:2])
        coarse_ref[j:j + 1, 128:256] = jnp.where(here1, got[2:3], got[3:4])

    blocks4 = sup.shape[0]
    lane_s = lanes((blocks4, size))
    sup_hots = jnp.concatenate(
        [jnp.where(lane_s == sup[:, k:k + 1], 1.0, 0.0).astype(BF16) for k in range(4)], axis=0)
    high, low = pick(dot(sup_hots, hi_lo(u)), blocks4)
    left = lanes((8, 128)) < 64
    upper = rows((8, 128)) < 4
    for g in range(blocks4 // 16):
        b_high, b_low = split(basis[256 * g:256 * g + 256, :])
        near = slice(16 * g, 16 * g + 16)
        both = dot_t(jnp.concatenate([high[near], low[near]], axis=0), b_high)
        got = both[0:16] + both[16:32] + dot_t(high[near], b_low)
        halves = [jnp.where(upper, got[8 * h:8 * h + 8, 0:128], got[8 * h:8 * h + 8, 128:256]) for h in range(2)]
        by_row[8 * g:8 * g + 8, :] = jnp.where(left, halves[0], halves[1])
    line, _ = place()
    even = lax.rem(line, 2) == 0
    adjoints, grid_rows, _ = x_ref.shape
    for a in range(adjoints):
        y = x_ref[a] + by_row[pl.ds(a, grid_rows, stride=4), :]
        y_ref[a] = y
        top, bottom = y[0:2], y[grid_rows - 2:grid_rows]
        first[2 * a:2 * a + 2, :] = jnp.where(even, bottom, top)
        second[2 * a:2 * a + 2, :] = jnp.where(even, top, bottom)


def post_kernel(r, b, e, n, from_first, from_second, y_ref, y_first, y_second, out, rx, bx, ex, nx, field, yx):
    fine = Fine(r, b, e, n, from_first, from_second, rx, bx, ex, nx, field)
    one, two = y_first[...], y_second[...]
    low = jnp.where(fine.low_ok, jnp.where(fine.even, two, one), 0.0)
    high = jnp.where(fine.high_ok, jnp.where(fine.even, one, two), 0.0)
    top = HALO + fine.grid_rows
    for a in range(fine.adjoints):
        yx[a, 0:8, :] = jnp.zeros((8, fine.width), F32)
        yx[a, 16:24, :] = jnp.zeros((8, fine.width), F32)
        yx[a, HALO - 2:HALO, :] = low[2 * a:2 * a + 2]
        yx[a, HALO:top, :] = y_ref[a]
        yx[a, top:top + 2, :] = high[2 * a:2 * a + 2]
    x = yx[...]
    for step in range(SWEEPS):
        x = fine.sweep(x)
    field[:, 8:32, :] = x
    for a in range(fine.adjoints):
        out[a] = field[a, 8 + HALO:8 + HALO + fine.grid_rows, :]


def shape(*dims):
    return jax.ShapeDtypeStruct(dims, F32)


def params(mebibytes):
    return pltpu.CompilerParams(vmem_limit_bytes=mebibytes * 2 ** 20)


def body(right_sides, brinkman, east_faces, north_faces, support, basis, links, coarse_block_inverses, coarse_coupling):
    adjoints, grid_rows, width = right_sides.shape
    blocks, block_size, _ = basis.shape
    owned = coarse_block_inverses.shape[0]
    coarse_rows = owned * lax.axis_size("wide")
    zs = lax.axis_size("wide") // 2
    size = 4 * coarse_rows
    basis = basis.reshape(blocks * block_size, -1)

    message = shape(24, width)
    to_first, to_second = pl.pallas_call(
        edges_kernel, out_shape=(message, message), compiler_params=params(16), name="edges",
    )(right_sides, brinkman, east_faces, north_faces)
    from_first, from_second = pair_swaps(to_first, to_second)

    in_vmem = pl.BlockSpec(memory_space=pltpu.VMEM)
    block, own = pl.pallas_call(
        functools.partial(pack_kernel, owned),
        out_shape=(shape(owned * PIECE, 256), shape(PIECE, 256)),
        in_specs=[pl.BlockSpec(memory_space=pltpu.SMEM), in_vmem, in_vmem],
        compiler_params=params(16), name="pack",
    )(links, coarse_coupling, coarse_block_inverses)

    fetched = jnp.concatenate([swap(own, "wide", 2 * k) for k in range(1, zs)], axis=0)
    pieces = [block, fetched] + [swap(fetched, "narrow", k) for k in range(1, owned)]
    pieces = pieces + [swap(piece, "wide", 1) for piece in pieces]

    mine = lax.axis_index("wide") * owned + lax.rem(lax.axis_index("narrow"), owned)
    by_k = support.reshape(blocks // 4, 2, 2, 4).transpose(3, 0, 2, 1).reshape(4, blocks, 1)
    a_row = jnp.arange(adjoints, dtype=jnp.int32)
    sup = (by_k * 4 + a_row).reshape(4, blocks * adjoints)
    sup_rel = (jnp.bitwise_xor(by_k, mine) * 4 + a_row).reshape(4, blocks * adjoints).T

    rhs, x = pl.pallas_call(
        functools.partial(restrict_kernel, coarse_rows),
        out_shape=(shape(size // 2, 128), shape(adjoints, grid_rows, width)),
        scratch_shapes=fine_scratch(adjoints, width) + [
            pltpu.VMEM((4 * grid_rows, width), F32), pltpu.VMEM((4 * blocks, 256), F32)],
        compiler_params=params(24), name="restrict",
    )(right_sides, brinkman, east_faces, north_faces, from_first, from_second, basis, sup)

    rhs = sum_all(rhs)

    def coarse_body(*refs):
        coarse_kernel(owned, coarse_rows, zs, refs)

    y, coarse, y_first, y_second = pl.pallas_call(
        coarse_body,
        out_shape=(shape(adjoints, grid_rows, width), shape(owned, 256), shape(8, width), shape(8, width)),
        scratch_shapes=[
            pltpu.VMEM((64 * coarse_rows, 256), BF16), pltpu.VMEM((64 * coarse_rows, 256), BF16),
            pltpu.VMEM((64 * coarse_rows, 256), BF16), pltpu.VMEM((size, 128), F32),
            pltpu.VMEM((4 * size, size), BF16), pltpu.VMEM((size, 256), F32),
            pltpu.VMEM((4 * owned, 128), F32), pltpu.VMEM((4 * grid_rows, width), F32)],
        compiler_params=params(min(56, 16 + coarse_rows // 2)), name="coarse",
    )(rhs, *pieces, basis, sup_rel, x)

    y_first, y_second = pair_swaps(y_first, y_second)
    solution_field = pl.pallas_call(
        post_kernel,
        out_shape=shape(adjoints, grid_rows, width),
        scratch_shapes=fine_scratch(adjoints, width) + [pltpu.VMEM((adjoints, FIELD, width), F32)],
        compiler_params=params(16), name="post",
    )(right_sides, brinkman, east_faces, north_faces, from_first, from_second, y, y_first, y_second)
    return solution_field, coarse


def solution(mesh):
    return jax.shard_map(
        body,
        mesh=mesh,
        in_specs=(
            P(None, ("wide", "narrow"), None),
            P(("wide", "narrow"), None),
            P(("wide", "narrow"), None),
            P(("wide", "narrow"), None),
            P(("wide", "narrow"), None),
            P(("wide", "narrow"), None, None),
            P("wide", None),
            P("wide", None, None),
            P("wide", None, None),
        ),
        out_specs=(P(None, ("wide", "narrow"), None), P("wide", None)),
        check_vma=False,
    )
```

time: 171 us -> 67.4 us (0.39); the launches traced: 168 us -> 66.8 us
  blocking collectives: 110 us -> 0 us
  waiting for transfers between devices: 4.19 us -> 25.2 us
  starting transfers between devices: 35.7 us -> 21.7 us
  Pallas kernels: 0 us -> 8.03 us
  matrix products: 6.21 us -> 0 us
  local copies, waits for them, and re-layouts: 6.62 us -> 10.3 us
  other arithmetic: 4.28 us -> 0.8 us
    all_gather x5 -> x0, blocking collectives: 64.9 us -> none  [the longest x4 56.1 us: spread(): lax.all_gather(adjoint_vector.reshape(owned, adjoints * block_size), 'wid...]
    unnamed x1 -> x0, blocking collectives: 45 us -> none
    ppermute x11 -> x22, waiting for transfers between devices: 4.19 us -> 25.2 us  [the longest x18 20.4 us: swap(): return lax.ppermute(value, axis, [(i, i ^ bits) for i in range(size)])]
    ppermute x11 -> x22, starting transfers between devices: 35.7 us -> 21.7 us  [the longest x18 13 us: swap(): return lax.ppermute(value, axis, [(i, i ^ bits) for i in range(size)])]
    unnamed x23 -> x36, local copies, waits for them, and re-layouts: 1.31 us -> 9.86 us
    pallas_call x0 -> x5, Pallas kernels: none -> 8.03 us  [the longest x1 5.48 us: body(): pl.pallas_call(coarse_body, out_shape=(shape(adjoints, grid_rows, width),...]
    dot_general x14 -> x0, matrix products: 6.21 us -> none  [the longest x1 1.83 us: body(): jnp.einsum('bfm,bam->abf', basis, chosen, precision=top_precision)]
    reshape x18 -> x0, local copies, waits for them, and re-layouts: 2.27 us -> none  [the longest x1 0.68 us: spread(): adjoint_vector.reshape(owned, adjoints * block_size)]
  transfers between devices with their start and end apart: 11 -> 22, of which waited for: 4 -> 10; matrix products, arithmetic and copies ran while one was open for 3% -> 2% of each run, Pallas kernels for 0% -> 3%
where the time goes in v1:
time: 67.4 us; the launch traced here: 66.8 us
  waiting for transfers between devices  25.2 us (37%)
  starting transfers between devices  21.7 us (32%)
  local copies, waits for them, and re-layouts  10.3 us (15%)
  Pallas kernels  8.03 us (12%)
  between operations  0.82 us (1%)
  other arithmetic  0.8 us (1%)
    ppermute x18, waiting for transfers between devices, swap(): return lax.ppermute(value, axis, [(i, i ^ bits) for i in range(size)])  20.4 us
    ppermute x18, starting transfers between devices, swap(): return lax.ppermute(value, axis, [(i, i ^ bits) for i in range(size)])  13 us
    unnamed x36, local copies, waits for them, and re-layouts  9.86 us
    ppermute x2, starting transfers between devices, pair_swaps(): lax.ppermute(to_second, BOTH, odd + [(target, source) for source, target...  5.51 us
    pallas_call x1, Pallas kernels, body(): pl.pallas_call(coarse_body, out_shape=(shape(adjoints, grid_rows, width),...  5.48 us
    ppermute x2, waiting for transfers between devices, pair_swaps(): lax.ppermute(to_second, BOTH, odd + [(target, source) for source, target...  3.17 us
    ppermute x2, starting transfers between devices, pair_swaps(): first = lax.ppermute(to_first, BOTH, [(i, i ^ 1) for i in range(count)])  3.15 us
    ppermute x2, waiting for transfers between devices, pair_swaps(): first = lax.ppermute(to_first, BOTH, [(i, i ^ 1) for i in range(count)])  1.63 us
  transfers between devices with their start and end apart: 22, of which 10 were waited for; matrix products, arithmetic and copies ran while one was open for 2% of the time, Pallas kernels for 3%

profile of v1, /device:TPU:0, one launch (start us, length us, event | category | flops | bytes accessed | tf_op | source)
XLA Modules:
  0.0 66.8 jit_solution(11416587203934657466)
XLA Ops:
  0.6 0.7 %copy-done.2 = f32[4,16,128]{2,1,0:T(8,128)S(1)} copy-done((f32[4,16,128]{2,1,0:T(8,128)S(1)}, f32[4,16,128]{2,1,0:T(8,128)}, u32[]{:S(2)}) %copy-start.2) | copy-done | bytes 32792
  1.4 0.7 %copy-done.7 = f32[16,128]{1,0:T(8,128)S(1)} copy-done((f32[16,128]{1,0:T(8,128)S(1)}, f32[16,128]{1,0:T(8,128)}, u32[]{:S(2)}) %copy-start.7) | copy-done | bytes 8216
  2.1 0.7 %copy-done.10 = f32[16,128]{1,0:T(8,128)S(1)} copy-done((f32[16,128]{1,0:T(8,128)S(1)}, f32[16,128]{1,0:T(8,128)}, u32[]{:S(2)}) %copy-start.10) | copy-done | bytes 8216
  2.8 0.7 %copy-done.13 = f32[16,128]{1,0:T(8,128)S(1)} copy-done((f32[16,128]{1,0:T(8,128)S(1)}, f32[16,128]{1,0:T(8,128)}, u32[]{:S(2)}) %copy-start.13) | copy-done | bytes 8216
  3.5 3.0 %collective-permute-start = (f32[24,128]{1,0:T(8,128)S(1)}, f32[24,128]{1,0:T(8,128)S(1)}, u32[]{:S(2)}, u32[]{:S(2)}) collective-permute-start(f32[24,128]{1,0:T(8,128)S(1)} %get-tuple-element.12), channel_id=1, source_target_pairs={{0,1},{1,0},{2,3},{3,2},{4,5},{5,4},{6,7},{7,6},{8,9},{9,8},{10,11... | collective-permute-start | bytes 36872 | tf_op jit(solution)/shard_map/ppermute | solution.py:29
  6.5 3.7 %collective-permute-start.1 = (f32[24,128]{1,0:T(8,128)S(1)}, f32[24,128]{1,0:T(8,128)S(1)}, u32[]{:S(2)}, u32[]{:S(2)}) collective-permute-start(f32[24,128]{1,0:T(8,128)S(1)} %get-tuple-element.13), channel_id=1, source_target_pairs={{1,2},{3,4},{5,6},{7,8},{9,10},{11,12},{13,14},{15,16},{17,18},{19... | collective-permute-start | bytes 36872 | tf_op jit(solution)/shard_map/ppermute | solution.py:31
  10.2 0.9 %copy-done.5 = f32[4,64,256]{2,1,0:T(8,128)S(1)} copy-done((f32[4,64,256]{2,1,0:T(8,128)S(1)}, f32[4,64,256]{2,1,0:T(8,128)}, u32[]{:S(2)}) %copy-start.5) | copy-done | bytes 262168
  11.1 0.9 %copy-done.6 = f32[4,64,64]{2,1,0:T(8,128)S(1)} copy-done((f32[4,64,64]{2,1,0:T(8,128)S(1)}, f32[4,64,64]{2,1,0:T(8,128)}, u32[]{:S(2)}) %copy-start.6) | copy-done | bytes 65560
  12.0 0.7 %copy-done.16 = s32[4,4]{1,0:T(4,128)S(1)} copy-done((s32[4,4]{1,0:T(4,128)S(1)}, s32[4,4]{1,0:T(4,128)}, u32[]{:S(2)}) %copy-start.16) | copy-done | bytes 88
  12.7 0.7 %pack.1 = (f32[352,256]{1,0:T(8,128)S(1)}, f32[88,256]{1,0:T(8,128)S(1)}) custom-call(s32[4,4]{1,0:T(4,128)S(1)} %copy-done.16, f32[4,64,256]{2,1,0:T(8,128)S(1)} %copy-done.5, f32[4,64,64]{2,1,0:T(8,128)S(1)} %copy-done.6), custom_call_target="tpu_custom_call" | custom-call | tf_op jit(solution)/shard_map/pack/pallas_call | solution.py:406
  13.4 0.1 collective-permute-start.9
  13.5 0.7 %xor_multiply_fusion = (s32[32,4]{0,1:T(4,128)S(1)}, s32[32,4]{0,1:T(4,128)S(1)}) fusion(s32[32,4]{0,1:T(4,128)} %param.13, s32[]{:T(128)S(6)} %add.77), kind=kLoop, calls=%fused_computation.7 | loop fusion | flops 384 | bytes 1540 | tf_op jit(solution)/shard_map/mul | solution.py:421
  14.2 0.1 copy.19
  14.3 0.1 copy.16
  14.4 0.1 add.67
  14.5 0.1 add_bitcast_fusion
  14.7 1.6 %copy-done = f32[32,64,256]{2,1,0:T(8,128)S(1)} copy-done((f32[32,64,256]{2,1,0:T(8,128)S(1)}, f32[32,64,256]{2,1,0:T(8,128)}, u32[]{:S(2)}) %copy-start) | copy-done | bytes 2097176
  16.3 0.8 %copy-done.3 = f32[4,16,128]{2,1,0:T(8,128)S(1)} copy-done((f32[4,16,128]{2,1,0:T(8,128)S(1)}, f32[4,16,128]{2,1,0:T(8,128)}, u32[]{:S(2)}) %copy-start.3) | copy-done | bytes 32792
  17.1 0.7 %copy-done.8 = f32[16,128]{1,0:T(8,128)S(1)} copy-done((f32[16,128]{1,0:T(8,128)S(1)}, f32[16,128]{1,0:T(8,128)}, u32[]{:S(2)}) %copy-start.8) | copy-done | bytes 8216
  17.8 0.7 %copy-done.11 = f32[16,128]{1,0:T(8,128)S(1)} copy-done((f32[16,128]{1,0:T(8,128)S(1)}, f32[16,128]{1,0:T(8,128)}, u32[]{:S(2)}) %copy-start.11) | copy-done | bytes 8216
  18.5 0.7 %copy-done.14 = f32[16,128]{1,0:T(8,128)S(1)} copy-done((f32[16,128]{1,0:T(8,128)S(1)}, f32[16,128]{1,0:T(8,128)}, u32[]{:S(2)}) %copy-start.14) | copy-done | bytes 8216
  19.2 1.0 %restrict.1 = (f32[64,128]{1,0:T(8,128)S(1)}, f32[4,16,128]{2,1,0:T(8,128)S(1)}) custom-call(f32[4,16,128]{2,1,0:T(8,128)S(1)} %copy-done.3, f32[16,128]{1,0:T(8,128)S(1)} %copy-done.8, f32[16,128]{1,0:T(8,128)S(1)} %copy-done.11, f32[16,128]{1,0:T(8,128)S(1)} %copy-done.14, f32[24,128]{1,0:T(8,128)S(1)} %collective-permute-done.from_first, ...), custom_call_target="tpu_custom_call" | custom-call | tf_op jit(solution)/shard_map/restrict/pallas_call | solution.py:423
  20.2 0.1 collective-permute-start.2
  20.3 1.7 %collective-permute-start.11 = (f32[88,256]{1,0:T(8,128)S(1)}, f32[88,256]{1,0:T(8,128)S(1)}, u32[]{:S(2)}, u32[]{:S(2)}) collective-permute-start(f32[88,256]{1,0:T(8,128)S(1)} %get-tuple-element.16), channel_id=1, source_target_pairs={{0,24},{4,28},{8,16},{12,20},{16,8},{20,12},{24,0},{28,4},{1,25},{... | collective-permute-start | bytes 270344 | tf_op jit(solution)/shard_map/ppermute | solution.py:24
  21.9 1.9 %collective-permute-start.10 = (f32[88,256]{1,0:T(8,128)S(1)}, f32[88,256]{1,0:T(8,128)S(1)}, u32[]{:S(2)}, u32[]{:S(2)}) collective-permute-start(f32[88,256]{1,0:T(8,128)S(1)} %get-tuple-element.16), channel_id=1, source_target_pairs={{0,16},{4,20},{8,24},{12,28},{16,0},{20,4},{24,8},{28,12},{1,17},{... | collective-permute-start | bytes 270344 | tf_op jit(solution)/shard_map/ppermute | solution.py:24
  23.8 0.6 collective-permute-start.5
  24.4 0.9 %collective-permute-start.4 = (f32[64,128]{1,0:T(8,128)S(1)}, f32[64,128]{1,0:T(8,128)S(1)}, u32[]{:S(2)}, u32[]{:S(2)}) collective-permute-start(f32[64,128]{1,0:T(8,128)S(1)} %add.70), channel_id=1, source_target_pairs={{0,2},{1,3},{2,0},{3,1},{4,6},{5,7},{6,4},{7,5},{8,10},{9,11},{10,... | collective-permute-start | bytes 98312 | tf_op jit(solution)/shard_map/ppermute | solution.py:24
  25.4 2.0 %collective-permute-start.3 = (f32[64,128]{1,0:T(8,128)S(1)}, f32[64,128]{1,0:T(8,128)S(1)}, u32[]{:S(2)}, u32[]{:S(2)}) collective-permute-start(f32[64,128]{1,0:T(8,128)S(1)} %add.70), channel_id=1, source_target_pairs={{0,1},{1,0},{2,3},{3,2},{4,5},{5,4},{6,7},{7,6},{8,9},{9,8},{10,11... | collective-permute-start | bytes 98312 | tf_op jit(solution)/shard_map/ppermute | solution.py:24
  27.4 5.2 %collective-permute-done.10 = f32[88,256]{1,0:T(8,128)S(1)} collective-permute-done((f32[88,256]{1,0:T(8,128)S(1)}, f32[88,256]{1,0:T(8,128)S(1)}, u32[]{:S(2)}, u32[]{:S(2)}) %collective-permute-start.10) | collective-permute-done | bytes 90144 | tf_op jit(solution)/shard_map/ppermute | solution.py:24
  32.6 0.1 collective-permute-start.14
  32.7 1.7 %collective-permute-start.13 = (f32[264,256]{1,0:T(8,128)S(1)}, f32[264,256]{1,0:T(8,128)S(1)}, u32[]{:S(2)}, u32[]{:S(2)}) collective-permute-start(f32[264,256]{1,0:T(8,128)S(1)} %constant_dynamic-update-slice_fusion.refs_2_), channel_id=1, source_target_pairs={{0,2},{1,3},{2,0},{3,1},{4,6},{5,7},{6,4},{7,5},{8,10},{9,11},{10,... | collective-permute-start | bytes 811016 | tf_op jit(solution)/shard_map/ppermute | solution.py:24
  34.3 1.8 %collective-permute-start.12 = (f32[264,256]{1,0:T(8,128)S(1)}, f32[264,256]{1,0:T(8,128)S(1)}, u32[]{:S(2)}, u32[]{:S(2)}) collective-permute-start(f32[264,256]{1,0:T(8,128)S(1)} %constant_dynamic-update-slice_fusion.refs_2_), channel_id=1, source_target_pairs={{0,1},{1,0},{2,3},{3,2},{4,5},{5,4},{6,7},{7,6},{8,9},{9,8},{10,11... | collective-permute-start | bytes 811016 | tf_op jit(solution)/shard_map/ppermute | solution.py:24
  36.2 1.2 %collective-permute-start.8 = (f32[64,128]{1,0:T(8,128)S(1)}, f32[64,128]{1,0:T(8,128)S(1)}, u32[]{:S(2)}, u32[]{:S(2)}) collective-permute-start(f32[64,128]{1,0:T(8,128)S(1)} %add_add_fusion.1), channel_id=1, source_target_pairs={{0,24},{4,28},{8,16},{12,20},{16,8},{20,12},{24,0},{28,4},{1,25},{... | collective-permute-start | bytes 98312 | tf_op jit(solution)/shard_map/ppermute | solution.py:24
  37.4 4.8 %collective-permute-done.8 = f32[64,128]{1,0:T(8,128)S(1)} collective-permute-done((f32[64,128]{1,0:T(8,128)S(1)}, f32[64,128]{1,0:T(8,128)S(1)}, u32[]{:S(2)}, u32[]{:S(2)}) %collective-permute-start.8) | collective-permute-done | bytes 32800 | tf_op jit(solution)/shard_map/ppermute | solution.py:24
  42.2 4.8 %collective-permute-done.7 = f32[64,128]{1,0:T(8,128)S(1)} collective-permute-done((f32[64,128]{1,0:T(8,128)S(1)}, f32[64,128]{1,0:T(8,128)S(1)}, u32[]{:S(2)}, u32[]{:S(2)}) %collective-permute-start.7) | collective-permute-done | bytes 32800 | tf_op jit(solution)/shard_map/ppermute | solution.py:24
  47.0 3.9 %collective-permute-done.6 = f32[64,128]{1,0:T(8,128)S(1)} collective-permute-done((f32[64,128]{1,0:T(8,128)S(1)}, f32[64,128]{1,0:T(8,128)S(1)}, u32[]{:S(2)}, u32[]{:S(2)}) %collective-permute-start.6) | collective-permute-done | bytes 32800 | tf_op jit(solution)/shard_map/ppermute | solution.py:24
  51.0 0.5 collective-permute-start.19
  51.5 0.4 collective-permute-start.17
  52.0 0.5 collective-permute-done.16.refs_7_
  52.5 0.4 collective-permute-done.19.refs_10_
  52.9 0.4 collective-permute-done.18.refs_9_
  53.3 0.4 collective-permute-done.17.refs_8_
  53.7 5.5 %coarse.1 = (f32[4,16,128]{2,1,0:T(8,128)S(1)}, f32[4,256]{1,0:T(4,128)}, f32[8,128]{1,0:T(8,128)S(1)}, f32[8,128]{1,0:T(8,128)S(1)}) custom-call(f32[64,128]{1,0:T(8,128)S(1)} %add_add_fusion.refs_0_, f32[352,256]{1,0:T(8,128)S(1)} %get-tuple-element.15.refs_1_, f32[264,256]{1,0:T(8,128)S(1)} %constant_dynamic-update-slice_fusion.refs_2_, ...), custom_call_target="tpu_custom_call" | custom-call | tf_op jit(solution)/shard_map/coarse/pallas_call | solution.py:436
  59.2 0.1 collective-permute-start.20
  59.3 1.8 %collective-permute-start.21 = (f32[8,128]{1,0:T(8,128)S(1)}, f32[8,128]{1,0:T(8,128)S(1)}, u32[]{:S(2)}, u32[]{:S(2)}) collective-permute-start(f32[8,128]{1,0:T(8,128)S(1)} %get-tuple-element.20), channel_id=1, source_target_pairs={{1,2},{3,4},{5,6},{7,8},{9,10},{11,12},{13,14},{15,16},{17,18},{19... | collective-permute-start | bytes 12296 | tf_op jit(solution)/shard_map/ppermute | solution.py:31
  61.1 1.6 %collective-permute-done.20.y_first = f32[8,128]{1,0:T(8,128)S(1)} collective-permute-done((f32[8,128]{1,0:T(8,128)S(1)}, f32[8,128]{1,0:T(8,128)S(1)}, u32[]{:S(2)}, u32[]{:S(2)}) %collective-permute-start.20) | collective-permute-done | bytes 4128 | tf_op jit(solution)/shard_map/ppermute | solution.py:29
  62.8 3.2 %collective-permute-done.21.y_second = f32[8,128]{1,0:T(8,128)S(1)} collective-permute-done((f32[8,128]{1,0:T(8,128)S(1)}, f32[8,128]{1,0:T(8,128)S(1)}, u32[]{:S(2)}, u32[]{:S(2)}) %collective-permute-start.21) | collective-permute-done | bytes 4128 | tf_op jit(solution)/shard_map/ppermute | solution.py:31
  66.0 0.8 %post.1 = f32[4,16,128]{2,1,0:T(8,128)} custom-call(f32[4,16,128]{2,1,0:T(8,128)S(1)} %copy-done.4, f32[16,128]{1,0:T(8,128)S(1)} %copy-done.9, f32[16,128]{1,0:T(8,128)S(1)} %copy-done.12, f32[16,128]{1,0:T(8,128)S(1)} %copy-done.15, f32[24,128]{1,0:T(8,128)S(1)} %collective-permute-done.from_first, f32[24,128]{1,0:T(8,128)S(1)} %collective-permute-done.1.from_second, ...), custom_call_target="tpu_custom_call" | custom-call | tf_op jit(solution)/shard_map/post/pallas_call | solution.py:448
  (52 shorter events, 0.3 us)
Async XLA Ops:
  0.6 0.8 %copy-start.2 = (f32[4,16,128]{2,1,0:T(8,128)S(1)}, f32[4,16,128]{2,1,0:T(8,128)}, u32[]{:S(2)}) copy-start(f32[4,16,128]{2,1,0:T(8,128)} %r.5) | copy-start | bytes 98308
  1.4 0.7 %copy-start.7 = (f32[16,128]{1,0:T(8,128)S(1)}, f32[16,128]{1,0:T(8,128)}, u32[]{:S(2)}) copy-start(f32[16,128]{1,0:T(8,128)} %b.5) | copy-start | bytes 24580
  2.1 0.7 %copy-start.10 = (f32[16,128]{1,0:T(8,128)S(1)}, f32[16,128]{1,0:T(8,128)}, u32[]{:S(2)}) copy-start(f32[16,128]{1,0:T(8,128)} %e.5) | copy-start | bytes 24580
  2.8 0.7 %copy-start.13 = (f32[16,128]{1,0:T(8,128)S(1)}, f32[16,128]{1,0:T(8,128)}, u32[]{:S(2)}) copy-start(f32[16,128]{1,0:T(8,128)} %n.5) | copy-start | bytes 24580
  3.5 11.2 %collective-permute-start = (f32[24,128]{1,0:T(8,128)S(1)}, f32[24,128]{1,0:T(8,128)S(1)}, u32[]{:S(2)}, u32[]{:S(2)}) collective-permute-start(f32[24,128]{1,0:T(8,128)S(1)} %get-tuple-element.12), channel_id=1, source_target_pairs={{0,1},{1,0},{2,3},{3,2},{4,5},{5,4},{6,7},{7,6},{8,9},{9,8},{10,11... | collective-permute-start | bytes 36872 | tf_op jit(solution)/shard_map/ppermute | solution.py:29
  6.5 8.2 %collective-permute-start.1 = (f32[24,128]{1,0:T(8,128)S(1)}, f32[24,128]{1,0:T(8,128)S(1)}, u32[]{:S(2)}, u32[]{:S(2)}) collective-permute-start(f32[24,128]{1,0:T(8,128)S(1)} %get-tuple-element.13), channel_id=1, source_target_pairs={{1,2},{3,4},{5,6},{7,8},{9,10},{11,12},{13,14},{15,16},{17,18},{19... | collective-permute-start | bytes 36872 | tf_op jit(solution)/shard_map/ppermute | solution.py:31
  10.2 0.9 %copy-start.5 = (f32[4,64,256]{2,1,0:T(8,128)S(1)}, f32[4,64,256]{2,1,0:T(8,128)}, u32[]{:S(2)}) copy-start(f32[4,64,256]{2,1,0:T(8,128)} %coupling.1) | copy-start | bytes 786436
  11.1 0.9 %copy-start.6 = (f32[4,64,64]{2,1,0:T(8,128)S(1)}, f32[4,64,64]{2,1,0:T(8,128)}, u32[]{:S(2)}) copy-start(f32[4,64,64]{2,1,0:T(8,128)} %inverses.1) | copy-start | bytes 196612
  12.0 0.7 %copy-start.16 = (s32[4,4]{1,0:T(4,128)S(1)}, s32[4,4]{1,0:T(4,128)}, u32[]{:S(2)}) copy-start(s32[4,4]{1,0:T(4,128)} %links.1) | copy-start | bytes 196
  13.4 12.0 %collective-permute-start.9 = (f32[88,256]{1,0:T(8,128)S(1)}, f32[88,256]{1,0:T(8,128)S(1)}, u32[]{:S(2)}, u32[]{:S(2)}) collective-permute-start(f32[88,256]{1,0:T(8,128)S(1)} %get-tuple-element.16), channel_id=1, source_target_pairs={{0,8},{4,12},{8,0},{12,4},{16,24},{20,28},{24,16},{28,20},{1,9},{5... | collective-permute-start | bytes 270344 | tf_op jit(solution)/shard_map/ppermute | solution.py:24
  14.7 1.6 %copy-start = (f32[32,64,256]{2,1,0:T(8,128)S(1)}, f32[32,64,256]{2,1,0:T(8,128)}, u32[]{:S(2)}) copy-start(f32[32,64,256]{2,1,0:T(8,128)} %param.14) | copy-start | bytes 6291460
  16.3 0.8 %copy-start.3 = (f32[4,16,128]{2,1,0:T(8,128)S(1)}, f32[4,16,128]{2,1,0:T(8,128)}, u32[]{:S(2)}) copy-start(f32[4,16,128]{2,1,0:T(8,128)} %r.5) | copy-start | bytes 98308
  17.1 0.7 %copy-start.8 = (f32[16,128]{1,0:T(8,128)S(1)}, f32[16,128]{1,0:T(8,128)}, u32[]{:S(2)}) copy-start(f32[16,128]{1,0:T(8,128)} %b.5) | copy-start | bytes 24580
  17.8 0.7 %copy-start.11 = (f32[16,128]{1,0:T(8,128)S(1)}, f32[16,128]{1,0:T(8,128)}, u32[]{:S(2)}) copy-start(f32[16,128]{1,0:T(8,128)} %e.5) | copy-start | bytes 24580
  18.5 0.7 %copy-start.14 = (f32[16,128]{1,0:T(8,128)S(1)}, f32[16,128]{1,0:T(8,128)}, u32[]{:S(2)}) copy-start(f32[16,128]{1,0:T(8,128)} %n.5) | copy-start | bytes 24580
  19.2 34.5 %copy-start.1 = (f32[32,64,256]{2,1,0:T(8,128)S(1)}, f32[32,64,256]{2,1,0:T(8,128)}, u32[]{:S(2)}) copy-start(f32[32,64,256]{2,1,0:T(8,128)} %param.14) | copy-start | bytes 6291460
  20.2 3.6 %collective-permute-start.2 = (f32[64,128]{1,0:T(8,128)S(1)}, f32[64,128]{1,0:T(8,128)S(1)}, u32[]{:S(2)}, u32[]{:S(2)}) collective-permute-start(f32[64,128]{1,0:T(8,128)S(1)} %get-tuple-element.14), channel_id=1, source_target_pairs={{0,4},{4,0},{8,12},{12,8},{16,20},{20,16},{24,28},{28,24},{1,5},{5... | collective-permute-start | bytes 98312 | tf_op jit(solution)/shard_map/ppermute | solution.py:24
  20.3 12.3 %collective-permute-start.11 = (f32[88,256]{1,0:T(8,128)S(1)}, f32[88,256]{1,0:T(8,128)S(1)}, u32[]{:S(2)}, u32[]{:S(2)}) collective-permute-start(f32[88,256]{1,0:T(8,128)S(1)} %get-tuple-element.16), channel_id=1, source_target_pairs={{0,24},{4,28},{8,16},{12,20},{16,8},{20,12},{24,0},{28,4},{1,25},{... | collective-permute-start | bytes 270344 | tf_op jit(solution)/shard_map/ppermute | solution.py:24
  21.9 10.6 %collective-permute-start.10 = (f32[88,256]{1,0:T(8,128)S(1)}, f32[88,256]{1,0:T(8,128)S(1)}, u32[]{:S(2)}, u32[]{:S(2)}) collective-permute-start(f32[88,256]{1,0:T(8,128)S(1)} %get-tuple-element.16), channel_id=1, source_target_pairs={{0,16},{4,20},{8,24},{12,28},{16,0},{20,4},{24,8},{28,12},{1,17},{... | collective-permute-start | bytes 270344 | tf_op jit(solution)/shard_map/ppermute | solution.py:24
  23.8 10.5 %collective-permute-start.5 = (f32[64,128]{1,0:T(8,128)S(1)}, f32[64,128]{1,0:T(8,128)S(1)}, u32[]{:S(2)}, u32[]{:S(2)}) collective-permute-start(f32[64,128]{1,0:T(8,128)S(1)} %add.70), channel_id=1, source_target_pairs={{0,3},{1,2},{2,1},{3,0},{4,7},{5,6},{6,5},{7,4},{8,11},{9,10},{10,... | collective-permute-start | bytes 98312 | tf_op jit(solution)/shard_map/ppermute | solution.py:24
  24.4 11.7 %collective-permute-start.4 = (f32[64,128]{1,0:T(8,128)S(1)}, f32[64,128]{1,0:T(8,128)S(1)}, u32[]{:S(2)}, u32[]{:S(2)}) collective-permute-start(f32[64,128]{1,0:T(8,128)S(1)} %add.70), channel_id=1, source_target_pairs={{0,2},{1,3},{2,0},{3,1},{4,6},{5,7},{6,4},{7,5},{8,10},{9,11},{10,... | collective-permute-start | bytes 98312 | tf_op jit(solution)/shard_map/ppermute | solution.py:24
  25.4 10.7 %collective-permute-start.3 = (f32[64,128]{1,0:T(8,128)S(1)}, f32[64,128]{1,0:T(8,128)S(1)}, u32[]{:S(2)}, u32[]{:S(2)}) collective-permute-start(f32[64,128]{1,0:T(8,128)S(1)} %add.70), channel_id=1, source_target_pairs={{0,1},{1,0},{2,3},{3,2},{4,5},{5,4},{6,7},{7,6},{8,9},{9,8},{10,11... | collective-permute-start | bytes 98312 | tf_op jit(solution)/shard_map/ppermute | solution.py:24
  32.6 18.4 %collective-permute-start.14 = (f32[264,256]{1,0:T(8,128)S(1)}, f32[264,256]{1,0:T(8,128)S(1)}, u32[]{:S(2)}, u32[]{:S(2)}) collective-permute-start(f32[264,256]{1,0:T(8,128)S(1)} %constant_dynamic-update-slice_fusion.refs_2_), channel_id=1, source_target_pairs={{0,3},{1,2},{2,1},{3,0},{4,7},{5,6},{6,5},{7,4},{8,11},{9,10},{10,... | collective-permute-start | bytes 811016 | tf_op jit(solution)/shard_map/ppermute | solution.py:24
  32.7 18.8 %collective-permute-start.13 = (f32[264,256]{1,0:T(8,128)S(1)}, f32[264,256]{1,0:T(8,128)S(1)}, u32[]{:S(2)}, u32[]{:S(2)}) collective-permute-start(f32[264,256]{1,0:T(8,128)S(1)} %constant_dynamic-update-slice_fusion.refs_2_), channel_id=1, source_target_pairs={{0,2},{1,3},{2,0},{3,1},{4,6},{5,7},{6,4},{7,5},{8,10},{9,11},{10,... | collective-permute-start | bytes 811016 | tf_op jit(solution)/shard_map/ppermute | solution.py:24
  34.3 17.2 %collective-permute-start.12 = (f32[264,256]{1,0:T(8,128)S(1)}, f32[264,256]{1,0:T(8,128)S(1)}, u32[]{:S(2)}, u32[]{:S(2)}) collective-permute-start(f32[264,256]{1,0:T(8,128)S(1)} %constant_dynamic-update-slice_fusion.refs_2_), channel_id=1, source_target_pairs={{0,1},{1,0},{2,3},{3,2},{4,5},{5,4},{6,7},{7,6},{8,9},{9,8},{10,11... | collective-permute-start | bytes 811016 | tf_op jit(solution)/shard_map/ppermute | solution.py:24
  36.2 6.1 %collective-permute-start.8 = (f32[64,128]{1,0:T(8,128)S(1)}, f32[64,128]{1,0:T(8,128)S(1)}, u32[]{:S(2)}, u32[]{:S(2)}) collective-permute-start(f32[64,128]{1,0:T(8,128)S(1)} %add_add_fusion.1), channel_id=1, source_target_pairs={{0,24},{4,28},{8,16},{12,20},{16,8},{20,12},{24,0},{28,4},{1,25},{... | collective-permute-start | bytes 98312 | tf_op jit(solution)/shard_map/ppermute | solution.py:24
  37.4 15.1 %collective-permute-start.15 = (f32[352,256]{1,0:T(8,128)S(1)}, f32[352,256]{1,0:T(8,128)S(1)}, u32[]{:S(2)}, u32[]{:S(2)}) collective-permute-start(f32[352,256]{1,0:T(8,128)S(1)} %get-tuple-element.15.refs_1_), channel_id=1, source_target_pairs={{0,4},{4,0},{8,12},{12,8},{16,20},{20,16},{24,28},{28,24},{1,5},{5... | collective-permute-start | bytes 1081352 | tf_op jit(solution)/shard_map/ppermute | solution.py:24
  42.2 4.8 %collective-permute-start.7 = (f32[64,128]{1,0:T(8,128)S(1)}, f32[64,128]{1,0:T(8,128)S(1)}, u32[]{:S(2)}, u32[]{:S(2)}) collective-permute-start(f32[64,128]{1,0:T(8,128)S(1)} %add_add_fusion.1), channel_id=1, source_target_pairs={{0,16},{4,20},{8,24},{12,28},{16,0},{20,4},{24,8},{28,12},{1,17},{... | collective-permute-start | bytes 98312 | tf_op jit(solution)/shard_map/ppermute | solution.py:24
  47.0 3.9 %collective-permute-start.6 = (f32[64,128]{1,0:T(8,128)S(1)}, f32[64,128]{1,0:T(8,128)S(1)}, u32[]{:S(2)}, u32[]{:S(2)}) collective-permute-start(f32[64,128]{1,0:T(8,128)S(1)} %add_add_fusion.1), channel_id=1, source_target_pairs={{0,8},{4,12},{8,0},{12,4},{16,24},{20,28},{24,16},{28,20},{1,9},{5... | collective-permute-start | bytes 98312 | tf_op jit(solution)/shard_map/ppermute | solution.py:24
  51.0 1.5 %collective-permute-start.16 = (f32[264,256]{1,0:T(8,128)S(1)}, f32[264,256]{1,0:T(8,128)S(1)}, u32[]{:S(2)}, u32[]{:S(2)}) collective-permute-start(f32[264,256]{1,0:T(8,128)S(1)} %constant_dynamic-update-slice_fusion.refs_2_), channel_id=1, source_target_pairs={{0,4},{4,0},{8,12},{12,8},{16,20},{20,16},{24,28},{28,24},{1,5},{5... | collective-permute-start | bytes 811016 | tf_op jit(solution)/shard_map/ppermute | solution.py:24
  51.0 1.9 %collective-permute-start.19 = (f32[264,256]{1,0:T(8,128)S(1)}, f32[264,256]{1,0:T(8,128)S(1)}, u32[]{:S(2)}, u32[]{:S(2)}) collective-permute-start(f32[264,256]{1,0:T(8,128)S(1)} %collective-permute-done.14.refs_5_), channel_id=1, source_target_pairs={{0,4},{4,0},{8,12},{12,8},{16,20},{20,16},{24,28},{28,24},{1,5},{5... | collective-permute-start | bytes 811016 | tf_op jit(solution)/shard_map/ppermute | solution.py:24
  51.5 1.8 %collective-permute-start.18 = (f32[264,256]{1,0:T(8,128)S(1)}, f32[264,256]{1,0:T(8,128)S(1)}, u32[]{:S(2)}, u32[]{:S(2)}) collective-permute-start(f32[264,256]{1,0:T(8,128)S(1)} %collective-permute-done.13.refs_4_), channel_id=1, source_target_pairs={{0,4},{4,0},{8,12},{12,8},{16,20},{20,16},{24,28},{28,24},{1,5},{5... | collective-permute-start | bytes 811016 | tf_op jit(solution)/shard_map/ppermute | solution.py:24
  51.5 2.1 %collective-permute-start.17 = (f32[264,256]{1,0:T(8,128)S(1)}, f32[264,256]{1,0:T(8,128)S(1)}, u32[]{:S(2)}, u32[]{:S(2)}) collective-permute-start(f32[264,256]{1,0:T(8,128)S(1)} %collective-permute-done.12.refs_3_), channel_id=1, source_target_pairs={{0,4},{4,0},{8,12},{12,8},{16,20},{20,16},{24,28},{28,24},{1,5},{5... | collective-permute-start | bytes 811016 | tf_op jit(solution)/shard_map/ppermute | solution.py:24
  53.7 12.3 %copy-start.4 = (f32[4,16,128]{2,1,0:T(8,128)S(1)}, f32[4,16,128]{2,1,0:T(8,128)}, u32[]{:S(2)}) copy-start(f32[4,16,128]{2,1,0:T(8,128)} %r.5) | copy-start | bytes 98308
  53.7 12.3 %copy-start.9 = (f32[16,128]{1,0:T(8,128)S(1)}, f32[16,128]{1,0:T(8,128)}, u32[]{:S(2)}) copy-start(f32[16,128]{1,0:T(8,128)} %b.5) | copy-start | bytes 24580
  53.7 12.3 %copy-start.12 = (f32[16,128]{1,0:T(8,128)S(1)}, f32[16,128]{1,0:T(8,128)}, u32[]{:S(2)}) copy-start(f32[16,128]{1,0:T(8,128)} %e.5) | copy-start | bytes 24580
  53.7 12.3 %copy-start.15 = (f32[16,128]{1,0:T(8,128)S(1)}, f32[16,128]{1,0:T(8,128)}, u32[]{:S(2)}) copy-start(f32[16,128]{1,0:T(8,128)} %n.5) | copy-start | bytes 24580
  59.2 3.6 %collective-permute-start.20 = (f32[8,128]{1,0:T(8,128)S(1)}, f32[8,128]{1,0:T(8,128)S(1)}, u32[]{:S(2)}, u32[]{:S(2)}) collective-permute-start(f32[8,128]{1,0:T(8,128)S(1)} %get-tuple-element.19), channel_id=1, source_target_pairs={{0,1},{1,0},{2,3},{3,2},{4,5},{5,4},{6,7},{7,6},{8,9},{9,8},{10,11... | collective-permute-start | bytes 12296 | tf_op jit(solution)/shard_map/ppermute | solution.py:29
  59.3 6.6 %collective-permute-start.21 = (f32[8,128]{1,0:T(8,128)S(1)}, f32[8,128]{1,0:T(8,128)S(1)}, u32[]{:S(2)}, u32[]{:S(2)}) collective-permute-start(f32[8,128]{1,0:T(8,128)S(1)} %get-tuple-element.20), channel_id=1, source_target_pairs={{1,2},{3,4},{5,6},{7,8},{9,10},{11,12},{13,14},{15,16},{17,18},{19... | collective-permute-start | bytes 12296 | tf_op jit(solution)/shard_map/ppermute | solution.py:31

commit v2 on v1

--- a/solution.py
+++ b/solution.py
@@ -32,7 +32,17 @@
     return first, second
 
 
-def groups_of(size):
+def tie(values, after):
+    count = len(values)
+    spec = pl.BlockSpec(memory_space=pl.ANY)
+    return list(pl.pallas_call(
+        lambda *refs: None, out_shape=[jax.ShapeDtypeStruct(v.shape, v.dtype) for v in values],
+        in_specs=[spec] * (count + 1), out_specs=[spec] * count,
+        input_output_aliases={i: i for i in range(count)}, cost_estimate=CHEAP, compiler_params=params(1), name="tie",
+    )(*values, after))
+
+
+def rounds_of(size):
     rounds, base = [], 1
     while base < size:
         span = 4 if base * 4 <= size else 2
@@ -41,13 +51,8 @@
     return rounds
 
 
-def sum_all(value):
-    value = value + swap(value, "wide", 1)
-    for masks in groups_of(lax.axis_size("narrow")):
-        value = sum([swap(value, "narrow", k) for k in masks], value)
-    for masks in groups_of(lax.axis_size("wide") // 2):
-        value = sum([swap(value, "wide", 2 * k) for k in masks], value)
-    return value
+def bits_of(size):
+    return [1 << i for i in range(size.bit_length() - 1)]
 
 
 def place():
@@ -82,7 +87,31 @@
     return pltpu.roll(value, 64, 1)
 
 
-def edges_kernel(r, b, e, n, first, second):
+def copy_all(pairs, sems):
+    copies = [pltpu.make_async_copy(source, target, sems.at[i]) for i, (source, target) in enumerate(pairs)]
+    for copy in copies:
+        copy.start()
+
+    def wait():
+        for copy in copies:
+            copy.wait()
+
+    return wait
+
+
+def pack_row(matrix, inverse, links, j, put):
+    packed = jnp.concatenate([inverse[16 * t:16 * t + 16, :] for t in range(4)], axis=1)
+    lane = lanes((8, 256))
+    tail = jnp.zeros((8, 256), F32)
+    for l in range(links.shape[1]):
+        tail = jnp.where(lane == l, links[j, l].astype(F32), tail)
+    put(0, matrix)
+    put(64, packed)
+    put(80, tail)
+
+
+def begin_kernel(r_in, b_in, e_in, n_in, first, second, r, b, e, n, sems):
+    copy_all([(r_in, r), (b_in, b), (e_in, e), (n_in, n)], sems)()
     grid_rows = b.shape[0]
     line, _ = place()
     even = lax.rem(line, 2) == 0
@@ -103,25 +132,67 @@
         at += size
 
 
-def pack_kernel(owned, links, coupling, inverses, block, own):
+def pack_kernel(owned, links_in, coupling_in, inverses_in, after, own, block, links, coupling, inverses, sems):
+    del after
     q = lax.rem(lax.axis_index("narrow"), owned)
-    lane = lanes((8, 256))
+    copy_all([(links_in, links), (coupling_in, coupling), (inverses_in, inverses)], sems)()
     for j_rel in range(owned):
         j = jnp.bitwise_xor(q, j_rel)
-        base = j_rel * PIECE
-        matrix = coupling[j]
-        inverse = inverses[j]
-        packed = jnp.concatenate([inverse[16 * t:16 * t + 16, :] for t in range(4)], axis=1)
-        tail = jnp.zeros((8, 256), F32)
-        for l in range(links.shape[1]):
-            tail = jnp.where(lane == l, links[j, l].astype(F32), tail)
-        block[base:base + 64, :] = matrix
-        block[base + 64:base + 80, :] = packed
-        block[base + 80:base + 88, :] = tail
-        if j_rel == 0:
-            own[0:64, :] = matrix
-            own[64:80, :] = packed
-            own[80:88, :] = tail
+
+        def put(at, value, base=j_rel * PIECE):
+            block[base + at:base + at + value.shape[0], :] = value
+            if base == 0:
+                own[at:at + value.shape[0], :] = value
+
+        pack_row(coupling[j], inverses[j], links, j, put)
+
+
+def prepare_kernel(owned, coarse_rows, r_in, b_in, e_in, n_in, support_in, basis_in,
+                   r_out, b_out, e_out, n_out, basis_high, basis_low, hots, sup_hots,
+                   support, basis, sems, basis_sems):
+    q = lax.rem(lax.axis_index("narrow"), owned)
+    mine = lax.axis_index("wide") * owned + q
+    wait = copy_all([(r_in, r_out), (b_in, b_out), (e_in, e_out), (n_in, n_out), (support_in, support)], sems)
+    parts = basis_sems.shape[0]
+    part = basis.shape[0] // parts
+    copies = [pltpu.make_async_copy(basis_in.at[pl.ds(part * i, part)], basis.at[pl.ds(part * i, part)],
+                                    basis_sems.at[i]) for i in range(parts)]
+    for copy in copies:
+        copy.start()
+    wait()
+
+    blocks = support.shape[1]
+    rows4 = 4 * blocks
+    size = 4 * coarse_rows
+
+    def chosen(which, index):
+        g, h = lax.shift_right_logical(index, 4), jnp.bitwise_and(lax.shift_right_logical(index, 3), 1)
+        p = jnp.bitwise_and(lax.shift_right_logical(index, 2), 1)
+        return jnp.where(which == g * 4 + p * 2 + h, 1.0, 0.0).astype(BF16)
+
+    value = support[...].astype(F32).astype(BF16)
+    column = dot_t(chosen(lanes((rows4, blocks)), rows((rows4, blocks))), value)
+    line = dot(value, chosen(rows((blocks, rows4)), lanes((blocks, rows4))))
+    line = line.astype(jnp.int32) * 4 + jnp.bitwise_and(lanes((4, rows4)), 3)
+    at = rows((size, rows4))
+    for k in range(4):
+        base, left = (k % 2) * size, (k // 2) * rows4
+        hots[base:base + size, left:left + rows4] = jnp.where(at == line[k:k + 1, :], 1.0, 0.0).astype(BF16)
+    column = jnp.bitwise_xor(column.astype(jnp.int32), mine) * 4 + jnp.bitwise_and(rows((rows4, 4)), 3)
+    across = lanes((rows4, size))
+    for k in range(4):
+        sup_hots[rows4 * k:rows4 * k + rows4, :] = jnp.where(across == column[:, k:k + 1], 1.0, 0.0).astype(BF16)
+
+    for i in range(parts):
+        copies[i].wait()
+        for at in range(part * i, part * i + part, 256):
+            basis_high[at:at + 256, :], basis_low[at:at + 256, :] = split(basis[at:at + 256, :])
+
+
+def stack_kernel(*refs):
+    fetched, gathered = refs[:-4], refs[-1]
+    for i, piece in enumerate(fetched):
+        gathered[PIECE * i:PIECE * i + PIECE, :] = piece[...]
 
 
 class Fine:
@@ -190,8 +261,8 @@
     ]
 
 
-def restrict_kernel(coarse_rows, r, b, e, n, from_first, from_second, basis, sup, out, x_out,
-                    rx, bx, ex, nx, field, by_row, contrib):
+def restrict_kernel(coarse_rows, r, b, e, n, from_first, from_second, basis_high, basis_low, hots, *refs):
+    out, x_out, rx, bx, ex, nx, field, by_row, contrib = refs[-9:]
     fine = Fine(r, b, e, n, from_first, from_second, rx, bx, ex, nx, field)
     x = fine.scale * fine.r
     for step in range(SWEEPS - 1):
@@ -211,19 +282,15 @@
             held = jnp.where(here, z, 0.0)
             parts.append(jnp.concatenate([jnp.where(upper, held, 0.0), jnp.where(upper, 0.0, held)], axis=1))
         high, low = split(jnp.concatenate(parts, axis=0))
-        w_high, w_low = split(basis[256 * g:256 * g + 256, :])
-        both = dot(jnp.concatenate([high, low], axis=0), w_high)
-        contrib[16 * g:16 * g + 16, :] = both[0:16] + both[16:32] + dot(high, w_low)
+        near = slice(256 * g, 256 * g + 256)
+        both = dot(jnp.concatenate([high, low], axis=0), basis_high[near, :])
+        contrib[16 * g:16 * g + 16, :] = both[0:16] + both[16:32] + dot(high, basis_low[near, :])
     c_high, c_low = split(contrib[...])
     weights = jnp.concatenate([
         jnp.concatenate([c_high[:, 0:128], c_low[:, 0:128]], axis=1),
         jnp.concatenate([c_high[:, 128:256], c_low[:, 128:256]], axis=1)], axis=0)
     size = 4 * coarse_rows
-    at = rows((size, 128))
-    hot = [jnp.where(at == sup[k:k + 1, :], 1.0, 0.0).astype(BF16) for k in range(4)]
-    hots = jnp.concatenate([
-        jnp.concatenate([hot[0], hot[2]], axis=1), jnp.concatenate([hot[1], hot[3]], axis=1)], axis=0)
-    total = dot(hots, weights)
+    total = dot(hots[...], weights)
     total = total[:, 0:128] + total[:, 128:256]
     here = lanes((size, 128)) < 64
     even = jnp.where(here, total[0:size], 0.0)
@@ -242,7 +309,7 @@
 
     (rhs_ref,) = take(1)
     pieces = take(2 * (1 + owned))
-    basis, sup, x_ref = take(3)
+    basis_high, basis_low, sup_hots, x_ref = take(4)
     y_ref, coarse_ref, first, second = take(4)
     w_high, w_low, w_inv, link_rows, hots, product, u_ref, by_row = refs
     size = 4 * coarse_rows
@@ -334,18 +401,15 @@
         coarse_ref[j:j + 1, 0:128] = jnp.where(here1, got[0:1], got[1:2])
         coarse_ref[j:j + 1, 128:256] = jnp.where(here1, got[2:3], got[3:4])
 
-    blocks4 = sup.shape[0]
-    lane_s = lanes((blocks4, size))
-    sup_hots = jnp.concatenate(
-        [jnp.where(lane_s == sup[:, k:k + 1], 1.0, 0.0).astype(BF16) for k in range(4)], axis=0)
-    high, low = pick(dot(sup_hots, hi_lo(u)), blocks4)
+    blocks4 = sup_hots.shape[0] // 4
+    high, low = pick(dot(sup_hots[...], hi_lo(u)), blocks4)
     left = lanes((8, 128)) < 64
     upper = rows((8, 128)) < 4
     for g in range(blocks4 // 16):
-        b_high, b_low = split(basis[256 * g:256 * g + 256, :])
         near = slice(16 * g, 16 * g + 16)
-        both = dot_t(jnp.concatenate([high[near], low[near]], axis=0), b_high)
-        got = both[0:16] + both[16:32] + dot_t(high[near], b_low)
+        block = slice(256 * g, 256 * g + 256)
+        both = dot_t(jnp.concatenate([high[near], low[near]], axis=0), basis_high[block, :])
+        got = both[0:16] + both[16:32] + dot_t(high[near], basis_low[block, :])
         halves = [jnp.where(upper, got[8 * h:8 * h + 8, 0:128], got[8 * h:8 * h + 8, 128:256]) for h in range(2)]
         by_row[8 * g:8 * g + 8, :] = jnp.where(left, halves[0], halves[1])
     line, _ = place()
@@ -379,12 +443,19 @@
         out[a] = field[a, 8 + HALO:8 + HALO + fine.grid_rows, :]
 
 
-def shape(*dims):
-    return jax.ShapeDtypeStruct(dims, F32)
+def shape(*dims, kind=F32):
+    return jax.ShapeDtypeStruct(dims, kind)
 
 
 def params(mebibytes):
     return pltpu.CompilerParams(vmem_limit_bytes=mebibytes * 2 ** 20)
+
+
+def stay(array):
+    return pltpu.with_memory_space_constraint(array, pltpu.HBM)
+
+
+CHEAP = pl.CostEstimate(flops=1, bytes_accessed=1, transcendentals=0)
 
 
 def body(right_sides, brinkman, east_faces, north_faces, support, basis, links, coarse_block_inverses, coarse_coupling):
@@ -396,61 +467,96 @@
     size = 4 * coarse_rows
     basis = basis.reshape(blocks * block_size, -1)
 
+    in_hbm = pl.BlockSpec(memory_space=pltpu.HBM)
+    anywhere = pl.BlockSpec(memory_space=pl.ANY)
+    in_vmem = pl.BlockSpec(memory_space=pltpu.VMEM)
+    row_dims = (grid_rows, width)
     message = shape(24, width)
+    fine_inputs = tuple(map(stay, (right_sides, brinkman, east_faces, north_faces)))
+    coarse_inputs = tuple(map(stay, (links, coarse_coupling, coarse_block_inverses)))
     to_first, to_second = pl.pallas_call(
-        edges_kernel, out_shape=(message, message), compiler_params=params(16), name="edges",
-    )(right_sides, brinkman, east_faces, north_faces)
+        begin_kernel,
+        out_shape=(message, message),
+        in_specs=[in_hbm] * 4,
+        scratch_shapes=[
+            pltpu.VMEM((adjoints, *row_dims), F32), pltpu.VMEM(row_dims, F32), pltpu.VMEM(row_dims, F32),
+            pltpu.VMEM(row_dims, F32), pltpu.SemaphoreType.DMA((4,))],
+        cost_estimate=CHEAP, compiler_params=params(16), name="begin",
+    )(*fine_inputs)
     from_first, from_second = pair_swaps(to_first, to_second)
 
-    in_vmem = pl.BlockSpec(memory_space=pltpu.VMEM)
-    block, own = pl.pallas_call(
+    own, block = pl.pallas_call(
         functools.partial(pack_kernel, owned),
-        out_shape=(shape(owned * PIECE, 256), shape(PIECE, 256)),
-        in_specs=[pl.BlockSpec(memory_space=pltpu.SMEM), in_vmem, in_vmem],
-        compiler_params=params(16), name="pack",
-    )(links, coarse_coupling, coarse_block_inverses)
-
-    fetched = jnp.concatenate([swap(own, "wide", 2 * k) for k in range(1, zs)], axis=0)
-    pieces = [block, fetched] + [swap(fetched, "narrow", k) for k in range(1, owned)]
-    pieces = pieces + [swap(piece, "wide", 1) for piece in pieces]
-
-    mine = lax.axis_index("wide") * owned + lax.rem(lax.axis_index("narrow"), owned)
-    by_k = support.reshape(blocks // 4, 2, 2, 4).transpose(3, 0, 2, 1).reshape(4, blocks, 1)
-    a_row = jnp.arange(adjoints, dtype=jnp.int32)
-    sup = (by_k * 4 + a_row).reshape(4, blocks * adjoints)
-    sup_rel = (jnp.bitwise_xor(by_k, mine) * 4 + a_row).reshape(4, blocks * adjoints).T
+        out_shape=(shape(PIECE, 256), shape(owned * PIECE, 256)),
+        in_specs=[in_hbm] * 3 + [anywhere],
+        scratch_shapes=[
+            pltpu.SMEM(links.shape, jnp.int32), pltpu.VMEM(coarse_coupling.shape, F32),
+            pltpu.VMEM(coarse_block_inverses.shape, F32), pltpu.SemaphoreType.DMA((3,))],
+        cost_estimate=CHEAP, compiler_params=params(16), name="pack",
+    )(*coarse_inputs, to_first)
+    fetched = [swap(own, "wide", 2 * k) for k in range(1, zs)]
+
+    rows4 = adjoints * blocks
+    r, b, e, n, basis_high, basis_low, hots, sup_hots = pl.pallas_call(
+        functools.partial(prepare_kernel, owned, coarse_rows),
+        out_shape=(shape(adjoints, *row_dims), shape(*row_dims), shape(*row_dims),
+                   shape(*row_dims), shape(*basis.shape, kind=BF16), shape(*basis.shape, kind=BF16),
+                   shape(2 * size, 2 * rows4, kind=BF16), shape(4 * rows4, size, kind=BF16)),
+        in_specs=[in_hbm] * 6,
+        scratch_shapes=[
+            pltpu.VMEM((4, blocks), jnp.int32),
+            pltpu.VMEM(basis.shape, F32), pltpu.SemaphoreType.DMA((5,)), pltpu.SemaphoreType.DMA((4,))],
+        cost_estimate=CHEAP, compiler_params=params(24), name="prepare",
+    )(*fine_inputs, stay(support.T), stay(basis))
+
+    gathered = pl.pallas_call(
+        stack_kernel, out_shape=shape((zs - 1) * PIECE, 256),
+        in_specs=[in_vmem] * (zs - 1) + [anywhere] * 3,
+        cost_estimate=CHEAP, compiler_params=params(4), name="stack",
+    )(*fetched, from_first, from_second, hots)
+    spread = [swap(gathered, "narrow", k) for k in range(1, owned)]
 
     rhs, x = pl.pallas_call(
         functools.partial(restrict_kernel, coarse_rows),
-        out_shape=(shape(size // 2, 128), shape(adjoints, grid_rows, width)),
+        out_shape=(shape(size // 2, 128), shape(adjoints, *row_dims)),
         scratch_shapes=fine_scratch(adjoints, width) + [
-            pltpu.VMEM((4 * grid_rows, width), F32), pltpu.VMEM((4 * blocks, 256), F32)],
-        compiler_params=params(24), name="restrict",
-    )(right_sides, brinkman, east_faces, north_faces, from_first, from_second, basis, sup)
-
-    rhs = sum_all(rhs)
+            pltpu.VMEM((4 * grid_rows, width), F32), pltpu.VMEM((rows4, 256), F32)],
+        in_specs=[in_vmem] * 9 + [anywhere],
+        cost_estimate=CHEAP, compiler_params=params(16), name="restrict",
+    )(r, b, e, n, from_first, from_second, basis_high, basis_low, hots, gathered)
+
+    rhs = rhs + swap(rhs, "wide", 1)
+    for bit in bits_of(zs):
+        rhs = rhs + swap(rhs, "wide", 2 * bit)
+    block, gathered_late = tie([block, gathered], rhs)
+    block_other = swap(block, "wide", 1)
+    gathered_other = swap(gathered_late, "wide", 1)
+    spread = tie(spread, rhs)
+    for masks in rounds_of(lax.axis_size("narrow")):
+        rhs = sum([swap(rhs, "narrow", k) for k in masks], rhs)
+    pieces = [block, gathered_late] + spread + [block_other, gathered_other] + [swap(piece, "wide", 1) for piece in spread]
 
     def coarse_body(*refs):
         coarse_kernel(owned, coarse_rows, zs, refs)
 
     y, coarse, y_first, y_second = pl.pallas_call(
         coarse_body,
-        out_shape=(shape(adjoints, grid_rows, width), shape(owned, 256), shape(8, width), shape(8, width)),
+        out_shape=(shape(adjoints, *row_dims), shape(owned, 256), shape(8, width), shape(8, width)),
         scratch_shapes=[
             pltpu.VMEM((64 * coarse_rows, 256), BF16), pltpu.VMEM((64 * coarse_rows, 256), BF16),
             pltpu.VMEM((64 * coarse_rows, 256), BF16), pltpu.VMEM((size, 128), F32),
             pltpu.VMEM((4 * size, size), BF16), pltpu.VMEM((size, 256), F32),
             pltpu.VMEM((4 * owned, 128), F32), pltpu.VMEM((4 * grid_rows, width), F32)],
-        compiler_params=params(min(56, 16 + coarse_rows // 2)), name="coarse",
-    )(rhs, *pieces, basis, sup_rel, x)
+        cost_estimate=CHEAP, compiler_params=params(min(48, 8 + coarse_rows // 3)), name="coarse",
+    )(rhs, *pieces, basis_high, basis_low, sup_hots, x)
 
     y_first, y_second = pair_swaps(y_first, y_second)
     solution_field = pl.pallas_call(
         post_kernel,
         out_shape=shape(adjoints, grid_rows, width),
         scratch_shapes=fine_scratch(adjoints, width) + [pltpu.VMEM((adjoints, FIELD, width), F32)],
-        compiler_params=params(16), name="post",
-    )(right_sides, brinkman, east_faces, north_faces, from_first, from_second, y, y_first, y_second)
+        cost_estimate=CHEAP, compiler_params=params(16), name="post",
+    )(r, b, e, n, from_first, from_second, y, y_first, y_second)
     return solution_field, coarse
 
 

time: 67.4 us -> 53.2 us (0.79)
  local copies, waits for them, and re-layouts: 10.3 us -> 0 us
  waiting for transfers between devices: 25.2 us -> 17.1 us
  Pallas kernels: 8.03 us -> 10.8 us
  starting transfers between devices: 21.7 us -> 24.3 us
  other arithmetic: 0.8 us -> 0.03 us
    unnamed x36 -> x0, local copies, waits for them, and re-layouts: 9.86 us -> none
    ppermute x18 -> x17, waiting for transfers between devices: 20.4 us -> 11.4 us  [swap(): return lax.ppermute(value, axis, [(i, i ^ bits) for i in range(size)])]
    pallas_call x3 -> x7, Pallas kernels: 6.16 us -> 8.94 us  [the longest x1 5.08 us: body(): pl.pallas_call(coarse_body, out_shape=(shape(adjoints, *row_dims), shape(...]
    ppermute x18 -> x17, starting transfers between devices: 13 us -> 15.7 us  [swap(): return lax.ppermute(value, axis, [(i, i ^ bits) for i in range(size)])]
    ppermute x2, waiting for transfers between devices: 3.17 us -> 4.86 us  [pair_swaps(): lax.ppermute(to_second, BOTH, odd + [(target, source) for source, target...]
    ppermute x2, starting transfers between devices: 3.15 us -> 1.61 us  [pair_swaps(): first = lax.ppermute(to_first, BOTH, [(i, i ^ 1) for i in range(count)])]
    ppermute x2, starting transfers between devices: 5.51 us -> 6.94 us  [pair_swaps(): lax.ppermute(to_second, BOTH, odd + [(target, source) for source, target...]
    ppermute x2, waiting for transfers between devices: 1.63 us -> 0.83 us  [pair_swaps(): first = lax.ppermute(to_first, BOTH, [(i, i ^ 1) for i in range(count)])]
  transfers between devices with their start and end apart: 22 -> 21, of which waited for: 10 -> 12; matrix products, arithmetic and copies ran while one was open for 2% -> 0% of each run, Pallas kernels for 3% -> 5%
where the time goes in v2:
time: 53.2 us; the launch traced here: 53 us
  starting transfers between devices  24.3 us (46%)
  waiting for transfers between devices  17.1 us (32%)
  Pallas kernels  10.8 us (20%)
  between operations  0.75 us (1%)
    ppermute x17, starting transfers between devices, swap(): return lax.ppermute(value, axis, [(i, i ^ bits) for i in range(size)])  15.7 us
    ppermute x17, waiting for transfers between devices, swap(): return lax.ppermute(value, axis, [(i, i ^ bits) for i in range(size)])  11.4 us
    ppermute x2, starting transfers between devices, pair_swaps(): lax.ppermute(to_second, BOTH, odd + [(target, source) for source, target...  6.94 us
    pallas_call x1, Pallas kernels, body(): pl.pallas_call(coarse_body, out_shape=(shape(adjoints, *row_dims), shape(...  5.08 us
    ppermute x2, waiting for transfers between devices, pair_swaps(): lax.ppermute(to_second, BOTH, odd + [(target, source) for source, target...  4.86 us
    pallas_call x1, Pallas kernels, body(): pl.pallas_call(functools.partial(prepare_kernel, owned, coarse_rows), out...  1.91 us
    ppermute x2, starting transfers between devices, pair_swaps(): first = lax.ppermute(to_first, BOTH, [(i, i ^ 1) for i in range(count)])  1.61 us
    pallas_call x1, Pallas kernels, body(): pl.pallas_call(functools.partial(pack_kernel, owned), out_shape=(shape(PI...  1.11 us
  transfers between devices with their start and end apart: 21, of which 12 were waited for; matrix products, arithmetic and copies ran while one was open for 0% of the time, Pallas kernels for 5%

profile of v2, /device:TPU:0, one launch (start us, length us, event | category | flops | bytes accessed | tf_op | source)
XLA Modules:
  0.0 53.0 jit_solution(16072591997559378665)
XLA Ops:
  0.6 0.8 %begin.1 = (f32[24,128]{1,0:T(8,128)S(1)}, f32[24,128]{1,0:T(8,128)S(1)}) custom-call(f32[4,16,128]{2,1,0:T(8,128)} %r_in.3, f32[16,128]{1,0:T(8,128)} %b_in.3, f32[16,128]{1,0:T(8,128)} %e_in.3, f32[16,128]{1,0:T(8,128)} %n_in.3), custom_call_target="tpu_custom_call" | custom-call | flops 1 | bytes 1 | tf_op jit(solution)/shard_map/begin/pallas_call | solution.py:477
  1.4 1.1 %pack.1 = (f32[88,256]{1,0:T(8,128)S(1)}, f32[352,256]{1,0:T(8,128)S(1)}) custom-call(s32[4,4]{1,0:T(4,128)} %links_in.1, f32[4,64,256]{2,1,0:T(8,128)} %coupling_in.1, f32[4,64,64]{2,1,0:T(8,128)} %inverses_in.1, f32[24,128]{1,0:T(8,128)S(1)} %get-tuple-element.29.after), custom_call_target="tpu_custom_call" | custom-call | flops 1 | bytes 1 | tf_op jit(solution)/shard_map/pack/pallas_call | solution.py:488
  2.6 5.1 %collective-permute-start.4 = (f32[88,256]{1,0:T(8,128)S(1)}, f32[88,256]{1,0:T(8,128)S(1)}, u32[]{:S(2)}, u32[]{:S(2)}) collective-permute-start(f32[88,256]{1,0:T(8,128)S(1)} %get-tuple-element.34), channel_id=1, source_target_pairs={{0,24},{4,28},{8,16},{12,20},{16,8},{20,12},{24,0},{28,4},{1,25},{... | collective-permute-start | bytes 270344 | tf_op jit(solution)/shard_map/ppermute | solution.py:24
  7.7 0.0 collective-permute-start.3
  7.7 0.6 %collective-permute-start.2 = (f32[88,256]{1,0:T(8,128)S(1)}, f32[88,256]{1,0:T(8,128)S(1)}, u32[]{:S(2)}, u32[]{:S(2)}) collective-permute-start(f32[88,256]{1,0:T(8,128)S(1)} %get-tuple-element.34), channel_id=1, source_target_pairs={{0,8},{4,12},{8,0},{12,4},{16,24},{20,28},{24,16},{28,20},{1,9},{5... | collective-permute-start | bytes 270344 | tf_op jit(solution)/shard_map/ppermute | solution.py:24
  8.3 4.2 %collective-permute-start.1 = (f32[24,128]{1,0:T(8,128)S(1)}, f32[24,128]{1,0:T(8,128)S(1)}, u32[]{:S(2)}, u32[]{:S(2)}) collective-permute-start(f32[24,128]{1,0:T(8,128)S(1)} %get-tuple-element.30), channel_id=1, source_target_pairs={{1,2},{3,4},{5,6},{7,8},{9,10},{11,12},{13,14},{15,16},{17,18},{19... | collective-permute-start | bytes 36872 | tf_op jit(solution)/shard_map/ppermute | solution.py:31
  12.6 0.0 collective-permute-start
  12.6 1.9 %prepare.1 = (f32[4,16,128]{2,1,0:T(8,128)S(1)}, f32[16,128]{1,0:T(8,128)S(1)}, f32[16,128]{1,0:T(8,128)S(1)}, f32[16,128]{1,0:T(8,128)S(1)}, bf16[2048,256]{1,0...) custom-call(f32[4,16,128]{2,1,0:T(8,128)} %r_in.3, ...), custom_call_target="tpu_custom_call" | custom-call | flops 1 | bytes 1 | tf_op jit(solution)/shard_map/prepare/pallas_call | solution.py:500
  14.5 0.9 %collective-permute-done.1.refs_4_.from_second = f32[24,128]{1,0:T(8,128)S(1)} collective-permute-done((f32[24,128]{1,0:T(8,128)S(1)}, f32[24,128]{1,0:T(8,128)S(1)}, u32[]{:S(2)}, u32[]{:S(2)}) %collective-permute-start.1) | collective-permute-done | bytes 12320 | tf_op jit(solution)/shard_map/ppermute | solution.py:31
  15.4 0.8 %collective-permute-done.refs_3_.from_first = f32[24,128]{1,0:T(8,128)S(1)} collective-permute-done((f32[24,128]{1,0:T(8,128)S(1)}, f32[24,128]{1,0:T(8,128)S(1)}, u32[]{:S(2)}, u32[]{:S(2)}) %collective-permute-start) | collective-permute-done | bytes 12320 | tf_op jit(solution)/shard_map/ppermute | solution.py:29
  16.2 0.0 collective-permute-done.4.refs_2_
  16.3 0.0 collective-permute-done.3.refs_1_
  16.3 0.0 collective-permute-done.2.refs_0_
  16.3 1.6 %collective-permute-start.13 = (f32[264,256]{1,0:T(8,128)S(1)}, f32[264,256]{1,0:T(8,128)S(1)}, u32[]{:S(2)}, u32[]{:S(2)}) collective-permute-start(f32[264,256]{1,0:T(8,128)S(1)} %stack.1.refs_0_.refs_1_), channel_id=1, source_target_pairs={{0,3},{1,2},{2,1},{3,0},{4,7},{5,6},{6,5},{7,4},{8,11},{9,10},{10,... | collective-permute-start | bytes 811016 | tf_op jit(solution)/shard_map/ppermute | solution.py:24
  17.9 0.4 collective-permute-start.12
  18.3 1.6 %collective-permute-start.11 = (f32[264,256]{1,0:T(8,128)S(1)}, f32[264,256]{1,0:T(8,128)S(1)}, u32[]{:S(2)}, u32[]{:S(2)}) collective-permute-start(f32[264,256]{1,0:T(8,128)S(1)} %stack.1.refs_0_.refs_1_), channel_id=1, source_target_pairs={{0,1},{1,0},{2,3},{3,2},{4,5},{5,4},{6,7},{7,6},{8,9},{9,8},{10,11... | collective-permute-start | bytes 811016 | tf_op jit(solution)/shard_map/ppermute | solution.py:24
  19.8 1.0 %restrict.1 = (f32[64,128]{1,0:T(8,128)S(1)}, f32[4,16,128]{2,1,0:T(8,128)S(1)}) custom-call(f32[4,16,128]{2,1,0:T(8,128)S(1)} %get-tuple-element.25.r, f32[16,128]{1,0:T(8,128)S(1)} %get-tuple-element.26.b, f32[16,128]{1,0:T(8,128)S(1)} %get-tuple-element.27.e, f32[16,128]{1,0:T(8,128)S(1)} %get-tuple-element.28.n, ...), custom_call_target="tpu_custom_call" | custom-call | flops 1 | bytes 1 | tf_op jit(solution)/shard_map/restrict/pallas_call | solution.py:519
  20.8 0.1 collective-permute-start.5
  20.9 1.2 %collective-permute-done.5 = f32[64,128]{1,0:T(8,128)S(1)} collective-permute-done((f32[64,128]{1,0:T(8,128)S(1)}, f32[64,128]{1,0:T(8,128)S(1)}, u32[]{:S(2)}, u32[]{:S(2)}) %collective-permute-start.5) | collective-permute-done | bytes 32800 | tf_op jit(solution)/shard_map/ppermute | solution.py:24
  22.1 0.7 %collective-permute-start.6 = (f32[64,128]{1,0:T(8,128)S(1)}, f32[64,128]{1,0:T(8,128)S(1)}, u32[]{:S(2)}, u32[]{:S(2)}) collective-permute-start(f32[64,128]{1,0:T(8,128)S(1)} %add.18), channel_id=1, source_target_pairs={{0,8},{4,12},{8,0},{12,4},{16,24},{20,28},{24,16},{28,20},{1,9},{5... | collective-permute-start | bytes 98312 | tf_op jit(solution)/shard_map/ppermute | solution.py:24
  22.9 3.2 %collective-permute-done.6 = f32[64,128]{1,0:T(8,128)S(1)} collective-permute-done((f32[64,128]{1,0:T(8,128)S(1)}, f32[64,128]{1,0:T(8,128)S(1)}, u32[]{:S(2)}, u32[]{:S(2)}) %collective-permute-start.6) | collective-permute-done | bytes 32800 | tf_op jit(solution)/shard_map/ppermute | solution.py:24
  26.0 1.8 %collective-permute-start.7 = (f32[64,128]{1,0:T(8,128)S(1)}, f32[64,128]{1,0:T(8,128)S(1)}, u32[]{:S(2)}, u32[]{:S(2)}) collective-permute-start(f32[64,128]{1,0:T(8,128)S(1)} %add.19), channel_id=1, source_target_pairs={{0,16},{4,20},{8,24},{12,28},{16,0},{20,4},{24,8},{28,12},{1,17},{... | collective-permute-start | bytes 98312 | tf_op jit(solution)/shard_map/ppermute | solution.py:24
  27.9 3.3 %collective-permute-done.7 = f32[64,128]{1,0:T(8,128)S(1)} collective-permute-done((f32[64,128]{1,0:T(8,128)S(1)}, f32[64,128]{1,0:T(8,128)S(1)}, u32[]{:S(2)}, u32[]{:S(2)}) %collective-permute-start.7) | collective-permute-done | bytes 32800 | tf_op jit(solution)/shard_map/ppermute | solution.py:24
  31.2 0.0 collective-permute-done.13.refs_2_
  31.2 0.0 collective-permute-done.12.refs_1_
  31.2 0.0 collective-permute-done.11.refs_0_
  31.2 0.1 collective-permute-start.14
  31.3 1.6 %collective-permute-start.10 = (f32[64,128]{1,0:T(8,128)S(1)}, f32[64,128]{1,0:T(8,128)S(1)}, u32[]{:S(2)}, u32[]{:S(2)}) collective-permute-start(f32[64,128]{1,0:T(8,128)S(1)} %add.20.refs_2_.refs_3_), channel_id=1, source_target_pairs={{0,3},{1,2},{2,1},{3,0},{4,7},{5,6},{6,5},{7,4},{8,11},{9,10},{10,... | collective-permute-start | bytes 98312 | tf_op jit(solution)/shard_map/ppermute | solution.py:24
  32.9 0.4 collective-permute-start.9
  33.3 1.6 %collective-permute-start.8 = (f32[64,128]{1,0:T(8,128)S(1)}, f32[64,128]{1,0:T(8,128)S(1)}, u32[]{:S(2)}, u32[]{:S(2)}) collective-permute-start(f32[64,128]{1,0:T(8,128)S(1)} %add.20.refs_2_.refs_3_), channel_id=1, source_target_pairs={{0,1},{1,0},{2,3},{3,2},{4,5},{5,4},{6,7},{7,6},{8,9},{9,8},{10,11... | collective-permute-start | bytes 98312 | tf_op jit(solution)/shard_map/ppermute | solution.py:24
  34.9 0.0 collective-permute-start.16
  34.9 1.4 %collective-permute-done.10 = f32[64,128]{1,0:T(8,128)S(1)} collective-permute-done((f32[64,128]{1,0:T(8,128)S(1)}, f32[64,128]{1,0:T(8,128)S(1)}, u32[]{:S(2)}, u32[]{:S(2)}) %collective-permute-start.10) | collective-permute-done | bytes 32800 | tf_op jit(solution)/shard_map/ppermute | solution.py:24
  36.3 0.0 collective-permute-start.17
  36.3 0.5 %collective-permute-done.9 = f32[64,128]{1,0:T(8,128)S(1)} collective-permute-done((f32[64,128]{1,0:T(8,128)S(1)}, f32[64,128]{1,0:T(8,128)S(1)}, u32[]{:S(2)}, u32[]{:S(2)}) %collective-permute-start.9) | collective-permute-done | bytes 32800 | tf_op jit(solution)/shard_map/ppermute | solution.py:24
  36.9 0.0 collective-permute-start.18
  36.9 0.4 collective-permute-done.8
  37.2 0.1 collective-permute-start.15
  37.4 0.0 collective-permute-done.16.refs_8_
  37.4 0.5 collective-permute-done.17.refs_9_
  37.8 0.6 %collective-permute-done.18.refs_10_ = f32[264,256]{1,0:T(8,128)S(1)} collective-permute-done((f32[264,256]{1,0:T(8,128)S(1)}, f32[264,256]{1,0:T(8,128)S(1)}, u32[]{:S(2)}, u32[]{:S(2)}) %collective-permute-start.18) | collective-permute-done | bytes 270368 | tf_op jit(solution)/shard_map/ppermute | solution.py:24
  38.4 0.4 collective-permute-done.15.refs_7_
  38.8 0.0 collective-permute-done.14.refs_6_
  38.8 5.1 %coarse.1 = (f32[4,16,128]{2,1,0:T(8,128)S(1)}, f32[4,256]{1,0:T(4,128)}, f32[8,128]{1,0:T(8,128)S(1)}, f32[8,128]{1,0:T(8,128)S(1)}) custom-call(f32[64,128]{1,0:T(8,128)S(1)} %add_add_fusion.refs_0_, f32[352,256]{1,0:T(8,128)S(1)} %get-tuple-element.37.refs_1_, f32[264,256]{1,0:T(8,128)S(1)} %get-tuple-element.38.refs_2_, ...), custom_call_target="tpu_custom_call" | custom-call | flops 1 | bytes 1 | tf_op jit(solution)/shard_map/coarse/pallas_call | solution.py:542
  43.9 1.6 %collective-permute-start.19 = (f32[8,128]{1,0:T(8,128)S(1)}, f32[8,128]{1,0:T(8,128)S(1)}, u32[]{:S(2)}, u32[]{:S(2)}) collective-permute-start(f32[8,128]{1,0:T(8,128)S(1)} %get-tuple-element.45), channel_id=1, source_target_pairs={{0,1},{1,0},{2,3},{3,2},{4,5},{5,4},{6,7},{7,6},{8,9},{9,8},{10,11... | collective-permute-start | bytes 12296 | tf_op jit(solution)/shard_map/ppermute | solution.py:29
  45.5 2.7 %collective-permute-start.20 = (f32[8,128]{1,0:T(8,128)S(1)}, f32[8,128]{1,0:T(8,128)S(1)}, u32[]{:S(2)}, u32[]{:S(2)}) collective-permute-start(f32[8,128]{1,0:T(8,128)S(1)} %get-tuple-element.46), channel_id=1, source_target_pairs={{1,2},{3,4},{5,6},{7,8},{9,10},{11,12},{13,14},{15,16},{17,18},{19... | collective-permute-start | bytes 12296 | tf_op jit(solution)/shard_map/ppermute | solution.py:31
  48.2 0.0 collective-permute-done.19.y_first
  48.2 3.9 %collective-permute-done.20.y_second = f32[8,128]{1,0:T(8,128)S(1)} collective-permute-done((f32[8,128]{1,0:T(8,128)S(1)}, f32[8,128]{1,0:T(8,128)S(1)}, u32[]{:S(2)}, u32[]{:S(2)}) %collective-permute-start.20) | collective-permute-done | bytes 4128 | tf_op jit(solution)/shard_map/ppermute | solution.py:31
  52.1 0.8 %post.1 = f32[4,16,128]{2,1,0:T(8,128)} custom-call(f32[4,16,128]{2,1,0:T(8,128)S(1)} %get-tuple-element.25.r, f32[16,128]{1,0:T(8,128)S(1)} %get-tuple-element.26.b, f32[16,128]{1,0:T(8,128)S(1)} %get-tuple-element.27.e, f32[16,128]{1,0:T(8,128)S(1)} %get-tuple-element.28.n, f32[24,128]{1,0:T(8,128)S(1)} %collective-permute-done.refs_3_.from_first, ...), custom_call_target="tpu_custom_call" | custom-call | flops 1 | bytes 1 | tf_op jit(solution)/shard_map/post/pallas_call | solution.py:554
  (7 shorter events, 0.1 us)
Async XLA Ops:
  2.6 13.7 %collective-permute-start.4 = (f32[88,256]{1,0:T(8,128)S(1)}, f32[88,256]{1,0:T(8,128)S(1)}, u32[]{:S(2)}, u32[]{:S(2)}) collective-permute-start(f32[88,256]{1,0:T(8,128)S(1)} %get-tuple-element.34), channel_id=1, source_target_pairs={{0,24},{4,28},{8,16},{12,20},{16,8},{20,12},{24,0},{28,4},{1,25},{... | collective-permute-start | bytes 270344 | tf_op jit(solution)/shard_map/ppermute | solution.py:24
  7.7 8.6 %collective-permute-start.3 = (f32[88,256]{1,0:T(8,128)S(1)}, f32[88,256]{1,0:T(8,128)S(1)}, u32[]{:S(2)}, u32[]{:S(2)}) collective-permute-start(f32[88,256]{1,0:T(8,128)S(1)} %get-tuple-element.34), channel_id=1, source_target_pairs={{0,16},{4,20},{8,24},{12,28},{16,0},{20,4},{24,8},{28,12},{1,17},{... | collective-permute-start | bytes 270344 | tf_op jit(solution)/shard_map/ppermute | solution.py:24
  7.7 8.6 %collective-permute-start.2 = (f32[88,256]{1,0:T(8,128)S(1)}, f32[88,256]{1,0:T(8,128)S(1)}, u32[]{:S(2)}, u32[]{:S(2)}) collective-permute-start(f32[88,256]{1,0:T(8,128)S(1)} %get-tuple-element.34), channel_id=1, source_target_pairs={{0,8},{4,12},{8,0},{12,4},{16,24},{20,28},{24,16},{28,20},{1,9},{5... | collective-permute-start | bytes 270344 | tf_op jit(solution)/shard_map/ppermute | solution.py:24
  8.3 7.1 %collective-permute-start.1 = (f32[24,128]{1,0:T(8,128)S(1)}, f32[24,128]{1,0:T(8,128)S(1)}, u32[]{:S(2)}, u32[]{:S(2)}) collective-permute-start(f32[24,128]{1,0:T(8,128)S(1)} %get-tuple-element.30), channel_id=1, source_target_pairs={{1,2},{3,4},{5,6},{7,8},{9,10},{11,12},{13,14},{15,16},{17,18},{19... | collective-permute-start | bytes 36872 | tf_op jit(solution)/shard_map/ppermute | solution.py:31
  12.6 3.7 %collective-permute-start = (f32[24,128]{1,0:T(8,128)S(1)}, f32[24,128]{1,0:T(8,128)S(1)}, u32[]{:S(2)}, u32[]{:S(2)}) collective-permute-start(f32[24,128]{1,0:T(8,128)S(1)} %get-tuple-element.29.after), channel_id=1, source_target_pairs={{0,1},{1,0},{2,3},{3,2},{4,5},{5,4},{6,7},{7,6},{8,9},{9,8},{10,11... | collective-permute-start | bytes 36872 | tf_op jit(solution)/shard_map/ppermute | solution.py:29
  16.3 14.9 %collective-permute-start.13 = (f32[264,256]{1,0:T(8,128)S(1)}, f32[264,256]{1,0:T(8,128)S(1)}, u32[]{:S(2)}, u32[]{:S(2)}) collective-permute-start(f32[264,256]{1,0:T(8,128)S(1)} %stack.1.refs_0_.refs_1_), channel_id=1, source_target_pairs={{0,3},{1,2},{2,1},{3,0},{4,7},{5,6},{6,5},{7,4},{8,11},{9,10},{10,... | collective-permute-start | bytes 811016 | tf_op jit(solution)/shard_map/ppermute | solution.py:24
  17.9 13.3 %collective-permute-start.12 = (f32[264,256]{1,0:T(8,128)S(1)}, f32[264,256]{1,0:T(8,128)S(1)}, u32[]{:S(2)}, u32[]{:S(2)}) collective-permute-start(f32[264,256]{1,0:T(8,128)S(1)} %stack.1.refs_0_.refs_1_), channel_id=1, source_target_pairs={{0,2},{1,3},{2,0},{3,1},{4,6},{5,7},{6,4},{7,5},{8,10},{9,11},{10,... | collective-permute-start | bytes 811016 | tf_op jit(solution)/shard_map/ppermute | solution.py:24
  18.3 12.9 %collective-permute-start.11 = (f32[264,256]{1,0:T(8,128)S(1)}, f32[264,256]{1,0:T(8,128)S(1)}, u32[]{:S(2)}, u32[]{:S(2)}) collective-permute-start(f32[264,256]{1,0:T(8,128)S(1)} %stack.1.refs_0_.refs_1_), channel_id=1, source_target_pairs={{0,1},{1,0},{2,3},{3,2},{4,5},{5,4},{6,7},{7,6},{8,9},{9,8},{10,11... | collective-permute-start | bytes 811016 | tf_op jit(solution)/shard_map/ppermute | solution.py:24
  20.8 1.3 %collective-permute-start.5 = (f32[64,128]{1,0:T(8,128)S(1)}, f32[64,128]{1,0:T(8,128)S(1)}, u32[]{:S(2)}, u32[]{:S(2)}) collective-permute-start(f32[64,128]{1,0:T(8,128)S(1)} %get-tuple-element.35), channel_id=1, source_target_pairs={{0,4},{4,0},{8,12},{12,8},{16,20},{20,16},{24,28},{28,24},{1,5},{5... | collective-permute-start | bytes 98312 | tf_op jit(solution)/shard_map/ppermute | solution.py:24
  22.1 3.9 %collective-permute-start.6 = (f32[64,128]{1,0:T(8,128)S(1)}, f32[64,128]{1,0:T(8,128)S(1)}, u32[]{:S(2)}, u32[]{:S(2)}) collective-permute-start(f32[64,128]{1,0:T(8,128)S(1)} %add.18), channel_id=1, source_target_pairs={{0,8},{4,12},{8,0},{12,4},{16,24},{20,28},{24,16},{28,20},{1,9},{5... | collective-permute-start | bytes 98312 | tf_op jit(solution)/shard_map/ppermute | solution.py:24
  26.0 5.2 %collective-permute-start.7 = (f32[64,128]{1,0:T(8,128)S(1)}, f32[64,128]{1,0:T(8,128)S(1)}, u32[]{:S(2)}, u32[]{:S(2)}) collective-permute-start(f32[64,128]{1,0:T(8,128)S(1)} %add.19), channel_id=1, source_target_pairs={{0,16},{4,20},{8,24},{12,28},{16,0},{20,4},{24,8},{28,12},{1,17},{... | collective-permute-start | bytes 98312 | tf_op jit(solution)/shard_map/ppermute | solution.py:24
  31.2 7.6 %collective-permute-start.14 = (f32[352,256]{1,0:T(8,128)S(1)}, f32[352,256]{1,0:T(8,128)S(1)}, u32[]{:S(2)}, u32[]{:S(2)}) collective-permute-start(f32[352,256]{1,0:T(8,128)S(1)} %get-tuple-element.37.refs_1_), channel_id=1, source_target_pairs={{0,4},{4,0},{8,12},{12,8},{16,20},{20,16},{24,28},{28,24},{1,5},{5... | collective-permute-start | bytes 1081352 | tf_op jit(solution)/shard_map/ppermute | solution.py:24
  31.3 5.0 %collective-permute-start.10 = (f32[64,128]{1,0:T(8,128)S(1)}, f32[64,128]{1,0:T(8,128)S(1)}, u32[]{:S(2)}, u32[]{:S(2)}) collective-permute-start(f32[64,128]{1,0:T(8,128)S(1)} %add.20.refs_2_.refs_3_), channel_id=1, source_target_pairs={{0,3},{1,2},{2,1},{3,0},{4,7},{5,6},{6,5},{7,4},{8,11},{9,10},{10,... | collective-permute-start | bytes 98312 | tf_op jit(solution)/shard_map/ppermute | solution.py:24
  32.9 3.9 %collective-permute-start.9 = (f32[64,128]{1,0:T(8,128)S(1)}, f32[64,128]{1,0:T(8,128)S(1)}, u32[]{:S(2)}, u32[]{:S(2)}) collective-permute-start(f32[64,128]{1,0:T(8,128)S(1)} %add.20.refs_2_.refs_3_), channel_id=1, source_target_pairs={{0,2},{1,3},{2,0},{3,1},{4,6},{5,7},{6,4},{7,5},{8,10},{9,11},{10,... | collective-permute-start | bytes 98312 | tf_op jit(solution)/shard_map/ppermute | solution.py:24
  33.3 3.9 %collective-permute-start.8 = (f32[64,128]{1,0:T(8,128)S(1)}, f32[64,128]{1,0:T(8,128)S(1)}, u32[]{:S(2)}, u32[]{:S(2)}) collective-permute-start(f32[64,128]{1,0:T(8,128)S(1)} %add.20.refs_2_.refs_3_), channel_id=1, source_target_pairs={{0,1},{1,0},{2,3},{3,2},{4,5},{5,4},{6,7},{7,6},{8,9},{9,8},{10,11... | collective-permute-start | bytes 98312 | tf_op jit(solution)/shard_map/ppermute | solution.py:24
  34.9 2.5 %collective-permute-start.16 = (f32[264,256]{1,0:T(8,128)S(1)}, f32[264,256]{1,0:T(8,128)S(1)}, u32[]{:S(2)}, u32[]{:S(2)}) collective-permute-start(f32[264,256]{1,0:T(8,128)S(1)} %get-tuple-element.39.refs_3_), channel_id=1, source_target_pairs={{0,4},{4,0},{8,12},{12,8},{16,20},{20,16},{24,28},{28,24},{1,5},{5... | collective-permute-start | bytes 811016 | tf_op jit(solution)/shard_map/ppermute | solution.py:24
  36.3 1.5 %collective-permute-start.17 = (f32[264,256]{1,0:T(8,128)S(1)}, f32[264,256]{1,0:T(8,128)S(1)}, u32[]{:S(2)}, u32[]{:S(2)}) collective-permute-start(f32[264,256]{1,0:T(8,128)S(1)} %get-tuple-element.40.refs_4_), channel_id=1, source_target_pairs={{0,4},{4,0},{8,12},{12,8},{16,20},{20,16},{24,28},{28,24},{1,5},{5... | collective-permute-start | bytes 811016 | tf_op jit(solution)/shard_map/ppermute | solution.py:24
  36.9 1.5 %collective-permute-start.18 = (f32[264,256]{1,0:T(8,128)S(1)}, f32[264,256]{1,0:T(8,128)S(1)}, u32[]{:S(2)}, u32[]{:S(2)}) collective-permute-start(f32[264,256]{1,0:T(8,128)S(1)} %get-tuple-element.41.refs_5_), channel_id=1, source_target_pairs={{0,4},{4,0},{8,12},{12,8},{16,20},{20,16},{24,28},{28,24},{1,5},{5... | collective-permute-start | bytes 811016 | tf_op jit(solution)/shard_map/ppermute | solution.py:24
  37.2 1.6 %collective-permute-start.15 = (f32[264,256]{1,0:T(8,128)S(1)}, f32[264,256]{1,0:T(8,128)S(1)}, u32[]{:S(2)}, u32[]{:S(2)}) collective-permute-start(f32[264,256]{1,0:T(8,128)S(1)} %get-tuple-element.38.refs_2_), channel_id=1, source_target_pairs={{0,4},{4,0},{8,12},{12,8},{16,20},{20,16},{24,28},{28,24},{1,5},{5... | collective-permute-start | bytes 811016 | tf_op jit(solution)/shard_map/ppermute | solution.py:24
  43.9 4.3 %collective-permute-start.19 = (f32[8,128]{1,0:T(8,128)S(1)}, f32[8,128]{1,0:T(8,128)S(1)}, u32[]{:S(2)}, u32[]{:S(2)}) collective-permute-start(f32[8,128]{1,0:T(8,128)S(1)} %get-tuple-element.45), channel_id=1, source_target_pairs={{0,1},{1,0},{2,3},{3,2},{4,5},{5,4},{6,7},{7,6},{8,9},{9,8},{10,11... | collective-permute-start | bytes 12296 | tf_op jit(solution)/shard_map/ppermute | solution.py:29
  45.5 6.6 %collective-permute-start.20 = (f32[8,128]{1,0:T(8,128)S(1)}, f32[8,128]{1,0:T(8,128)S(1)}, u32[]{:S(2)}, u32[]{:S(2)}) collective-permute-start(f32[8,128]{1,0:T(8,128)S(1)} %get-tuple-element.46), channel_id=1, source_target_pairs={{1,2},{3,4},{5,6},{7,8},{9,10},{11,12},{13,14},{15,16},{17,18},{19... | collective-permute-start | bytes 12296 | tf_op jit(solution)/shard_map/ppermute | solution.py:31

commit v3 on v2

--- a/solution.py
+++ b/solution.py
@@ -14,7 +14,7 @@
 BOTH = ("wide", "narrow")
 HALO = 3
 FIELD = 24
-PIECE = 88
+PIECE = 80
 F32 = jnp.float32
 BF16 = jnp.bfloat16
 
@@ -30,6 +30,17 @@
     odd = [(i, i + 1) for i in range(1, count - 1, 2)] + [(count - 1, 0)]
     second = lax.ppermute(to_second, BOTH, odd + [(target, source) for source, target in odd])
     return first, second
+
+
+def pair_swaps_near(to_first, to_second):
+    count = lax.axis_size(BOTH)
+    first = lax.ppermute(to_first, BOTH, [(i, i ^ 1) for i in range(count)])
+    inner = lax.ppermute(to_second, BOTH, [(i, i ^ 3) for i in range(count)])
+    outer = [(i, i + 1) for i in range(3, count - 1, 4)]
+    rest = sorted(set(range(count)) - {i for pair in outer for i in pair})
+    outer += list(zip(rest[::2], rest[1::2]))
+    outer = lax.ppermute(to_second, BOTH, outer + [(target, source) for source, target in outer])
+    return first, inner, outer
 
 
 def tie(values, after):
@@ -62,6 +73,10 @@
     return line, count
 
 
+def packed_rows(count):
+    return count * PIECE + 8 * ((count + 7) // 8)
+
+
 def lanes(shape):
     return lax.broadcasted_iota(jnp.int32, shape, len(shape) - 1)
 
@@ -99,22 +114,20 @@
     return wait
 
 
-def pack_row(matrix, inverse, links, j, put):
-    packed = jnp.concatenate([inverse[16 * t:16 * t + 16, :] for t in range(4)], axis=1)
-    lane = lanes((8, 256))
-    tail = jnp.zeros((8, 256), F32)
-    for l in range(links.shape[1]):
-        tail = jnp.where(lane == l, links[j, l].astype(F32), tail)
+def pack_row(matrix, inverse, put):
     put(0, matrix)
-    put(64, packed)
-    put(80, tail)
-
-
-def begin_kernel(r_in, b_in, e_in, n_in, first, second, r, b, e, n, sems):
-    copy_all([(r_in, r), (b_in, b), (e_in, e), (n_in, n)], sems)()
+    put(64, jnp.concatenate([inverse[16 * t:16 * t + 16, :] for t in range(4)], axis=1))
+
+
+def begin_kernel(owned, r_in, b_in, e_in, n_in, links_in, coupling_in, inverses_in, first, second, own, block,
+                 r, b, e, n, links, coupling, inverses, sems):
+    wait = copy_all([(r_in, r), (b_in, b), (e_in, e), (n_in, n), (links_in, links), (coupling_in, coupling),
+                     (inverses_in, inverses)], sems)
     grid_rows = b.shape[0]
     line, _ = place()
     even = lax.rem(line, 2) == 0
+    q = lax.rem(lax.axis_index("narrow"), owned)
+    wait()
 
     def message(start, north_start):
         parts = [r[a, start:start + HALO, :] for a in range(r.shape[0])]
@@ -131,11 +144,8 @@
         second[at:at + size, :] = jnp.where(even, low, high)
         at += size
 
-
-def pack_kernel(owned, links_in, coupling_in, inverses_in, after, own, block, links, coupling, inverses, sems):
-    del after
-    q = lax.rem(lax.axis_index("narrow"), owned)
-    copy_all([(links_in, links), (coupling_in, coupling), (inverses_in, inverses)], sems)()
+    lane, row = lanes((8, 256)), rows((8, 256))
+    tail = jnp.zeros((8, 256), F32)
     for j_rel in range(owned):
         j = jnp.bitwise_xor(q, j_rel)
 
@@ -144,22 +154,23 @@
             if base == 0:
                 own[at:at + value.shape[0], :] = value
 
-        pack_row(coupling[j], inverses[j], links, j, put)
+        pack_row(coupling[j], inverses[j], put)
+        for l in range(links.shape[1]):
+            tail = jnp.where((row == j_rel) & (lane == l), links[j, l].astype(F32), tail)
+    block[owned * PIECE:owned * PIECE + 8, :] = tail
+    own[PIECE:PIECE + 8, :] = tail
 
 
 def prepare_kernel(owned, coarse_rows, r_in, b_in, e_in, n_in, support_in, basis_in,
-                   r_out, b_out, e_out, n_out, basis_high, basis_low, hots, sup_hots,
-                   support, basis, sems, basis_sems):
+                   r_out, b_out, e_out, n_out, basis, hots, sup_hots, support, sems):
     q = lax.rem(lax.axis_index("narrow"), owned)
     mine = lax.axis_index("wide") * owned + q
-    wait = copy_all([(r_in, r_out), (b_in, b_out), (e_in, e_out), (n_in, n_out), (support_in, support)], sems)
-    parts = basis_sems.shape[0]
-    part = basis.shape[0] // parts
-    copies = [pltpu.make_async_copy(basis_in.at[pl.ds(part * i, part)], basis.at[pl.ds(part * i, part)],
-                                    basis_sems.at[i]) for i in range(parts)]
-    for copy in copies:
-        copy.start()
-    wait()
+    wait_support = copy_all([(support_in, support)], sems.at[pl.ds(0, 1)])
+    part = basis.shape[0] // 8
+    parts = [pl.ds(part * i, part) for i in range(8)]
+    wait = copy_all([(basis_in.at[at], basis.at[at]) for at in parts]
+                    + [(r_in, r_out), (b_in, b_out), (e_in, e_out), (n_in, n_out)], sems.at[pl.ds(1, 12)])
+    wait_support()
 
     blocks = support.shape[1]
     rows4 = 4 * blocks
@@ -183,16 +194,23 @@
     for k in range(4):
         sup_hots[rows4 * k:rows4 * k + rows4, :] = jnp.where(across == column[:, k:k + 1], 1.0, 0.0).astype(BF16)
 
-    for i in range(parts):
-        copies[i].wait()
-        for at in range(part * i, part * i + part, 256):
-            basis_high[at:at + 256, :], basis_low[at:at + 256, :] = split(basis[at:at + 256, :])
+    wait()
 
 
 def stack_kernel(*refs):
     fetched, gathered = refs[:-4], refs[-1]
+    count = len(fetched)
+    gathered[count * PIECE:, :] = jnp.zeros((gathered.shape[0] - count * PIECE, gathered.shape[1]), F32)
     for i, piece in enumerate(fetched):
-        gathered[PIECE * i:PIECE * i + PIECE, :] = piece[...]
+        gathered[PIECE * i:PIECE * i + PIECE, :] = piece[0:PIECE, :]
+        gathered[PIECE * count + i:PIECE * count + i + 1, :] = piece[PIECE:PIECE + 1, :]
+
+
+def add_kernel(one, two, out):
+    half = out.shape[0] // 2
+    for i in range(2):
+        block = slice(128 * i, 128 * i + 128)
+        out[half * i:half * i + half, :] = one[0:half, block] + two[0:half, block]
 
 
 class Fine:
@@ -251,6 +269,21 @@
         return x + self.scale * (self.r - self.apply(x))
 
 
+    def keep(self, r_out, coef_out):
+        r_out[...] = self.r
+        for i, value in enumerate((self.diagonal, self.scale, self.north, self.south, self.east, self.west)):
+            coef_out[i] = value
+
+
+class Kept(Fine):
+    def __init__(self, r, coef, field):
+        line, count = place()
+        self.even, self.low_ok, self.high_ok = lax.rem(line, 2) == 0, line > 0, line < count - 1
+        self.r, self.field = r[...], field
+        self.diagonal, self.scale, self.north, self.south, self.east, self.west = [coef[i] for i in range(6)]
+        self.adjoints, _, self.width = r.shape
+
+
 def fine_scratch(adjoints, width):
     return [
         pltpu.VMEM((adjoints, FIELD, width), F32),
@@ -261,8 +294,8 @@
     ]
 
 
-def restrict_kernel(coarse_rows, r, b, e, n, from_first, from_second, basis_high, basis_low, hots, *refs):
-    out, x_out, rx, bx, ex, nx, field, by_row, contrib = refs[-9:]
+def restrict_kernel(coarse_rows, r, b, e, n, from_first, from_second, basis, hots,
+                    block, gathered, out, x_out, rx, bx, ex, nx, field, by_row, contrib):
     fine = Fine(r, b, e, n, from_first, from_second, rx, bx, ex, nx, field)
     x = fine.scale * fine.r
     for step in range(SWEEPS - 1):
@@ -283,8 +316,9 @@
             parts.append(jnp.concatenate([jnp.where(upper, held, 0.0), jnp.where(upper, 0.0, held)], axis=1))
         high, low = split(jnp.concatenate(parts, axis=0))
         near = slice(256 * g, 256 * g + 256)
-        both = dot(jnp.concatenate([high, low], axis=0), basis_high[near, :])
-        contrib[16 * g:16 * g + 16, :] = both[0:16] + both[16:32] + dot(high, basis_low[near, :])
+        w_high, w_low = split(basis[near, :])
+        both = dot(jnp.concatenate([high, low], axis=0), w_high)
+        contrib[16 * g:16 * g + 16, :] = both[0:16] + both[16:32] + dot(high, w_low)
     c_high, c_low = split(contrib[...])
     weights = jnp.concatenate([
         jnp.concatenate([c_high[:, 0:128], c_low[:, 0:128]], axis=1),
@@ -296,36 +330,50 @@
     even = jnp.where(here, total[0:size], 0.0)
     odd = jnp.where(here, 0.0, total[size:2 * size])
     mid = size // 2
-    out[...] = even[0:mid] + half_turn(odd[0:mid]) + half_turn(even[mid:size]) + odd[mid:size]
-
-
-def coarse_kernel(owned, coarse_rows, zs, refs):
-    refs = list(refs)
-
-    def take(count):
-        got = refs[:count]
-        del refs[:count]
-        return got
-
-    (rhs_ref,) = take(1)
-    pieces = take(2 * (1 + owned))
-    basis_high, basis_low, sup_hots, x_ref = take(4)
-    y_ref, coarse_ref, first, second = take(4)
-    w_high, w_low, w_inv, link_rows, hots, product, u_ref, by_row = refs
+    packed = even[0:mid] + half_turn(odd[0:mid]) + half_turn(even[mid:size]) + odd[mid:size]
+    half = mid // 2
+    out[0:half, 0:128] = packed[0:half]
+    out[0:half, 128:256] = packed[half:mid]
+    out[half:half + block.shape[0], :] = block[...]
+    out[half + block.shape[0]:, :] = gathered[...]
+
+
+def prolong(group, high, low, basis):
+    near = slice(16 * group, 16 * group + 16)
+    block = slice(256 * group, 256 * group + 256)
+    high = high[near, :]
+    w_high, w_low = split(basis[block, :])
+    both = dot_t(jnp.concatenate([high, low[near, :]], axis=0), w_high)
+    got = both[0:16] + both[16:32] + dot_t(high, w_low)
+    upper = rows((8, 128)) < 4
+    halves = [jnp.where(upper, got[8 * h:8 * h + 8, 0:128], got[8 * h:8 * h + 8, 128:256]) for h in range(2)]
+    return jnp.where(lanes((8, 128)) < 64, halves[0], halves[1])
+
+
+def coarse_kernel(owned, coarse_rows, zs, rhs_ref, message, message_other, *refs):
+    spread, spread_other = refs[:owned - 1], refs[owned - 1:2 * owned - 2]
+    (basis, sup_hots, x_ref, coarse_ref, high_out, low_out, first, second,
+     w_high, w_low, w_inv, link_rows, hots, product, u_ref, by_row) = refs[2 * owned - 2:]
     size = 4 * coarse_rows
     wide, narrow = lax.axis_index("wide"), lax.axis_index("narrow")
     q = lax.rem(narrow, owned)
     mine = wide * owned + q
 
     lane16 = lanes((16, 128)) < 64
+    at_own = coarse_rows
+    at_fetched = at_own + packed_rows(owned)
     for z_rel in range(zs):
-        for c_rel in range(2):
+        for c_rel, (fetched, others) in enumerate(((message, spread), (message_other, spread_other))):
             for j_rel in range(owned):
                 i = (z_rel * 2 + c_rel) * owned + j_rel
                 if z_rel == 0:
-                    piece, base = pieces[c_rel * (1 + owned)], j_rel * PIECE
+                    piece, start, index, count = fetched, at_own, j_rel, owned
+                elif j_rel == 0:
+                    piece, start, index, count = fetched, at_fetched, z_rel - 1, zs - 1
                 else:
-                    piece, base = pieces[c_rel * (1 + owned) + 1 + j_rel], (z_rel - 1) * PIECE
+                    piece, start, index, count = others[j_rel - 1], 0, z_rel - 1, zs - 1
+                base = start + index * PIECE
+                at_links = start + count * PIECE + index
                 high, low = split(piece[base:base + 64, :])
                 w_high[64 * i:64 * i + 64, :] = high
                 w_low[64 * i:64 * i + 64, :] = low
@@ -337,7 +385,7 @@
                 high, low = split(jnp.concatenate(quarters, axis=0))
                 w_inv[64 * i:64 * i + 64, 0:128] = high
                 w_inv[64 * i:64 * i + 64, 128:256] = low
-                link_rows[4 * i:4 * i + 4, :] = piece[base + 80:base + 84, 0:128]
+                link_rows[4 * i:4 * i + 4, :] = jnp.broadcast_to(piece[at_links:at_links + 1, 0:128], (4, 128))
 
     lane = lanes((size, size))
     a_col = jnp.bitwise_and(rows((size, 1)), 3)
@@ -403,44 +451,53 @@
 
     blocks4 = sup_hots.shape[0] // 4
     high, low = pick(dot(sup_hots[...], hi_lo(u)), blocks4)
-    left = lanes((8, 128)) < 64
-    upper = rows((8, 128)) < 4
-    for g in range(blocks4 // 16):
-        near = slice(16 * g, 16 * g + 16)
-        block = slice(256 * g, 256 * g + 256)
-        both = dot_t(jnp.concatenate([high[near], low[near]], axis=0), basis_high[block, :])
-        got = both[0:16] + both[16:32] + dot_t(high[near], basis_low[block, :])
-        halves = [jnp.where(upper, got[8 * h:8 * h + 8, 0:128], got[8 * h:8 * h + 8, 128:256]) for h in range(2)]
-        by_row[8 * g:8 * g + 8, :] = jnp.where(left, halves[0], halves[1])
+    high_out[...] = high
+    low_out[...] = low
     line, _ = place()
     even = lax.rem(line, 2) == 0
     adjoints, grid_rows, _ = x_ref.shape
+    by_row[0:8, :] = prolong(0, high, low, basis)
+    by_row[8:16, :] = prolong(grid_rows // 2 - 1, high, low, basis)
     for a in range(adjoints):
-        y = x_ref[a] + by_row[pl.ds(a, grid_rows, stride=4), :]
-        y_ref[a] = y
-        top, bottom = y[0:2], y[grid_rows - 2:grid_rows]
+        edge = by_row[pl.ds(a, 4, stride=4), :]
+        top = x_ref[a, 0:2, :] + edge[0:2]
+        bottom = x_ref[a, grid_rows - 2:grid_rows, :] + edge[2:4]
         first[2 * a:2 * a + 2, :] = jnp.where(even, bottom, top)
         second[2 * a:2 * a + 2, :] = jnp.where(even, top, bottom)
 
 
-def post_kernel(r, b, e, n, from_first, from_second, y_ref, y_first, y_second, out, rx, bx, ex, nx, field, yx):
-    fine = Fine(r, b, e, n, from_first, from_second, rx, bx, ex, nx, field)
-    one, two = y_first[...], y_second[...]
+def correct_kernel(r, b, e, n, from_first, from_second, x_ref, high, low, basis,
+                   r_out, coef_out, y_out, rx, bx, ex, nx, field, by_row):
+    Fine(r, b, e, n, from_first, from_second, rx, bx, ex, nx, field).keep(r_out, coef_out)
+    adjoints, grid_rows, width = x_ref.shape
+    for g in range(grid_rows // 2):
+        by_row[8 * g:8 * g + 8, :] = prolong(g, high, low, basis)
+    for a in range(adjoints):
+        y_out[a, 0:8, :] = jnp.zeros((8, width), F32)
+        y_out[a, 16:24, :] = jnp.zeros((8, width), F32)
+        y_out[a, HALO:HALO + grid_rows, :] = x_ref[a] + by_row[pl.ds(a, grid_rows, stride=4), :]
+
+
+def post_kernel(r, coef, y_ref, y_first, y_inner, y_outer, out, field):
+    fine = Kept(r, coef, field)
+    in_line = lax.rem(place()[0], 4)
+    one, two = y_first[...], jnp.where((in_line == 1) | (in_line == 2), y_inner[...], y_outer[...])
     low = jnp.where(fine.low_ok, jnp.where(fine.even, two, one), 0.0)
     high = jnp.where(fine.high_ok, jnp.where(fine.even, one, two), 0.0)
-    top = HALO + fine.grid_rows
+    grid_rows = out.shape[1]
+    start, top = 8 + HALO, 8 + HALO + grid_rows
+    field[:, 0:8, :] = jnp.zeros((fine.adjoints, 8, fine.width), F32)
+    field[:, 32:40, :] = jnp.zeros((fine.adjoints, 8, fine.width), F32)
+    field[:, 8:32, :] = y_ref[...]
     for a in range(fine.adjoints):
-        yx[a, 0:8, :] = jnp.zeros((8, fine.width), F32)
-        yx[a, 16:24, :] = jnp.zeros((8, fine.width), F32)
-        yx[a, HALO - 2:HALO, :] = low[2 * a:2 * a + 2]
-        yx[a, HALO:top, :] = y_ref[a]
-        yx[a, top:top + 2, :] = high[2 * a:2 * a + 2]
-    x = yx[...]
+        field[a, start - 2:start, :] = low[2 * a:2 * a + 2]
+        field[a, top:top + 2, :] = high[2 * a:2 * a + 2]
+    x = field[:, 8:32, :]
     for step in range(SWEEPS):
         x = fine.sweep(x)
     field[:, 8:32, :] = x
     for a in range(fine.adjoints):
-        out[a] = field[a, 8 + HALO:8 + HALO + fine.grid_rows, :]
+        out[a] = field[a, start:top, :]
 
 
 def shape(*dims, kind=F32):
@@ -474,90 +531,83 @@
     message = shape(24, width)
     fine_inputs = tuple(map(stay, (right_sides, brinkman, east_faces, north_faces)))
     coarse_inputs = tuple(map(stay, (links, coarse_coupling, coarse_block_inverses)))
-    to_first, to_second = pl.pallas_call(
-        begin_kernel,
-        out_shape=(message, message),
-        in_specs=[in_hbm] * 4,
+    to_first, to_second, own, block = pl.pallas_call(
+        functools.partial(begin_kernel, owned),
+        out_shape=(message, message, shape(packed_rows(1), 256), shape(packed_rows(owned), 256)),
+        in_specs=[in_hbm] * 7,
         scratch_shapes=[
             pltpu.VMEM((adjoints, *row_dims), F32), pltpu.VMEM(row_dims, F32), pltpu.VMEM(row_dims, F32),
-            pltpu.VMEM(row_dims, F32), pltpu.SemaphoreType.DMA((4,))],
+            pltpu.VMEM(row_dims, F32), pltpu.SMEM(links.shape, jnp.int32), pltpu.VMEM(coarse_coupling.shape, F32),
+            pltpu.VMEM(coarse_block_inverses.shape, F32), pltpu.SemaphoreType.DMA((7,))],
         cost_estimate=CHEAP, compiler_params=params(16), name="begin",
-    )(*fine_inputs)
+    )(*fine_inputs, *coarse_inputs)
     from_first, from_second = pair_swaps(to_first, to_second)
-
-    own, block = pl.pallas_call(
-        functools.partial(pack_kernel, owned),
-        out_shape=(shape(PIECE, 256), shape(owned * PIECE, 256)),
-        in_specs=[in_hbm] * 3 + [anywhere],
-        scratch_shapes=[
-            pltpu.SMEM(links.shape, jnp.int32), pltpu.VMEM(coarse_coupling.shape, F32),
-            pltpu.VMEM(coarse_block_inverses.shape, F32), pltpu.SemaphoreType.DMA((3,))],
-        cost_estimate=CHEAP, compiler_params=params(16), name="pack",
-    )(*coarse_inputs, to_first)
     fetched = [swap(own, "wide", 2 * k) for k in range(1, zs)]
 
     rows4 = adjoints * blocks
-    r, b, e, n, basis_high, basis_low, hots, sup_hots = pl.pallas_call(
+    r, b, e, n, basis, hots, sup_hots = pl.pallas_call(
         functools.partial(prepare_kernel, owned, coarse_rows),
-        out_shape=(shape(adjoints, *row_dims), shape(*row_dims), shape(*row_dims),
-                   shape(*row_dims), shape(*basis.shape, kind=BF16), shape(*basis.shape, kind=BF16),
-                   shape(2 * size, 2 * rows4, kind=BF16), shape(4 * rows4, size, kind=BF16)),
+        out_shape=(shape(adjoints, *row_dims), shape(*row_dims), shape(*row_dims), shape(*row_dims),
+                   shape(*basis.shape), shape(2 * size, 2 * rows4, kind=BF16), shape(4 * rows4, size, kind=BF16)),
         in_specs=[in_hbm] * 6,
-        scratch_shapes=[
-            pltpu.VMEM((4, blocks), jnp.int32),
-            pltpu.VMEM(basis.shape, F32), pltpu.SemaphoreType.DMA((5,)), pltpu.SemaphoreType.DMA((4,))],
-        cost_estimate=CHEAP, compiler_params=params(24), name="prepare",
+        scratch_shapes=[pltpu.VMEM((4, blocks), jnp.int32), pltpu.SemaphoreType.DMA((13,))],
+        cost_estimate=CHEAP, compiler_params=params(16), name="prepare",
     )(*fine_inputs, stay(support.T), stay(basis))
 
     gathered = pl.pallas_call(
-        stack_kernel, out_shape=shape((zs - 1) * PIECE, 256),
+        stack_kernel, out_shape=shape(packed_rows(zs - 1), 256),
         in_specs=[in_vmem] * (zs - 1) + [anywhere] * 3,
         cost_estimate=CHEAP, compiler_params=params(4), name="stack",
     )(*fetched, from_first, from_second, hots)
     spread = [swap(gathered, "narrow", k) for k in range(1, owned)]
 
-    rhs, x = pl.pallas_call(
+    half = coarse_rows
+    message, x = pl.pallas_call(
         functools.partial(restrict_kernel, coarse_rows),
-        out_shape=(shape(size // 2, 128), shape(adjoints, *row_dims)),
+        out_shape=(shape(half + packed_rows(owned) + packed_rows(zs - 1), 256), shape(adjoints, *row_dims)),
         scratch_shapes=fine_scratch(adjoints, width) + [
             pltpu.VMEM((4 * grid_rows, width), F32), pltpu.VMEM((rows4, 256), F32)],
-        in_specs=[in_vmem] * 9 + [anywhere],
         cost_estimate=CHEAP, compiler_params=params(16), name="restrict",
-    )(r, b, e, n, from_first, from_second, basis_high, basis_low, hots, gathered)
-
-    rhs = rhs + swap(rhs, "wide", 1)
+    )(r, b, e, n, from_first, from_second, basis, hots, block, gathered)
+
+    message_other = swap(message, "wide", 1)
+    rhs = pl.pallas_call(
+        add_kernel, out_shape=shape(2 * half, 128), cost_estimate=CHEAP, compiler_params=params(4), name="add",
+    )(message, message_other)
     for bit in bits_of(zs):
         rhs = rhs + swap(rhs, "wide", 2 * bit)
-    block, gathered_late = tie([block, gathered], rhs)
-    block_other = swap(block, "wide", 1)
-    gathered_other = swap(gathered_late, "wide", 1)
     spread = tie(spread, rhs)
+    spread_other = [swap(piece, "wide", 1) for piece in spread]
     for masks in rounds_of(lax.axis_size("narrow")):
         rhs = sum([swap(rhs, "narrow", k) for k in masks], rhs)
-    pieces = [block, gathered_late] + spread + [block_other, gathered_other] + [swap(piece, "wide", 1) for piece in spread]
-
-    def coarse_body(*refs):
-        coarse_kernel(owned, coarse_rows, zs, refs)
-
-    y, coarse, y_first, y_second = pl.pallas_call(
-        coarse_body,
-        out_shape=(shape(adjoints, *row_dims), shape(owned, 256), shape(8, width), shape(8, width)),
+
+    near = shape(rows4, 256, kind=BF16)
+    coarse, high, low, y_first, y_second = pl.pallas_call(
+        functools.partial(coarse_kernel, owned, coarse_rows, zs),
+        out_shape=(shape(owned, 256), near, near, shape(8, width), shape(8, width)),
         scratch_shapes=[
             pltpu.VMEM((64 * coarse_rows, 256), BF16), pltpu.VMEM((64 * coarse_rows, 256), BF16),
             pltpu.VMEM((64 * coarse_rows, 256), BF16), pltpu.VMEM((size, 128), F32),
             pltpu.VMEM((4 * size, size), BF16), pltpu.VMEM((size, 256), F32),
-            pltpu.VMEM((4 * owned, 128), F32), pltpu.VMEM((4 * grid_rows, width), F32)],
+            pltpu.VMEM((4 * owned, 128), F32), pltpu.VMEM((16, width), F32)],
         cost_estimate=CHEAP, compiler_params=params(min(48, 8 + coarse_rows // 3)), name="coarse",
-    )(rhs, *pieces, basis_high, basis_low, sup_hots, x)
-
-    y_first, y_second = pair_swaps(y_first, y_second)
-    solution_field = pl.pallas_call(
+    )(rhs, message, message_other, *spread, *spread_other, basis, sup_hots, x)
+
+    y_from = pair_swaps_near(y_first, y_second)
+    extended = shape(adjoints, FIELD, width)
+    r, coef, y = pl.pallas_call(
+        correct_kernel,
+        out_shape=(extended, shape(6, FIELD, width), extended),
+        scratch_shapes=fine_scratch(adjoints, width) + [pltpu.VMEM((4 * grid_rows, width), F32)],
+        cost_estimate=CHEAP, compiler_params=params(16), name="correct",
+    )(r, b, e, n, from_first, from_second, x, high, low, basis)
+    field = pl.pallas_call(
         post_kernel,
-        out_shape=shape(adjoints, grid_rows, width),
-        scratch_shapes=fine_scratch(adjoints, width) + [pltpu.VMEM((adjoints, FIELD, width), F32)],
+        out_shape=shape(adjoints, *row_dims),
+        scratch_shapes=[pltpu.VMEM((adjoints, 40, width), F32)],
         cost_estimate=CHEAP, compiler_params=params(16), name="post",
-    )(r, b, e, n, from_first, from_second, y, y_first, y_second)
-    return solution_field, coarse
+    )(r, coef, y, *y_from)
+    return field, coarse
 
 
 def solution(mesh):

time: 53.2 us -> 48.2 us (0.906)
  waiting for transfers between devices: 17.1 us -> 14.9 us
  starting transfers between devices: 24.3 us -> 22.2 us
  Pallas kernels: 10.8 us -> 10.2 us
    ppermute x2 -> x1, starting transfers between devices: 6.94 us -> 2.85 us  [pair_swaps(): lax.ppermute(to_second, BOTH, odd + [(target, source) for source, target...]
    ppermute x0 -> x3, waiting for transfers between devices: none -> 3.09 us  [the longest x1 1.81 us: pair_swaps_near(): inner = lax.ppermute(to_second, BOTH, [(i, i ^ 3) for i in range(count)])]
    ppermute x0 -> x3, starting transfers between devices: none -> 2.74 us  [the longest x1 1.12 us: pair_swaps_near(): first = lax.ppermute(to_first, BOTH, [(i, i ^ 1) for i in range(count)])]
    ppermute x2 -> x1, waiting for transfers between devices: 4.86 us -> 2.31 us  [pair_swaps(): lax.ppermute(to_second, BOTH, odd + [(target, source) for source, target...]
    ppermute x17 -> x15, waiting for transfers between devices: 11.4 us -> 9.52 us  [swap(): return lax.ppermute(value, axis, [(i, i ^ bits) for i in range(size)])]
    ppermute x2 -> x1, waiting for transfers between devices: 0.83 us -> 0.01 us  [pair_swaps(): first = lax.ppermute(to_first, BOTH, [(i, i ^ 1) for i in range(count)])]
    ppermute x17 -> x15, starting transfers between devices: 15.7 us -> 15 us  [swap(): return lax.ppermute(value, axis, [(i, i ^ bits) for i in range(size)])]
    pallas_call x5 -> x6, Pallas kernels: 7.87 us -> 7.54 us  [the longest x1 4.76 us: body(): pl.pallas_call(functools.partial(coarse_kernel, owned, coarse_rows, zs),...]
  transfers between devices with their start and end apart: 21 -> 20, of which waited for: 12 -> 10; matrix products, arithmetic and copies ran while one was open for 0% -> 0% of each run, Pallas kernels for 5% -> 5%
where the time goes in v3:
time: 48.2 us; the launch traced here: 48.1 us
  starting transfers between devices  22.2 us (46%)
  waiting for transfers between devices  14.9 us (31%)
  Pallas kernels  10.2 us (21%)
  between operations  0.73 us (2%)
    ppermute x15, starting transfers between devices, swap(): return lax.ppermute(value, axis, [(i, i ^ bits) for i in range(size)])  15 us
    ppermute x15, waiting for transfers between devices, swap(): return lax.ppermute(value, axis, [(i, i ^ bits) for i in range(size)])  9.52 us
    pallas_call x1, Pallas kernels, body(): pl.pallas_call(functools.partial(coarse_kernel, owned, coarse_rows, zs),...  4.76 us
    ppermute x1, starting transfers between devices, pair_swaps(): lax.ppermute(to_second, BOTH, odd + [(target, source) for source, target...  2.85 us
    ppermute x1, waiting for transfers between devices, pair_swaps(): lax.ppermute(to_second, BOTH, odd + [(target, source) for source, target...  2.31 us
    ppermute x1, waiting for transfers between devices, pair_swaps_near(): inner = lax.ppermute(to_second, BOTH, [(i, i ^ 3) for i in range(count)])  1.81 us
    pallas_call x1, Pallas kernels, body(): pl.pallas_call(functools.partial(prepare_kernel, owned, coarse_rows), out...  1.64 us
    ppermute x1, starting transfers between devices, pair_swaps(): first = lax.ppermute(to_first, BOTH, [(i, i ^ 1) for i in range(count)])  1.63 us
  transfers between devices with their start and end apart: 20, of which 10 were waited for; matrix products, arithmetic and copies ran while one was open for 0% of the time, Pallas kernels for 5%

profile of v3, /device:TPU:0, one launch (start us, length us, event | category | flops | bytes accessed | tf_op | source)
XLA Modules:
  0.0 48.1 jit_solution(8777471417785620453)
XLA Ops:
  0.6 1.2 %begin.1 = (f32[24,128]{1,0:T(8,128)S(1)}, f32[24,128]{1,0:T(8,128)S(1)}, f32[88,256]{1,0:T(8,128)S(1)}, f32[328,256]{1,0:T(8,128)S(1)}) custom-call(f32[4,16,128]{2,1,0:T(8,128)} %r_in.3, f32[16,128]{1,0:T(8,128)} %b_in.3, f32[16,128]{1,0:T(8,128)} %e_in.3, f32[16,128]{1,0:T(8,128)} %n_in.3, s32[4,4]{1,0:T(4,128)} %links_in.1, f32[4,64,256]{2,1,0:T(8,128)} %coupling_in.1, ...), custom_call_target="tpu_custom_call" | custom-call | flops 1 | bytes 1 | tf_op jit(solution)/shard_map/begin/pallas_call | solution.py:534
  1.9 5.1 %collective-permute-start.4 = (f32[88,256]{1,0:T(8,128)S(1)}, f32[88,256]{1,0:T(8,128)S(1)}, u32[]{:S(2)}, u32[]{:S(2)}) collective-permute-start(f32[88,256]{1,0:T(8,128)S(1)} %get-tuple-element.35), channel_id=1, source_target_pairs={{0,24},{4,28},{8,16},{12,20},{16,8},{20,12},{24,0},{28,4},{1,25},{... | collective-permute-start | bytes 270344 | tf_op jit(solution)/shard_map/ppermute | solution.py:24
  7.0 0.0 collective-permute-start.3
  7.0 0.6 %collective-permute-start.2 = (f32[88,256]{1,0:T(8,128)S(1)}, f32[88,256]{1,0:T(8,128)S(1)}, u32[]{:S(2)}, u32[]{:S(2)}) collective-permute-start(f32[88,256]{1,0:T(8,128)S(1)} %get-tuple-element.35), channel_id=1, source_target_pairs={{0,8},{4,12},{8,0},{12,4},{16,24},{20,28},{24,16},{28,20},{1,9},{5... | collective-permute-start | bytes 270344 | tf_op jit(solution)/shard_map/ppermute | solution.py:24
  7.6 1.6 %collective-permute-start = (f32[24,128]{1,0:T(8,128)S(1)}, f32[24,128]{1,0:T(8,128)S(1)}, u32[]{:S(2)}, u32[]{:S(2)}) collective-permute-start(f32[24,128]{1,0:T(8,128)S(1)} %get-tuple-element.30), channel_id=1, source_target_pairs={{0,1},{1,0},{2,3},{3,2},{4,5},{5,4},{6,7},{7,6},{8,9},{9,8},{10,11... | collective-permute-start | bytes 36872 | tf_op jit(solution)/shard_map/ppermute | solution.py:29
  9.3 2.8 %collective-permute-start.1 = (f32[24,128]{1,0:T(8,128)S(1)}, f32[24,128]{1,0:T(8,128)S(1)}, u32[]{:S(2)}, u32[]{:S(2)}) collective-permute-start(f32[24,128]{1,0:T(8,128)S(1)} %get-tuple-element.31), channel_id=1, source_target_pairs={{1,2},{3,4},{5,6},{7,8},{9,10},{11,12},{13,14},{15,16},{17,18},{19... | collective-permute-start | bytes 36872 | tf_op jit(solution)/shard_map/ppermute | solution.py:31
  12.1 1.6 %prepare.1 = (f32[4,16,128]{2,1,0:T(8,128)S(1)}, f32[16,128]{1,0:T(8,128)S(1)}, f32[16,128]{1,0:T(8,128)S(1)}, f32[16,128]{1,0:T(8,128)S(1)}, f32[2048,256]{1,0:...) custom-call(f32[4,16,128]{2,1,0:T(8,128)} %r_in.3, f32[16,128]{1,0:T(8,128)} %b_in.3, ...), custom_call_target="tpu_custom_call" | custom-call | flops 1 | bytes 1 | tf_op jit(solution)/shard_map/prepare/pallas_call | solution.py:548
  13.7 0.0 collective-permute-done.refs_3_.from_first
  13.8 2.3 %collective-permute-done.1.refs_4_.from_second = f32[24,128]{1,0:T(8,128)S(1)} collective-permute-done((f32[24,128]{1,0:T(8,128)S(1)}, f32[24,128]{1,0:T(8,128)S(1)}, u32[]{:S(2)}, u32[]{:S(2)}) %collective-permute-start.1) | collective-permute-done | bytes 12320 | tf_op jit(solution)/shard_map/ppermute | solution.py:31
  16.1 0.0 collective-permute-done.4.refs_2_
  16.1 0.0 collective-permute-done.3.refs_1_
  16.1 0.0 collective-permute-done.2.refs_0_
  16.1 1.0 %restrict.1 = (f32[608,256]{1,0:T(8,128)S(1)}, f32[4,16,128]{2,1,0:T(8,128)S(1)}) custom-call(f32[4,16,128]{2,1,0:T(8,128)S(1)} %get-tuple-element.26.r, f32[16,128]{1,0:T(8,128)S(1)} %get-tuple-element.27.b, f32[16,128]{1,0:T(8,128)S(1)} %get-tuple-element.28.e, f32[16,128]{1,0:T(8,128)S(1)} %get-tuple-element.29.n, ...), custom_call_target="tpu_custom_call" | custom-call | flops 1 | bytes 1 | tf_op jit(solution)/shard_map/restrict/pallas_call | solution.py:565
  17.2 0.1 collective-permute-start.5
  17.2 1.1 %collective-permute-start.13 = (f32[248,256]{1,0:T(8,128)S(1)}, f32[248,256]{1,0:T(8,128)S(1)}, u32[]{:S(2)}, u32[]{:S(2)}) collective-permute-start(f32[248,256]{1,0:T(8,128)S(1)} %stack.1.gathered), channel_id=1, source_target_pairs={{0,3},{1,2},{2,1},{3,0},{4,7},{5,6},{6,5},{7,4},{8,11},{9,10},{10,... | collective-permute-start | bytes 761864 | tf_op jit(solution)/shard_map/ppermute | solution.py:24
  18.3 0.4 collective-permute-start.12
  18.7 2.1 %collective-permute-start.11 = (f32[248,256]{1,0:T(8,128)S(1)}, f32[248,256]{1,0:T(8,128)S(1)}, u32[]{:S(2)}, u32[]{:S(2)}) collective-permute-start(f32[248,256]{1,0:T(8,128)S(1)} %stack.1.gathered), channel_id=1, source_target_pairs={{0,1},{1,0},{2,3},{3,2},{4,5},{5,4},{6,7},{7,6},{8,9},{9,8},{10,11... | collective-permute-start | bytes 761864 | tf_op jit(solution)/shard_map/ppermute | solution.py:24
  20.8 0.0 collective-permute-done.5.two.message_other
  20.8 0.3 collective-permute-start.6
  21.1 3.7 %collective-permute-done.6 = f32[64,128]{1,0:T(8,128)S(1)} collective-permute-done((f32[64,128]{1,0:T(8,128)S(1)}, f32[64,128]{1,0:T(8,128)S(1)}, u32[]{:S(2)}, u32[]{:S(2)}) %collective-permute-start.6) | collective-permute-done | bytes 32800 | tf_op jit(solution)/shard_map/ppermute | solution.py:24
  24.8 1.3 %collective-permute-start.7 = (f32[64,128]{1,0:T(8,128)S(1)}, f32[64,128]{1,0:T(8,128)S(1)}, u32[]{:S(2)}, u32[]{:S(2)}) collective-permute-start(f32[64,128]{1,0:T(8,128)S(1)} %add.16), channel_id=1, source_target_pairs={{0,16},{4,20},{8,24},{12,28},{16,0},{20,4},{24,8},{28,12},{1,17},{... | collective-permute-start | bytes 98312 | tf_op jit(solution)/shard_map/ppermute | solution.py:24
  26.1 3.5 %collective-permute-done.7 = f32[64,128]{1,0:T(8,128)S(1)} collective-permute-done((f32[64,128]{1,0:T(8,128)S(1)}, f32[64,128]{1,0:T(8,128)S(1)}, u32[]{:S(2)}, u32[]{:S(2)}) %collective-permute-start.7) | collective-permute-done | bytes 32800 | tf_op jit(solution)/shard_map/ppermute | solution.py:24
  29.6 1.4 %collective-permute-start.10 = (f32[64,128]{1,0:T(8,128)S(1)}, f32[64,128]{1,0:T(8,128)S(1)}, u32[]{:S(2)}, u32[]{:S(2)}) collective-permute-start(f32[64,128]{1,0:T(8,128)S(1)} %add.17.refs_3_), channel_id=1, source_target_pairs={{0,3},{1,2},{2,1},{3,0},{4,7},{5,6},{6,5},{7,4},{8,11},{9,10},{10,... | collective-permute-start | bytes 98312 | tf_op jit(solution)/shard_map/ppermute | solution.py:24
  31.0 0.4 collective-permute-start.9
  31.4 0.0 collective-permute-done.13.refs_2_
  31.4 1.7 %collective-permute-start.8 = (f32[64,128]{1,0:T(8,128)S(1)}, f32[64,128]{1,0:T(8,128)S(1)}, u32[]{:S(2)}, u32[]{:S(2)}) collective-permute-start(f32[64,128]{1,0:T(8,128)S(1)} %add.17.refs_3_), channel_id=1, source_target_pairs={{0,1},{1,0},{2,3},{3,2},{4,5},{5,4},{6,7},{7,6},{8,9},{9,8},{10,11... | collective-permute-start | bytes 98312 | tf_op jit(solution)/shard_map/ppermute | solution.py:24
  33.1 0.0 collective-permute-done.12.refs_1_
  33.1 0.0 collective-permute-done.11.refs_0_
  33.1 0.0 collective-permute-start.14
  33.1 0.5 %collective-permute-start.15 = (f32[248,256]{1,0:T(8,128)S(1)}, f32[248,256]{1,0:T(8,128)S(1)}, u32[]{:S(2)}, u32[]{:S(2)}) collective-permute-start(f32[248,256]{1,0:T(8,128)S(1)} %get-tuple-element.39.refs_1_), channel_id=1, source_target_pairs={{0,4},{4,0},{8,12},{12,8},{16,20},{20,16},{24,28},{28,24},{1,5},{5... | collective-permute-start | bytes 761864 | tf_op jit(solution)/shard_map/ppermute | solution.py:24
  33.6 0.8 %collective-permute-done.10 = f32[64,128]{1,0:T(8,128)S(1)} collective-permute-done((f32[64,128]{1,0:T(8,128)S(1)}, f32[64,128]{1,0:T(8,128)S(1)}, u32[]{:S(2)}, u32[]{:S(2)}) %collective-permute-start.10) | collective-permute-done | bytes 32800 | tf_op jit(solution)/shard_map/ppermute | solution.py:24
  34.4 0.0 collective-permute-start.16
  34.4 0.5 collective-permute-done.9
  34.9 0.4 collective-permute-done.8
  35.4 0.0 collective-permute-done.14.refs_3_
  35.4 0.0 collective-permute-done.15.refs_4_
  35.4 0.6 %collective-permute-done.16.refs_5_ = f32[248,256]{1,0:T(8,128)S(1)} collective-permute-done((f32[248,256]{1,0:T(8,128)S(1)}, f32[248,256]{1,0:T(8,128)S(1)}, u32[]{:S(2)}, u32[]{:S(2)}) %collective-permute-start.16) | collective-permute-done | bytes 253984 | tf_op jit(solution)/shard_map/ppermute | solution.py:24
  35.9 4.8 %coarse.1 = (f32[4,256]{1,0:T(4,128)}, bf16[128,256]{1,0:T(8,128)(2,1)S(1)}, bf16[128,256]{1,0:T(8,128)(2,1)S(1)}, f32[8,128]{1,0:T(8,128)S(1)}, f32[8,128]{1,0:T(8,128)S(1)}) custom-call(f32[64,128]{1,0:T(8,128)S(1)} %add_add_fusion.rhs_ref, f32[608,256]{1,0:T(8,128)S(1)} %get-tuple-element.37.one.message, ...), custom_call_target="tpu_custom_call" | custom-call | flops 1 | bytes 1 | tf_op jit(solution)/shard_map/coarse/pallas_call | solution.py:585
  40.7 1.1 %collective-permute-start.17 = (f32[8,128]{1,0:T(8,128)S(1)}, f32[8,128]{1,0:T(8,128)S(1)}, u32[]{:S(2)}, u32[]{:S(2)}) collective-permute-start(f32[8,128]{1,0:T(8,128)S(1)} %get-tuple-element.47), channel_id=1, source_target_pairs={{0,1},{1,0},{2,3},{3,2},{4,5},{5,4},{6,7},{7,6},{8,9},{9,8},{10,11... | collective-permute-start | bytes 12296 | tf_op jit(solution)/shard_map/ppermute | solution.py:37
  41.8 0.9 %collective-permute-start.19 = (f32[8,128]{1,0:T(8,128)S(1)}, f32[8,128]{1,0:T(8,128)S(1)}, u32[]{:S(2)}, u32[]{:S(2)}) collective-permute-start(f32[8,128]{1,0:T(8,128)S(1)} %get-tuple-element.48), channel_id=1, source_target_pairs={{3,4},{7,8},{11,12},{15,16},{19,20},{23,24},{27,28},{0,1},{2,5},{6... | collective-permute-start | bytes 12296 | tf_op jit(solution)/shard_map/ppermute | solution.py:42
  42.7 0.7 %collective-permute-start.18 = (f32[8,128]{1,0:T(8,128)S(1)}, f32[8,128]{1,0:T(8,128)S(1)}, u32[]{:S(2)}, u32[]{:S(2)}) collective-permute-start(f32[8,128]{1,0:T(8,128)S(1)} %get-tuple-element.48), channel_id=1, source_target_pairs={{0,3},{1,2},{2,1},{3,0},{4,7},{5,6},{6,5},{7,4},{8,11},{9,10},{10,... | collective-permute-start | bytes 12296 | tf_op jit(solution)/shard_map/ppermute | solution.py:38
  43.5 0.7 %correct.1 = (f32[4,24,128]{2,1,0:T(8,128)S(1)}, f32[6,24,128]{2,1,0:T(8,128)S(1)}, f32[4,24,128]{2,1,0:T(8,128)S(1)}) custom-call(f32[4,16,128]{2,1,0:T(8,128)S(1)} %get-tuple-element.26.r, f32[16,128]{1,0:T(8,128)S(1)} %get-tuple-element.27.b, f32[16,128]{1,0:T(8,128)S(1)} %get-tuple-element.28.e, f32[16,128]{1,0:T(8,128)S(1)} %get-tuple-element.29.n, ...), custom_call_target="tpu_custom_call" | custom-call | flops 1 | bytes 1 | tf_op jit(solution)/shard_map/correct/pallas_call | solution.py:598
  44.2 0.2 collective-permute-done.17.y_first
  44.3 1.1 %collective-permute-done.19.y_outer = f32[8,128]{1,0:T(8,128)S(1)} collective-permute-done((f32[8,128]{1,0:T(8,128)S(1)}, f32[8,128]{1,0:T(8,128)S(1)}, u32[]{:S(2)}, u32[]{:S(2)}) %collective-permute-start.19) | collective-permute-done | bytes 4128 | tf_op jit(solution)/shard_map/ppermute | solution.py:42
  45.4 1.8 %collective-permute-done.18.y_inner = f32[8,128]{1,0:T(8,128)S(1)} collective-permute-done((f32[8,128]{1,0:T(8,128)S(1)}, f32[8,128]{1,0:T(8,128)S(1)}, u32[]{:S(2)}, u32[]{:S(2)}) %collective-permute-start.18) | collective-permute-done | bytes 4128 | tf_op jit(solution)/shard_map/ppermute | solution.py:38
  47.2 0.8 %post.1 = f32[4,16,128]{2,1,0:T(8,128)} custom-call(f32[4,24,128]{2,1,0:T(8,128)S(1)} %get-tuple-element.44.r, f32[6,24,128]{2,1,0:T(8,128)S(1)} %get-tuple-element.45.coef, f32[4,24,128]{2,1,0:T(8,128)S(1)} %get-tuple-element.46.y_ref, f32[8,128]{1,0:T(8,128)S(1)} %collective-permute-done.17.y_first, f32[8,128]{1,0:T(8,128)S(1)} %collective-permute-done.18.y_inner, ...), custom_call_target="tpu_custom_call" | custom-call | flops 1 | bytes 1 | tf_op jit(solution)/shard_map/post/pallas_call | solution.py:604
  (6 shorter events, 0.0 us)
Async XLA Ops:
  1.9 14.2 %collective-permute-start.4 = (f32[88,256]{1,0:T(8,128)S(1)}, f32[88,256]{1,0:T(8,128)S(1)}, u32[]{:S(2)}, u32[]{:S(2)}) collective-permute-start(f32[88,256]{1,0:T(8,128)S(1)} %get-tuple-element.35), channel_id=1, source_target_pairs={{0,24},{4,28},{8,16},{12,20},{16,8},{20,12},{24,0},{28,4},{1,25},{... | collective-permute-start | bytes 270344 | tf_op jit(solution)/shard_map/ppermute | solution.py:24
  7.0 9.1 %collective-permute-start.3 = (f32[88,256]{1,0:T(8,128)S(1)}, f32[88,256]{1,0:T(8,128)S(1)}, u32[]{:S(2)}, u32[]{:S(2)}) collective-permute-start(f32[88,256]{1,0:T(8,128)S(1)} %get-tuple-element.35), channel_id=1, source_target_pairs={{0,16},{4,20},{8,24},{12,28},{16,0},{20,4},{24,8},{28,12},{1,17},{... | collective-permute-start | bytes 270344 | tf_op jit(solution)/shard_map/ppermute | solution.py:24
  7.0 9.1 %collective-permute-start.2 = (f32[88,256]{1,0:T(8,128)S(1)}, f32[88,256]{1,0:T(8,128)S(1)}, u32[]{:S(2)}, u32[]{:S(2)}) collective-permute-start(f32[88,256]{1,0:T(8,128)S(1)} %get-tuple-element.35), channel_id=1, source_target_pairs={{0,8},{4,12},{8,0},{12,4},{16,24},{20,28},{24,16},{28,20},{1,9},{5... | collective-permute-start | bytes 270344 | tf_op jit(solution)/shard_map/ppermute | solution.py:24
  7.6 6.1 %collective-permute-start = (f32[24,128]{1,0:T(8,128)S(1)}, f32[24,128]{1,0:T(8,128)S(1)}, u32[]{:S(2)}, u32[]{:S(2)}) collective-permute-start(f32[24,128]{1,0:T(8,128)S(1)} %get-tuple-element.30), channel_id=1, source_target_pairs={{0,1},{1,0},{2,3},{3,2},{4,5},{5,4},{6,7},{7,6},{8,9},{9,8},{10,11... | collective-permute-start | bytes 36872 | tf_op jit(solution)/shard_map/ppermute | solution.py:29
  9.3 6.8 %collective-permute-start.1 = (f32[24,128]{1,0:T(8,128)S(1)}, f32[24,128]{1,0:T(8,128)S(1)}, u32[]{:S(2)}, u32[]{:S(2)}) collective-permute-start(f32[24,128]{1,0:T(8,128)S(1)} %get-tuple-element.31), channel_id=1, source_target_pairs={{1,2},{3,4},{5,6},{7,8},{9,10},{11,12},{13,14},{15,16},{17,18},{19... | collective-permute-start | bytes 36872 | tf_op jit(solution)/shard_map/ppermute | solution.py:31
  17.2 3.6 %collective-permute-start.5 = (f32[608,256]{1,0:T(8,128)S(1)}, f32[608,256]{1,0:T(8,128)S(1)}, u32[]{:S(2)}, u32[]{:S(2)}) collective-permute-start(f32[608,256]{1,0:T(8,128)S(1)} %get-tuple-element.37.one.message), channel_id=1, source_target_pairs={{0,4},{4,0},{8,12},{12,8},{16,20},{20,16},{24,28},{28,24},{1,5},{5... | collective-permute-start | bytes 1867784 | tf_op jit(solution)/shard_map/ppermute | solution.py:24
  17.2 14.2 %collective-permute-start.13 = (f32[248,256]{1,0:T(8,128)S(1)}, f32[248,256]{1,0:T(8,128)S(1)}, u32[]{:S(2)}, u32[]{:S(2)}) collective-permute-start(f32[248,256]{1,0:T(8,128)S(1)} %stack.1.gathered), channel_id=1, source_target_pairs={{0,3},{1,2},{2,1},{3,0},{4,7},{5,6},{6,5},{7,4},{8,11},{9,10},{10,... | collective-permute-start | bytes 761864 | tf_op jit(solution)/shard_map/ppermute | solution.py:24
  18.3 14.8 %collective-permute-start.12 = (f32[248,256]{1,0:T(8,128)S(1)}, f32[248,256]{1,0:T(8,128)S(1)}, u32[]{:S(2)}, u32[]{:S(2)}) collective-permute-start(f32[248,256]{1,0:T(8,128)S(1)} %stack.1.gathered), channel_id=1, source_target_pairs={{0,2},{1,3},{2,0},{3,1},{4,6},{5,7},{6,4},{7,5},{8,10},{9,11},{10,... | collective-permute-start | bytes 761864 | tf_op jit(solution)/shard_map/ppermute | solution.py:24
  18.7 14.4 %collective-permute-start.11 = (f32[248,256]{1,0:T(8,128)S(1)}, f32[248,256]{1,0:T(8,128)S(1)}, u32[]{:S(2)}, u32[]{:S(2)}) collective-permute-start(f32[248,256]{1,0:T(8,128)S(1)} %stack.1.gathered), channel_id=1, source_target_pairs={{0,1},{1,0},{2,3},{3,2},{4,5},{5,4},{6,7},{7,6},{8,9},{9,8},{10,11... | collective-permute-start | bytes 761864 | tf_op jit(solution)/shard_map/ppermute | solution.py:24
  20.8 4.0 %collective-permute-start.6 = (f32[64,128]{1,0:T(8,128)S(1)}, f32[64,128]{1,0:T(8,128)S(1)}, u32[]{:S(2)}, u32[]{:S(2)}) collective-permute-start(f32[64,128]{1,0:T(8,128)S(1)} %add.24), channel_id=1, source_target_pairs={{0,8},{4,12},{8,0},{12,4},{16,24},{20,28},{24,16},{28,20},{1,9},{5... | collective-permute-start | bytes 98312 | tf_op jit(solution)/shard_map/ppermute | solution.py:24
  24.8 4.8 %collective-permute-start.7 = (f32[64,128]{1,0:T(8,128)S(1)}, f32[64,128]{1,0:T(8,128)S(1)}, u32[]{:S(2)}, u32[]{:S(2)}) collective-permute-start(f32[64,128]{1,0:T(8,128)S(1)} %add.16), channel_id=1, source_target_pairs={{0,16},{4,20},{8,24},{12,28},{16,0},{20,4},{24,8},{28,12},{1,17},{... | collective-permute-start | bytes 98312 | tf_op jit(solution)/shard_map/ppermute | solution.py:24
  29.6 4.8 %collective-permute-start.10 = (f32[64,128]{1,0:T(8,128)S(1)}, f32[64,128]{1,0:T(8,128)S(1)}, u32[]{:S(2)}, u32[]{:S(2)}) collective-permute-start(f32[64,128]{1,0:T(8,128)S(1)} %add.17.refs_3_), channel_id=1, source_target_pairs={{0,3},{1,2},{2,1},{3,0},{4,7},{5,6},{6,5},{7,4},{8,11},{9,10},{10,... | collective-permute-start | bytes 98312 | tf_op jit(solution)/shard_map/ppermute | solution.py:24
  31.0 3.9 %collective-permute-start.9 = (f32[64,128]{1,0:T(8,128)S(1)}, f32[64,128]{1,0:T(8,128)S(1)}, u32[]{:S(2)}, u32[]{:S(2)}) collective-permute-start(f32[64,128]{1,0:T(8,128)S(1)} %add.17.refs_3_), channel_id=1, source_target_pairs={{0,2},{1,3},{2,0},{3,1},{4,6},{5,7},{6,4},{7,5},{8,10},{9,11},{10,... | collective-permute-start | bytes 98312 | tf_op jit(solution)/shard_map/ppermute | solution.py:24
  31.4 3.9 %collective-permute-start.8 = (f32[64,128]{1,0:T(8,128)S(1)}, f32[64,128]{1,0:T(8,128)S(1)}, u32[]{:S(2)}, u32[]{:S(2)}) collective-permute-start(f32[64,128]{1,0:T(8,128)S(1)} %add.17.refs_3_), channel_id=1, source_target_pairs={{0,1},{1,0},{2,3},{3,2},{4,5},{5,4},{6,7},{7,6},{8,9},{9,8},{10,11... | collective-permute-start | bytes 98312 | tf_op jit(solution)/shard_map/ppermute | solution.py:24
  33.1 2.3 %collective-permute-start.14 = (f32[248,256]{1,0:T(8,128)S(1)}, f32[248,256]{1,0:T(8,128)S(1)}, u32[]{:S(2)}, u32[]{:S(2)}) collective-permute-start(f32[248,256]{1,0:T(8,128)S(1)} %get-tuple-element.38.refs_0_), channel_id=1, source_target_pairs={{0,4},{4,0},{8,12},{12,8},{16,20},{20,16},{24,28},{28,24},{1,5},{5... | collective-permute-start | bytes 761864 | tf_op jit(solution)/shard_map/ppermute | solution.py:24
  33.1 2.3 %collective-permute-start.15 = (f32[248,256]{1,0:T(8,128)S(1)}, f32[248,256]{1,0:T(8,128)S(1)}, u32[]{:S(2)}, u32[]{:S(2)}) collective-permute-start(f32[248,256]{1,0:T(8,128)S(1)} %get-tuple-element.39.refs_1_), channel_id=1, source_target_pairs={{0,4},{4,0},{8,12},{12,8},{16,20},{20,16},{24,28},{28,24},{1,5},{5... | collective-permute-start | bytes 761864 | tf_op jit(solution)/shard_map/ppermute | solution.py:24
  34.4 1.5 %collective-permute-start.16 = (f32[248,256]{1,0:T(8,128)S(1)}, f32[248,256]{1,0:T(8,128)S(1)}, u32[]{:S(2)}, u32[]{:S(2)}) collective-permute-start(f32[248,256]{1,0:T(8,128)S(1)} %get-tuple-element.40.refs_2_), channel_id=1, source_target_pairs={{0,4},{4,0},{8,12},{12,8},{16,20},{20,16},{24,28},{28,24},{1,5},{5... | collective-permute-start | bytes 761864 | tf_op jit(solution)/shard_map/ppermute | solution.py:24
  40.7 3.6 %collective-permute-start.17 = (f32[8,128]{1,0:T(8,128)S(1)}, f32[8,128]{1,0:T(8,128)S(1)}, u32[]{:S(2)}, u32[]{:S(2)}) collective-permute-start(f32[8,128]{1,0:T(8,128)S(1)} %get-tuple-element.47), channel_id=1, source_target_pairs={{0,1},{1,0},{2,3},{3,2},{4,5},{5,4},{6,7},{7,6},{8,9},{9,8},{10,11... | collective-permute-start | bytes 12296 | tf_op jit(solution)/shard_map/ppermute | solution.py:37
  41.8 3.6 %collective-permute-start.19 = (f32[8,128]{1,0:T(8,128)S(1)}, f32[8,128]{1,0:T(8,128)S(1)}, u32[]{:S(2)}, u32[]{:S(2)}) collective-permute-start(f32[8,128]{1,0:T(8,128)S(1)} %get-tuple-element.48), channel_id=1, source_target_pairs={{3,4},{7,8},{11,12},{15,16},{19,20},{23,24},{27,28},{0,1},{2,5},{6... | collective-permute-start | bytes 12296 | tf_op jit(solution)/shard_map/ppermute | solution.py:42
  42.7 4.5 %collective-permute-start.18 = (f32[8,128]{1,0:T(8,128)S(1)}, f32[8,128]{1,0:T(8,128)S(1)}, u32[]{:S(2)}, u32[]{:S(2)}) collective-permute-start(f32[8,128]{1,0:T(8,128)S(1)} %get-tuple-element.48), channel_id=1, source_target_pairs={{0,3},{1,2},{2,1},{3,0},{4,7},{5,6},{6,5},{7,4},{8,11},{9,10},{10,... | collective-permute-start | bytes 12296 | tf_op jit(solution)/shard_map/ppermute | solution.py:38

commit v4 on v3

--- a/solution.py
+++ b/solution.py
@@ -33,11 +33,12 @@
 
 
 def pair_swaps_near(to_first, to_second):
-    count = lax.axis_size(BOTH)
+    count, across = lax.axis_size(BOTH), lax.axis_size("narrow")
     first = lax.ppermute(to_first, BOTH, [(i, i ^ 1) for i in range(count)])
-    inner = lax.ppermute(to_second, BOTH, [(i, i ^ 3) for i in range(count)])
+    inner = lax.ppermute(to_second, BOTH, [(i, i ^ (3 if i % 4 in (1, 2) else across)) for i in range(count)])
     outer = [(i, i + 1) for i in range(3, count - 1, 4)]
-    rest = sorted(set(range(count)) - {i for pair in outer for i in pair})
+    outer += [(i, i ^ across) for i in range(2, count, 4) if i < i ^ across]
+    rest = [0] + list(range(1, count, 4)) + [count - 1]
     outer += list(zip(rest[::2], rest[1::2]))
     outer = lax.ppermute(to_second, BOTH, outer + [(target, source) for source, target in outer])
     return first, inner, outer
@@ -360,6 +361,7 @@
     mine = wide * owned + q
 
     lane16 = lanes((16, 128)) < 64
+    lane64 = lanes((64, 128)) < 64
     at_own = coarse_rows
     at_fetched = at_own + packed_rows(owned)
     for z_rel in range(zs):
@@ -383,8 +385,7 @@
                     turned = half_turn(packed)
                     quarters += [jnp.where(lane16, packed, turned), jnp.where(lane16, turned, packed)]
                 high, low = split(jnp.concatenate(quarters, axis=0))
-                w_inv[64 * i:64 * i + 64, 0:128] = high
-                w_inv[64 * i:64 * i + 64, 128:256] = low
+                w_inv[64 * i:64 * i + 64, :] = jnp.where(lane64, high.astype(F32), low.astype(F32)).astype(BF16)
                 link_rows[4 * i:4 * i + 4, :] = jnp.broadcast_to(piece[at_links:at_links + 1, 0:128], (4, 128))
 
     lane = lanes((size, size))
@@ -403,10 +404,10 @@
         high, low = split(value)
         return jnp.concatenate([high, low], axis=1)
 
-    source = jnp.bitwise_xor(rows((size, 1)), mine * 4)
-    order = jnp.where(lane == source, 1.0, 0.0).astype(BF16)
-    rhs = dot(order, hi_lo(rhs))
-    rhs = rhs[:, 0:128] + rhs[:, 128:256]
+    u_ref[...] = rhs
+    for i in range(coarse_rows):
+        link_rows[4 * i:4 * i + 4, :] = u_ref[pl.ds(jnp.bitwise_xor(mine, i) * 4, 4), :]
+    rhs = link_rows[...]
 
     own_block = jnp.bitwise_and(lax.shift_right_logical(rows((size, 256)), 2), 3) == lax.shift_right_logical(
         lanes((size, 256)), 6)
@@ -418,10 +419,11 @@
 
     def apply_inverse(value):
         high, low = split(value)
-        mixed = jnp.where(here, high.astype(F32), low.astype(F32)).astype(BF16)
-        mixed = jnp.concatenate([mixed, mixed], axis=1)
+        low = jnp.where(here, low.astype(F32), 0.0).astype(BF16)
         for g in range(coarse_rows // 4):
-            product[16 * g:16 * g + 16, :] = dot_t(mixed[16 * g:16 * g + 16], w_inv[256 * g:256 * g + 256, :])
+            near = slice(16 * g, 16 * g + 16)
+            both = dot_t(jnp.concatenate([high[near], low[near]], axis=0), w_inv[256 * g:256 * g + 256, :])
+            product[near, :] = both[0:16] + both[16:32]
         return fold()
 
     def pick(got, step):
@@ -442,7 +444,7 @@
             product[near, :] = both[0:16] + both[16:32] + dot_t(high[near], w_low[block, :])
         u = apply_inverse(rhs + fold())
 
-    u_ref[...] = u[0:4 * owned]
+    u_ref[0:4 * owned, :] = u[0:4 * owned]
     here1 = lanes((1, 128)) < 64
     for j in range(owned):
         got = u_ref[pl.ds(jnp.bitwise_xor(q, j) * 4, 4), :]
@@ -587,9 +589,9 @@
         out_shape=(shape(owned, 256), near, near, shape(8, width), shape(8, width)),
         scratch_shapes=[
             pltpu.VMEM((64 * coarse_rows, 256), BF16), pltpu.VMEM((64 * coarse_rows, 256), BF16),
-            pltpu.VMEM((64 * coarse_rows, 256), BF16), pltpu.VMEM((size, 128), F32),
+            pltpu.VMEM((64 * coarse_rows, 128), BF16), pltpu.VMEM((size, 128), F32),
             pltpu.VMEM((4 * size, size), BF16), pltpu.VMEM((size, 256), F32),
-            pltpu.VMEM((4 * owned, 128), F32), pltpu.VMEM((16, width), F32)],
+            pltpu.VMEM((size, 128), F32), pltpu.VMEM((16, width), F32)],
         cost_estimate=CHEAP, compiler_params=params(min(48, 8 + coarse_rows // 3)), name="coarse",
     )(rhs, message, message_other, *spread, *spread_other, basis, sup_hots, x)
 

time: 48.2 us -> 46 us (0.954)
  waiting for transfers between devices: 14.9 us -> 13.3 us
    ppermute x1, waiting for transfers between devices: 1.81 us -> 0.01 us  [pair_swaps_near(): lax.ppermute(to_second, BOTH, [(i, i ^ (3 if i % 4 in (1, 2) else across)...]
  transfers between devices with their start and end apart: 20 -> 20, of which waited for: 10 -> 9; matrix products, arithmetic and copies ran while one was open for 0% -> 0% of each run, Pallas kernels for 5% -> 5%
where the time goes in v4:
time: 46 us; the launch traced here: 45.9 us
  starting transfers between devices  22.1 us (48%)
  waiting for transfers between devices  13.3 us (29%)
  Pallas kernels  9.8 us (21%)
  between operations  0.73 us (2%)
    ppermute x15, starting transfers between devices, swap(): return lax.ppermute(value, axis, [(i, i ^ bits) for i in range(size)])  15 us
    ppermute x15, waiting for transfers between devices, swap(): return lax.ppermute(value, axis, [(i, i ^ bits) for i in range(size)])  9.52 us
    pallas_call x1, Pallas kernels, body(): pl.pallas_call(functools.partial(coarse_kernel, owned, coarse_rows, zs),...  4.35 us
    ppermute x1, starting transfers between devices, pair_swaps(): lax.ppermute(to_second, BOTH, odd + [(target, source) for source, target...  2.85 us
    ppermute x1, waiting for transfers between devices, pair_swaps(): lax.ppermute(to_second, BOTH, odd + [(target, source) for source, target...  2.31 us
    pallas_call x1, Pallas kernels, body(): pl.pallas_call(functools.partial(prepare_kernel, owned, coarse_rows), out...  1.64 us
    ppermute x1, starting transfers between devices, pair_swaps(): first = lax.ppermute(to_first, BOTH, [(i, i ^ 1) for i in range(count)])  1.63 us
    pallas_call x1, Pallas kernels, body(): pl.pallas_call(functools.partial(begin_kernel, owned), out_shape=(message...  1.22 us
  transfers between devices with their start and end apart: 20, of which 9 were waited for; matrix products, arithmetic and copies ran while one was open for 0% of the time, Pallas kernels for 5%

profile of v4, /device:TPU:0, one launch (start us, length us, event | category | flops | bytes accessed | tf_op | source)
XLA Modules:
  0.0 45.9 jit_solution(9527856162676642461)
XLA Ops:
  0.6 1.2 %begin.1 = (f32[24,128]{1,0:T(8,128)S(1)}, f32[24,128]{1,0:T(8,128)S(1)}, f32[88,256]{1,0:T(8,128)S(1)}, f32[328,256]{1,0:T(8,128)S(1)}) custom-call(f32[4,16,128]{2,1,0:T(8,128)} %r_in.3, f32[16,128]{1,0:T(8,128)} %b_in.3, f32[16,128]{1,0:T(8,128)} %e_in.3, f32[16,128]{1,0:T(8,128)} %n_in.3, s32[4,4]{1,0:T(4,128)} %links_in.1, f32[4,64,256]{2,1,0:T(8,128)} %coupling_in.1, ...), custom_call_target="tpu_custom_call" | custom-call | flops 1 | bytes 1 | tf_op jit(solution)/shard_map/begin/pallas_call | solution.py:536
  1.9 5.1 %collective-permute-start.4 = (f32[88,256]{1,0:T(8,128)S(1)}, f32[88,256]{1,0:T(8,128)S(1)}, u32[]{:S(2)}, u32[]{:S(2)}) collective-permute-start(f32[88,256]{1,0:T(8,128)S(1)} %get-tuple-element.35), channel_id=1, source_target_pairs={{0,24},{4,28},{8,16},{12,20},{16,8},{20,12},{24,0},{28,4},{1,25},{... | collective-permute-start | bytes 270344 | tf_op jit(solution)/shard_map/ppermute | solution.py:24
  7.0 0.0 collective-permute-start.3
  7.0 0.6 %collective-permute-start.2 = (f32[88,256]{1,0:T(8,128)S(1)}, f32[88,256]{1,0:T(8,128)S(1)}, u32[]{:S(2)}, u32[]{:S(2)}) collective-permute-start(f32[88,256]{1,0:T(8,128)S(1)} %get-tuple-element.35), channel_id=1, source_target_pairs={{0,8},{4,12},{8,0},{12,4},{16,24},{20,28},{24,16},{28,20},{1,9},{5... | collective-permute-start | bytes 270344 | tf_op jit(solution)/shard_map/ppermute | solution.py:24
  7.6 1.6 %collective-permute-start = (f32[24,128]{1,0:T(8,128)S(1)}, f32[24,128]{1,0:T(8,128)S(1)}, u32[]{:S(2)}, u32[]{:S(2)}) collective-permute-start(f32[24,128]{1,0:T(8,128)S(1)} %get-tuple-element.30), channel_id=1, source_target_pairs={{0,1},{1,0},{2,3},{3,2},{4,5},{5,4},{6,7},{7,6},{8,9},{9,8},{10,11... | collective-permute-start | bytes 36872 | tf_op jit(solution)/shard_map/ppermute | solution.py:29
  9.3 2.8 %collective-permute-start.1 = (f32[24,128]{1,0:T(8,128)S(1)}, f32[24,128]{1,0:T(8,128)S(1)}, u32[]{:S(2)}, u32[]{:S(2)}) collective-permute-start(f32[24,128]{1,0:T(8,128)S(1)} %get-tuple-element.31), channel_id=1, source_target_pairs={{1,2},{3,4},{5,6},{7,8},{9,10},{11,12},{13,14},{15,16},{17,18},{19... | collective-permute-start | bytes 36872 | tf_op jit(solution)/shard_map/ppermute | solution.py:31
  12.1 1.6 %prepare.1 = (f32[4,16,128]{2,1,0:T(8,128)S(1)}, f32[16,128]{1,0:T(8,128)S(1)}, f32[16,128]{1,0:T(8,128)S(1)}, f32[16,128]{1,0:T(8,128)S(1)}, f32[2048,256]{1,0:...) custom-call(f32[4,16,128]{2,1,0:T(8,128)} %r_in.3, f32[16,128]{1,0:T(8,128)} %b_in.3, ...), custom_call_target="tpu_custom_call" | custom-call | flops 1 | bytes 1 | tf_op jit(solution)/shard_map/prepare/pallas_call | solution.py:550
  13.7 0.0 collective-permute-done.refs_3_.from_first
  13.8 2.3 %collective-permute-done.1.refs_4_.from_second = f32[24,128]{1,0:T(8,128)S(1)} collective-permute-done((f32[24,128]{1,0:T(8,128)S(1)}, f32[24,128]{1,0:T(8,128)S(1)}, u32[]{:S(2)}, u32[]{:S(2)}) %collective-permute-start.1) | collective-permute-done | bytes 12320 | tf_op jit(solution)/shard_map/ppermute | solution.py:31
  16.1 0.0 collective-permute-done.4.refs_2_
  16.1 0.0 collective-permute-done.3.refs_1_
  16.1 0.0 collective-permute-done.2.refs_0_
  16.1 1.0 %restrict.1 = (f32[608,256]{1,0:T(8,128)S(1)}, f32[4,16,128]{2,1,0:T(8,128)S(1)}) custom-call(f32[4,16,128]{2,1,0:T(8,128)S(1)} %get-tuple-element.26.r, f32[16,128]{1,0:T(8,128)S(1)} %get-tuple-element.27.b, f32[16,128]{1,0:T(8,128)S(1)} %get-tuple-element.28.e, f32[16,128]{1,0:T(8,128)S(1)} %get-tuple-element.29.n, ...), custom_call_target="tpu_custom_call" | custom-call | flops 1 | bytes 1 | tf_op jit(solution)/shard_map/restrict/pallas_call | solution.py:567
  17.2 0.1 collective-permute-start.5
  17.2 1.1 %collective-permute-start.13 = (f32[248,256]{1,0:T(8,128)S(1)}, f32[248,256]{1,0:T(8,128)S(1)}, u32[]{:S(2)}, u32[]{:S(2)}) collective-permute-start(f32[248,256]{1,0:T(8,128)S(1)} %stack.1.gathered), channel_id=1, source_target_pairs={{0,3},{1,2},{2,1},{3,0},{4,7},{5,6},{6,5},{7,4},{8,11},{9,10},{10,... | collective-permute-start | bytes 761864 | tf_op jit(solution)/shard_map/ppermute | solution.py:24
  18.3 0.4 collective-permute-start.12
  18.7 2.1 %collective-permute-start.11 = (f32[248,256]{1,0:T(8,128)S(1)}, f32[248,256]{1,0:T(8,128)S(1)}, u32[]{:S(2)}, u32[]{:S(2)}) collective-permute-start(f32[248,256]{1,0:T(8,128)S(1)} %stack.1.gathered), channel_id=1, source_target_pairs={{0,1},{1,0},{2,3},{3,2},{4,5},{5,4},{6,7},{7,6},{8,9},{9,8},{10,11... | collective-permute-start | bytes 761864 | tf_op jit(solution)/shard_map/ppermute | solution.py:24
  20.8 0.0 collective-permute-done.5.two.message_other
  20.8 0.3 collective-permute-start.6
  21.1 3.7 %collective-permute-done.6 = f32[64,128]{1,0:T(8,128)S(1)} collective-permute-done((f32[64,128]{1,0:T(8,128)S(1)}, f32[64,128]{1,0:T(8,128)S(1)}, u32[]{:S(2)}, u32[]{:S(2)}) %collective-permute-start.6) | collective-permute-done | bytes 32800 | tf_op jit(solution)/shard_map/ppermute | solution.py:24
  24.8 1.3 %collective-permute-start.7 = (f32[64,128]{1,0:T(8,128)S(1)}, f32[64,128]{1,0:T(8,128)S(1)}, u32[]{:S(2)}, u32[]{:S(2)}) collective-permute-start(f32[64,128]{1,0:T(8,128)S(1)} %add.16), channel_id=1, source_target_pairs={{0,16},{4,20},{8,24},{12,28},{16,0},{20,4},{24,8},{28,12},{1,17},{... | collective-permute-start | bytes 98312 | tf_op jit(solution)/shard_map/ppermute | solution.py:24
  26.1 3.5 %collective-permute-done.7 = f32[64,128]{1,0:T(8,128)S(1)} collective-permute-done((f32[64,128]{1,0:T(8,128)S(1)}, f32[64,128]{1,0:T(8,128)S(1)}, u32[]{:S(2)}, u32[]{:S(2)}) %collective-permute-start.7) | collective-permute-done | bytes 32800 | tf_op jit(solution)/shard_map/ppermute | solution.py:24
  29.6 1.4 %collective-permute-start.10 = (f32[64,128]{1,0:T(8,128)S(1)}, f32[64,128]{1,0:T(8,128)S(1)}, u32[]{:S(2)}, u32[]{:S(2)}) collective-permute-start(f32[64,128]{1,0:T(8,128)S(1)} %add.17.refs_3_), channel_id=1, source_target_pairs={{0,3},{1,2},{2,1},{3,0},{4,7},{5,6},{6,5},{7,4},{8,11},{9,10},{10,... | collective-permute-start | bytes 98312 | tf_op jit(solution)/shard_map/ppermute | solution.py:24
  31.0 0.4 collective-permute-start.9
  31.4 0.0 collective-permute-done.13.refs_2_
  31.4 1.7 %collective-permute-start.8 = (f32[64,128]{1,0:T(8,128)S(1)}, f32[64,128]{1,0:T(8,128)S(1)}, u32[]{:S(2)}, u32[]{:S(2)}) collective-permute-start(f32[64,128]{1,0:T(8,128)S(1)} %add.17.refs_3_), channel_id=1, source_target_pairs={{0,1},{1,0},{2,3},{3,2},{4,5},{5,4},{6,7},{7,6},{8,9},{9,8},{10,11... | collective-permute-start | bytes 98312 | tf_op jit(solution)/shard_map/ppermute | solution.py:24
  33.1 0.0 collective-permute-done.12.refs_1_
  33.1 0.0 collective-permute-done.11.refs_0_
  33.1 0.0 collective-permute-start.14
  33.1 0.5 %collective-permute-start.15 = (f32[248,256]{1,0:T(8,128)S(1)}, f32[248,256]{1,0:T(8,128)S(1)}, u32[]{:S(2)}, u32[]{:S(2)}) collective-permute-start(f32[248,256]{1,0:T(8,128)S(1)} %get-tuple-element.39.refs_1_), channel_id=1, source_target_pairs={{0,4},{4,0},{8,12},{12,8},{16,20},{20,16},{24,28},{28,24},{1,5},{5... | collective-permute-start | bytes 761864 | tf_op jit(solution)/shard_map/ppermute | solution.py:24
  33.6 0.8 %collective-permute-done.10 = f32[64,128]{1,0:T(8,128)S(1)} collective-permute-done((f32[64,128]{1,0:T(8,128)S(1)}, f32[64,128]{1,0:T(8,128)S(1)}, u32[]{:S(2)}, u32[]{:S(2)}) %collective-permute-start.10) | collective-permute-done | bytes 32800 | tf_op jit(solution)/shard_map/ppermute | solution.py:24
  34.4 0.0 collective-permute-start.16
  34.4 0.5 %collective-permute-done.9 = f32[64,128]{1,0:T(8,128)S(1)} collective-permute-done((f32[64,128]{1,0:T(8,128)S(1)}, f32[64,128]{1,0:T(8,128)S(1)}, u32[]{:S(2)}, u32[]{:S(2)}) %collective-permute-start.9) | collective-permute-done | bytes 32800 | tf_op jit(solution)/shard_map/ppermute | solution.py:24
  34.9 0.4 collective-permute-done.8
  35.4 0.0 collective-permute-done.14.refs_3_
  35.4 0.0 collective-permute-done.15.refs_4_
  35.4 0.6 %collective-permute-done.16.refs_5_ = f32[248,256]{1,0:T(8,128)S(1)} collective-permute-done((f32[248,256]{1,0:T(8,128)S(1)}, f32[248,256]{1,0:T(8,128)S(1)}, u32[]{:S(2)}, u32[]{:S(2)}) %collective-permute-start.16) | collective-permute-done | bytes 253984 | tf_op jit(solution)/shard_map/ppermute | solution.py:24
  35.9 4.3 %coarse.1 = (f32[4,256]{1,0:T(4,128)}, bf16[128,256]{1,0:T(8,128)(2,1)S(1)}, bf16[128,256]{1,0:T(8,128)(2,1)S(1)}, f32[8,128]{1,0:T(8,128)S(1)}, f32[8,128]{1,0:T(8,128)S(1)}) custom-call(f32[64,128]{1,0:T(8,128)S(1)} %add_add_fusion.rhs_ref, f32[608,256]{1,0:T(8,128)S(1)} %get-tuple-element.37.one.message, ...), custom_call_target="tpu_custom_call" | custom-call | flops 1 | bytes 1 | tf_op jit(solution)/shard_map/coarse/pallas_call | solution.py:587
  40.3 1.1 %collective-permute-start.17 = (f32[8,128]{1,0:T(8,128)S(1)}, f32[8,128]{1,0:T(8,128)S(1)}, u32[]{:S(2)}, u32[]{:S(2)}) collective-permute-start(f32[8,128]{1,0:T(8,128)S(1)} %get-tuple-element.47), channel_id=1, source_target_pairs={{0,1},{1,0},{2,3},{3,2},{4,5},{5,4},{6,7},{7,6},{8,9},{9,8},{10,11... | collective-permute-start | bytes 12296 | tf_op jit(solution)/shard_map/ppermute | solution.py:37
  41.4 0.9 %collective-permute-start.19 = (f32[8,128]{1,0:T(8,128)S(1)}, f32[8,128]{1,0:T(8,128)S(1)}, u32[]{:S(2)}, u32[]{:S(2)}) collective-permute-start(f32[8,128]{1,0:T(8,128)S(1)} %get-tuple-element.48), channel_id=1, source_target_pairs={{3,4},{7,8},{11,12},{15,16},{19,20},{23,24},{27,28},{2,6},{10,14},... | collective-permute-start | bytes 12296 | tf_op jit(solution)/shard_map/ppermute | solution.py:43
  42.3 0.6 %collective-permute-start.18 = (f32[8,128]{1,0:T(8,128)S(1)}, f32[8,128]{1,0:T(8,128)S(1)}, u32[]{:S(2)}, u32[]{:S(2)}) collective-permute-start(f32[8,128]{1,0:T(8,128)S(1)} %get-tuple-element.48), channel_id=1, source_target_pairs={{0,4},{1,2},{2,1},{3,7},{4,0},{5,6},{6,5},{7,3},{8,12},{9,10},{10,... | collective-permute-start | bytes 12296 | tf_op jit(solution)/shard_map/ppermute | solution.py:38
  42.9 0.7 %correct.1 = (f32[4,24,128]{2,1,0:T(8,128)S(1)}, f32[6,24,128]{2,1,0:T(8,128)S(1)}, f32[4,24,128]{2,1,0:T(8,128)S(1)}) custom-call(f32[4,16,128]{2,1,0:T(8,128)S(1)} %get-tuple-element.26.r, f32[16,128]{1,0:T(8,128)S(1)} %get-tuple-element.27.b, f32[16,128]{1,0:T(8,128)S(1)} %get-tuple-element.28.e, f32[16,128]{1,0:T(8,128)S(1)} %get-tuple-element.29.n, ...), custom_call_target="tpu_custom_call" | custom-call | flops 1 | bytes 1 | tf_op jit(solution)/shard_map/correct/pallas_call | solution.py:600
  43.6 0.3 collective-permute-done.17.y_first
  43.9 1.1 %collective-permute-done.19.y_outer = f32[8,128]{1,0:T(8,128)S(1)} collective-permute-done((f32[8,128]{1,0:T(8,128)S(1)}, f32[8,128]{1,0:T(8,128)S(1)}, u32[]{:S(2)}, u32[]{:S(2)}) %collective-permute-start.19) | collective-permute-done | bytes 4128 | tf_op jit(solution)/shard_map/ppermute | solution.py:43
  45.0 0.0 collective-permute-done.18.y_inner
  45.0 0.8 %post.1 = f32[4,16,128]{2,1,0:T(8,128)} custom-call(f32[4,24,128]{2,1,0:T(8,128)S(1)} %get-tuple-element.44.r, f32[6,24,128]{2,1,0:T(8,128)S(1)} %get-tuple-element.45.coef, f32[4,24,128]{2,1,0:T(8,128)S(1)} %get-tuple-element.46.y_ref, f32[8,128]{1,0:T(8,128)S(1)} %collective-permute-done.17.y_first, f32[8,128]{1,0:T(8,128)S(1)} %collective-permute-done.18.y_inner, ...), custom_call_target="tpu_custom_call" | custom-call | flops 1 | bytes 1 | tf_op jit(solution)/shard_map/post/pallas_call | solution.py:606
  (6 shorter events, 0.0 us)
Async XLA Ops:
  1.9 14.2 %collective-permute-start.4 = (f32[88,256]{1,0:T(8,128)S(1)}, f32[88,256]{1,0:T(8,128)S(1)}, u32[]{:S(2)}, u32[]{:S(2)}) collective-permute-start(f32[88,256]{1,0:T(8,128)S(1)} %get-tuple-element.35), channel_id=1, source_target_pairs={{0,24},{4,28},{8,16},{12,20},{16,8},{20,12},{24,0},{28,4},{1,25},{... | collective-permute-start | bytes 270344 | tf_op jit(solution)/shard_map/ppermute | solution.py:24
  7.0 9.1 %collective-permute-start.3 = (f32[88,256]{1,0:T(8,128)S(1)}, f32[88,256]{1,0:T(8,128)S(1)}, u32[]{:S(2)}, u32[]{:S(2)}) collective-permute-start(f32[88,256]{1,0:T(8,128)S(1)} %get-tuple-element.35), channel_id=1, source_target_pairs={{0,16},{4,20},{8,24},{12,28},{16,0},{20,4},{24,8},{28,12},{1,17},{... | collective-permute-start | bytes 270344 | tf_op jit(solution)/shard_map/ppermute | solution.py:24
  7.0 9.1 %collective-permute-start.2 = (f32[88,256]{1,0:T(8,128)S(1)}, f32[88,256]{1,0:T(8,128)S(1)}, u32[]{:S(2)}, u32[]{:S(2)}) collective-permute-start(f32[88,256]{1,0:T(8,128)S(1)} %get-tuple-element.35), channel_id=1, source_target_pairs={{0,8},{4,12},{8,0},{12,4},{16,24},{20,28},{24,16},{28,20},{1,9},{5... | collective-permute-start | bytes 270344 | tf_op jit(solution)/shard_map/ppermute | solution.py:24
  7.6 6.1 %collective-permute-start = (f32[24,128]{1,0:T(8,128)S(1)}, f32[24,128]{1,0:T(8,128)S(1)}, u32[]{:S(2)}, u32[]{:S(2)}) collective-permute-start(f32[24,128]{1,0:T(8,128)S(1)} %get-tuple-element.30), channel_id=1, source_target_pairs={{0,1},{1,0},{2,3},{3,2},{4,5},{5,4},{6,7},{7,6},{8,9},{9,8},{10,11... | collective-permute-start | bytes 36872 | tf_op jit(solution)/shard_map/ppermute | solution.py:29
  9.3 6.8 %collective-permute-start.1 = (f32[24,128]{1,0:T(8,128)S(1)}, f32[24,128]{1,0:T(8,128)S(1)}, u32[]{:S(2)}, u32[]{:S(2)}) collective-permute-start(f32[24,128]{1,0:T(8,128)S(1)} %get-tuple-element.31), channel_id=1, source_target_pairs={{1,2},{3,4},{5,6},{7,8},{9,10},{11,12},{13,14},{15,16},{17,18},{19... | collective-permute-start | bytes 36872 | tf_op jit(solution)/shard_map/ppermute | solution.py:31
  17.2 3.6 %collective-permute-start.5 = (f32[608,256]{1,0:T(8,128)S(1)}, f32[608,256]{1,0:T(8,128)S(1)}, u32[]{:S(2)}, u32[]{:S(2)}) collective-permute-start(f32[608,256]{1,0:T(8,128)S(1)} %get-tuple-element.37.one.message), channel_id=1, source_target_pairs={{0,4},{4,0},{8,12},{12,8},{16,20},{20,16},{24,28},{28,24},{1,5},{5... | collective-permute-start | bytes 1867784 | tf_op jit(solution)/shard_map/ppermute | solution.py:24
  17.2 14.2 %collective-permute-start.13 = (f32[248,256]{1,0:T(8,128)S(1)}, f32[248,256]{1,0:T(8,128)S(1)}, u32[]{:S(2)}, u32[]{:S(2)}) collective-permute-start(f32[248,256]{1,0:T(8,128)S(1)} %stack.1.gathered), channel_id=1, source_target_pairs={{0,3},{1,2},{2,1},{3,0},{4,7},{5,6},{6,5},{7,4},{8,11},{9,10},{10,... | collective-permute-start | bytes 761864 | tf_op jit(solution)/shard_map/ppermute | solution.py:24
  18.3 14.8 %collective-permute-start.12 = (f32[248,256]{1,0:T(8,128)S(1)}, f32[248,256]{1,0:T(8,128)S(1)}, u32[]{:S(2)}, u32[]{:S(2)}) collective-permute-start(f32[248,256]{1,0:T(8,128)S(1)} %stack.1.gathered), channel_id=1, source_target_pairs={{0,2},{1,3},{2,0},{3,1},{4,6},{5,7},{6,4},{7,5},{8,10},{9,11},{10,... | collective-permute-start | bytes 761864 | tf_op jit(solution)/shard_map/ppermute | solution.py:24
  18.7 14.4 %collective-permute-start.11 = (f32[248,256]{1,0:T(8,128)S(1)}, f32[248,256]{1,0:T(8,128)S(1)}, u32[]{:S(2)}, u32[]{:S(2)}) collective-permute-start(f32[248,256]{1,0:T(8,128)S(1)} %stack.1.gathered), channel_id=1, source_target_pairs={{0,1},{1,0},{2,3},{3,2},{4,5},{5,4},{6,7},{7,6},{8,9},{9,8},{10,11... | collective-permute-start | bytes 761864 | tf_op jit(solution)/shard_map/ppermute | solution.py:24
  20.8 4.0 %collective-permute-start.6 = (f32[64,128]{1,0:T(8,128)S(1)}, f32[64,128]{1,0:T(8,128)S(1)}, u32[]{:S(2)}, u32[]{:S(2)}) collective-permute-start(f32[64,128]{1,0:T(8,128)S(1)} %add.24), channel_id=1, source_target_pairs={{0,8},{4,12},{8,0},{12,4},{16,24},{20,28},{24,16},{28,20},{1,9},{5... | collective-permute-start | bytes 98312 | tf_op jit(solution)/shard_map/ppermute | solution.py:24
  24.8 4.8 %collective-permute-start.7 = (f32[64,128]{1,0:T(8,128)S(1)}, f32[64,128]{1,0:T(8,128)S(1)}, u32[]{:S(2)}, u32[]{:S(2)}) collective-permute-start(f32[64,128]{1,0:T(8,128)S(1)} %add.16), channel_id=1, source_target_pairs={{0,16},{4,20},{8,24},{12,28},{16,0},{20,4},{24,8},{28,12},{1,17},{... | collective-permute-start | bytes 98312 | tf_op jit(solution)/shard_map/ppermute | solution.py:24
  29.6 4.8 %collective-permute-start.10 = (f32[64,128]{1,0:T(8,128)S(1)}, f32[64,128]{1,0:T(8,128)S(1)}, u32[]{:S(2)}, u32[]{:S(2)}) collective-permute-start(f32[64,128]{1,0:T(8,128)S(1)} %add.17.refs_3_), channel_id=1, source_target_pairs={{0,3},{1,2},{2,1},{3,0},{4,7},{5,6},{6,5},{7,4},{8,11},{9,10},{10,... | collective-permute-start | bytes 98312 | tf_op jit(solution)/shard_map/ppermute | solution.py:24
  31.0 3.9 %collective-permute-start.9 = (f32[64,128]{1,0:T(8,128)S(1)}, f32[64,128]{1,0:T(8,128)S(1)}, u32[]{:S(2)}, u32[]{:S(2)}) collective-permute-start(f32[64,128]{1,0:T(8,128)S(1)} %add.17.refs_3_), channel_id=1, source_target_pairs={{0,2},{1,3},{2,0},{3,1},{4,6},{5,7},{6,4},{7,5},{8,10},{9,11},{10,... | collective-permute-start | bytes 98312 | tf_op jit(solution)/shard_map/ppermute | solution.py:24
  31.4 3.9 %collective-permute-start.8 = (f32[64,128]{1,0:T(8,128)S(1)}, f32[64,128]{1,0:T(8,128)S(1)}, u32[]{:S(2)}, u32[]{:S(2)}) collective-permute-start(f32[64,128]{1,0:T(8,128)S(1)} %add.17.refs_3_), channel_id=1, source_target_pairs={{0,1},{1,0},{2,3},{3,2},{4,5},{5,4},{6,7},{7,6},{8,9},{9,8},{10,11... | collective-permute-start | bytes 98312 | tf_op jit(solution)/shard_map/ppermute | solution.py:24
  33.1 2.3 %collective-permute-start.14 = (f32[248,256]{1,0:T(8,128)S(1)}, f32[248,256]{1,0:T(8,128)S(1)}, u32[]{:S(2)}, u32[]{:S(2)}) collective-permute-start(f32[248,256]{1,0:T(8,128)S(1)} %get-tuple-element.38.refs_0_), channel_id=1, source_target_pairs={{0,4},{4,0},{8,12},{12,8},{16,20},{20,16},{24,28},{28,24},{1,5},{5... | collective-permute-start | bytes 761864 | tf_op jit(solution)/shard_map/ppermute | solution.py:24
  33.1 2.3 %collective-permute-start.15 = (f32[248,256]{1,0:T(8,128)S(1)}, f32[248,256]{1,0:T(8,128)S(1)}, u32[]{:S(2)}, u32[]{:S(2)}) collective-permute-start(f32[248,256]{1,0:T(8,128)S(1)} %get-tuple-element.39.refs_1_), channel_id=1, source_target_pairs={{0,4},{4,0},{8,12},{12,8},{16,20},{20,16},{24,28},{28,24},{1,5},{5... | collective-permute-start | bytes 761864 | tf_op jit(solution)/shard_map/ppermute | solution.py:24
  34.4 1.5 %collective-permute-start.16 = (f32[248,256]{1,0:T(8,128)S(1)}, f32[248,256]{1,0:T(8,128)S(1)}, u32[]{:S(2)}, u32[]{:S(2)}) collective-permute-start(f32[248,256]{1,0:T(8,128)S(1)} %get-tuple-element.40.refs_2_), channel_id=1, source_target_pairs={{0,4},{4,0},{8,12},{12,8},{16,20},{20,16},{24,28},{28,24},{1,5},{5... | collective-permute-start | bytes 761864 | tf_op jit(solution)/shard_map/ppermute | solution.py:24
  40.3 3.6 %collective-permute-start.17 = (f32[8,128]{1,0:T(8,128)S(1)}, f32[8,128]{1,0:T(8,128)S(1)}, u32[]{:S(2)}, u32[]{:S(2)}) collective-permute-start(f32[8,128]{1,0:T(8,128)S(1)} %get-tuple-element.47), channel_id=1, source_target_pairs={{0,1},{1,0},{2,3},{3,2},{4,5},{5,4},{6,7},{7,6},{8,9},{9,8},{10,11... | collective-permute-start | bytes 12296 | tf_op jit(solution)/shard_map/ppermute | solution.py:37
  41.4 3.6 %collective-permute-start.19 = (f32[8,128]{1,0:T(8,128)S(1)}, f32[8,128]{1,0:T(8,128)S(1)}, u32[]{:S(2)}, u32[]{:S(2)}) collective-permute-start(f32[8,128]{1,0:T(8,128)S(1)} %get-tuple-element.48), channel_id=1, source_target_pairs={{3,4},{7,8},{11,12},{15,16},{19,20},{23,24},{27,28},{2,6},{10,14},... | collective-permute-start | bytes 12296 | tf_op jit(solution)/shard_map/ppermute | solution.py:43
  42.3 2.7 %collective-permute-start.18 = (f32[8,128]{1,0:T(8,128)S(1)}, f32[8,128]{1,0:T(8,128)S(1)}, u32[]{:S(2)}, u32[]{:S(2)}) collective-permute-start(f32[8,128]{1,0:T(8,128)S(1)} %get-tuple-element.48), channel_id=1, source_target_pairs={{0,4},{1,2},{2,1},{3,7},{4,0},{5,6},{6,5},{7,3},{8,12},{9,10},{10,... | collective-permute-start | bytes 12296 | tf_op jit(solution)/shard_map/ppermute | solution.py:38

commit v5 on v4

--- a/solution.py
+++ b/solution.py
@@ -61,6 +61,26 @@
         rounds.append([base * k for k in range(1, span)])
         base *= span
     return rounds
+
+
+def share_kernel(value, one, two, out):
+    second = lax.rem(lax.axis_index("wide"), 2) == 1
+    out[...] = one[...] + jnp.where(second, two[...], value[...])
+
+
+def sum_shared(value, axis, masks):
+    if len(masks) == 1:
+        return value + swap(value, axis, masks[0])
+    count, across = lax.axis_size(BOTH), lax.axis_size("narrow")
+    unit = across if axis == "wide" else 1
+    near, far, farthest = [unit * mask for mask in masks]
+    one = lax.ppermute(value, BOTH, [(i, i ^ (far if i & across else near)) for i in range(count)])
+    two = lax.ppermute(value, BOTH, [(i, i ^ (farthest if i & across else near)) for i in range(count)])
+    value = pl.pallas_call(
+        share_kernel, out_shape=jax.ShapeDtypeStruct(value.shape, value.dtype),
+        cost_estimate=CHEAP, compiler_params=params(1), name="share",
+    )(value, one, two)
+    return value + swap(value, "wide", 1)
 
 
 def bits_of(size):
@@ -295,7 +315,7 @@
     ]
 
 
-def restrict_kernel(coarse_rows, r, b, e, n, from_first, from_second, basis, hots,
+def restrict_kernel(coarse_rows, r, b, e, n, from_second, from_first, basis, hots,
                     block, gathered, out, x_out, rx, bx, ex, nx, field, by_row, contrib):
     fine = Fine(r, b, e, n, from_first, from_second, rx, bx, ex, nx, field)
     x = fine.scale * fine.r
@@ -468,7 +488,7 @@
         second[2 * a:2 * a + 2, :] = jnp.where(even, top, bottom)
 
 
-def correct_kernel(r, b, e, n, from_first, from_second, x_ref, high, low, basis,
+def correct_kernel(r, b, e, n, from_second, from_first, x_ref, high, low, basis,
                    r_out, coef_out, y_out, rx, bx, ex, nx, field, by_row):
     Fine(r, b, e, n, from_first, from_second, rx, bx, ex, nx, field).keep(r_out, coef_out)
     adjoints, grid_rows, width = x_ref.shape
@@ -560,7 +580,7 @@
         stack_kernel, out_shape=shape(packed_rows(zs - 1), 256),
         in_specs=[in_vmem] * (zs - 1) + [anywhere] * 3,
         cost_estimate=CHEAP, compiler_params=params(4), name="stack",
-    )(*fetched, from_first, from_second, hots)
+    )(*fetched, from_second, from_first, hots)
     spread = [swap(gathered, "narrow", k) for k in range(1, owned)]
 
     half = coarse_rows
@@ -570,14 +590,14 @@
         scratch_shapes=fine_scratch(adjoints, width) + [
             pltpu.VMEM((4 * grid_rows, width), F32), pltpu.VMEM((rows4, 256), F32)],
         cost_estimate=CHEAP, compiler_params=params(16), name="restrict",
-    )(r, b, e, n, from_first, from_second, basis, hots, block, gathered)
+    )(r, b, e, n, from_second, from_first, basis, hots, block, gathered)
 
     message_other = swap(message, "wide", 1)
     rhs = pl.pallas_call(
         add_kernel, out_shape=shape(2 * half, 128), cost_estimate=CHEAP, compiler_params=params(4), name="add",
     )(message, message_other)
-    for bit in bits_of(zs):
-        rhs = rhs + swap(rhs, "wide", 2 * bit)
+    for masks in rounds_of(zs):
+        rhs = sum_shared(rhs, "wide", [2 * k for k in masks])
     spread = tie(spread, rhs)
     spread_other = [swap(piece, "wide", 1) for piece in spread]
     for masks in rounds_of(lax.axis_size("narrow")):
@@ -602,7 +622,7 @@
         out_shape=(extended, shape(6, FIELD, width), extended),
         scratch_shapes=fine_scratch(adjoints, width) + [pltpu.VMEM((4 * grid_rows, width), F32)],
         cost_estimate=CHEAP, compiler_params=params(16), name="correct",
-    )(r, b, e, n, from_first, from_second, x, high, low, basis)
+    )(r, b, e, n, from_second, from_first, x, high, low, basis)
     field = pl.pallas_call(
         post_kernel,
         out_shape=shape(adjoints, *row_dims),

time: 46 us -> 44 us (0.957)
  waiting for transfers between devices: 13.3 us -> 11.2 us
    ppermute x15 -> x14, waiting for transfers between devices: 9.52 us -> 4.58 us  [swap(): return lax.ppermute(value, axis, [(i, i ^ bits) for i in range(size)])]
    ppermute x0 -> x2, waiting for transfers between devices: none -> 3 us  [the longest x1 1.89 us: sum_shared(): lax.ppermute(value, BOTH, [(i, i ^ (farthest if i & across else near)) fo...]
    ppermute x0 -> x2, starting transfers between devices: none -> 2.09 us  [the longest x1 1.28 us: sum_shared(): lax.ppermute(value, BOTH, [(i, i ^ (far if i & across else near)) for i i...]
    ppermute x1, starting transfers between devices: 1.63 us -> 0.01 us  [pair_swaps(): first = lax.ppermute(to_first, BOTH, [(i, i ^ 1) for i in range(count)])]
    ppermute x1, starting transfers between devices: 2.85 us -> 4.23 us  [pair_swaps(): lax.ppermute(to_second, BOTH, odd + [(target, source) for source, target...]
    ppermute x15 -> x14, starting transfers between devices: 15 us -> 13.7 us  [swap(): return lax.ppermute(value, axis, [(i, i ^ bits) for i in range(size)])]
    ppermute x1, waiting for transfers between devices: 2.31 us -> 1.22 us  [pair_swaps(): lax.ppermute(to_second, BOTH, odd + [(target, source) for source, target...]
    ppermute x1, waiting for transfers between devices: 0.01 us -> 0.83 us  [pair_swaps(): first = lax.ppermute(to_first, BOTH, [(i, i ^ 1) for i in range(count)])]
  transfers between devices with their start and end apart: 20 -> 21, of which waited for: 9 -> 12; matrix products, arithmetic and copies ran while one was open for 0% -> 0% of each run, Pallas kernels for 5% -> 5%
where the time goes in v5:
time: 44 us; the launch traced here: 43.8 us
  starting transfers between devices  22.1 us (50%)
  waiting for transfers between devices  11.2 us (25%)
  Pallas kernels  9.82 us (22%)
  between operations  0.7 us (2%)
    ppermute x14, starting transfers between devices, swap(): return lax.ppermute(value, axis, [(i, i ^ bits) for i in range(size)])  13.7 us
    ppermute x14, waiting for transfers between devices, swap(): return lax.ppermute(value, axis, [(i, i ^ bits) for i in range(size)])  4.58 us
    pallas_call x1, Pallas kernels, body(): pl.pallas_call(functools.partial(coarse_kernel, owned, coarse_rows, zs),...  4.35 us
    ppermute x1, starting transfers between devices, pair_swaps(): lax.ppermute(to_second, BOTH, odd + [(target, source) for source, target...  4.23 us
    ppermute x1, waiting for transfers between devices, sum_shared(): lax.ppermute(value, BOTH, [(i, i ^ (farthest if i & across else near)) fo...  1.89 us
    pallas_call x1, Pallas kernels, body(): pl.pallas_call(functools.partial(prepare_kernel, owned, coarse_rows), out...  1.64 us
    ppermute x1, starting transfers between devices, pair_swaps_near(): lax.ppermute(to_second, BOTH, outer + [(target, source) for source, targe...  1.31 us
    ppermute x1, starting transfers between devices, sum_shared(): lax.ppermute(value, BOTH, [(i, i ^ (far if i & across else near)) for i i...  1.28 us
  transfers between devices with their start and end apart: 21, of which 12 were waited for; matrix products, arithmetic and copies ran while one was open for 0% of the time, Pallas kernels for 5%

profile of v5, /device:TPU:0, one launch (start us, length us, event | category | flops | bytes accessed | tf_op | source)
XLA Modules:
  0.0 43.8 jit_solution(12792753973446574317)
XLA Ops:
  0.6 1.2 %begin.1 = (f32[24,128]{1,0:T(8,128)S(1)}, f32[24,128]{1,0:T(8,128)S(1)}, f32[88,256]{1,0:T(8,128)S(1)}, f32[328,256]{1,0:T(8,128)S(1)}) custom-call(f32[4,16,128]{2,1,0:T(8,128)} %r_in.3, f32[16,128]{1,0:T(8,128)} %b_in.3, f32[16,128]{1,0:T(8,128)} %e_in.3, f32[16,128]{1,0:T(8,128)} %n_in.3, s32[4,4]{1,0:T(4,128)} %links_in.1, f32[4,64,256]{2,1,0:T(8,128)} %coupling_in.1, ...), custom_call_target="tpu_custom_call" | custom-call | flops 1 | bytes 1 | tf_op jit(solution)/shard_map/begin/pallas_call | solution.py:556
  1.9 5.1 %collective-permute-start.4 = (f32[88,256]{1,0:T(8,128)S(1)}, f32[88,256]{1,0:T(8,128)S(1)}, u32[]{:S(2)}, u32[]{:S(2)}) collective-permute-start(f32[88,256]{1,0:T(8,128)S(1)} %get-tuple-element.35), channel_id=1, source_target_pairs={{0,24},{4,28},{8,16},{12,20},{16,8},{20,12},{24,0},{28,4},{1,25},{... | collective-permute-start | bytes 270344 | tf_op jit(solution)/shard_map/ppermute | solution.py:24
  7.0 0.0 collective-permute-start.3
  7.0 0.6 %collective-permute-start.2 = (f32[88,256]{1,0:T(8,128)S(1)}, f32[88,256]{1,0:T(8,128)S(1)}, u32[]{:S(2)}, u32[]{:S(2)}) collective-permute-start(f32[88,256]{1,0:T(8,128)S(1)} %get-tuple-element.35), channel_id=1, source_target_pairs={{0,8},{4,12},{8,0},{12,4},{16,24},{20,28},{24,16},{28,20},{1,9},{5... | collective-permute-start | bytes 270344 | tf_op jit(solution)/shard_map/ppermute | solution.py:24
  7.6 4.2 %collective-permute-start = (f32[24,128]{1,0:T(8,128)S(1)}, f32[24,128]{1,0:T(8,128)S(1)}, u32[]{:S(2)}, u32[]{:S(2)}) collective-permute-start(f32[24,128]{1,0:T(8,128)S(1)} %get-tuple-element.30), channel_id=1, source_target_pairs={{1,2},{3,4},{5,6},{7,8},{9,10},{11,12},{13,14},{15,16},{17,18},{19... | collective-permute-start | bytes 36872 | tf_op jit(solution)/shard_map/ppermute | solution.py:31
  11.8 0.0 collective-permute-start.1
  11.8 1.6 %prepare.1 = (f32[4,16,128]{2,1,0:T(8,128)S(1)}, f32[16,128]{1,0:T(8,128)S(1)}, f32[16,128]{1,0:T(8,128)S(1)}, f32[16,128]{1,0:T(8,128)S(1)}, f32[2048,256]{1,0:...) custom-call(f32[4,16,128]{2,1,0:T(8,128)} %r_in.3, f32[16,128]{1,0:T(8,128)} %b_in.3, ...), custom_call_target="tpu_custom_call" | custom-call | flops 1 | bytes 1 | tf_op jit(solution)/shard_map/prepare/pallas_call | solution.py:570
  13.5 1.2 %collective-permute-done.refs_3_.from_second = f32[24,128]{1,0:T(8,128)S(1)} collective-permute-done((f32[24,128]{1,0:T(8,128)S(1)}, f32[24,128]{1,0:T(8,128)S(1)}, u32[]{:S(2)}, u32[]{:S(2)}) %collective-permute-start) | collective-permute-done | bytes 12320 | tf_op jit(solution)/shard_map/ppermute | solution.py:31
  14.7 0.8 %collective-permute-done.1.refs_4_.from_first = f32[24,128]{1,0:T(8,128)S(1)} collective-permute-done((f32[24,128]{1,0:T(8,128)S(1)}, f32[24,128]{1,0:T(8,128)S(1)}, u32[]{:S(2)}, u32[]{:S(2)}) %collective-permute-start.1) | collective-permute-done | bytes 12320 | tf_op jit(solution)/shard_map/ppermute | solution.py:29
  15.5 0.0 collective-permute-done.4.refs_2_
  15.5 0.0 collective-permute-done.3.refs_1_
  15.5 0.0 collective-permute-done.2.refs_0_
  15.6 1.0 %restrict.1 = (f32[608,256]{1,0:T(8,128)S(1)}, f32[4,16,128]{2,1,0:T(8,128)S(1)}) custom-call(f32[4,16,128]{2,1,0:T(8,128)S(1)} %get-tuple-element.26.r, f32[16,128]{1,0:T(8,128)S(1)} %get-tuple-element.27.b, f32[16,128]{1,0:T(8,128)S(1)} %get-tuple-element.28.e, f32[16,128]{1,0:T(8,128)S(1)} %get-tuple-element.29.n, ...), custom_call_target="tpu_custom_call" | custom-call | flops 1 | bytes 1 | tf_op jit(solution)/shard_map/restrict/pallas_call | solution.py:587
  16.6 0.1 collective-permute-start.5
  16.7 1.6 %collective-permute-start.14 = (f32[248,256]{1,0:T(8,128)S(1)}, f32[248,256]{1,0:T(8,128)S(1)}, u32[]{:S(2)}, u32[]{:S(2)}) collective-permute-start(f32[248,256]{1,0:T(8,128)S(1)} %stack.1.gathered), channel_id=1, source_target_pairs={{0,3},{1,2},{2,1},{3,0},{4,7},{5,6},{6,5},{7,4},{8,11},{9,10},{10,... | collective-permute-start | bytes 761864 | tf_op jit(solution)/shard_map/ppermute | solution.py:24
  18.3 0.4 collective-permute-start.13
  18.7 1.6 %collective-permute-start.12 = (f32[248,256]{1,0:T(8,128)S(1)}, f32[248,256]{1,0:T(8,128)S(1)}, u32[]{:S(2)}, u32[]{:S(2)}) collective-permute-start(f32[248,256]{1,0:T(8,128)S(1)} %stack.1.gathered), channel_id=1, source_target_pairs={{0,1},{1,0},{2,3},{3,2},{4,5},{5,4},{6,7},{7,6},{8,9},{9,8},{10,11... | collective-permute-start | bytes 761864 | tf_op jit(solution)/shard_map/ppermute | solution.py:24
  20.3 0.0 collective-permute-done.5.two.message_other
  20.3 0.8 %collective-permute-start.7 = (f32[64,128]{1,0:T(8,128)S(1)}, f32[64,128]{1,0:T(8,128)S(1)}, u32[]{:S(2)}, u32[]{:S(2)}) collective-permute-start(f32[64,128]{1,0:T(8,128)S(1)} %add.20.value), channel_id=1, source_target_pairs={{0,8},{1,9},{2,10},{3,11},{4,28},{5,29},{6,30},{7,31},{8,0},{9,1},... | collective-permute-start | bytes 98312 | tf_op jit(solution)/shard_map/ppermute | solution.py:78
  21.1 1.3 %collective-permute-start.6 = (f32[64,128]{1,0:T(8,128)S(1)}, f32[64,128]{1,0:T(8,128)S(1)}, u32[]{:S(2)}, u32[]{:S(2)}) collective-permute-start(f32[64,128]{1,0:T(8,128)S(1)} %add.20.value), channel_id=1, source_target_pairs={{0,8},{1,9},{2,10},{3,11},{4,20},{5,21},{6,22},{7,23},{8,0},{9,1},... | collective-permute-start | bytes 98312 | tf_op jit(solution)/shard_map/ppermute | solution.py:77
  22.4 1.9 %collective-permute-done.7.two = f32[64,128]{1,0:T(8,128)S(1)} collective-permute-done((f32[64,128]{1,0:T(8,128)S(1)}, f32[64,128]{1,0:T(8,128)S(1)}, u32[]{:S(2)}, u32[]{:S(2)}) %collective-permute-start.7) | collective-permute-done | bytes 32800 | tf_op jit(solution)/shard_map/ppermute | solution.py:78
  24.3 1.1 %collective-permute-done.6.one = f32[64,128]{1,0:T(8,128)S(1)} collective-permute-done((f32[64,128]{1,0:T(8,128)S(1)}, f32[64,128]{1,0:T(8,128)S(1)}, u32[]{:S(2)}, u32[]{:S(2)}) %collective-permute-start.6) | collective-permute-done | bytes 32800 | tf_op jit(solution)/shard_map/ppermute | solution.py:77
  25.4 0.2 collective-permute-start.8
  25.6 1.0 %collective-permute-done.8 = f32[64,128]{1,0:T(8,128)S(1)} collective-permute-done((f32[64,128]{1,0:T(8,128)S(1)}, f32[64,128]{1,0:T(8,128)S(1)}, u32[]{:S(2)}, u32[]{:S(2)}) %collective-permute-start.8) | collective-permute-done | bytes 32800 | tf_op jit(solution)/shard_map/ppermute | solution.py:24
  26.7 2.1 %collective-permute-start.11 = (f32[64,128]{1,0:T(8,128)S(1)}, f32[64,128]{1,0:T(8,128)S(1)}, u32[]{:S(2)}, u32[]{:S(2)}) collective-permute-start(f32[64,128]{1,0:T(8,128)S(1)} %add.13.refs_3_), channel_id=1, source_target_pairs={{0,3},{1,2},{2,1},{3,0},{4,7},{5,6},{6,5},{7,4},{8,11},{9,10},{10,... | collective-permute-start | bytes 98312 | tf_op jit(solution)/shard_map/ppermute | solution.py:24
  28.7 0.4 collective-permute-start.10
  29.1 0.0 collective-permute-done.14.refs_2_
  29.1 1.0 %collective-permute-start.9 = (f32[64,128]{1,0:T(8,128)S(1)}, f32[64,128]{1,0:T(8,128)S(1)}, u32[]{:S(2)}, u32[]{:S(2)}) collective-permute-start(f32[64,128]{1,0:T(8,128)S(1)} %add.13.refs_3_), channel_id=1, source_target_pairs={{0,1},{1,0},{2,3},{3,2},{4,5},{5,4},{6,7},{7,6},{8,9},{9,8},{10,11... | collective-permute-start | bytes 98312 | tf_op jit(solution)/shard_map/ppermute | solution.py:24
  30.2 1.9 %collective-permute-done.13.refs_1_ = f32[248,256]{1,0:T(8,128)S(1)} collective-permute-done((f32[248,256]{1,0:T(8,128)S(1)}, f32[248,256]{1,0:T(8,128)S(1)}, u32[]{:S(2)}, u32[]{:S(2)}) %collective-permute-start.13) | collective-permute-done | bytes 253984 | tf_op jit(solution)/shard_map/ppermute | solution.py:24
  32.0 0.0 collective-permute-done.12.refs_0_
  32.0 0.0 collective-permute-start.15
  32.0 0.5 %collective-permute-start.16 = (f32[248,256]{1,0:T(8,128)S(1)}, f32[248,256]{1,0:T(8,128)S(1)}, u32[]{:S(2)}, u32[]{:S(2)}) collective-permute-start(f32[248,256]{1,0:T(8,128)S(1)} %get-tuple-element.39.refs_1_), channel_id=1, source_target_pairs={{0,4},{4,0},{8,12},{12,8},{16,20},{20,16},{24,28},{28,24},{1,5},{5... | collective-permute-start | bytes 761864 | tf_op jit(solution)/shard_map/ppermute | solution.py:24
  32.5 0.0 collective-permute-done.11
  32.5 0.1 collective-permute-start.17
  32.6 0.4 collective-permute-done.10
  33.0 0.0 collective-permute-done.9
  33.0 0.5 %collective-permute-done.15.refs_3_ = f32[248,256]{1,0:T(8,128)S(1)} collective-permute-done((f32[248,256]{1,0:T(8,128)S(1)}, f32[248,256]{1,0:T(8,128)S(1)}, u32[]{:S(2)}, u32[]{:S(2)}) %collective-permute-start.15) | collective-permute-done | bytes 253984 | tf_op jit(solution)/shard_map/ppermute | solution.py:24
  33.6 0.4 collective-permute-done.16.refs_4_
  33.9 0.4 collective-permute-done.17.refs_5_
  34.3 4.3 %coarse.1 = (f32[4,256]{1,0:T(4,128)}, bf16[128,256]{1,0:T(8,128)(2,1)S(1)}, bf16[128,256]{1,0:T(8,128)(2,1)S(1)}, f32[8,128]{1,0:T(8,128)S(1)}, f32[8,128]{1,0:T(8,128)S(1)}) custom-call(f32[64,128]{1,0:T(8,128)S(1)} %add_add_fusion.rhs_ref, f32[608,256]{1,0:T(8,128)S(1)} %get-tuple-element.37.one.message, ...), custom_call_target="tpu_custom_call" | custom-call | flops 1 | bytes 1 | tf_op jit(solution)/shard_map/coarse/pallas_call | solution.py:607
  38.6 0.7 %collective-permute-start.18 = (f32[8,128]{1,0:T(8,128)S(1)}, f32[8,128]{1,0:T(8,128)S(1)}, u32[]{:S(2)}, u32[]{:S(2)}) collective-permute-start(f32[8,128]{1,0:T(8,128)S(1)} %get-tuple-element.47), channel_id=1, source_target_pairs={{0,1},{1,0},{2,3},{3,2},{4,5},{5,4},{6,7},{7,6},{8,9},{9,8},{10,11... | collective-permute-start | bytes 12296 | tf_op jit(solution)/shard_map/ppermute | solution.py:37
  39.3 1.3 %collective-permute-start.20 = (f32[8,128]{1,0:T(8,128)S(1)}, f32[8,128]{1,0:T(8,128)S(1)}, u32[]{:S(2)}, u32[]{:S(2)}) collective-permute-start(f32[8,128]{1,0:T(8,128)S(1)} %get-tuple-element.48), channel_id=1, source_target_pairs={{3,4},{7,8},{11,12},{15,16},{19,20},{23,24},{27,28},{2,6},{10,14},... | collective-permute-start | bytes 12296 | tf_op jit(solution)/shard_map/ppermute | solution.py:43
  40.7 0.1 collective-permute-start.19
  40.7 0.7 %correct.1 = (f32[4,24,128]{2,1,0:T(8,128)S(1)}, f32[6,24,128]{2,1,0:T(8,128)S(1)}, f32[4,24,128]{2,1,0:T(8,128)S(1)}) custom-call(f32[4,16,128]{2,1,0:T(8,128)S(1)} %get-tuple-element.26.r, f32[16,128]{1,0:T(8,128)S(1)} %get-tuple-element.27.b, f32[16,128]{1,0:T(8,128)S(1)} %get-tuple-element.28.e, f32[16,128]{1,0:T(8,128)S(1)} %get-tuple-element.29.n, ...), custom_call_target="tpu_custom_call" | custom-call | flops 1 | bytes 1 | tf_op jit(solution)/shard_map/correct/pallas_call | solution.py:620
  41.4 0.8 %collective-permute-done.18.y_first = f32[8,128]{1,0:T(8,128)S(1)} collective-permute-done((f32[8,128]{1,0:T(8,128)S(1)}, f32[8,128]{1,0:T(8,128)S(1)}, u32[]{:S(2)}, u32[]{:S(2)}) %collective-permute-start.18) | collective-permute-done | bytes 4128 | tf_op jit(solution)/shard_map/ppermute | solution.py:37
  42.2 0.7 %collective-permute-done.20.y_outer = f32[8,128]{1,0:T(8,128)S(1)} collective-permute-done((f32[8,128]{1,0:T(8,128)S(1)}, f32[8,128]{1,0:T(8,128)S(1)}, u32[]{:S(2)}, u32[]{:S(2)}) %collective-permute-start.20) | collective-permute-done | bytes 4128 | tf_op jit(solution)/shard_map/ppermute | solution.py:43
  43.0 0.0 collective-permute-done.19.y_inner
  43.0 0.8 %post.1 = f32[4,16,128]{2,1,0:T(8,128)} custom-call(f32[4,24,128]{2,1,0:T(8,128)S(1)} %get-tuple-element.44.r, f32[6,24,128]{2,1,0:T(8,128)S(1)} %get-tuple-element.45.coef, f32[4,24,128]{2,1,0:T(8,128)S(1)} %get-tuple-element.46.y_ref, f32[8,128]{1,0:T(8,128)S(1)} %collective-permute-done.18.y_first, f32[8,128]{1,0:T(8,128)S(1)} %collective-permute-done.19.y_inner, ...), custom_call_target="tpu_custom_call" | custom-call | flops 1 | bytes 1 | tf_op jit(solution)/shard_map/post/pallas_call | solution.py:626
  (6 shorter events, 0.1 us)
Async XLA Ops:
  1.9 13.7 %collective-permute-start.4 = (f32[88,256]{1,0:T(8,128)S(1)}, f32[88,256]{1,0:T(8,128)S(1)}, u32[]{:S(2)}, u32[]{:S(2)}) collective-permute-start(f32[88,256]{1,0:T(8,128)S(1)} %get-tuple-element.35), channel_id=1, source_target_pairs={{0,24},{4,28},{8,16},{12,20},{16,8},{20,12},{24,0},{28,4},{1,25},{... | collective-permute-start | bytes 270344 | tf_op jit(solution)/shard_map/ppermute | solution.py:24
  7.0 8.6 %collective-permute-start.3 = (f32[88,256]{1,0:T(8,128)S(1)}, f32[88,256]{1,0:T(8,128)S(1)}, u32[]{:S(2)}, u32[]{:S(2)}) collective-permute-start(f32[88,256]{1,0:T(8,128)S(1)} %get-tuple-element.35), channel_id=1, source_target_pairs={{0,16},{4,20},{8,24},{12,28},{16,0},{20,4},{24,8},{28,12},{1,17},{... | collective-permute-start | bytes 270344 | tf_op jit(solution)/shard_map/ppermute | solution.py:24
  7.0 8.6 %collective-permute-start.2 = (f32[88,256]{1,0:T(8,128)S(1)}, f32[88,256]{1,0:T(8,128)S(1)}, u32[]{:S(2)}, u32[]{:S(2)}) collective-permute-start(f32[88,256]{1,0:T(8,128)S(1)} %get-tuple-element.35), channel_id=1, source_target_pairs={{0,8},{4,12},{8,0},{12,4},{16,24},{20,28},{24,16},{28,20},{1,9},{5... | collective-permute-start | bytes 270344 | tf_op jit(solution)/shard_map/ppermute | solution.py:24
  7.6 7.1 %collective-permute-start = (f32[24,128]{1,0:T(8,128)S(1)}, f32[24,128]{1,0:T(8,128)S(1)}, u32[]{:S(2)}, u32[]{:S(2)}) collective-permute-start(f32[24,128]{1,0:T(8,128)S(1)} %get-tuple-element.30), channel_id=1, source_target_pairs={{1,2},{3,4},{5,6},{7,8},{9,10},{11,12},{13,14},{15,16},{17,18},{19... | collective-permute-start | bytes 36872 | tf_op jit(solution)/shard_map/ppermute | solution.py:31
  11.8 3.7 %collective-permute-start.1 = (f32[24,128]{1,0:T(8,128)S(1)}, f32[24,128]{1,0:T(8,128)S(1)}, u32[]{:S(2)}, u32[]{:S(2)}) collective-permute-start(f32[24,128]{1,0:T(8,128)S(1)} %get-tuple-element.31), channel_id=1, source_target_pairs={{0,1},{1,0},{2,3},{3,2},{4,5},{5,4},{6,7},{7,6},{8,9},{9,8},{10,11... | collective-permute-start | bytes 36872 | tf_op jit(solution)/shard_map/ppermute | solution.py:29
  16.6 3.6 %collective-permute-start.5 = (f32[608,256]{1,0:T(8,128)S(1)}, f32[608,256]{1,0:T(8,128)S(1)}, u32[]{:S(2)}, u32[]{:S(2)}) collective-permute-start(f32[608,256]{1,0:T(8,128)S(1)} %get-tuple-element.37.one.message), channel_id=1, source_target_pairs={{0,4},{4,0},{8,12},{12,8},{16,20},{20,16},{24,28},{28,24},{1,5},{5... | collective-permute-start | bytes 1867784 | tf_op jit(solution)/shard_map/ppermute | solution.py:24
  16.7 12.4 %collective-permute-start.14 = (f32[248,256]{1,0:T(8,128)S(1)}, f32[248,256]{1,0:T(8,128)S(1)}, u32[]{:S(2)}, u32[]{:S(2)}) collective-permute-start(f32[248,256]{1,0:T(8,128)S(1)} %stack.1.gathered), channel_id=1, source_target_pairs={{0,3},{1,2},{2,1},{3,0},{4,7},{5,6},{6,5},{7,4},{8,11},{9,10},{10,... | collective-permute-start | bytes 761864 | tf_op jit(solution)/shard_map/ppermute | solution.py:24
  18.3 13.7 %collective-permute-start.13 = (f32[248,256]{1,0:T(8,128)S(1)}, f32[248,256]{1,0:T(8,128)S(1)}, u32[]{:S(2)}, u32[]{:S(2)}) collective-permute-start(f32[248,256]{1,0:T(8,128)S(1)} %stack.1.gathered), channel_id=1, source_target_pairs={{0,2},{1,3},{2,0},{3,1},{4,6},{5,7},{6,4},{7,5},{8,10},{9,11},{10,... | collective-permute-start | bytes 761864 | tf_op jit(solution)/shard_map/ppermute | solution.py:24
  18.7 13.3 %collective-permute-start.12 = (f32[248,256]{1,0:T(8,128)S(1)}, f32[248,256]{1,0:T(8,128)S(1)}, u32[]{:S(2)}, u32[]{:S(2)}) collective-permute-start(f32[248,256]{1,0:T(8,128)S(1)} %stack.1.gathered), channel_id=1, source_target_pairs={{0,1},{1,0},{2,3},{3,2},{4,5},{5,4},{6,7},{7,6},{8,9},{9,8},{10,11... | collective-permute-start | bytes 761864 | tf_op jit(solution)/shard_map/ppermute | solution.py:24
  20.3 4.0 %collective-permute-start.7 = (f32[64,128]{1,0:T(8,128)S(1)}, f32[64,128]{1,0:T(8,128)S(1)}, u32[]{:S(2)}, u32[]{:S(2)}) collective-permute-start(f32[64,128]{1,0:T(8,128)S(1)} %add.20.value), channel_id=1, source_target_pairs={{0,8},{1,9},{2,10},{3,11},{4,28},{5,29},{6,30},{7,31},{8,0},{9,1},... | collective-permute-start | bytes 98312 | tf_op jit(solution)/shard_map/ppermute | solution.py:78
  21.1 4.3 %collective-permute-start.6 = (f32[64,128]{1,0:T(8,128)S(1)}, f32[64,128]{1,0:T(8,128)S(1)}, u32[]{:S(2)}, u32[]{:S(2)}) collective-permute-start(f32[64,128]{1,0:T(8,128)S(1)} %add.20.value), channel_id=1, source_target_pairs={{0,8},{1,9},{2,10},{3,11},{4,20},{5,21},{6,22},{7,23},{8,0},{9,1},... | collective-permute-start | bytes 98312 | tf_op jit(solution)/shard_map/ppermute | solution.py:77
  25.4 1.3 %collective-permute-start.8 = (f32[64,128]{1,0:T(8,128)S(1)}, f32[64,128]{1,0:T(8,128)S(1)}, u32[]{:S(2)}, u32[]{:S(2)}) collective-permute-start(f32[64,128]{1,0:T(8,128)S(1)} %share.1), channel_id=1, source_target_pairs={{0,4},{4,0},{8,12},{12,8},{16,20},{20,16},{24,28},{28,24},{1,5},{5... | collective-permute-start | bytes 98312 | tf_op jit(solution)/shard_map/ppermute | solution.py:24
  26.7 5.9 %collective-permute-start.11 = (f32[64,128]{1,0:T(8,128)S(1)}, f32[64,128]{1,0:T(8,128)S(1)}, u32[]{:S(2)}, u32[]{:S(2)}) collective-permute-start(f32[64,128]{1,0:T(8,128)S(1)} %add.13.refs_3_), channel_id=1, source_target_pairs={{0,3},{1,2},{2,1},{3,0},{4,7},{5,6},{6,5},{7,4},{8,11},{9,10},{10,... | collective-permute-start | bytes 98312 | tf_op jit(solution)/shard_map/ppermute | solution.py:24
  28.7 4.3 %collective-permute-start.10 = (f32[64,128]{1,0:T(8,128)S(1)}, f32[64,128]{1,0:T(8,128)S(1)}, u32[]{:S(2)}, u32[]{:S(2)}) collective-permute-start(f32[64,128]{1,0:T(8,128)S(1)} %add.13.refs_3_), channel_id=1, source_target_pairs={{0,2},{1,3},{2,0},{3,1},{4,6},{5,7},{6,4},{7,5},{8,10},{9,11},{10,... | collective-permute-start | bytes 98312 | tf_op jit(solution)/shard_map/ppermute | solution.py:24
  29.1 3.9 %collective-permute-start.9 = (f32[64,128]{1,0:T(8,128)S(1)}, f32[64,128]{1,0:T(8,128)S(1)}, u32[]{:S(2)}, u32[]{:S(2)}) collective-permute-start(f32[64,128]{1,0:T(8,128)S(1)} %add.13.refs_3_), channel_id=1, source_target_pairs={{0,1},{1,0},{2,3},{3,2},{4,5},{5,4},{6,7},{7,6},{8,9},{9,8},{10,11... | collective-permute-start | bytes 98312 | tf_op jit(solution)/shard_map/ppermute | solution.py:24
  32.0 1.5 %collective-permute-start.15 = (f32[248,256]{1,0:T(8,128)S(1)}, f32[248,256]{1,0:T(8,128)S(1)}, u32[]{:S(2)}, u32[]{:S(2)}) collective-permute-start(f32[248,256]{1,0:T(8,128)S(1)} %get-tuple-element.38.refs_0_), channel_id=1, source_target_pairs={{0,4},{4,0},{8,12},{12,8},{16,20},{20,16},{24,28},{28,24},{1,5},{5... | collective-permute-start | bytes 761864 | tf_op jit(solution)/shard_map/ppermute | solution.py:24
  32.0 1.9 %collective-permute-start.16 = (f32[248,256]{1,0:T(8,128)S(1)}, f32[248,256]{1,0:T(8,128)S(1)}, u32[]{:S(2)}, u32[]{:S(2)}) collective-permute-start(f32[248,256]{1,0:T(8,128)S(1)} %get-tuple-element.39.refs_1_), channel_id=1, source_target_pairs={{0,4},{4,0},{8,12},{12,8},{16,20},{20,16},{24,28},{28,24},{1,5},{5... | collective-permute-start | bytes 761864 | tf_op jit(solution)/shard_map/ppermute | solution.py:24
  32.5 1.7 %collective-permute-start.17 = (f32[248,256]{1,0:T(8,128)S(1)}, f32[248,256]{1,0:T(8,128)S(1)}, u32[]{:S(2)}, u32[]{:S(2)}) collective-permute-start(f32[248,256]{1,0:T(8,128)S(1)} %get-tuple-element.40.refs_2_), channel_id=1, source_target_pairs={{0,4},{4,0},{8,12},{12,8},{16,20},{20,16},{24,28},{28,24},{1,5},{5... | collective-permute-start | bytes 761864 | tf_op jit(solution)/shard_map/ppermute | solution.py:24
  38.6 3.6 %collective-permute-start.18 = (f32[8,128]{1,0:T(8,128)S(1)}, f32[8,128]{1,0:T(8,128)S(1)}, u32[]{:S(2)}, u32[]{:S(2)}) collective-permute-start(f32[8,128]{1,0:T(8,128)S(1)} %get-tuple-element.47), channel_id=1, source_target_pairs={{0,1},{1,0},{2,3},{3,2},{4,5},{5,4},{6,7},{7,6},{8,9},{9,8},{10,11... | collective-permute-start | bytes 12296 | tf_op jit(solution)/shard_map/ppermute | solution.py:37
  39.3 3.6 %collective-permute-start.20 = (f32[8,128]{1,0:T(8,128)S(1)}, f32[8,128]{1,0:T(8,128)S(1)}, u32[]{:S(2)}, u32[]{:S(2)}) collective-permute-start(f32[8,128]{1,0:T(8,128)S(1)} %get-tuple-element.48), channel_id=1, source_target_pairs={{3,4},{7,8},{11,12},{15,16},{19,20},{23,24},{27,28},{2,6},{10,14},... | collective-permute-start | bytes 12296 | tf_op jit(solution)/shard_map/ppermute | solution.py:43
  40.7 2.3 %collective-permute-start.19 = (f32[8,128]{1,0:T(8,128)S(1)}, f32[8,128]{1,0:T(8,128)S(1)}, u32[]{:S(2)}, u32[]{:S(2)}) collective-permute-start(f32[8,128]{1,0:T(8,128)S(1)} %get-tuple-element.48), channel_id=1, source_target_pairs={{0,4},{1,2},{2,1},{3,7},{4,0},{5,6},{6,5},{7,3},{8,12},{9,10},{10,... | collective-permute-start | bytes 12296 | tf_op jit(solution)/shard_map/ppermute | solution.py:38

commit v6 on v5

--- a/solution.py
+++ b/solution.py
@@ -219,12 +219,11 @@
 
 
 def stack_kernel(*refs):
-    fetched, gathered = refs[:-4], refs[-1]
-    count = len(fetched)
-    gathered[count * PIECE:, :] = jnp.zeros((gathered.shape[0] - count * PIECE, gathered.shape[1]), F32)
+    fetched, gathered, far = refs[:-5], refs[-2], refs[-1]
+    owned = far.shape[0] // len(fetched)
     for i, piece in enumerate(fetched):
         gathered[PIECE * i:PIECE * i + PIECE, :] = piece[0:PIECE, :]
-        gathered[PIECE * count + i:PIECE * count + i + 1, :] = piece[PIECE:PIECE + 1, :]
+        far[owned * i:owned * i + owned, :] = piece[PIECE:PIECE + owned, :]
 
 
 def add_kernel(one, two, out):
@@ -316,7 +315,7 @@
 
 
 def restrict_kernel(coarse_rows, r, b, e, n, from_second, from_first, basis, hots,
-                    block, gathered, out, x_out, rx, bx, ex, nx, field, by_row, contrib):
+                    block, gathered, far, out, x_out, rx, bx, ex, nx, field, by_row, contrib):
     fine = Fine(r, b, e, n, from_first, from_second, rx, bx, ex, nx, field)
     x = fine.scale * fine.r
     for step in range(SWEEPS - 1):
@@ -356,7 +355,10 @@
     out[0:half, 0:128] = packed[0:half]
     out[0:half, 128:256] = packed[half:mid]
     out[half:half + block.shape[0], :] = block[...]
-    out[half + block.shape[0]:, :] = gathered[...]
+    at = half + block.shape[0]
+    out[at:at + gathered.shape[0], :] = gathered[...]
+    at += gathered.shape[0]
+    out[at:at + far.shape[0], :] = far[...]
 
 
 def prolong(group, high, low, basis):
@@ -388,14 +390,15 @@
         for c_rel, (fetched, others) in enumerate(((message, spread), (message_other, spread_other))):
             for j_rel in range(owned):
                 i = (z_rel * 2 + c_rel) * owned + j_rel
+                at_links = at_own + owned * PIECE + j_rel
+                if z_rel > 0:
+                    at_links = at_fetched + (zs - 1) * PIECE + (z_rel - 1) * owned + j_rel
                 if z_rel == 0:
-                    piece, start, index, count = fetched, at_own, j_rel, owned
+                    piece, base = fetched, at_own + j_rel * PIECE
                 elif j_rel == 0:
-                    piece, start, index, count = fetched, at_fetched, z_rel - 1, zs - 1
+                    piece, base = fetched, at_fetched + (z_rel - 1) * PIECE
                 else:
-                    piece, start, index, count = others[j_rel - 1], 0, z_rel - 1, zs - 1
-                base = start + index * PIECE
-                at_links = start + count * PIECE + index
+                    piece, base = others[j_rel - 1], (z_rel - 1) * PIECE
                 high, low = split(piece[base:base + 64, :])
                 w_high[64 * i:64 * i + 64, :] = high
                 w_low[64 * i:64 * i + 64, :] = low
@@ -406,7 +409,7 @@
                     quarters += [jnp.where(lane16, packed, turned), jnp.where(lane16, turned, packed)]
                 high, low = split(jnp.concatenate(quarters, axis=0))
                 w_inv[64 * i:64 * i + 64, :] = jnp.where(lane64, high.astype(F32), low.astype(F32)).astype(BF16)
-                link_rows[4 * i:4 * i + 4, :] = jnp.broadcast_to(piece[at_links:at_links + 1, 0:128], (4, 128))
+                link_rows[4 * i:4 * i + 4, :] = jnp.broadcast_to(fetched[at_links:at_links + 1, 0:128], (4, 128))
 
     lane = lanes((size, size))
     a_col = jnp.bitwise_and(rows((size, 1)), 3)
@@ -576,8 +579,10 @@
         cost_estimate=CHEAP, compiler_params=params(16), name="prepare",
     )(*fine_inputs, stay(support.T), stay(basis))
 
-    gathered = pl.pallas_call(
-        stack_kernel, out_shape=shape(packed_rows(zs - 1), 256),
+    height = (zs - 1) * PIECE
+    far_rows = (zs - 1) * owned
+    gathered, far = pl.pallas_call(
+        stack_kernel, out_shape=(shape(height, 256), shape(far_rows, 256)),
         in_specs=[in_vmem] * (zs - 1) + [anywhere] * 3,
         cost_estimate=CHEAP, compiler_params=params(4), name="stack",
     )(*fetched, from_second, from_first, hots)
@@ -586,11 +591,11 @@
     half = coarse_rows
     message, x = pl.pallas_call(
         functools.partial(restrict_kernel, coarse_rows),
-        out_shape=(shape(half + packed_rows(owned) + packed_rows(zs - 1), 256), shape(adjoints, *row_dims)),
+        out_shape=(shape(half + packed_rows(owned) + height + far_rows, 256), shape(adjoints, *row_dims)),
         scratch_shapes=fine_scratch(adjoints, width) + [
             pltpu.VMEM((4 * grid_rows, width), F32), pltpu.VMEM((rows4, 256), F32)],
         cost_estimate=CHEAP, compiler_params=params(16), name="restrict",
-    )(r, b, e, n, from_second, from_first, basis, hots, block, gathered)
+    )(r, b, e, n, from_second, from_first, basis, hots, block, gathered, far)
 
     message_other = swap(message, "wide", 1)
     rhs = pl.pallas_call(

time: 44 us -> 43.4 us (0.986)
  waiting for transfers between devices: 11.2 us -> 10.2 us
  transfers between devices with their start and end apart: 21 -> 21, of which waited for: 12 -> 13; matrix products, arithmetic and copies ran while one was open for 0% -> 0% of each run, Pallas kernels for 5% -> 5%
where the time goes in v6:
time: 43.4 us; the launch traced here: 43.2 us
  starting transfers between devices  22.4 us (52%)
  waiting for transfers between devices  10.2 us (24%)
  Pallas kernels  9.82 us (23%)
  between operations  0.7 us (2%)
    ppermute x14, starting transfers between devices, swap(): return lax.ppermute(value, axis, [(i, i ^ bits) for i in range(size)])  13.7 us
    pallas_call x1, Pallas kernels, body(): pl.pallas_call(functools.partial(coarse_kernel, owned, coarse_rows, zs),...  4.35 us
    ppermute x1, starting transfers between devices, pair_swaps(): lax.ppermute(to_second, BOTH, odd + [(target, source) for source, target...  4.23 us
    ppermute x14, waiting for transfers between devices, swap(): return lax.ppermute(value, axis, [(i, i ^ bits) for i in range(size)])  4.19 us
    ppermute x1, waiting for transfers between devices, sum_shared(): lax.ppermute(value, BOTH, [(i, i ^ (farthest if i & across else near)) fo...  1.89 us
    pallas_call x1, Pallas kernels, body(): pl.pallas_call(functools.partial(prepare_kernel, owned, coarse_rows), out...  1.64 us
    ppermute x1, starting transfers between devices, pair_swaps_near(): lax.ppermute(to_second, BOTH, outer + [(target, source) for source, targe...  1.55 us
    ppermute x1, starting transfers between devices, sum_shared(): lax.ppermute(value, BOTH, [(i, i ^ (far if i & across else near)) for i i...  1.28 us
  transfers between devices with their start and end apart: 21, of which 13 were waited for; matrix products, arithmetic and copies ran while one was open for 0% of the time, Pallas kernels for 5%

profile of v6, /device:TPU:0, one launch (start us, length us, event | category | flops | bytes accessed | tf_op | source)
XLA Modules:
  0.0 43.2 jit_solution(15935941589653355305)
XLA Ops:
  0.6 1.2 %begin.1 = (f32[24,128]{1,0:T(8,128)S(1)}, f32[24,128]{1,0:T(8,128)S(1)}, f32[88,256]{1,0:T(8,128)S(1)}, f32[328,256]{1,0:T(8,128)S(1)}) custom-call(f32[4,16,128]{2,1,0:T(8,128)} %r_in.3, f32[16,128]{1,0:T(8,128)} %b_in.3, f32[16,128]{1,0:T(8,128)} %e_in.3, f32[16,128]{1,0:T(8,128)} %n_in.3, s32[4,4]{1,0:T(4,128)} %links_in.1, f32[4,64,256]{2,1,0:T(8,128)} %coupling_in.1, ...), custom_call_target="tpu_custom_call" | custom-call | flops 1 | bytes 1 | tf_op jit(solution)/shard_map/begin/pallas_call | solution.py:559
  1.9 5.1 %collective-permute-start.4 = (f32[88,256]{1,0:T(8,128)S(1)}, f32[88,256]{1,0:T(8,128)S(1)}, u32[]{:S(2)}, u32[]{:S(2)}) collective-permute-start(f32[88,256]{1,0:T(8,128)S(1)} %get-tuple-element.37), channel_id=1, source_target_pairs={{0,24},{4,28},{8,16},{12,20},{16,8},{20,12},{24,0},{28,4},{1,25},{... | collective-permute-start | bytes 270344 | tf_op jit(solution)/shard_map/ppermute | solution.py:24
  7.0 0.0 collective-permute-start.3
  7.0 0.6 %collective-permute-start.2 = (f32[88,256]{1,0:T(8,128)S(1)}, f32[88,256]{1,0:T(8,128)S(1)}, u32[]{:S(2)}, u32[]{:S(2)}) collective-permute-start(f32[88,256]{1,0:T(8,128)S(1)} %get-tuple-element.37), channel_id=1, source_target_pairs={{0,8},{4,12},{8,0},{12,4},{16,24},{20,28},{24,16},{28,20},{1,9},{5... | collective-permute-start | bytes 270344 | tf_op jit(solution)/shard_map/ppermute | solution.py:24
  7.6 4.2 %collective-permute-start = (f32[24,128]{1,0:T(8,128)S(1)}, f32[24,128]{1,0:T(8,128)S(1)}, u32[]{:S(2)}, u32[]{:S(2)}) collective-permute-start(f32[24,128]{1,0:T(8,128)S(1)} %get-tuple-element.32), channel_id=1, source_target_pairs={{1,2},{3,4},{5,6},{7,8},{9,10},{11,12},{13,14},{15,16},{17,18},{19... | collective-permute-start | bytes 36872 | tf_op jit(solution)/shard_map/ppermute | solution.py:31
  11.8 0.0 collective-permute-start.1
  11.8 1.6 %prepare.1 = (f32[4,16,128]{2,1,0:T(8,128)S(1)}, f32[16,128]{1,0:T(8,128)S(1)}, f32[16,128]{1,0:T(8,128)S(1)}, f32[16,128]{1,0:T(8,128)S(1)}, f32[2048,256]{1,0:...) custom-call(f32[4,16,128]{2,1,0:T(8,128)} %r_in.3, f32[16,128]{1,0:T(8,128)} %b_in.3, ...), custom_call_target="tpu_custom_call" | custom-call | flops 1 | bytes 1 | tf_op jit(solution)/shard_map/prepare/pallas_call | solution.py:573
  13.5 1.2 %collective-permute-done.refs_3_.from_second = f32[24,128]{1,0:T(8,128)S(1)} collective-permute-done((f32[24,128]{1,0:T(8,128)S(1)}, f32[24,128]{1,0:T(8,128)S(1)}, u32[]{:S(2)}, u32[]{:S(2)}) %collective-permute-start) | collective-permute-done | bytes 12320 | tf_op jit(solution)/shard_map/ppermute | solution.py:31
  14.7 0.8 %collective-permute-done.1.refs_4_.from_first = f32[24,128]{1,0:T(8,128)S(1)} collective-permute-done((f32[24,128]{1,0:T(8,128)S(1)}, f32[24,128]{1,0:T(8,128)S(1)}, u32[]{:S(2)}, u32[]{:S(2)}) %collective-permute-start.1) | collective-permute-done | bytes 12320 | tf_op jit(solution)/shard_map/ppermute | solution.py:29
  15.5 0.0 collective-permute-done.4.refs_2_
  15.5 0.0 collective-permute-done.3.refs_1_
  15.5 0.0 collective-permute-done.2.refs_0_
  15.6 1.0 %restrict.1 = (f32[612,256]{1,0:T(8,128)S(1)}, f32[4,16,128]{2,1,0:T(8,128)S(1)}) custom-call(f32[4,16,128]{2,1,0:T(8,128)S(1)} %get-tuple-element.28.r, f32[16,128]{1,0:T(8,128)S(1)} %get-tuple-element.29.b, f32[16,128]{1,0:T(8,128)S(1)} %get-tuple-element.30.e, f32[16,128]{1,0:T(8,128)S(1)} %get-tuple-element.31.n, ...), custom_call_target="tpu_custom_call" | custom-call | flops 1 | bytes 1 | tf_op jit(solution)/shard_map/restrict/pallas_call | solution.py:592
  16.6 0.1 collective-permute-start.5
  16.7 1.6 %collective-permute-start.14 = (f32[240,256]{1,0:T(8,128)S(1)}, f32[240,256]{1,0:T(8,128)S(1)}, u32[]{:S(2)}, u32[]{:S(2)}) collective-permute-start(f32[240,256]{1,0:T(8,128)S(1)} %get-tuple-element.38.gathered), channel_id=1, source_target_pairs={{0,3},{1,2},{2,1},{3,0},{4,7},{5,6},{6,5},{7,4},{8,11},{9,10},{10,... | collective-permute-start | bytes 737288 | tf_op jit(solution)/shard_map/ppermute | solution.py:24
  18.3 0.4 collective-permute-start.13
  18.7 1.6 %collective-permute-start.12 = (f32[240,256]{1,0:T(8,128)S(1)}, f32[240,256]{1,0:T(8,128)S(1)}, u32[]{:S(2)}, u32[]{:S(2)}) collective-permute-start(f32[240,256]{1,0:T(8,128)S(1)} %get-tuple-element.38.gathered), channel_id=1, source_target_pairs={{0,1},{1,0},{2,3},{3,2},{4,5},{5,4},{6,7},{7,6},{8,9},{9,8},{10,11... | collective-permute-start | bytes 737288 | tf_op jit(solution)/shard_map/ppermute | solution.py:24
  20.3 0.0 collective-permute-done.5.two.message_other
  20.3 0.8 %collective-permute-start.7 = (f32[64,128]{1,0:T(8,128)S(1)}, f32[64,128]{1,0:T(8,128)S(1)}, u32[]{:S(2)}, u32[]{:S(2)}) collective-permute-start(f32[64,128]{1,0:T(8,128)S(1)} %add.20.value), channel_id=1, source_target_pairs={{0,8},{1,9},{2,10},{3,11},{4,28},{5,29},{6,30},{7,31},{8,0},{9,1},... | collective-permute-start | bytes 98312 | tf_op jit(solution)/shard_map/ppermute | solution.py:78
  21.1 1.3 %collective-permute-start.6 = (f32[64,128]{1,0:T(8,128)S(1)}, f32[64,128]{1,0:T(8,128)S(1)}, u32[]{:S(2)}, u32[]{:S(2)}) collective-permute-start(f32[64,128]{1,0:T(8,128)S(1)} %add.20.value), channel_id=1, source_target_pairs={{0,8},{1,9},{2,10},{3,11},{4,20},{5,21},{6,22},{7,23},{8,0},{9,1},... | collective-permute-start | bytes 98312 | tf_op jit(solution)/shard_map/ppermute | solution.py:77
  22.4 1.9 %collective-permute-done.7.two = f32[64,128]{1,0:T(8,128)S(1)} collective-permute-done((f32[64,128]{1,0:T(8,128)S(1)}, f32[64,128]{1,0:T(8,128)S(1)}, u32[]{:S(2)}, u32[]{:S(2)}) %collective-permute-start.7) | collective-permute-done | bytes 32800 | tf_op jit(solution)/shard_map/ppermute | solution.py:78
  24.3 1.1 %collective-permute-done.6.one = f32[64,128]{1,0:T(8,128)S(1)} collective-permute-done((f32[64,128]{1,0:T(8,128)S(1)}, f32[64,128]{1,0:T(8,128)S(1)}, u32[]{:S(2)}, u32[]{:S(2)}) %collective-permute-start.6) | collective-permute-done | bytes 32800 | tf_op jit(solution)/shard_map/ppermute | solution.py:77
  25.4 0.3 collective-permute-start.8
  25.6 1.0 %collective-permute-done.8 = f32[64,128]{1,0:T(8,128)S(1)} collective-permute-done((f32[64,128]{1,0:T(8,128)S(1)}, f32[64,128]{1,0:T(8,128)S(1)}, u32[]{:S(2)}, u32[]{:S(2)}) %collective-permute-start.8) | collective-permute-done | bytes 32800 | tf_op jit(solution)/shard_map/ppermute | solution.py:24
  26.7 2.1 %collective-permute-start.11 = (f32[64,128]{1,0:T(8,128)S(1)}, f32[64,128]{1,0:T(8,128)S(1)}, u32[]{:S(2)}, u32[]{:S(2)}) collective-permute-start(f32[64,128]{1,0:T(8,128)S(1)} %add.13.refs_3_), channel_id=1, source_target_pairs={{0,3},{1,2},{2,1},{3,0},{4,7},{5,6},{6,5},{7,4},{8,11},{9,10},{10,... | collective-permute-start | bytes 98312 | tf_op jit(solution)/shard_map/ppermute | solution.py:24
  28.7 0.4 collective-permute-start.10
  29.1 0.0 collective-permute-done.14.refs_2_
  29.1 1.0 %collective-permute-start.9 = (f32[64,128]{1,0:T(8,128)S(1)}, f32[64,128]{1,0:T(8,128)S(1)}, u32[]{:S(2)}, u32[]{:S(2)}) collective-permute-start(f32[64,128]{1,0:T(8,128)S(1)} %add.13.refs_3_), channel_id=1, source_target_pairs={{0,1},{1,0},{2,3},{3,2},{4,5},{5,4},{6,7},{7,6},{8,9},{9,8},{10,11... | collective-permute-start | bytes 98312 | tf_op jit(solution)/shard_map/ppermute | solution.py:24
  30.1 1.5 %collective-permute-done.13.refs_1_ = f32[240,256]{1,0:T(8,128)S(1)} collective-permute-done((f32[240,256]{1,0:T(8,128)S(1)}, f32[240,256]{1,0:T(8,128)S(1)}, u32[]{:S(2)}, u32[]{:S(2)}) %collective-permute-start.13) | collective-permute-done | bytes 245792 | tf_op jit(solution)/shard_map/ppermute | solution.py:24
  31.7 0.0 collective-permute-done.12.refs_0_
  31.7 0.0 collective-permute-start.15
  31.7 0.5 %collective-permute-start.16 = (f32[240,256]{1,0:T(8,128)S(1)}, f32[240,256]{1,0:T(8,128)S(1)}, u32[]{:S(2)}, u32[]{:S(2)}) collective-permute-start(f32[240,256]{1,0:T(8,128)S(1)} %get-tuple-element.43.refs_1_), channel_id=1, source_target_pairs={{0,4},{4,0},{8,12},{12,8},{16,20},{20,16},{24,28},{28,24},{1,5},{5... | collective-permute-start | bytes 737288 | tf_op jit(solution)/shard_map/ppermute | solution.py:24
  32.2 0.0 collective-permute-done.11
  32.2 0.1 collective-permute-start.17
  32.3 0.4 collective-permute-done.10
  32.6 0.4 collective-permute-done.9
  33.0 0.2 collective-permute-done.15.refs_3_
  33.2 0.4 collective-permute-done.16.refs_4_
  33.5 0.4 collective-permute-done.17.refs_5_
  33.9 4.4 %coarse.1 = (f32[4,256]{1,0:T(4,128)}, bf16[128,256]{1,0:T(8,128)(2,1)S(1)}, bf16[128,256]{1,0:T(8,128)(2,1)S(1)}, f32[8,128]{1,0:T(8,128)S(1)}, f32[8,128]{1,0:T(8,128)S(1)}) custom-call(f32[64,128]{1,0:T(8,128)S(1)} %add_add_fusion.rhs_ref, f32[612,256]{1,0:T(8,128)S(1)} %get-tuple-element.41.one.message, ...), custom_call_target="tpu_custom_call" | custom-call | flops 1 | bytes 1 | tf_op jit(solution)/shard_map/coarse/pallas_call | solution.py:612
  38.3 0.5 %collective-permute-start.18 = (f32[8,128]{1,0:T(8,128)S(1)}, f32[8,128]{1,0:T(8,128)S(1)}, u32[]{:S(2)}, u32[]{:S(2)}) collective-permute-start(f32[8,128]{1,0:T(8,128)S(1)} %get-tuple-element.51), channel_id=1, source_target_pairs={{0,1},{1,0},{2,3},{3,2},{4,5},{5,4},{6,7},{7,6},{8,9},{9,8},{10,11... | collective-permute-start | bytes 12296 | tf_op jit(solution)/shard_map/ppermute | solution.py:37
  38.7 1.5 %collective-permute-start.20 = (f32[8,128]{1,0:T(8,128)S(1)}, f32[8,128]{1,0:T(8,128)S(1)}, u32[]{:S(2)}, u32[]{:S(2)}) collective-permute-start(f32[8,128]{1,0:T(8,128)S(1)} %get-tuple-element.52), channel_id=1, source_target_pairs={{3,4},{7,8},{11,12},{15,16},{19,20},{23,24},{27,28},{2,6},{10,14},... | collective-permute-start | bytes 12296 | tf_op jit(solution)/shard_map/ppermute | solution.py:43
  40.3 0.4 collective-permute-start.19
  40.7 0.7 %correct.1 = (f32[4,24,128]{2,1,0:T(8,128)S(1)}, f32[6,24,128]{2,1,0:T(8,128)S(1)}, f32[4,24,128]{2,1,0:T(8,128)S(1)}) custom-call(f32[4,16,128]{2,1,0:T(8,128)S(1)} %get-tuple-element.28.r, f32[16,128]{1,0:T(8,128)S(1)} %get-tuple-element.29.b, f32[16,128]{1,0:T(8,128)S(1)} %get-tuple-element.30.e, f32[16,128]{1,0:T(8,128)S(1)} %get-tuple-element.31.n, ...), custom_call_target="tpu_custom_call" | custom-call | flops 1 | bytes 1 | tf_op jit(solution)/shard_map/correct/pallas_call | solution.py:625
  41.4 0.5 %collective-permute-done.18.y_first = f32[8,128]{1,0:T(8,128)S(1)} collective-permute-done((f32[8,128]{1,0:T(8,128)S(1)}, f32[8,128]{1,0:T(8,128)S(1)}, u32[]{:S(2)}, u32[]{:S(2)}) %collective-permute-start.18) | collective-permute-done | bytes 4128 | tf_op jit(solution)/shard_map/ppermute | solution.py:37
  41.9 0.5 %collective-permute-done.20.y_outer = f32[8,128]{1,0:T(8,128)S(1)} collective-permute-done((f32[8,128]{1,0:T(8,128)S(1)}, f32[8,128]{1,0:T(8,128)S(1)}, u32[]{:S(2)}, u32[]{:S(2)}) %collective-permute-start.20) | collective-permute-done | bytes 4128 | tf_op jit(solution)/shard_map/ppermute | solution.py:43
  42.3 0.0 collective-permute-done.19.y_inner
  42.3 0.8 %post.1 = f32[4,16,128]{2,1,0:T(8,128)} custom-call(f32[4,24,128]{2,1,0:T(8,128)S(1)} %get-tuple-element.48.r, f32[6,24,128]{2,1,0:T(8,128)S(1)} %get-tuple-element.49.coef, f32[4,24,128]{2,1,0:T(8,128)S(1)} %get-tuple-element.50.y_ref, f32[8,128]{1,0:T(8,128)S(1)} %collective-permute-done.18.y_first, f32[8,128]{1,0:T(8,128)S(1)} %collective-permute-done.19.y_inner, ...), custom_call_target="tpu_custom_call" | custom-call | flops 1 | bytes 1 | tf_op jit(solution)/shard_map/post/pallas_call | solution.py:631
  (6 shorter events, 0.1 us)
Async XLA Ops:
  1.9 13.7 %collective-permute-start.4 = (f32[88,256]{1,0:T(8,128)S(1)}, f32[88,256]{1,0:T(8,128)S(1)}, u32[]{:S(2)}, u32[]{:S(2)}) collective-permute-start(f32[88,256]{1,0:T(8,128)S(1)} %get-tuple-element.37), channel_id=1, source_target_pairs={{0,24},{4,28},{8,16},{12,20},{16,8},{20,12},{24,0},{28,4},{1,25},{... | collective-permute-start | bytes 270344 | tf_op jit(solution)/shard_map/ppermute | solution.py:24
  7.0 8.6 %collective-permute-start.3 = (f32[88,256]{1,0:T(8,128)S(1)}, f32[88,256]{1,0:T(8,128)S(1)}, u32[]{:S(2)}, u32[]{:S(2)}) collective-permute-start(f32[88,256]{1,0:T(8,128)S(1)} %get-tuple-element.37), channel_id=1, source_target_pairs={{0,16},{4,20},{8,24},{12,28},{16,0},{20,4},{24,8},{28,12},{1,17},{... | collective-permute-start | bytes 270344 | tf_op jit(solution)/shard_map/ppermute | solution.py:24
  7.0 8.6 %collective-permute-start.2 = (f32[88,256]{1,0:T(8,128)S(1)}, f32[88,256]{1,0:T(8,128)S(1)}, u32[]{:S(2)}, u32[]{:S(2)}) collective-permute-start(f32[88,256]{1,0:T(8,128)S(1)} %get-tuple-element.37), channel_id=1, source_target_pairs={{0,8},{4,12},{8,0},{12,4},{16,24},{20,28},{24,16},{28,20},{1,9},{5... | collective-permute-start | bytes 270344 | tf_op jit(solution)/shard_map/ppermute | solution.py:24
  7.6 7.1 %collective-permute-start = (f32[24,128]{1,0:T(8,128)S(1)}, f32[24,128]{1,0:T(8,128)S(1)}, u32[]{:S(2)}, u32[]{:S(2)}) collective-permute-start(f32[24,128]{1,0:T(8,128)S(1)} %get-tuple-element.32), channel_id=1, source_target_pairs={{1,2},{3,4},{5,6},{7,8},{9,10},{11,12},{13,14},{15,16},{17,18},{19... | collective-permute-start | bytes 36872 | tf_op jit(solution)/shard_map/ppermute | solution.py:31
  11.8 3.7 %collective-permute-start.1 = (f32[24,128]{1,0:T(8,128)S(1)}, f32[24,128]{1,0:T(8,128)S(1)}, u32[]{:S(2)}, u32[]{:S(2)}) collective-permute-start(f32[24,128]{1,0:T(8,128)S(1)} %get-tuple-element.33), channel_id=1, source_target_pairs={{0,1},{1,0},{2,3},{3,2},{4,5},{5,4},{6,7},{7,6},{8,9},{9,8},{10,11... | collective-permute-start | bytes 36872 | tf_op jit(solution)/shard_map/ppermute | solution.py:29
  16.6 3.6 %collective-permute-start.5 = (f32[612,256]{1,0:T(8,128)S(1)}, f32[612,256]{1,0:T(8,128)S(1)}, u32[]{:S(2)}, u32[]{:S(2)}) collective-permute-start(f32[612,256]{1,0:T(8,128)S(1)} %get-tuple-element.41.one.message), channel_id=1, source_target_pairs={{0,4},{4,0},{8,12},{12,8},{16,20},{20,16},{24,28},{28,24},{1,5},{5... | collective-permute-start | bytes 1880072 | tf_op jit(solution)/shard_map/ppermute | solution.py:24
  16.7 12.4 %collective-permute-start.14 = (f32[240,256]{1,0:T(8,128)S(1)}, f32[240,256]{1,0:T(8,128)S(1)}, u32[]{:S(2)}, u32[]{:S(2)}) collective-permute-start(f32[240,256]{1,0:T(8,128)S(1)} %get-tuple-element.38.gathered), channel_id=1, source_target_pairs={{0,3},{1,2},{2,1},{3,0},{4,7},{5,6},{6,5},{7,4},{8,11},{9,10},{10,... | collective-permute-start | bytes 737288 | tf_op jit(solution)/shard_map/ppermute | solution.py:24
  18.3 13.3 %collective-permute-start.13 = (f32[240,256]{1,0:T(8,128)S(1)}, f32[240,256]{1,0:T(8,128)S(1)}, u32[]{:S(2)}, u32[]{:S(2)}) collective-permute-start(f32[240,256]{1,0:T(8,128)S(1)} %get-tuple-element.38.gathered), channel_id=1, source_target_pairs={{0,2},{1,3},{2,0},{3,1},{4,6},{5,7},{6,4},{7,5},{8,10},{9,11},{10,... | collective-permute-start | bytes 737288 | tf_op jit(solution)/shard_map/ppermute | solution.py:24
  18.7 13.0 %collective-permute-start.12 = (f32[240,256]{1,0:T(8,128)S(1)}, f32[240,256]{1,0:T(8,128)S(1)}, u32[]{:S(2)}, u32[]{:S(2)}) collective-permute-start(f32[240,256]{1,0:T(8,128)S(1)} %get-tuple-element.38.gathered), channel_id=1, source_target_pairs={{0,1},{1,0},{2,3},{3,2},{4,5},{5,4},{6,7},{7,6},{8,9},{9,8},{10,11... | collective-permute-start | bytes 737288 | tf_op jit(solution)/shard_map/ppermute | solution.py:24
  20.3 4.0 %collective-permute-start.7 = (f32[64,128]{1,0:T(8,128)S(1)}, f32[64,128]{1,0:T(8,128)S(1)}, u32[]{:S(2)}, u32[]{:S(2)}) collective-permute-start(f32[64,128]{1,0:T(8,128)S(1)} %add.20.value), channel_id=1, source_target_pairs={{0,8},{1,9},{2,10},{3,11},{4,28},{5,29},{6,30},{7,31},{8,0},{9,1},... | collective-permute-start | bytes 98312 | tf_op jit(solution)/shard_map/ppermute | solution.py:78
  21.1 4.3 %collective-permute-start.6 = (f32[64,128]{1,0:T(8,128)S(1)}, f32[64,128]{1,0:T(8,128)S(1)}, u32[]{:S(2)}, u32[]{:S(2)}) collective-permute-start(f32[64,128]{1,0:T(8,128)S(1)} %add.20.value), channel_id=1, source_target_pairs={{0,8},{1,9},{2,10},{3,11},{4,20},{5,21},{6,22},{7,23},{8,0},{9,1},... | collective-permute-start | bytes 98312 | tf_op jit(solution)/shard_map/ppermute | solution.py:77
  25.4 1.3 %collective-permute-start.8 = (f32[64,128]{1,0:T(8,128)S(1)}, f32[64,128]{1,0:T(8,128)S(1)}, u32[]{:S(2)}, u32[]{:S(2)}) collective-permute-start(f32[64,128]{1,0:T(8,128)S(1)} %share.1), channel_id=1, source_target_pairs={{0,4},{4,0},{8,12},{12,8},{16,20},{20,16},{24,28},{28,24},{1,5},{5... | collective-permute-start | bytes 98312 | tf_op jit(solution)/shard_map/ppermute | solution.py:24
  26.7 5.5 %collective-permute-start.11 = (f32[64,128]{1,0:T(8,128)S(1)}, f32[64,128]{1,0:T(8,128)S(1)}, u32[]{:S(2)}, u32[]{:S(2)}) collective-permute-start(f32[64,128]{1,0:T(8,128)S(1)} %add.13.refs_3_), channel_id=1, source_target_pairs={{0,3},{1,2},{2,1},{3,0},{4,7},{5,6},{6,5},{7,4},{8,11},{9,10},{10,... | collective-permute-start | bytes 98312 | tf_op jit(solution)/shard_map/ppermute | solution.py:24
  28.7 3.9 %collective-permute-start.10 = (f32[64,128]{1,0:T(8,128)S(1)}, f32[64,128]{1,0:T(8,128)S(1)}, u32[]{:S(2)}, u32[]{:S(2)}) collective-permute-start(f32[64,128]{1,0:T(8,128)S(1)} %add.13.refs_3_), channel_id=1, source_target_pairs={{0,2},{1,3},{2,0},{3,1},{4,6},{5,7},{6,4},{7,5},{8,10},{9,11},{10,... | collective-permute-start | bytes 98312 | tf_op jit(solution)/shard_map/ppermute | solution.py:24
  29.1 3.9 %collective-permute-start.9 = (f32[64,128]{1,0:T(8,128)S(1)}, f32[64,128]{1,0:T(8,128)S(1)}, u32[]{:S(2)}, u32[]{:S(2)}) collective-permute-start(f32[64,128]{1,0:T(8,128)S(1)} %add.13.refs_3_), channel_id=1, source_target_pairs={{0,1},{1,0},{2,3},{3,2},{4,5},{5,4},{6,7},{7,6},{8,9},{9,8},{10,11... | collective-permute-start | bytes 98312 | tf_op jit(solution)/shard_map/ppermute | solution.py:24
  31.7 1.5 %collective-permute-start.15 = (f32[240,256]{1,0:T(8,128)S(1)}, f32[240,256]{1,0:T(8,128)S(1)}, u32[]{:S(2)}, u32[]{:S(2)}) collective-permute-start(f32[240,256]{1,0:T(8,128)S(1)} %get-tuple-element.42.refs_0_), channel_id=1, source_target_pairs={{0,4},{4,0},{8,12},{12,8},{16,20},{20,16},{24,28},{28,24},{1,5},{5... | collective-permute-start | bytes 737288 | tf_op jit(solution)/shard_map/ppermute | solution.py:24
  31.7 1.9 %collective-permute-start.16 = (f32[240,256]{1,0:T(8,128)S(1)}, f32[240,256]{1,0:T(8,128)S(1)}, u32[]{:S(2)}, u32[]{:S(2)}) collective-permute-start(f32[240,256]{1,0:T(8,128)S(1)} %get-tuple-element.43.refs_1_), channel_id=1, source_target_pairs={{0,4},{4,0},{8,12},{12,8},{16,20},{20,16},{24,28},{28,24},{1,5},{5... | collective-permute-start | bytes 737288 | tf_op jit(solution)/shard_map/ppermute | solution.py:24
  32.2 1.7 %collective-permute-start.17 = (f32[240,256]{1,0:T(8,128)S(1)}, f32[240,256]{1,0:T(8,128)S(1)}, u32[]{:S(2)}, u32[]{:S(2)}) collective-permute-start(f32[240,256]{1,0:T(8,128)S(1)} %get-tuple-element.44.refs_2_), channel_id=1, source_target_pairs={{0,4},{4,0},{8,12},{12,8},{16,20},{20,16},{24,28},{28,24},{1,5},{5... | collective-permute-start | bytes 737288 | tf_op jit(solution)/shard_map/ppermute | solution.py:24
  38.3 3.6 %collective-permute-start.18 = (f32[8,128]{1,0:T(8,128)S(1)}, f32[8,128]{1,0:T(8,128)S(1)}, u32[]{:S(2)}, u32[]{:S(2)}) collective-permute-start(f32[8,128]{1,0:T(8,128)S(1)} %get-tuple-element.51), channel_id=1, source_target_pairs={{0,1},{1,0},{2,3},{3,2},{4,5},{5,4},{6,7},{7,6},{8,9},{9,8},{10,11... | collective-permute-start | bytes 12296 | tf_op jit(solution)/shard_map/ppermute | solution.py:37
  38.7 3.6 %collective-permute-start.20 = (f32[8,128]{1,0:T(8,128)S(1)}, f32[8,128]{1,0:T(8,128)S(1)}, u32[]{:S(2)}, u32[]{:S(2)}) collective-permute-start(f32[8,128]{1,0:T(8,128)S(1)} %get-tuple-element.52), channel_id=1, source_target_pairs={{3,4},{7,8},{11,12},{15,16},{19,20},{23,24},{27,28},{2,6},{10,14},... | collective-permute-start | bytes 12296 | tf_op jit(solution)/shard_map/ppermute | solution.py:43
  40.3 2.1 %collective-permute-start.19 = (f32[8,128]{1,0:T(8,128)S(1)}, f32[8,128]{1,0:T(8,128)S(1)}, u32[]{:S(2)}, u32[]{:S(2)}) collective-permute-start(f32[8,128]{1,0:T(8,128)S(1)} %get-tuple-element.52), channel_id=1, source_target_pairs={{0,4},{1,2},{2,1},{3,7},{4,0},{5,6},{6,5},{7,3},{8,12},{9,10},{10,... | collective-permute-start | bytes 12296 | tf_op jit(solution)/shard_map/ppermute | solution.py:38

commit v7 on v6

--- a/solution.py
+++ b/solution.py
@@ -135,19 +135,28 @@
     return wait
 
 
-def pack_row(matrix, inverse, put):
-    put(0, matrix)
-    put(64, jnp.concatenate([inverse[16 * t:16 * t + 16, :] for t in range(4)], axis=1))
-
-
-def begin_kernel(owned, r_in, b_in, e_in, n_in, links_in, coupling_in, inverses_in, first, second, own, block,
-                 r, b, e, n, links, coupling, inverses, sems):
-    wait = copy_all([(r_in, r), (b_in, b), (e_in, e), (n_in, n), (links_in, links), (coupling_in, coupling),
-                     (inverses_in, inverses)], sems)
+def packed_inverse(inverse):
+    return jnp.concatenate([inverse[16 * t:16 * t + 16, :] for t in range(4)], axis=1)
+
+
+def link_rows_of(owned, links, q):
+    lane, row = lanes((8, 256)), rows((8, 256))
+    tail = jnp.zeros((8, 256), F32)
+    for j_rel in range(owned):
+        for l in range(links.shape[1]):
+            link = links[jnp.bitwise_xor(q, j_rel), l].astype(F32)
+            tail = jnp.where((row == j_rel) & (lane == l), link, tail)
+    return tail
+
+
+def begin_kernel(owned, r_in, b_in, e_in, n_in, links_in, coupling_in, inverses_in, first, second, own,
+                 r, b, e, n, links, inverse, sems):
+    q = lax.rem(lax.axis_index("narrow"), owned)
+    wait = copy_all([(r_in, r), (b_in, b), (e_in, e), (n_in, n), (links_in, links),
+                     (coupling_in.at[q], own.at[pl.ds(0, 64)]), (inverses_in.at[q], inverse)], sems)
     grid_rows = b.shape[0]
     line, _ = place()
     even = lax.rem(line, 2) == 0
-    q = lax.rem(lax.axis_index("narrow"), owned)
     wait()
 
     def message(start, north_start):
@@ -165,32 +174,25 @@
         second[at:at + size, :] = jnp.where(even, low, high)
         at += size
 
-    lane, row = lanes((8, 256)), rows((8, 256))
-    tail = jnp.zeros((8, 256), F32)
-    for j_rel in range(owned):
-        j = jnp.bitwise_xor(q, j_rel)
-
-        def put(at, value, base=j_rel * PIECE):
-            block[base + at:base + at + value.shape[0], :] = value
-            if base == 0:
-                own[at:at + value.shape[0], :] = value
-
-        pack_row(coupling[j], inverses[j], put)
-        for l in range(links.shape[1]):
-            tail = jnp.where((row == j_rel) & (lane == l), links[j, l].astype(F32), tail)
-    block[owned * PIECE:owned * PIECE + 8, :] = tail
-    own[PIECE:PIECE + 8, :] = tail
-
-
-def prepare_kernel(owned, coarse_rows, r_in, b_in, e_in, n_in, support_in, basis_in,
-                   r_out, b_out, e_out, n_out, basis, hots, sup_hots, support, sems):
+    own[64:PIECE, :] = packed_inverse(inverse[...])
+    own[PIECE:PIECE + 8, :] = link_rows_of(owned, links, q)
+
+
+def prepare_kernel(owned, coarse_rows, r_in, b_in, e_in, n_in, links_in, coupling_in, inverses_in, support_in, basis_in,
+                   block, r_out, b_out, e_out, n_out, basis, hots, sup_hots, support, links, inverses, sems):
     q = lax.rem(lax.axis_index("narrow"), owned)
     mine = lax.axis_index("wide") * owned + q
     wait_support = copy_all([(support_in, support)], sems.at[pl.ds(0, 1)])
+    wait_rows = copy_all([(coupling_in.at[jnp.bitwise_xor(q, j)], block.at[pl.ds(j * PIECE, 64)]) for j in range(owned)]
+                         + [(links_in, links), (inverses_in, inverses)], sems.at[pl.ds(13, owned + 2)])
     part = basis.shape[0] // 8
     parts = [pl.ds(part * i, part) for i in range(8)]
     wait = copy_all([(basis_in.at[at], basis.at[at]) for at in parts]
                     + [(r_in, r_out), (b_in, b_out), (e_in, e_out), (n_in, n_out)], sems.at[pl.ds(1, 12)])
+    wait_rows()
+    for j in range(owned):
+        block[j * PIECE + 64:j * PIECE + PIECE, :] = packed_inverse(inverses[jnp.bitwise_xor(q, j)])
+    block[owned * PIECE:owned * PIECE + 8, :] = link_rows_of(owned, links, q)
     wait_support()
 
     blocks = support.shape[1]
@@ -556,28 +558,31 @@
     message = shape(24, width)
     fine_inputs = tuple(map(stay, (right_sides, brinkman, east_faces, north_faces)))
     coarse_inputs = tuple(map(stay, (links, coarse_coupling, coarse_block_inverses)))
-    to_first, to_second, own, block = pl.pallas_call(
+    to_first, to_second, own = pl.pallas_call(
         functools.partial(begin_kernel, owned),
-        out_shape=(message, message, shape(packed_rows(1), 256), shape(packed_rows(owned), 256)),
+        out_shape=(message, message, shape(packed_rows(1), 256)),
         in_specs=[in_hbm] * 7,
         scratch_shapes=[
             pltpu.VMEM((adjoints, *row_dims), F32), pltpu.VMEM(row_dims, F32), pltpu.VMEM(row_dims, F32),
-            pltpu.VMEM(row_dims, F32), pltpu.SMEM(links.shape, jnp.int32), pltpu.VMEM(coarse_coupling.shape, F32),
-            pltpu.VMEM(coarse_block_inverses.shape, F32), pltpu.SemaphoreType.DMA((7,))],
+            pltpu.VMEM(row_dims, F32), pltpu.SMEM(links.shape, jnp.int32),
+            pltpu.VMEM(coarse_block_inverses.shape[1:], F32), pltpu.SemaphoreType.DMA((7,))],
         cost_estimate=CHEAP, compiler_params=params(16), name="begin",
     )(*fine_inputs, *coarse_inputs)
     from_first, from_second = pair_swaps(to_first, to_second)
     fetched = [swap(own, "wide", 2 * k) for k in range(1, zs)]
 
     rows4 = adjoints * blocks
-    r, b, e, n, basis, hots, sup_hots = pl.pallas_call(
+    block, r, b, e, n, basis, hots, sup_hots = pl.pallas_call(
         functools.partial(prepare_kernel, owned, coarse_rows),
-        out_shape=(shape(adjoints, *row_dims), shape(*row_dims), shape(*row_dims), shape(*row_dims),
-                   shape(*basis.shape), shape(2 * size, 2 * rows4, kind=BF16), shape(4 * rows4, size, kind=BF16)),
-        in_specs=[in_hbm] * 6,
-        scratch_shapes=[pltpu.VMEM((4, blocks), jnp.int32), pltpu.SemaphoreType.DMA((13,))],
+        out_shape=(shape(packed_rows(owned), 256), shape(adjoints, *row_dims), shape(*row_dims), shape(*row_dims),
+                   shape(*row_dims), shape(*basis.shape), shape(2 * size, 2 * rows4, kind=BF16),
+                   shape(4 * rows4, size, kind=BF16)),
+        in_specs=[in_hbm] * 9,
+        scratch_shapes=[
+            pltpu.VMEM((4, blocks), jnp.int32), pltpu.SMEM(links.shape, jnp.int32),
+            pltpu.VMEM(coarse_block_inverses.shape, F32), pltpu.SemaphoreType.DMA((13 + owned + 2,))],
         cost_estimate=CHEAP, compiler_params=params(16), name="prepare",
-    )(*fine_inputs, stay(support.T), stay(basis))
+    )(*fine_inputs, *coarse_inputs, stay(support.T), stay(basis))
 
     height = (zs - 1) * PIECE
     far_rows = (zs - 1) * owned

time: 43.4 us -> 43.2 us (level)
  transfers between devices with their start and end apart: 21 -> 21, of which waited for: 13 -> 13; matrix products, arithmetic and copies ran while one was open for 0% -> 0% of each run, Pallas kernels for 5% -> 6%
where the time goes in v7:
time: 43.2 us; the launch traced here: 43 us
  starting transfers between devices  22.4 us (52%)
  waiting for transfers between devices  9.96 us (23%)
  Pallas kernels  9.92 us (23%)
  between operations  0.7 us (2%)
    ppermute x14, starting transfers between devices, swap(): return lax.ppermute(value, axis, [(i, i ^ bits) for i in range(size)])  13.7 us
    pallas_call x1, Pallas kernels, body(): pl.pallas_call(functools.partial(coarse_kernel, owned, coarse_rows, zs),...  4.36 us
    ppermute x1, starting transfers between devices, pair_swaps(): lax.ppermute(to_second, BOTH, odd + [(target, source) for source, target...  4.23 us
    ppermute x14, waiting for transfers between devices, swap(): return lax.ppermute(value, axis, [(i, i ^ bits) for i in range(size)])  4.19 us
    pallas_call x1, Pallas kernels, body(): pl.pallas_call(functools.partial(prepare_kernel, owned, coarse_rows), out...  1.89 us
    ppermute x1, waiting for transfers between devices, sum_shared(): lax.ppermute(value, BOTH, [(i, i ^ (farthest if i & across else near)) fo...  1.89 us
    ppermute x1, starting transfers between devices, pair_swaps_near(): lax.ppermute(to_second, BOTH, outer + [(target, source) for source, targe...  1.55 us
    ppermute x1, starting transfers between devices, sum_shared(): lax.ppermute(value, BOTH, [(i, i ^ (far if i & across else near)) for i i...  1.28 us
  transfers between devices with their start and end apart: 21, of which 13 were waited for; matrix products, arithmetic and copies ran while one was open for 0% of the time, Pallas kernels for 6%

profile of v7, /device:TPU:0, one launch (start us, length us, event | category | flops | bytes accessed | tf_op | source)
XLA Modules:
  0.0 43.0 jit_solution(15328978282415528198)
XLA Ops:
  0.6 1.1 %begin.1 = (f32[24,128]{1,0:T(8,128)S(1)}, f32[24,128]{1,0:T(8,128)S(1)}, f32[88,256]{1,0:T(8,128)S(1)}) custom-call(f32[4,16,128]{2,1,0:T(8,128)} %r_in.3, f32[16,128]{1,0:T(8,128)} %b_in.3, f32[16,128]{1,0:T(8,128)} %e_in.3, f32[16,128]{1,0:T(8,128)} %n_in.3, s32[4,4]{1,0:T(4,128)} %links_in.3, f32[4,64,256]{2,1,0:T(8,128)} %coupling_in.3, ...), custom_call_target="tpu_custom_call" | custom-call | flops 1 | bytes 1 | tf_op jit(solution)/shard_map/begin/pallas_call | solution.py:561
  1.7 5.1 %collective-permute-start.4 = (f32[88,256]{1,0:T(8,128)S(1)}, f32[88,256]{1,0:T(8,128)S(1)}, u32[]{:S(2)}, u32[]{:S(2)}) collective-permute-start(f32[88,256]{1,0:T(8,128)S(1)} %get-tuple-element.37), channel_id=1, source_target_pairs={{0,24},{4,28},{8,16},{12,20},{16,8},{20,12},{24,0},{28,4},{1,25},{... | collective-permute-start | bytes 270344 | tf_op jit(solution)/shard_map/ppermute | solution.py:24
  6.8 0.0 collective-permute-start.3
  6.8 0.6 %collective-permute-start.2 = (f32[88,256]{1,0:T(8,128)S(1)}, f32[88,256]{1,0:T(8,128)S(1)}, u32[]{:S(2)}, u32[]{:S(2)}) collective-permute-start(f32[88,256]{1,0:T(8,128)S(1)} %get-tuple-element.37), channel_id=1, source_target_pairs={{0,8},{4,12},{8,0},{12,4},{16,24},{20,28},{24,16},{28,20},{1,9},{5... | collective-permute-start | bytes 270344 | tf_op jit(solution)/shard_map/ppermute | solution.py:24
  7.5 4.2 %collective-permute-start = (f32[24,128]{1,0:T(8,128)S(1)}, f32[24,128]{1,0:T(8,128)S(1)}, u32[]{:S(2)}, u32[]{:S(2)}) collective-permute-start(f32[24,128]{1,0:T(8,128)S(1)} %get-tuple-element.32), channel_id=1, source_target_pairs={{1,2},{3,4},{5,6},{7,8},{9,10},{11,12},{13,14},{15,16},{17,18},{19... | collective-permute-start | bytes 36872 | tf_op jit(solution)/shard_map/ppermute | solution.py:31
  11.7 0.0 collective-permute-start.1
  11.7 1.9 %prepare.1 = (f32[328,256]{1,0:T(8,128)S(1)}, f32[4,16,128]{2,1,0:T(8,128)S(1)}, f32[16,128]{1,0:T(8,128)S(1)}, f32[16,128]{1,0:T(8,128)S(1)}, f32[16,128]{1,0:T...) custom-call(f32[4,16,128]{2,1,0:T(8,128)} %r_in.3, ...), custom_call_target="tpu_custom_call" | custom-call | flops 1 | bytes 1 | tf_op jit(solution)/shard_map/prepare/pallas_call | solution.py:575
  13.6 1.0 %collective-permute-done.refs_3_.from_second = f32[24,128]{1,0:T(8,128)S(1)} collective-permute-done((f32[24,128]{1,0:T(8,128)S(1)}, f32[24,128]{1,0:T(8,128)S(1)}, u32[]{:S(2)}, u32[]{:S(2)}) %collective-permute-start) | collective-permute-done | bytes 12320 | tf_op jit(solution)/shard_map/ppermute | solution.py:31
  14.6 0.8 %collective-permute-done.1.refs_4_.from_first = f32[24,128]{1,0:T(8,128)S(1)} collective-permute-done((f32[24,128]{1,0:T(8,128)S(1)}, f32[24,128]{1,0:T(8,128)S(1)}, u32[]{:S(2)}, u32[]{:S(2)}) %collective-permute-start.1) | collective-permute-done | bytes 12320 | tf_op jit(solution)/shard_map/ppermute | solution.py:29
  15.4 0.0 collective-permute-done.4.refs_2_
  15.4 0.0 collective-permute-done.3.refs_1_
  15.4 0.0 collective-permute-done.2.refs_0_
  15.4 1.0 %restrict.1 = (f32[612,256]{1,0:T(8,128)S(1)}, f32[4,16,128]{2,1,0:T(8,128)S(1)}) custom-call(f32[4,16,128]{2,1,0:T(8,128)S(1)} %get-tuple-element.28.r, f32[16,128]{1,0:T(8,128)S(1)} %get-tuple-element.29.b, f32[16,128]{1,0:T(8,128)S(1)} %get-tuple-element.30.e, f32[16,128]{1,0:T(8,128)S(1)} %get-tuple-element.31.n, ...), custom_call_target="tpu_custom_call" | custom-call | flops 1 | bytes 1 | tf_op jit(solution)/shard_map/restrict/pallas_call | solution.py:597
  16.5 0.1 collective-permute-start.5
  16.5 1.6 %collective-permute-start.14 = (f32[240,256]{1,0:T(8,128)S(1)}, f32[240,256]{1,0:T(8,128)S(1)}, u32[]{:S(2)}, u32[]{:S(2)}) collective-permute-start(f32[240,256]{1,0:T(8,128)S(1)} %get-tuple-element.38.gathered), channel_id=1, source_target_pairs={{0,3},{1,2},{2,1},{3,0},{4,7},{5,6},{6,5},{7,4},{8,11},{9,10},{10,... | collective-permute-start | bytes 737288 | tf_op jit(solution)/shard_map/ppermute | solution.py:24
  18.2 0.4 collective-permute-start.13
  18.5 1.6 %collective-permute-start.12 = (f32[240,256]{1,0:T(8,128)S(1)}, f32[240,256]{1,0:T(8,128)S(1)}, u32[]{:S(2)}, u32[]{:S(2)}) collective-permute-start(f32[240,256]{1,0:T(8,128)S(1)} %get-tuple-element.38.gathered), channel_id=1, source_target_pairs={{0,1},{1,0},{2,3},{3,2},{4,5},{5,4},{6,7},{7,6},{8,9},{9,8},{10,11... | collective-permute-start | bytes 737288 | tf_op jit(solution)/shard_map/ppermute | solution.py:24
  20.1 0.0 collective-permute-done.5.two.message_other
  20.1 0.8 %collective-permute-start.7 = (f32[64,128]{1,0:T(8,128)S(1)}, f32[64,128]{1,0:T(8,128)S(1)}, u32[]{:S(2)}, u32[]{:S(2)}) collective-permute-start(f32[64,128]{1,0:T(8,128)S(1)} %add.20.value), channel_id=1, source_target_pairs={{0,8},{1,9},{2,10},{3,11},{4,28},{5,29},{6,30},{7,31},{8,0},{9,1},... | collective-permute-start | bytes 98312 | tf_op jit(solution)/shard_map/ppermute | solution.py:78
  20.9 1.3 %collective-permute-start.6 = (f32[64,128]{1,0:T(8,128)S(1)}, f32[64,128]{1,0:T(8,128)S(1)}, u32[]{:S(2)}, u32[]{:S(2)}) collective-permute-start(f32[64,128]{1,0:T(8,128)S(1)} %add.20.value), channel_id=1, source_target_pairs={{0,8},{1,9},{2,10},{3,11},{4,20},{5,21},{6,22},{7,23},{8,0},{9,1},... | collective-permute-start | bytes 98312 | tf_op jit(solution)/shard_map/ppermute | solution.py:77
  22.2 1.9 %collective-permute-done.7.two = f32[64,128]{1,0:T(8,128)S(1)} collective-permute-done((f32[64,128]{1,0:T(8,128)S(1)}, f32[64,128]{1,0:T(8,128)S(1)}, u32[]{:S(2)}, u32[]{:S(2)}) %collective-permute-start.7) | collective-permute-done | bytes 32800 | tf_op jit(solution)/shard_map/ppermute | solution.py:78
  24.1 1.1 %collective-permute-done.6.one = f32[64,128]{1,0:T(8,128)S(1)} collective-permute-done((f32[64,128]{1,0:T(8,128)S(1)}, f32[64,128]{1,0:T(8,128)S(1)}, u32[]{:S(2)}, u32[]{:S(2)}) %collective-permute-start.6) | collective-permute-done | bytes 32800 | tf_op jit(solution)/shard_map/ppermute | solution.py:77
  25.2 0.2 collective-permute-start.8
  25.5 1.0 %collective-permute-done.8 = f32[64,128]{1,0:T(8,128)S(1)} collective-permute-done((f32[64,128]{1,0:T(8,128)S(1)}, f32[64,128]{1,0:T(8,128)S(1)}, u32[]{:S(2)}, u32[]{:S(2)}) %collective-permute-start.8) | collective-permute-done | bytes 32800 | tf_op jit(solution)/shard_map/ppermute | solution.py:24
  26.5 2.1 %collective-permute-start.11 = (f32[64,128]{1,0:T(8,128)S(1)}, f32[64,128]{1,0:T(8,128)S(1)}, u32[]{:S(2)}, u32[]{:S(2)}) collective-permute-start(f32[64,128]{1,0:T(8,128)S(1)} %add.13.refs_3_), channel_id=1, source_target_pairs={{0,3},{1,2},{2,1},{3,0},{4,7},{5,6},{6,5},{7,4},{8,11},{9,10},{10,... | collective-permute-start | bytes 98312 | tf_op jit(solution)/shard_map/ppermute | solution.py:24
  28.6 0.4 collective-permute-start.10
  28.9 0.0 collective-permute-done.14.refs_2_
  28.9 1.0 %collective-permute-start.9 = (f32[64,128]{1,0:T(8,128)S(1)}, f32[64,128]{1,0:T(8,128)S(1)}, u32[]{:S(2)}, u32[]{:S(2)}) collective-permute-start(f32[64,128]{1,0:T(8,128)S(1)} %add.13.refs_3_), channel_id=1, source_target_pairs={{0,1},{1,0},{2,3},{3,2},{4,5},{5,4},{6,7},{7,6},{8,9},{9,8},{10,11... | collective-permute-start | bytes 98312 | tf_op jit(solution)/shard_map/ppermute | solution.py:24
  30.0 1.5 %collective-permute-done.13.refs_1_ = f32[240,256]{1,0:T(8,128)S(1)} collective-permute-done((f32[240,256]{1,0:T(8,128)S(1)}, f32[240,256]{1,0:T(8,128)S(1)}, u32[]{:S(2)}, u32[]{:S(2)}) %collective-permute-start.13) | collective-permute-done | bytes 245792 | tf_op jit(solution)/shard_map/ppermute | solution.py:24
  31.5 0.0 collective-permute-done.12.refs_0_
  31.5 0.0 collective-permute-start.15
  31.5 0.5 %collective-permute-start.16 = (f32[240,256]{1,0:T(8,128)S(1)}, f32[240,256]{1,0:T(8,128)S(1)}, u32[]{:S(2)}, u32[]{:S(2)}) collective-permute-start(f32[240,256]{1,0:T(8,128)S(1)} %get-tuple-element.43.refs_1_), channel_id=1, source_target_pairs={{0,4},{4,0},{8,12},{12,8},{16,20},{20,16},{24,28},{28,24},{1,5},{5... | collective-permute-start | bytes 737288 | tf_op jit(solution)/shard_map/ppermute | solution.py:24
  32.0 0.0 collective-permute-done.11
  32.0 0.1 collective-permute-start.17
  32.1 0.4 collective-permute-done.10
  32.5 0.4 collective-permute-done.9
  32.9 0.2 collective-permute-done.15.refs_3_
  33.0 0.4 collective-permute-done.16.refs_4_
  33.4 0.4 collective-permute-done.17.refs_5_
  33.7 4.4 %coarse.1 = (f32[4,256]{1,0:T(4,128)}, bf16[128,256]{1,0:T(8,128)(2,1)S(1)}, bf16[128,256]{1,0:T(8,128)(2,1)S(1)}, f32[8,128]{1,0:T(8,128)S(1)}, f32[8,128]{1,0:T(8,128)S(1)}) custom-call(f32[64,128]{1,0:T(8,128)S(1)} %add_add_fusion.rhs_ref, f32[612,256]{1,0:T(8,128)S(1)} %get-tuple-element.41.one.message, ...), custom_call_target="tpu_custom_call" | custom-call | flops 1 | bytes 1 | tf_op jit(solution)/shard_map/coarse/pallas_call | solution.py:617
  38.1 0.5 %collective-permute-start.18 = (f32[8,128]{1,0:T(8,128)S(1)}, f32[8,128]{1,0:T(8,128)S(1)}, u32[]{:S(2)}, u32[]{:S(2)}) collective-permute-start(f32[8,128]{1,0:T(8,128)S(1)} %get-tuple-element.51), channel_id=1, source_target_pairs={{0,1},{1,0},{2,3},{3,2},{4,5},{5,4},{6,7},{7,6},{8,9},{9,8},{10,11... | collective-permute-start | bytes 12296 | tf_op jit(solution)/shard_map/ppermute | solution.py:37
  38.6 1.5 %collective-permute-start.20 = (f32[8,128]{1,0:T(8,128)S(1)}, f32[8,128]{1,0:T(8,128)S(1)}, u32[]{:S(2)}, u32[]{:S(2)}) collective-permute-start(f32[8,128]{1,0:T(8,128)S(1)} %get-tuple-element.52), channel_id=1, source_target_pairs={{3,4},{7,8},{11,12},{15,16},{19,20},{23,24},{27,28},{2,6},{10,14},... | collective-permute-start | bytes 12296 | tf_op jit(solution)/shard_map/ppermute | solution.py:43
  40.1 0.4 collective-permute-start.19
  40.5 0.7 %correct.1 = (f32[4,24,128]{2,1,0:T(8,128)S(1)}, f32[6,24,128]{2,1,0:T(8,128)S(1)}, f32[4,24,128]{2,1,0:T(8,128)S(1)}) custom-call(f32[4,16,128]{2,1,0:T(8,128)S(1)} %get-tuple-element.28.r, f32[16,128]{1,0:T(8,128)S(1)} %get-tuple-element.29.b, f32[16,128]{1,0:T(8,128)S(1)} %get-tuple-element.30.e, f32[16,128]{1,0:T(8,128)S(1)} %get-tuple-element.31.n, ...), custom_call_target="tpu_custom_call" | custom-call | flops 1 | bytes 1 | tf_op jit(solution)/shard_map/correct/pallas_call | solution.py:630
  41.2 0.5 %collective-permute-done.18.y_first = f32[8,128]{1,0:T(8,128)S(1)} collective-permute-done((f32[8,128]{1,0:T(8,128)S(1)}, f32[8,128]{1,0:T(8,128)S(1)}, u32[]{:S(2)}, u32[]{:S(2)}) %collective-permute-start.18) | collective-permute-done | bytes 4128 | tf_op jit(solution)/shard_map/ppermute | solution.py:37
  41.7 0.5 %collective-permute-done.20.y_outer = f32[8,128]{1,0:T(8,128)S(1)} collective-permute-done((f32[8,128]{1,0:T(8,128)S(1)}, f32[8,128]{1,0:T(8,128)S(1)}, u32[]{:S(2)}, u32[]{:S(2)}) %collective-permute-start.20) | collective-permute-done | bytes 4128 | tf_op jit(solution)/shard_map/ppermute | solution.py:43
  42.2 0.0 collective-permute-done.19.y_inner
  42.2 0.8 %post.1 = f32[4,16,128]{2,1,0:T(8,128)} custom-call(f32[4,24,128]{2,1,0:T(8,128)S(1)} %get-tuple-element.48.r, f32[6,24,128]{2,1,0:T(8,128)S(1)} %get-tuple-element.49.coef, f32[4,24,128]{2,1,0:T(8,128)S(1)} %get-tuple-element.50.y_ref, f32[8,128]{1,0:T(8,128)S(1)} %collective-permute-done.18.y_first, f32[8,128]{1,0:T(8,128)S(1)} %collective-permute-done.19.y_inner, ...), custom_call_target="tpu_custom_call" | custom-call | flops 1 | bytes 1 | tf_op jit(solution)/shard_map/post/pallas_call | solution.py:636
  (6 shorter events, 0.1 us)
Async XLA Ops:
  1.7 13.7 %collective-permute-start.4 = (f32[88,256]{1,0:T(8,128)S(1)}, f32[88,256]{1,0:T(8,128)S(1)}, u32[]{:S(2)}, u32[]{:S(2)}) collective-permute-start(f32[88,256]{1,0:T(8,128)S(1)} %get-tuple-element.37), channel_id=1, source_target_pairs={{0,24},{4,28},{8,16},{12,20},{16,8},{20,12},{24,0},{28,4},{1,25},{... | collective-permute-start | bytes 270344 | tf_op jit(solution)/shard_map/ppermute | solution.py:24
  6.8 8.6 %collective-permute-start.3 = (f32[88,256]{1,0:T(8,128)S(1)}, f32[88,256]{1,0:T(8,128)S(1)}, u32[]{:S(2)}, u32[]{:S(2)}) collective-permute-start(f32[88,256]{1,0:T(8,128)S(1)} %get-tuple-element.37), channel_id=1, source_target_pairs={{0,16},{4,20},{8,24},{12,28},{16,0},{20,4},{24,8},{28,12},{1,17},{... | collective-permute-start | bytes 270344 | tf_op jit(solution)/shard_map/ppermute | solution.py:24
  6.8 8.6 %collective-permute-start.2 = (f32[88,256]{1,0:T(8,128)S(1)}, f32[88,256]{1,0:T(8,128)S(1)}, u32[]{:S(2)}, u32[]{:S(2)}) collective-permute-start(f32[88,256]{1,0:T(8,128)S(1)} %get-tuple-element.37), channel_id=1, source_target_pairs={{0,8},{4,12},{8,0},{12,4},{16,24},{20,28},{24,16},{28,20},{1,9},{5... | collective-permute-start | bytes 270344 | tf_op jit(solution)/shard_map/ppermute | solution.py:24
  7.5 7.1 %collective-permute-start = (f32[24,128]{1,0:T(8,128)S(1)}, f32[24,128]{1,0:T(8,128)S(1)}, u32[]{:S(2)}, u32[]{:S(2)}) collective-permute-start(f32[24,128]{1,0:T(8,128)S(1)} %get-tuple-element.32), channel_id=1, source_target_pairs={{1,2},{3,4},{5,6},{7,8},{9,10},{11,12},{13,14},{15,16},{17,18},{19... | collective-permute-start | bytes 36872 | tf_op jit(solution)/shard_map/ppermute | solution.py:31
  11.7 3.7 %collective-permute-start.1 = (f32[24,128]{1,0:T(8,128)S(1)}, f32[24,128]{1,0:T(8,128)S(1)}, u32[]{:S(2)}, u32[]{:S(2)}) collective-permute-start(f32[24,128]{1,0:T(8,128)S(1)} %get-tuple-element.33), channel_id=1, source_target_pairs={{0,1},{1,0},{2,3},{3,2},{4,5},{5,4},{6,7},{7,6},{8,9},{9,8},{10,11... | collective-permute-start | bytes 36872 | tf_op jit(solution)/shard_map/ppermute | solution.py:29
  16.5 3.6 %collective-permute-start.5 = (f32[612,256]{1,0:T(8,128)S(1)}, f32[612,256]{1,0:T(8,128)S(1)}, u32[]{:S(2)}, u32[]{:S(2)}) collective-permute-start(f32[612,256]{1,0:T(8,128)S(1)} %get-tuple-element.41.one.message), channel_id=1, source_target_pairs={{0,4},{4,0},{8,12},{12,8},{16,20},{20,16},{24,28},{28,24},{1,5},{5... | collective-permute-start | bytes 1880072 | tf_op jit(solution)/shard_map/ppermute | solution.py:24
  16.5 12.4 %collective-permute-start.14 = (f32[240,256]{1,0:T(8,128)S(1)}, f32[240,256]{1,0:T(8,128)S(1)}, u32[]{:S(2)}, u32[]{:S(2)}) collective-permute-start(f32[240,256]{1,0:T(8,128)S(1)} %get-tuple-element.38.gathered), channel_id=1, source_target_pairs={{0,3},{1,2},{2,1},{3,0},{4,7},{5,6},{6,5},{7,4},{8,11},{9,10},{10,... | collective-permute-start | bytes 737288 | tf_op jit(solution)/shard_map/ppermute | solution.py:24
  18.2 13.3 %collective-permute-start.13 = (f32[240,256]{1,0:T(8,128)S(1)}, f32[240,256]{1,0:T(8,128)S(1)}, u32[]{:S(2)}, u32[]{:S(2)}) collective-permute-start(f32[240,256]{1,0:T(8,128)S(1)} %get-tuple-element.38.gathered), channel_id=1, source_target_pairs={{0,2},{1,3},{2,0},{3,1},{4,6},{5,7},{6,4},{7,5},{8,10},{9,11},{10,... | collective-permute-start | bytes 737288 | tf_op jit(solution)/shard_map/ppermute | solution.py:24
  18.5 13.0 %collective-permute-start.12 = (f32[240,256]{1,0:T(8,128)S(1)}, f32[240,256]{1,0:T(8,128)S(1)}, u32[]{:S(2)}, u32[]{:S(2)}) collective-permute-start(f32[240,256]{1,0:T(8,128)S(1)} %get-tuple-element.38.gathered), channel_id=1, source_target_pairs={{0,1},{1,0},{2,3},{3,2},{4,5},{5,4},{6,7},{7,6},{8,9},{9,8},{10,11... | collective-permute-start | bytes 737288 | tf_op jit(solution)/shard_map/ppermute | solution.py:24
  20.1 4.0 %collective-permute-start.7 = (f32[64,128]{1,0:T(8,128)S(1)}, f32[64,128]{1,0:T(8,128)S(1)}, u32[]{:S(2)}, u32[]{:S(2)}) collective-permute-start(f32[64,128]{1,0:T(8,128)S(1)} %add.20.value), channel_id=1, source_target_pairs={{0,8},{1,9},{2,10},{3,11},{4,28},{5,29},{6,30},{7,31},{8,0},{9,1},... | collective-permute-start | bytes 98312 | tf_op jit(solution)/shard_map/ppermute | solution.py:78
  20.9 4.3 %collective-permute-start.6 = (f32[64,128]{1,0:T(8,128)S(1)}, f32[64,128]{1,0:T(8,128)S(1)}, u32[]{:S(2)}, u32[]{:S(2)}) collective-permute-start(f32[64,128]{1,0:T(8,128)S(1)} %add.20.value), channel_id=1, source_target_pairs={{0,8},{1,9},{2,10},{3,11},{4,20},{5,21},{6,22},{7,23},{8,0},{9,1},... | collective-permute-start | bytes 98312 | tf_op jit(solution)/shard_map/ppermute | solution.py:77
  25.2 1.3 %collective-permute-start.8 = (f32[64,128]{1,0:T(8,128)S(1)}, f32[64,128]{1,0:T(8,128)S(1)}, u32[]{:S(2)}, u32[]{:S(2)}) collective-permute-start(f32[64,128]{1,0:T(8,128)S(1)} %share.1), channel_id=1, source_target_pairs={{0,4},{4,0},{8,12},{12,8},{16,20},{20,16},{24,28},{28,24},{1,5},{5... | collective-permute-start | bytes 98312 | tf_op jit(solution)/shard_map/ppermute | solution.py:24
  26.5 5.5 %collective-permute-start.11 = (f32[64,128]{1,0:T(8,128)S(1)}, f32[64,128]{1,0:T(8,128)S(1)}, u32[]{:S(2)}, u32[]{:S(2)}) collective-permute-start(f32[64,128]{1,0:T(8,128)S(1)} %add.13.refs_3_), channel_id=1, source_target_pairs={{0,3},{1,2},{2,1},{3,0},{4,7},{5,6},{6,5},{7,4},{8,11},{9,10},{10,... | collective-permute-start | bytes 98312 | tf_op jit(solution)/shard_map/ppermute | solution.py:24
  28.6 3.9 %collective-permute-start.10 = (f32[64,128]{1,0:T(8,128)S(1)}, f32[64,128]{1,0:T(8,128)S(1)}, u32[]{:S(2)}, u32[]{:S(2)}) collective-permute-start(f32[64,128]{1,0:T(8,128)S(1)} %add.13.refs_3_), channel_id=1, source_target_pairs={{0,2},{1,3},{2,0},{3,1},{4,6},{5,7},{6,4},{7,5},{8,10},{9,11},{10,... | collective-permute-start | bytes 98312 | tf_op jit(solution)/shard_map/ppermute | solution.py:24
  28.9 3.9 %collective-permute-start.9 = (f32[64,128]{1,0:T(8,128)S(1)}, f32[64,128]{1,0:T(8,128)S(1)}, u32[]{:S(2)}, u32[]{:S(2)}) collective-permute-start(f32[64,128]{1,0:T(8,128)S(1)} %add.13.refs_3_), channel_id=1, source_target_pairs={{0,1},{1,0},{2,3},{3,2},{4,5},{5,4},{6,7},{7,6},{8,9},{9,8},{10,11... | collective-permute-start | bytes 98312 | tf_op jit(solution)/shard_map/ppermute | solution.py:24
  31.5 1.5 %collective-permute-start.15 = (f32[240,256]{1,0:T(8,128)S(1)}, f32[240,256]{1,0:T(8,128)S(1)}, u32[]{:S(2)}, u32[]{:S(2)}) collective-permute-start(f32[240,256]{1,0:T(8,128)S(1)} %get-tuple-element.42.refs_0_), channel_id=1, source_target_pairs={{0,4},{4,0},{8,12},{12,8},{16,20},{20,16},{24,28},{28,24},{1,5},{5... | collective-permute-start | bytes 737288 | tf_op jit(solution)/shard_map/ppermute | solution.py:24
  31.5 1.9 %collective-permute-start.16 = (f32[240,256]{1,0:T(8,128)S(1)}, f32[240,256]{1,0:T(8,128)S(1)}, u32[]{:S(2)}, u32[]{:S(2)}) collective-permute-start(f32[240,256]{1,0:T(8,128)S(1)} %get-tuple-element.43.refs_1_), channel_id=1, source_target_pairs={{0,4},{4,0},{8,12},{12,8},{16,20},{20,16},{24,28},{28,24},{1,5},{5... | collective-permute-start | bytes 737288 | tf_op jit(solution)/shard_map/ppermute | solution.py:24
  32.0 1.7 %collective-permute-start.17 = (f32[240,256]{1,0:T(8,128)S(1)}, f32[240,256]{1,0:T(8,128)S(1)}, u32[]{:S(2)}, u32[]{:S(2)}) collective-permute-start(f32[240,256]{1,0:T(8,128)S(1)} %get-tuple-element.44.refs_2_), channel_id=1, source_target_pairs={{0,4},{4,0},{8,12},{12,8},{16,20},{20,16},{24,28},{28,24},{1,5},{5... | collective-permute-start | bytes 737288 | tf_op jit(solution)/shard_map/ppermute | solution.py:24
  38.1 3.6 %collective-permute-start.18 = (f32[8,128]{1,0:T(8,128)S(1)}, f32[8,128]{1,0:T(8,128)S(1)}, u32[]{:S(2)}, u32[]{:S(2)}) collective-permute-start(f32[8,128]{1,0:T(8,128)S(1)} %get-tuple-element.51), channel_id=1, source_target_pairs={{0,1},{1,0},{2,3},{3,2},{4,5},{5,4},{6,7},{7,6},{8,9},{9,8},{10,11... | collective-permute-start | bytes 12296 | tf_op jit(solution)/shard_map/ppermute | solution.py:37
  38.6 3.6 %collective-permute-start.20 = (f32[8,128]{1,0:T(8,128)S(1)}, f32[8,128]{1,0:T(8,128)S(1)}, u32[]{:S(2)}, u32[]{:S(2)}) collective-permute-start(f32[8,128]{1,0:T(8,128)S(1)} %get-tuple-element.52), channel_id=1, source_target_pairs={{3,4},{7,8},{11,12},{15,16},{19,20},{23,24},{27,28},{2,6},{10,14},... | collective-permute-start | bytes 12296 | tf_op jit(solution)/shard_map/ppermute | solution.py:43
  40.1 2.1 %collective-permute-start.19 = (f32[8,128]{1,0:T(8,128)S(1)}, f32[8,128]{1,0:T(8,128)S(1)}, u32[]{:S(2)}, u32[]{:S(2)}) collective-permute-start(f32[8,128]{1,0:T(8,128)S(1)} %get-tuple-element.52), channel_id=1, source_target_pairs={{0,4},{1,2},{2,1},{3,7},{4,0},{5,6},{6,5},{7,3},{8,12},{9,10},{10,... | collective-permute-start | bytes 12296 | tf_op jit(solution)/shard_map/ppermute | solution.py:38

commit v8 on v7

--- a/solution.py
+++ b/solution.py
@@ -136,6 +136,7 @@
 
 
 def packed_inverse(inverse):
+    inverse = inverse.T
     return jnp.concatenate([inverse[16 * t:16 * t + 16, :] for t in range(4)], axis=1)
 
 
@@ -409,8 +410,13 @@
                     packed = piece[base + 64:base + 80, 128 * half:128 * half + 128]
                     turned = half_turn(packed)
                     quarters += [jnp.where(lane16, packed, turned), jnp.where(lane16, turned, packed)]
-                high, low = split(jnp.concatenate(quarters, axis=0))
-                w_inv[64 * i:64 * i + 64, :] = jnp.where(lane64, high.astype(F32), low.astype(F32)).astype(BF16)
+                columns = jnp.concatenate(quarters, axis=0)
+                if j_rel % 2:
+                    high, low = split(jnp.where(lane64, before, columns))
+                    at, to = i // 4 * 128, j_rel % 4 // 2 * 128
+                    w_inv[at:at + 64, to:to + 128] = high
+                    w_inv[at + 64:at + 128, to:to + 128] = low
+                before = columns
                 link_rows[4 * i:4 * i + 4, :] = jnp.broadcast_to(fetched[at_links:at_links + 1, 0:128], (4, 128))
 
     lane = lanes((size, size))
@@ -447,7 +453,7 @@
         low = jnp.where(here, low.astype(F32), 0.0).astype(BF16)
         for g in range(coarse_rows // 4):
             near = slice(16 * g, 16 * g + 16)
-            both = dot_t(jnp.concatenate([high[near], low[near]], axis=0), w_inv[256 * g:256 * g + 256, :])
+            both = dot(jnp.concatenate([high[near], low[near]], axis=0), w_inv[128 * g:128 * g + 128, :])
             product[near, :] = both[0:16] + both[16:32]
         return fold()
 
@@ -611,7 +617,7 @@
     spread = tie(spread, rhs)
     spread_other = [swap(piece, "wide", 1) for piece in spread]
     for masks in rounds_of(lax.axis_size("narrow")):
-        rhs = sum([swap(rhs, "narrow", k) for k in masks], rhs)
+        rhs = sum([swap(rhs, "narrow", k) for k in masks[::-1]], rhs)
 
     near = shape(rows4, 256, kind=BF16)
     coarse, high, low, y_first, y_second = pl.pallas_call(
@@ -619,7 +625,7 @@
         out_shape=(shape(owned, 256), near, near, shape(8, width), shape(8, width)),
         scratch_shapes=[
             pltpu.VMEM((64 * coarse_rows, 256), BF16), pltpu.VMEM((64 * coarse_rows, 256), BF16),
-            pltpu.VMEM((64 * coarse_rows, 128), BF16), pltpu.VMEM((size, 128), F32),
+            pltpu.VMEM((32 * coarse_rows, 256), BF16), pltpu.VMEM((size, 128), F32),
             pltpu.VMEM((4 * size, size), BF16), pltpu.VMEM((size, 256), F32),
             pltpu.VMEM((size, 128), F32), pltpu.VMEM((16, width), F32)],
         cost_estimate=CHEAP, compiler_params=params(min(48, 8 + coarse_rows // 3)), name="coarse",

time: 43.2 us -> 43.4 us (level)
  waiting for transfers between devices: 9.96 us -> 10.5 us
  transfers between devices with their start and end apart: 21 -> 21, of which waited for: 13 -> 9; matrix products, arithmetic and copies ran while one was open for 0% -> 0% of each run, Pallas kernels for 6% -> 6%
where the time goes in v8:
time: 43.4 us; the launch traced here: 43.2 us
  starting transfers between devices  22.1 us (51%)
  waiting for transfers between devices  10.5 us (24%)
  Pallas kernels  9.89 us (23%)
  between operations  0.72 us (2%)
    ppermute x14, starting transfers between devices, swap(): return lax.ppermute(value, axis, [(i, i ^ bits) for i in range(size)])  13.7 us
    ppermute x14, waiting for transfers between devices, swap(): return lax.ppermute(value, axis, [(i, i ^ bits) for i in range(size)])  4.43 us
    pallas_call x1, Pallas kernels, body(): pl.pallas_call(functools.partial(coarse_kernel, owned, coarse_rows, zs),...  4.26 us
    ppermute x1, starting transfers between devices, pair_swaps(): lax.ppermute(to_second, BOTH, odd + [(target, source) for source, target...  4.23 us
    pallas_call x1, Pallas kernels, body(): pl.pallas_call(functools.partial(prepare_kernel, owned, coarse_rows), out...  1.89 us
    ppermute x1, waiting for transfers between devices, sum_shared(): lax.ppermute(value, BOTH, [(i, i ^ (farthest if i & across else near)) fo...  1.89 us
    ppermute x1, starting transfers between devices, pair_swaps_near(): lax.ppermute(to_second, BOTH, outer + [(target, source) for source, targe...  1.62 us
    ppermute x1, starting transfers between devices, sum_shared(): lax.ppermute(value, BOTH, [(i, i ^ (far if i & across else near)) for i i...  1.28 us
  transfers between devices with their start and end apart: 21, of which 9 were waited for; matrix products, arithmetic and copies ran while one was open for 0% of the time, Pallas kernels for 6%

profile of v8, /device:TPU:0, one launch (start us, length us, event | category | flops | bytes accessed | tf_op | source)
XLA Modules:
  0.0 43.2 jit_solution(1091840750409515113)
XLA Ops:
  0.6 1.1 %begin.1 = (f32[24,128]{1,0:T(8,128)S(1)}, f32[24,128]{1,0:T(8,128)S(1)}, f32[88,256]{1,0:T(8,128)S(1)}) custom-call(f32[4,16,128]{2,1,0:T(8,128)} %r_in.3, f32[16,128]{1,0:T(8,128)} %b_in.3, f32[16,128]{1,0:T(8,128)} %e_in.3, f32[16,128]{1,0:T(8,128)} %n_in.3, s32[4,4]{1,0:T(4,128)} %links_in.3, f32[4,64,256]{2,1,0:T(8,128)} %coupling_in.3, ...), custom_call_target="tpu_custom_call" | custom-call | flops 1 | bytes 1 | tf_op jit(solution)/shard_map/begin/pallas_call | solution.py:567
  1.8 5.1 %collective-permute-start.4 = (f32[88,256]{1,0:T(8,128)S(1)}, f32[88,256]{1,0:T(8,128)S(1)}, u32[]{:S(2)}, u32[]{:S(2)}) collective-permute-start(f32[88,256]{1,0:T(8,128)S(1)} %get-tuple-element.37), channel_id=1, source_target_pairs={{0,24},{4,28},{8,16},{12,20},{16,8},{20,12},{24,0},{28,4},{1,25},{... | collective-permute-start | bytes 270344 | tf_op jit(solution)/shard_map/ppermute | solution.py:24
  6.9 0.0 collective-permute-start.3
  6.9 0.6 %collective-permute-start.2 = (f32[88,256]{1,0:T(8,128)S(1)}, f32[88,256]{1,0:T(8,128)S(1)}, u32[]{:S(2)}, u32[]{:S(2)}) collective-permute-start(f32[88,256]{1,0:T(8,128)S(1)} %get-tuple-element.37), channel_id=1, source_target_pairs={{0,8},{4,12},{8,0},{12,4},{16,24},{20,28},{24,16},{28,20},{1,9},{5... | collective-permute-start | bytes 270344 | tf_op jit(solution)/shard_map/ppermute | solution.py:24
  7.5 4.2 %collective-permute-start = (f32[24,128]{1,0:T(8,128)S(1)}, f32[24,128]{1,0:T(8,128)S(1)}, u32[]{:S(2)}, u32[]{:S(2)}) collective-permute-start(f32[24,128]{1,0:T(8,128)S(1)} %get-tuple-element.32), channel_id=1, source_target_pairs={{1,2},{3,4},{5,6},{7,8},{9,10},{11,12},{13,14},{15,16},{17,18},{19... | collective-permute-start | bytes 36872 | tf_op jit(solution)/shard_map/ppermute | solution.py:31
  11.8 0.0 collective-permute-start.1
  11.8 1.9 %prepare.1 = (f32[328,256]{1,0:T(8,128)S(1)}, f32[4,16,128]{2,1,0:T(8,128)S(1)}, f32[16,128]{1,0:T(8,128)S(1)}, f32[16,128]{1,0:T(8,128)S(1)}, f32[16,128]{1,0:T...) custom-call(f32[4,16,128]{2,1,0:T(8,128)} %r_in.3, ...), custom_call_target="tpu_custom_call" | custom-call | flops 1 | bytes 1 | tf_op jit(solution)/shard_map/prepare/pallas_call | solution.py:581
  13.7 1.0 %collective-permute-done.refs_3_.from_second = f32[24,128]{1,0:T(8,128)S(1)} collective-permute-done((f32[24,128]{1,0:T(8,128)S(1)}, f32[24,128]{1,0:T(8,128)S(1)}, u32[]{:S(2)}, u32[]{:S(2)}) %collective-permute-start) | collective-permute-done | bytes 12320 | tf_op jit(solution)/shard_map/ppermute | solution.py:31
  14.6 0.8 %collective-permute-done.1.refs_4_.from_first = f32[24,128]{1,0:T(8,128)S(1)} collective-permute-done((f32[24,128]{1,0:T(8,128)S(1)}, f32[24,128]{1,0:T(8,128)S(1)}, u32[]{:S(2)}, u32[]{:S(2)}) %collective-permute-start.1) | collective-permute-done | bytes 12320 | tf_op jit(solution)/shard_map/ppermute | solution.py:29
  15.4 0.0 collective-permute-done.4.refs_2_
  15.5 0.0 collective-permute-done.3.refs_1_
  15.5 0.0 collective-permute-done.2.refs_0_
  15.5 1.0 %restrict.1 = (f32[612,256]{1,0:T(8,128)S(1)}, f32[4,16,128]{2,1,0:T(8,128)S(1)}) custom-call(f32[4,16,128]{2,1,0:T(8,128)S(1)} %get-tuple-element.28.r, f32[16,128]{1,0:T(8,128)S(1)} %get-tuple-element.29.b, f32[16,128]{1,0:T(8,128)S(1)} %get-tuple-element.30.e, f32[16,128]{1,0:T(8,128)S(1)} %get-tuple-element.31.n, ...), custom_call_target="tpu_custom_call" | custom-call | flops 1 | bytes 1 | tf_op jit(solution)/shard_map/restrict/pallas_call | solution.py:603
  16.5 0.1 collective-permute-start.5
  16.6 1.6 %collective-permute-start.14 = (f32[240,256]{1,0:T(8,128)S(1)}, f32[240,256]{1,0:T(8,128)S(1)}, u32[]{:S(2)}, u32[]{:S(2)}) collective-permute-start(f32[240,256]{1,0:T(8,128)S(1)} %get-tuple-element.38.gathered), channel_id=1, source_target_pairs={{0,3},{1,2},{2,1},{3,0},{4,7},{5,6},{6,5},{7,4},{8,11},{9,10},{10,... | collective-permute-start | bytes 737288 | tf_op jit(solution)/shard_map/ppermute | solution.py:24
  18.2 0.4 collective-permute-start.13
  18.6 1.6 %collective-permute-start.12 = (f32[240,256]{1,0:T(8,128)S(1)}, f32[240,256]{1,0:T(8,128)S(1)}, u32[]{:S(2)}, u32[]{:S(2)}) collective-permute-start(f32[240,256]{1,0:T(8,128)S(1)} %get-tuple-element.38.gathered), channel_id=1, source_target_pairs={{0,1},{1,0},{2,3},{3,2},{4,5},{5,4},{6,7},{7,6},{8,9},{9,8},{10,11... | collective-permute-start | bytes 737288 | tf_op jit(solution)/shard_map/ppermute | solution.py:24
  20.2 0.0 collective-permute-done.5.two.message_other
  20.2 0.8 %collective-permute-start.7 = (f32[64,128]{1,0:T(8,128)S(1)}, f32[64,128]{1,0:T(8,128)S(1)}, u32[]{:S(2)}, u32[]{:S(2)}) collective-permute-start(f32[64,128]{1,0:T(8,128)S(1)} %add.20.value), channel_id=1, source_target_pairs={{0,8},{1,9},{2,10},{3,11},{4,28},{5,29},{6,30},{7,31},{8,0},{9,1},... | collective-permute-start | bytes 98312 | tf_op jit(solution)/shard_map/ppermute | solution.py:78
  21.0 1.3 %collective-permute-start.6 = (f32[64,128]{1,0:T(8,128)S(1)}, f32[64,128]{1,0:T(8,128)S(1)}, u32[]{:S(2)}, u32[]{:S(2)}) collective-permute-start(f32[64,128]{1,0:T(8,128)S(1)} %add.20.value), channel_id=1, source_target_pairs={{0,8},{1,9},{2,10},{3,11},{4,20},{5,21},{6,22},{7,23},{8,0},{9,1},... | collective-permute-start | bytes 98312 | tf_op jit(solution)/shard_map/ppermute | solution.py:77
  22.3 1.9 %collective-permute-done.7.two = f32[64,128]{1,0:T(8,128)S(1)} collective-permute-done((f32[64,128]{1,0:T(8,128)S(1)}, f32[64,128]{1,0:T(8,128)S(1)}, u32[]{:S(2)}, u32[]{:S(2)}) %collective-permute-start.7) | collective-permute-done | bytes 32800 | tf_op jit(solution)/shard_map/ppermute | solution.py:78
  24.2 1.1 %collective-permute-done.6.one = f32[64,128]{1,0:T(8,128)S(1)} collective-permute-done((f32[64,128]{1,0:T(8,128)S(1)}, f32[64,128]{1,0:T(8,128)S(1)}, u32[]{:S(2)}, u32[]{:S(2)}) %collective-permute-start.6) | collective-permute-done | bytes 32800 | tf_op jit(solution)/shard_map/ppermute | solution.py:77
  25.3 0.2 collective-permute-start.8
  25.5 1.0 %collective-permute-done.8 = f32[64,128]{1,0:T(8,128)S(1)} collective-permute-done((f32[64,128]{1,0:T(8,128)S(1)}, f32[64,128]{1,0:T(8,128)S(1)}, u32[]{:S(2)}, u32[]{:S(2)}) %collective-permute-start.8) | collective-permute-done | bytes 32800 | tf_op jit(solution)/shard_map/ppermute | solution.py:24
  26.6 1.0 %collective-permute-start.11 = (f32[64,128]{1,0:T(8,128)S(1)}, f32[64,128]{1,0:T(8,128)S(1)}, u32[]{:S(2)}, u32[]{:S(2)}) collective-permute-start(f32[64,128]{1,0:T(8,128)S(1)} %add.13.refs_3_), channel_id=1, source_target_pairs={{0,1},{1,0},{2,3},{3,2},{4,5},{5,4},{6,7},{7,6},{8,9},{9,8},{10,11... | collective-permute-start | bytes 98312 | tf_op jit(solution)/shard_map/ppermute | solution.py:24
  27.6 1.6 %collective-permute-start.10 = (f32[64,128]{1,0:T(8,128)S(1)}, f32[64,128]{1,0:T(8,128)S(1)}, u32[]{:S(2)}, u32[]{:S(2)}) collective-permute-start(f32[64,128]{1,0:T(8,128)S(1)} %add.13.refs_3_), channel_id=1, source_target_pairs={{0,2},{1,3},{2,0},{3,1},{4,6},{5,7},{6,4},{7,5},{8,10},{9,11},{10,... | collective-permute-start | bytes 98312 | tf_op jit(solution)/shard_map/ppermute | solution.py:24
  29.2 0.0 collective-permute-done.14.refs_2_
  29.2 0.9 %collective-permute-start.9 = (f32[64,128]{1,0:T(8,128)S(1)}, f32[64,128]{1,0:T(8,128)S(1)}, u32[]{:S(2)}, u32[]{:S(2)}) collective-permute-start(f32[64,128]{1,0:T(8,128)S(1)} %add.13.refs_3_), channel_id=1, source_target_pairs={{0,3},{1,2},{2,1},{3,0},{4,7},{5,6},{6,5},{7,4},{8,11},{9,10},{10,... | collective-permute-start | bytes 98312 | tf_op jit(solution)/shard_map/ppermute | solution.py:24
  30.1 1.2 %collective-permute-done.13.refs_1_ = f32[240,256]{1,0:T(8,128)S(1)} collective-permute-done((f32[240,256]{1,0:T(8,128)S(1)}, f32[240,256]{1,0:T(8,128)S(1)}, u32[]{:S(2)}, u32[]{:S(2)}) %collective-permute-start.13) | collective-permute-done | bytes 245792 | tf_op jit(solution)/shard_map/ppermute | solution.py:24
  31.2 0.0 collective-permute-done.12.refs_0_
  31.2 0.0 collective-permute-start.15
  31.2 0.5 %collective-permute-start.16 = (f32[240,256]{1,0:T(8,128)S(1)}, f32[240,256]{1,0:T(8,128)S(1)}, u32[]{:S(2)}, u32[]{:S(2)}) collective-permute-start(f32[240,256]{1,0:T(8,128)S(1)} %get-tuple-element.43.refs_1_), channel_id=1, source_target_pairs={{0,4},{4,0},{8,12},{12,8},{16,20},{20,16},{24,28},{28,24},{1,5},{5... | collective-permute-start | bytes 737288 | tf_op jit(solution)/shard_map/ppermute | solution.py:24
  31.7 0.0 collective-permute-done.11
  31.7 0.1 collective-permute-start.17
  31.8 0.0 collective-permute-done.10
  31.9 2.2 %collective-permute-done.9 = f32[64,128]{1,0:T(8,128)S(1)} collective-permute-done((f32[64,128]{1,0:T(8,128)S(1)}, f32[64,128]{1,0:T(8,128)S(1)}, u32[]{:S(2)}, u32[]{:S(2)}) %collective-permute-start.9) | collective-permute-done | bytes 32800 | tf_op jit(solution)/shard_map/ppermute | solution.py:24
  34.0 0.0 collective-permute-done.15.refs_3_
  34.0 0.0 collective-permute-done.16.refs_4_
  34.1 0.0 collective-permute-done.17.refs_5_
  34.1 4.3 %coarse.1 = (f32[4,256]{1,0:T(4,128)}, bf16[128,256]{1,0:T(8,128)(2,1)S(1)}, bf16[128,256]{1,0:T(8,128)(2,1)S(1)}, f32[8,128]{1,0:T(8,128)S(1)}, f32[8,128]{1,0:T(8,128)S(1)}) custom-call(f32[64,128]{1,0:T(8,128)S(1)} %add_add_fusion.rhs_ref, f32[612,256]{1,0:T(8,128)S(1)} %get-tuple-element.41.one.message, ...), custom_call_target="tpu_custom_call" | custom-call | flops 1 | bytes 1 | tf_op jit(solution)/shard_map/coarse/pallas_call | solution.py:623
  38.3 0.4 collective-permute-start.18
  38.8 1.6 %collective-permute-start.20 = (f32[8,128]{1,0:T(8,128)S(1)}, f32[8,128]{1,0:T(8,128)S(1)}, u32[]{:S(2)}, u32[]{:S(2)}) collective-permute-start(f32[8,128]{1,0:T(8,128)S(1)} %get-tuple-element.52), channel_id=1, source_target_pairs={{3,4},{7,8},{11,12},{15,16},{19,20},{23,24},{27,28},{2,6},{10,14},... | collective-permute-start | bytes 12296 | tf_op jit(solution)/shard_map/ppermute | solution.py:43
  40.4 0.0 collective-permute-start.19
  40.4 0.7 %correct.1 = (f32[4,24,128]{2,1,0:T(8,128)S(1)}, f32[6,24,128]{2,1,0:T(8,128)S(1)}, f32[4,24,128]{2,1,0:T(8,128)S(1)}) custom-call(f32[4,16,128]{2,1,0:T(8,128)S(1)} %get-tuple-element.28.r, f32[16,128]{1,0:T(8,128)S(1)} %get-tuple-element.29.b, f32[16,128]{1,0:T(8,128)S(1)} %get-tuple-element.30.e, f32[16,128]{1,0:T(8,128)S(1)} %get-tuple-element.31.n, ...), custom_call_target="tpu_custom_call" | custom-call | flops 1 | bytes 1 | tf_op jit(solution)/shard_map/correct/pallas_call | solution.py:636
  41.1 0.9 %collective-permute-done.18.y_first = f32[8,128]{1,0:T(8,128)S(1)} collective-permute-done((f32[8,128]{1,0:T(8,128)S(1)}, f32[8,128]{1,0:T(8,128)S(1)}, u32[]{:S(2)}, u32[]{:S(2)}) %collective-permute-start.18) | collective-permute-done | bytes 4128 | tf_op jit(solution)/shard_map/ppermute | solution.py:37
  42.0 0.4 collective-permute-done.20.y_outer
  42.4 0.0 collective-permute-done.19.y_inner
  42.4 0.8 %post.1 = f32[4,16,128]{2,1,0:T(8,128)} custom-call(f32[4,24,128]{2,1,0:T(8,128)S(1)} %get-tuple-element.48.r, f32[6,24,128]{2,1,0:T(8,128)S(1)} %get-tuple-element.49.coef, f32[4,24,128]{2,1,0:T(8,128)S(1)} %get-tuple-element.50.y_ref, f32[8,128]{1,0:T(8,128)S(1)} %collective-permute-done.18.y_first, f32[8,128]{1,0:T(8,128)S(1)} %collective-permute-done.19.y_inner, ...), custom_call_target="tpu_custom_call" | custom-call | flops 1 | bytes 1 | tf_op jit(solution)/shard_map/post/pallas_call | solution.py:642
  (6 shorter events, 0.1 us)
Async XLA Ops:
  1.8 13.7 %collective-permute-start.4 = (f32[88,256]{1,0:T(8,128)S(1)}, f32[88,256]{1,0:T(8,128)S(1)}, u32[]{:S(2)}, u32[]{:S(2)}) collective-permute-start(f32[88,256]{1,0:T(8,128)S(1)} %get-tuple-element.37), channel_id=1, source_target_pairs={{0,24},{4,28},{8,16},{12,20},{16,8},{20,12},{24,0},{28,4},{1,25},{... | collective-permute-start | bytes 270344 | tf_op jit(solution)/shard_map/ppermute | solution.py:24
  6.9 8.6 %collective-permute-start.3 = (f32[88,256]{1,0:T(8,128)S(1)}, f32[88,256]{1,0:T(8,128)S(1)}, u32[]{:S(2)}, u32[]{:S(2)}) collective-permute-start(f32[88,256]{1,0:T(8,128)S(1)} %get-tuple-element.37), channel_id=1, source_target_pairs={{0,16},{4,20},{8,24},{12,28},{16,0},{20,4},{24,8},{28,12},{1,17},{... | collective-permute-start | bytes 270344 | tf_op jit(solution)/shard_map/ppermute | solution.py:24
  6.9 8.6 %collective-permute-start.2 = (f32[88,256]{1,0:T(8,128)S(1)}, f32[88,256]{1,0:T(8,128)S(1)}, u32[]{:S(2)}, u32[]{:S(2)}) collective-permute-start(f32[88,256]{1,0:T(8,128)S(1)} %get-tuple-element.37), channel_id=1, source_target_pairs={{0,8},{4,12},{8,0},{12,4},{16,24},{20,28},{24,16},{28,20},{1,9},{5... | collective-permute-start | bytes 270344 | tf_op jit(solution)/shard_map/ppermute | solution.py:24
  7.5 7.1 %collective-permute-start = (f32[24,128]{1,0:T(8,128)S(1)}, f32[24,128]{1,0:T(8,128)S(1)}, u32[]{:S(2)}, u32[]{:S(2)}) collective-permute-start(f32[24,128]{1,0:T(8,128)S(1)} %get-tuple-element.32), channel_id=1, source_target_pairs={{1,2},{3,4},{5,6},{7,8},{9,10},{11,12},{13,14},{15,16},{17,18},{19... | collective-permute-start | bytes 36872 | tf_op jit(solution)/shard_map/ppermute | solution.py:31
  11.8 3.7 %collective-permute-start.1 = (f32[24,128]{1,0:T(8,128)S(1)}, f32[24,128]{1,0:T(8,128)S(1)}, u32[]{:S(2)}, u32[]{:S(2)}) collective-permute-start(f32[24,128]{1,0:T(8,128)S(1)} %get-tuple-element.33), channel_id=1, source_target_pairs={{0,1},{1,0},{2,3},{3,2},{4,5},{5,4},{6,7},{7,6},{8,9},{9,8},{10,11... | collective-permute-start | bytes 36872 | tf_op jit(solution)/shard_map/ppermute | solution.py:29
  16.5 3.6 %collective-permute-start.5 = (f32[612,256]{1,0:T(8,128)S(1)}, f32[612,256]{1,0:T(8,128)S(1)}, u32[]{:S(2)}, u32[]{:S(2)}) collective-permute-start(f32[612,256]{1,0:T(8,128)S(1)} %get-tuple-element.41.one.message), channel_id=1, source_target_pairs={{0,4},{4,0},{8,12},{12,8},{16,20},{20,16},{24,28},{28,24},{1,5},{5... | collective-permute-start | bytes 1880072 | tf_op jit(solution)/shard_map/ppermute | solution.py:24
  16.6 12.6 %collective-permute-start.14 = (f32[240,256]{1,0:T(8,128)S(1)}, f32[240,256]{1,0:T(8,128)S(1)}, u32[]{:S(2)}, u32[]{:S(2)}) collective-permute-start(f32[240,256]{1,0:T(8,128)S(1)} %get-tuple-element.38.gathered), channel_id=1, source_target_pairs={{0,3},{1,2},{2,1},{3,0},{4,7},{5,6},{6,5},{7,4},{8,11},{9,10},{10,... | collective-permute-start | bytes 737288 | tf_op jit(solution)/shard_map/ppermute | solution.py:24
  18.2 13.0 %collective-permute-start.13 = (f32[240,256]{1,0:T(8,128)S(1)}, f32[240,256]{1,0:T(8,128)S(1)}, u32[]{:S(2)}, u32[]{:S(2)}) collective-permute-start(f32[240,256]{1,0:T(8,128)S(1)} %get-tuple-element.38.gathered), channel_id=1, source_target_pairs={{0,2},{1,3},{2,0},{3,1},{4,6},{5,7},{6,4},{7,5},{8,10},{9,11},{10,... | collective-permute-start | bytes 737288 | tf_op jit(solution)/shard_map/ppermute | solution.py:24
  18.6 12.6 %collective-permute-start.12 = (f32[240,256]{1,0:T(8,128)S(1)}, f32[240,256]{1,0:T(8,128)S(1)}, u32[]{:S(2)}, u32[]{:S(2)}) collective-permute-start(f32[240,256]{1,0:T(8,128)S(1)} %get-tuple-element.38.gathered), channel_id=1, source_target_pairs={{0,1},{1,0},{2,3},{3,2},{4,5},{5,4},{6,7},{7,6},{8,9},{9,8},{10,11... | collective-permute-start | bytes 737288 | tf_op jit(solution)/shard_map/ppermute | solution.py:24
  20.2 4.0 %collective-permute-start.7 = (f32[64,128]{1,0:T(8,128)S(1)}, f32[64,128]{1,0:T(8,128)S(1)}, u32[]{:S(2)}, u32[]{:S(2)}) collective-permute-start(f32[64,128]{1,0:T(8,128)S(1)} %add.20.value), channel_id=1, source_target_pairs={{0,8},{1,9},{2,10},{3,11},{4,28},{5,29},{6,30},{7,31},{8,0},{9,1},... | collective-permute-start | bytes 98312 | tf_op jit(solution)/shard_map/ppermute | solution.py:78
  21.0 4.3 %collective-permute-start.6 = (f32[64,128]{1,0:T(8,128)S(1)}, f32[64,128]{1,0:T(8,128)S(1)}, u32[]{:S(2)}, u32[]{:S(2)}) collective-permute-start(f32[64,128]{1,0:T(8,128)S(1)} %add.20.value), channel_id=1, source_target_pairs={{0,8},{1,9},{2,10},{3,11},{4,20},{5,21},{6,22},{7,23},{8,0},{9,1},... | collective-permute-start | bytes 98312 | tf_op jit(solution)/shard_map/ppermute | solution.py:77
  25.3 1.3 %collective-permute-start.8 = (f32[64,128]{1,0:T(8,128)S(1)}, f32[64,128]{1,0:T(8,128)S(1)}, u32[]{:S(2)}, u32[]{:S(2)}) collective-permute-start(f32[64,128]{1,0:T(8,128)S(1)} %share.1), channel_id=1, source_target_pairs={{0,4},{4,0},{8,12},{12,8},{16,20},{20,16},{24,28},{28,24},{1,5},{5... | collective-permute-start | bytes 98312 | tf_op jit(solution)/shard_map/ppermute | solution.py:24
  26.6 5.2 %collective-permute-start.11 = (f32[64,128]{1,0:T(8,128)S(1)}, f32[64,128]{1,0:T(8,128)S(1)}, u32[]{:S(2)}, u32[]{:S(2)}) collective-permute-start(f32[64,128]{1,0:T(8,128)S(1)} %add.13.refs_3_), channel_id=1, source_target_pairs={{0,1},{1,0},{2,3},{3,2},{4,5},{5,4},{6,7},{7,6},{8,9},{9,8},{10,11... | collective-permute-start | bytes 98312 | tf_op jit(solution)/shard_map/ppermute | solution.py:24
  27.6 4.3 %collective-permute-start.10 = (f32[64,128]{1,0:T(8,128)S(1)}, f32[64,128]{1,0:T(8,128)S(1)}, u32[]{:S(2)}, u32[]{:S(2)}) collective-permute-start(f32[64,128]{1,0:T(8,128)S(1)} %add.13.refs_3_), channel_id=1, source_target_pairs={{0,2},{1,3},{2,0},{3,1},{4,6},{5,7},{6,4},{7,5},{8,10},{9,11},{10,... | collective-permute-start | bytes 98312 | tf_op jit(solution)/shard_map/ppermute | solution.py:24
  29.2 4.8 %collective-permute-start.9 = (f32[64,128]{1,0:T(8,128)S(1)}, f32[64,128]{1,0:T(8,128)S(1)}, u32[]{:S(2)}, u32[]{:S(2)}) collective-permute-start(f32[64,128]{1,0:T(8,128)S(1)} %add.13.refs_3_), channel_id=1, source_target_pairs={{0,3},{1,2},{2,1},{3,0},{4,7},{5,6},{6,5},{7,4},{8,11},{9,10},{10,... | collective-permute-start | bytes 98312 | tf_op jit(solution)/shard_map/ppermute | solution.py:24
  31.2 2.8 %collective-permute-start.15 = (f32[240,256]{1,0:T(8,128)S(1)}, f32[240,256]{1,0:T(8,128)S(1)}, u32[]{:S(2)}, u32[]{:S(2)}) collective-permute-start(f32[240,256]{1,0:T(8,128)S(1)} %get-tuple-element.42.refs_0_), channel_id=1, source_target_pairs={{0,4},{4,0},{8,12},{12,8},{16,20},{20,16},{24,28},{28,24},{1,5},{5... | collective-permute-start | bytes 737288 | tf_op jit(solution)/shard_map/ppermute | solution.py:24
  31.2 2.8 %collective-permute-start.16 = (f32[240,256]{1,0:T(8,128)S(1)}, f32[240,256]{1,0:T(8,128)S(1)}, u32[]{:S(2)}, u32[]{:S(2)}) collective-permute-start(f32[240,256]{1,0:T(8,128)S(1)} %get-tuple-element.43.refs_1_), channel_id=1, source_target_pairs={{0,4},{4,0},{8,12},{12,8},{16,20},{20,16},{24,28},{28,24},{1,5},{5... | collective-permute-start | bytes 737288 | tf_op jit(solution)/shard_map/ppermute | solution.py:24
  31.7 2.3 %collective-permute-start.17 = (f32[240,256]{1,0:T(8,128)S(1)}, f32[240,256]{1,0:T(8,128)S(1)}, u32[]{:S(2)}, u32[]{:S(2)}) collective-permute-start(f32[240,256]{1,0:T(8,128)S(1)} %get-tuple-element.44.refs_2_), channel_id=1, source_target_pairs={{0,4},{4,0},{8,12},{12,8},{16,20},{20,16},{24,28},{28,24},{1,5},{5... | collective-permute-start | bytes 737288 | tf_op jit(solution)/shard_map/ppermute | solution.py:24
  38.3 3.6 %collective-permute-start.18 = (f32[8,128]{1,0:T(8,128)S(1)}, f32[8,128]{1,0:T(8,128)S(1)}, u32[]{:S(2)}, u32[]{:S(2)}) collective-permute-start(f32[8,128]{1,0:T(8,128)S(1)} %get-tuple-element.51), channel_id=1, source_target_pairs={{0,1},{1,0},{2,3},{3,2},{4,5},{5,4},{6,7},{7,6},{8,9},{9,8},{10,11... | collective-permute-start | bytes 12296 | tf_op jit(solution)/shard_map/ppermute | solution.py:37
  38.8 3.6 %collective-permute-start.20 = (f32[8,128]{1,0:T(8,128)S(1)}, f32[8,128]{1,0:T(8,128)S(1)}, u32[]{:S(2)}, u32[]{:S(2)}) collective-permute-start(f32[8,128]{1,0:T(8,128)S(1)} %get-tuple-element.52), channel_id=1, source_target_pairs={{3,4},{7,8},{11,12},{15,16},{19,20},{23,24},{27,28},{2,6},{10,14},... | collective-permute-start | bytes 12296 | tf_op jit(solution)/shard_map/ppermute | solution.py:43
  40.4 2.0 %collective-permute-start.19 = (f32[8,128]{1,0:T(8,128)S(1)}, f32[8,128]{1,0:T(8,128)S(1)}, u32[]{:S(2)}, u32[]{:S(2)}) collective-permute-start(f32[8,128]{1,0:T(8,128)S(1)} %get-tuple-element.52), channel_id=1, source_target_pairs={{0,4},{1,2},{2,1},{3,7},{4,0},{5,6},{6,5},{7,3},{8,12},{9,10},{10,... | collective-permute-start | bytes 12296 | tf_op jit(solution)/shard_map/ppermute | solution.py:38

commit v9 on v7

--- a/solution.py
+++ b/solution.py
@@ -73,7 +73,7 @@
         return value + swap(value, axis, masks[0])
     count, across = lax.axis_size(BOTH), lax.axis_size("narrow")
     unit = across if axis == "wide" else 1
-    near, far, farthest = [unit * mask for mask in masks]
+    near, farthest, far = [unit * mask for mask in masks]
     one = lax.ppermute(value, BOTH, [(i, i ^ (far if i & across else near)) for i in range(count)])
     two = lax.ppermute(value, BOTH, [(i, i ^ (farthest if i & across else near)) for i in range(count)])
     value = pl.pallas_call(

time: 43.2 us -> 43.4 us (level)
  starting transfers between devices: 22.4 us -> 23 us
  waiting for transfers between devices: 9.96 us -> 9.52 us
    ppermute x14, starting transfers between devices: 13.7 us -> 14.6 us  [swap(): return lax.ppermute(value, axis, [(i, i ^ bits) for i in range(size)])]
    ppermute x14, waiting for transfers between devices: 4.19 us -> 3.66 us  [swap(): return lax.ppermute(value, axis, [(i, i ^ bits) for i in range(size)])]
  transfers between devices with their start and end apart: 21 -> 21, of which waited for: 13 -> 12; matrix products, arithmetic and copies ran while one was open for 0% -> 0% of each run, Pallas kernels for 6% -> 6%
where the time goes in v9:
time: 43.4 us; the launch traced here: 43.2 us
  starting transfers between devices  23 us (53%)
  Pallas kernels  9.92 us (23%)
  waiting for transfers between devices  9.52 us (22%)
  between operations  0.7 us (2%)
    ppermute x14, starting transfers between devices, swap(): return lax.ppermute(value, axis, [(i, i ^ bits) for i in range(size)])  14.6 us
    pallas_call x1, Pallas kernels, body(): pl.pallas_call(functools.partial(coarse_kernel, owned, coarse_rows, zs),...  4.36 us
    ppermute x1, starting transfers between devices, pair_swaps(): lax.ppermute(to_second, BOTH, odd + [(target, source) for source, target...  4.23 us
    ppermute x14, waiting for transfers between devices, swap(): return lax.ppermute(value, axis, [(i, i ^ bits) for i in range(size)])  3.66 us
    ppermute x1, waiting for transfers between devices, sum_shared(): lax.ppermute(value, BOTH, [(i, i ^ (farthest if i & across else near)) fo...  1.95 us
    pallas_call x1, Pallas kernels, body(): pl.pallas_call(functools.partial(prepare_kernel, owned, coarse_rows), out...  1.89 us
    ppermute x1, starting transfers between devices, pair_swaps_near(): lax.ppermute(to_second, BOTH, outer + [(target, source) for source, targe...  1.4 us
    ppermute x1, starting transfers between devices, sum_shared(): lax.ppermute(value, BOTH, [(i, i ^ (far if i & across else near)) for i i...  1.28 us
  transfers between devices with their start and end apart: 21, of which 12 were waited for; matrix products, arithmetic and copies ran while one was open for 0% of the time, Pallas kernels for 6%

profile of v9, /device:TPU:0, one launch (start us, length us, event | category | flops | bytes accessed | tf_op | source)
XLA Modules:
  0.0 43.2 jit_solution(6835428241668052448)
XLA Ops:
  0.6 1.1 %begin.1 = (f32[24,128]{1,0:T(8,128)S(1)}, f32[24,128]{1,0:T(8,128)S(1)}, f32[88,256]{1,0:T(8,128)S(1)}) custom-call(f32[4,16,128]{2,1,0:T(8,128)} %r_in.3, f32[16,128]{1,0:T(8,128)} %b_in.3, f32[16,128]{1,0:T(8,128)} %e_in.3, f32[16,128]{1,0:T(8,128)} %n_in.3, s32[4,4]{1,0:T(4,128)} %links_in.3, f32[4,64,256]{2,1,0:T(8,128)} %coupling_in.3, ...), custom_call_target="tpu_custom_call" | custom-call | flops 1 | bytes 1 | tf_op jit(solution)/shard_map/begin/pallas_call | solution.py:561
  1.7 5.1 %collective-permute-start.4 = (f32[88,256]{1,0:T(8,128)S(1)}, f32[88,256]{1,0:T(8,128)S(1)}, u32[]{:S(2)}, u32[]{:S(2)}) collective-permute-start(f32[88,256]{1,0:T(8,128)S(1)} %get-tuple-element.37), channel_id=1, source_target_pairs={{0,24},{4,28},{8,16},{12,20},{16,8},{20,12},{24,0},{28,4},{1,25},{... | collective-permute-start | bytes 270344 | tf_op jit(solution)/shard_map/ppermute | solution.py:24
  6.8 0.0 collective-permute-start.3
  6.8 0.6 %collective-permute-start.2 = (f32[88,256]{1,0:T(8,128)S(1)}, f32[88,256]{1,0:T(8,128)S(1)}, u32[]{:S(2)}, u32[]{:S(2)}) collective-permute-start(f32[88,256]{1,0:T(8,128)S(1)} %get-tuple-element.37), channel_id=1, source_target_pairs={{0,8},{4,12},{8,0},{12,4},{16,24},{20,28},{24,16},{28,20},{1,9},{5... | collective-permute-start | bytes 270344 | tf_op jit(solution)/shard_map/ppermute | solution.py:24
  7.5 4.2 %collective-permute-start = (f32[24,128]{1,0:T(8,128)S(1)}, f32[24,128]{1,0:T(8,128)S(1)}, u32[]{:S(2)}, u32[]{:S(2)}) collective-permute-start(f32[24,128]{1,0:T(8,128)S(1)} %get-tuple-element.32), channel_id=1, source_target_pairs={{1,2},{3,4},{5,6},{7,8},{9,10},{11,12},{13,14},{15,16},{17,18},{19... | collective-permute-start | bytes 36872 | tf_op jit(solution)/shard_map/ppermute | solution.py:31
  11.7 0.0 collective-permute-start.1
  11.7 1.9 %prepare.1 = (f32[328,256]{1,0:T(8,128)S(1)}, f32[4,16,128]{2,1,0:T(8,128)S(1)}, f32[16,128]{1,0:T(8,128)S(1)}, f32[16,128]{1,0:T(8,128)S(1)}, f32[16,128]{1,0:T...) custom-call(f32[4,16,128]{2,1,0:T(8,128)} %r_in.3, ...), custom_call_target="tpu_custom_call" | custom-call | flops 1 | bytes 1 | tf_op jit(solution)/shard_map/prepare/pallas_call | solution.py:575
  13.6 1.0 %collective-permute-done.refs_3_.from_second = f32[24,128]{1,0:T(8,128)S(1)} collective-permute-done((f32[24,128]{1,0:T(8,128)S(1)}, f32[24,128]{1,0:T(8,128)S(1)}, u32[]{:S(2)}, u32[]{:S(2)}) %collective-permute-start) | collective-permute-done | bytes 12320 | tf_op jit(solution)/shard_map/ppermute | solution.py:31
  14.6 0.8 %collective-permute-done.1.refs_4_.from_first = f32[24,128]{1,0:T(8,128)S(1)} collective-permute-done((f32[24,128]{1,0:T(8,128)S(1)}, f32[24,128]{1,0:T(8,128)S(1)}, u32[]{:S(2)}, u32[]{:S(2)}) %collective-permute-start.1) | collective-permute-done | bytes 12320 | tf_op jit(solution)/shard_map/ppermute | solution.py:29
  15.4 0.0 collective-permute-done.4.refs_2_
  15.4 0.0 collective-permute-done.3.refs_1_
  15.4 0.0 collective-permute-done.2.refs_0_
  15.4 1.0 %restrict.1 = (f32[612,256]{1,0:T(8,128)S(1)}, f32[4,16,128]{2,1,0:T(8,128)S(1)}) custom-call(f32[4,16,128]{2,1,0:T(8,128)S(1)} %get-tuple-element.28.r, f32[16,128]{1,0:T(8,128)S(1)} %get-tuple-element.29.b, f32[16,128]{1,0:T(8,128)S(1)} %get-tuple-element.30.e, f32[16,128]{1,0:T(8,128)S(1)} %get-tuple-element.31.n, ...), custom_call_target="tpu_custom_call" | custom-call | flops 1 | bytes 1 | tf_op jit(solution)/shard_map/restrict/pallas_call | solution.py:597
  16.5 0.1 collective-permute-start.5
  16.5 1.6 %collective-permute-start.14 = (f32[240,256]{1,0:T(8,128)S(1)}, f32[240,256]{1,0:T(8,128)S(1)}, u32[]{:S(2)}, u32[]{:S(2)}) collective-permute-start(f32[240,256]{1,0:T(8,128)S(1)} %get-tuple-element.38.gathered), channel_id=1, source_target_pairs={{0,3},{1,2},{2,1},{3,0},{4,7},{5,6},{6,5},{7,4},{8,11},{9,10},{10,... | collective-permute-start | bytes 737288 | tf_op jit(solution)/shard_map/ppermute | solution.py:24
  18.2 0.4 collective-permute-start.13
  18.5 1.6 %collective-permute-start.12 = (f32[240,256]{1,0:T(8,128)S(1)}, f32[240,256]{1,0:T(8,128)S(1)}, u32[]{:S(2)}, u32[]{:S(2)}) collective-permute-start(f32[240,256]{1,0:T(8,128)S(1)} %get-tuple-element.38.gathered), channel_id=1, source_target_pairs={{0,1},{1,0},{2,3},{3,2},{4,5},{5,4},{6,7},{7,6},{8,9},{9,8},{10,11... | collective-permute-start | bytes 737288 | tf_op jit(solution)/shard_map/ppermute | solution.py:24
  20.1 0.0 collective-permute-done.5.two.message_other
  20.1 0.8 %collective-permute-start.7 = (f32[64,128]{1,0:T(8,128)S(1)}, f32[64,128]{1,0:T(8,128)S(1)}, u32[]{:S(2)}, u32[]{:S(2)}) collective-permute-start(f32[64,128]{1,0:T(8,128)S(1)} %add.20.value), channel_id=1, source_target_pairs={{0,8},{1,9},{2,10},{3,11},{4,20},{5,21},{6,22},{7,23},{8,0},{9,1},... | collective-permute-start | bytes 98312 | tf_op jit(solution)/shard_map/ppermute | solution.py:78
  20.9 1.3 %collective-permute-start.6 = (f32[64,128]{1,0:T(8,128)S(1)}, f32[64,128]{1,0:T(8,128)S(1)}, u32[]{:S(2)}, u32[]{:S(2)}) collective-permute-start(f32[64,128]{1,0:T(8,128)S(1)} %add.20.value), channel_id=1, source_target_pairs={{0,8},{1,9},{2,10},{3,11},{4,28},{5,29},{6,30},{7,31},{8,0},{9,1},... | collective-permute-start | bytes 98312 | tf_op jit(solution)/shard_map/ppermute | solution.py:77
  22.2 1.9 %collective-permute-done.7.two = f32[64,128]{1,0:T(8,128)S(1)} collective-permute-done((f32[64,128]{1,0:T(8,128)S(1)}, f32[64,128]{1,0:T(8,128)S(1)}, u32[]{:S(2)}, u32[]{:S(2)}) %collective-permute-start.7) | collective-permute-done | bytes 32800 | tf_op jit(solution)/shard_map/ppermute | solution.py:78
  24.2 0.7 %collective-permute-done.6.one = f32[64,128]{1,0:T(8,128)S(1)} collective-permute-done((f32[64,128]{1,0:T(8,128)S(1)}, f32[64,128]{1,0:T(8,128)S(1)}, u32[]{:S(2)}, u32[]{:S(2)}) %collective-permute-start.6) | collective-permute-done | bytes 32800 | tf_op jit(solution)/shard_map/ppermute | solution.py:77
  24.9 1.1 %collective-permute-start.8 = (f32[64,128]{1,0:T(8,128)S(1)}, f32[64,128]{1,0:T(8,128)S(1)}, u32[]{:S(2)}, u32[]{:S(2)}) collective-permute-start(f32[64,128]{1,0:T(8,128)S(1)} %share.1), channel_id=1, source_target_pairs={{0,4},{4,0},{8,12},{12,8},{16,20},{20,16},{24,28},{28,24},{1,5},{5... | collective-permute-start | bytes 98312 | tf_op jit(solution)/shard_map/ppermute | solution.py:24
  26.0 0.9 %collective-permute-done.8 = f32[64,128]{1,0:T(8,128)S(1)} collective-permute-done((f32[64,128]{1,0:T(8,128)S(1)}, f32[64,128]{1,0:T(8,128)S(1)}, u32[]{:S(2)}, u32[]{:S(2)}) %collective-permute-start.8) | collective-permute-done | bytes 32800 | tf_op jit(solution)/shard_map/ppermute | solution.py:24
  26.9 1.1 %collective-permute-start.11 = (f32[64,128]{1,0:T(8,128)S(1)}, f32[64,128]{1,0:T(8,128)S(1)}, u32[]{:S(2)}, u32[]{:S(2)}) collective-permute-start(f32[64,128]{1,0:T(8,128)S(1)} %add.13.refs_3_), channel_id=1, source_target_pairs={{0,3},{1,2},{2,1},{3,0},{4,7},{5,6},{6,5},{7,4},{8,11},{9,10},{10,... | collective-permute-start | bytes 98312 | tf_op jit(solution)/shard_map/ppermute | solution.py:24
  27.9 0.7 %collective-permute-start.10 = (f32[64,128]{1,0:T(8,128)S(1)}, f32[64,128]{1,0:T(8,128)S(1)}, u32[]{:S(2)}, u32[]{:S(2)}) collective-permute-start(f32[64,128]{1,0:T(8,128)S(1)} %add.13.refs_3_), channel_id=1, source_target_pairs={{0,2},{1,3},{2,0},{3,1},{4,6},{5,7},{6,4},{7,5},{8,10},{9,11},{10,... | collective-permute-start | bytes 98312 | tf_op jit(solution)/shard_map/ppermute | solution.py:24
  28.6 0.0 collective-permute-done.14.refs_2_
  28.6 1.7 %collective-permute-start.9 = (f32[64,128]{1,0:T(8,128)S(1)}, f32[64,128]{1,0:T(8,128)S(1)}, u32[]{:S(2)}, u32[]{:S(2)}) collective-permute-start(f32[64,128]{1,0:T(8,128)S(1)} %add.13.refs_3_), channel_id=1, source_target_pairs={{0,1},{1,0},{2,3},{3,2},{4,5},{5,4},{6,7},{7,6},{8,9},{9,8},{10,11... | collective-permute-start | bytes 98312 | tf_op jit(solution)/shard_map/ppermute | solution.py:24
  30.4 1.2 %collective-permute-done.13.refs_1_ = f32[240,256]{1,0:T(8,128)S(1)} collective-permute-done((f32[240,256]{1,0:T(8,128)S(1)}, f32[240,256]{1,0:T(8,128)S(1)}, u32[]{:S(2)}, u32[]{:S(2)}) %collective-permute-start.13) | collective-permute-done | bytes 245792 | tf_op jit(solution)/shard_map/ppermute | solution.py:24
  31.5 0.0 collective-permute-done.12.refs_0_
  31.5 0.0 collective-permute-start.15
  31.5 0.5 %collective-permute-start.16 = (f32[240,256]{1,0:T(8,128)S(1)}, f32[240,256]{1,0:T(8,128)S(1)}, u32[]{:S(2)}, u32[]{:S(2)}) collective-permute-start(f32[240,256]{1,0:T(8,128)S(1)} %get-tuple-element.43.refs_1_), channel_id=1, source_target_pairs={{0,4},{4,0},{8,12},{12,8},{16,20},{20,16},{24,28},{28,24},{1,5},{5... | collective-permute-start | bytes 737288 | tf_op jit(solution)/shard_map/ppermute | solution.py:24
  32.0 0.0 collective-permute-done.11
  32.0 0.1 collective-permute-start.17
  32.1 0.4 collective-permute-done.10
  32.5 0.0 collective-permute-done.9
  32.5 0.5 %collective-permute-done.15.refs_3_ = f32[240,256]{1,0:T(8,128)S(1)} collective-permute-done((f32[240,256]{1,0:T(8,128)S(1)}, f32[240,256]{1,0:T(8,128)S(1)}, u32[]{:S(2)}, u32[]{:S(2)}) %collective-permute-start.15) | collective-permute-done | bytes 245792 | tf_op jit(solution)/shard_map/ppermute | solution.py:24
  33.0 0.4 collective-permute-done.16.refs_4_
  33.4 0.4 collective-permute-done.17.refs_5_
  33.7 4.4 %coarse.1 = (f32[4,256]{1,0:T(4,128)}, bf16[128,256]{1,0:T(8,128)(2,1)S(1)}, bf16[128,256]{1,0:T(8,128)(2,1)S(1)}, f32[8,128]{1,0:T(8,128)S(1)}, f32[8,128]{1,0:T(8,128)S(1)}) custom-call(f32[64,128]{1,0:T(8,128)S(1)} %add_add_fusion.rhs_ref, f32[612,256]{1,0:T(8,128)S(1)} %get-tuple-element.41.one.message, ...), custom_call_target="tpu_custom_call" | custom-call | flops 1 | bytes 1 | tf_op jit(solution)/shard_map/coarse/pallas_call | solution.py:617
  38.1 0.6 %collective-permute-start.18 = (f32[8,128]{1,0:T(8,128)S(1)}, f32[8,128]{1,0:T(8,128)S(1)}, u32[]{:S(2)}, u32[]{:S(2)}) collective-permute-start(f32[8,128]{1,0:T(8,128)S(1)} %get-tuple-element.51), channel_id=1, source_target_pairs={{0,1},{1,0},{2,3},{3,2},{4,5},{5,4},{6,7},{7,6},{8,9},{9,8},{10,11... | collective-permute-start | bytes 12296 | tf_op jit(solution)/shard_map/ppermute | solution.py:37
  38.7 1.4 %collective-permute-start.20 = (f32[8,128]{1,0:T(8,128)S(1)}, f32[8,128]{1,0:T(8,128)S(1)}, u32[]{:S(2)}, u32[]{:S(2)}) collective-permute-start(f32[8,128]{1,0:T(8,128)S(1)} %get-tuple-element.52), channel_id=1, source_target_pairs={{3,4},{7,8},{11,12},{15,16},{19,20},{23,24},{27,28},{2,6},{10,14},... | collective-permute-start | bytes 12296 | tf_op jit(solution)/shard_map/ppermute | solution.py:43
  40.1 0.1 collective-permute-start.19
  40.2 0.7 %correct.1 = (f32[4,24,128]{2,1,0:T(8,128)S(1)}, f32[6,24,128]{2,1,0:T(8,128)S(1)}, f32[4,24,128]{2,1,0:T(8,128)S(1)}) custom-call(f32[4,16,128]{2,1,0:T(8,128)S(1)} %get-tuple-element.28.r, f32[16,128]{1,0:T(8,128)S(1)} %get-tuple-element.29.b, f32[16,128]{1,0:T(8,128)S(1)} %get-tuple-element.30.e, f32[16,128]{1,0:T(8,128)S(1)} %get-tuple-element.31.n, ...), custom_call_target="tpu_custom_call" | custom-call | flops 1 | bytes 1 | tf_op jit(solution)/shard_map/correct/pallas_call | solution.py:630
  40.9 0.8 %collective-permute-done.18.y_first = f32[8,128]{1,0:T(8,128)S(1)} collective-permute-done((f32[8,128]{1,0:T(8,128)S(1)}, f32[8,128]{1,0:T(8,128)S(1)}, u32[]{:S(2)}, u32[]{:S(2)}) %collective-permute-start.18) | collective-permute-done | bytes 4128 | tf_op jit(solution)/shard_map/ppermute | solution.py:37
  41.7 0.6 %collective-permute-done.20.y_outer = f32[8,128]{1,0:T(8,128)S(1)} collective-permute-done((f32[8,128]{1,0:T(8,128)S(1)}, f32[8,128]{1,0:T(8,128)S(1)}, u32[]{:S(2)}, u32[]{:S(2)}) %collective-permute-start.20) | collective-permute-done | bytes 4128 | tf_op jit(solution)/shard_map/ppermute | solution.py:43
  42.3 0.0 collective-permute-done.19.y_inner
  42.3 0.8 %post.1 = f32[4,16,128]{2,1,0:T(8,128)} custom-call(f32[4,24,128]{2,1,0:T(8,128)S(1)} %get-tuple-element.48.r, f32[6,24,128]{2,1,0:T(8,128)S(1)} %get-tuple-element.49.coef, f32[4,24,128]{2,1,0:T(8,128)S(1)} %get-tuple-element.50.y_ref, f32[8,128]{1,0:T(8,128)S(1)} %collective-permute-done.18.y_first, f32[8,128]{1,0:T(8,128)S(1)} %collective-permute-done.19.y_inner, ...), custom_call_target="tpu_custom_call" | custom-call | flops 1 | bytes 1 | tf_op jit(solution)/shard_map/post/pallas_call | solution.py:636
  (6 shorter events, 0.1 us)
Async XLA Ops:
  1.7 13.7 %collective-permute-start.4 = (f32[88,256]{1,0:T(8,128)S(1)}, f32[88,256]{1,0:T(8,128)S(1)}, u32[]{:S(2)}, u32[]{:S(2)}) collective-permute-start(f32[88,256]{1,0:T(8,128)S(1)} %get-tuple-element.37), channel_id=1, source_target_pairs={{0,24},{4,28},{8,16},{12,20},{16,8},{20,12},{24,0},{28,4},{1,25},{... | collective-permute-start | bytes 270344 | tf_op jit(solution)/shard_map/ppermute | solution.py:24
  6.8 8.6 %collective-permute-start.3 = (f32[88,256]{1,0:T(8,128)S(1)}, f32[88,256]{1,0:T(8,128)S(1)}, u32[]{:S(2)}, u32[]{:S(2)}) collective-permute-start(f32[88,256]{1,0:T(8,128)S(1)} %get-tuple-element.37), channel_id=1, source_target_pairs={{0,16},{4,20},{8,24},{12,28},{16,0},{20,4},{24,8},{28,12},{1,17},{... | collective-permute-start | bytes 270344 | tf_op jit(solution)/shard_map/ppermute | solution.py:24
  6.8 8.6 %collective-permute-start.2 = (f32[88,256]{1,0:T(8,128)S(1)}, f32[88,256]{1,0:T(8,128)S(1)}, u32[]{:S(2)}, u32[]{:S(2)}) collective-permute-start(f32[88,256]{1,0:T(8,128)S(1)} %get-tuple-element.37), channel_id=1, source_target_pairs={{0,8},{4,12},{8,0},{12,4},{16,24},{20,28},{24,16},{28,20},{1,9},{5... | collective-permute-start | bytes 270344 | tf_op jit(solution)/shard_map/ppermute | solution.py:24
  7.5 7.1 %collective-permute-start = (f32[24,128]{1,0:T(8,128)S(1)}, f32[24,128]{1,0:T(8,128)S(1)}, u32[]{:S(2)}, u32[]{:S(2)}) collective-permute-start(f32[24,128]{1,0:T(8,128)S(1)} %get-tuple-element.32), channel_id=1, source_target_pairs={{1,2},{3,4},{5,6},{7,8},{9,10},{11,12},{13,14},{15,16},{17,18},{19... | collective-permute-start | bytes 36872 | tf_op jit(solution)/shard_map/ppermute | solution.py:31
  11.7 3.7 %collective-permute-start.1 = (f32[24,128]{1,0:T(8,128)S(1)}, f32[24,128]{1,0:T(8,128)S(1)}, u32[]{:S(2)}, u32[]{:S(2)}) collective-permute-start(f32[24,128]{1,0:T(8,128)S(1)} %get-tuple-element.33), channel_id=1, source_target_pairs={{0,1},{1,0},{2,3},{3,2},{4,5},{5,4},{6,7},{7,6},{8,9},{9,8},{10,11... | collective-permute-start | bytes 36872 | tf_op jit(solution)/shard_map/ppermute | solution.py:29
  16.5 3.6 %collective-permute-start.5 = (f32[612,256]{1,0:T(8,128)S(1)}, f32[612,256]{1,0:T(8,128)S(1)}, u32[]{:S(2)}, u32[]{:S(2)}) collective-permute-start(f32[612,256]{1,0:T(8,128)S(1)} %get-tuple-element.41.one.message), channel_id=1, source_target_pairs={{0,4},{4,0},{8,12},{12,8},{16,20},{20,16},{24,28},{28,24},{1,5},{5... | collective-permute-start | bytes 1880072 | tf_op jit(solution)/shard_map/ppermute | solution.py:24
  16.5 12.1 %collective-permute-start.14 = (f32[240,256]{1,0:T(8,128)S(1)}, f32[240,256]{1,0:T(8,128)S(1)}, u32[]{:S(2)}, u32[]{:S(2)}) collective-permute-start(f32[240,256]{1,0:T(8,128)S(1)} %get-tuple-element.38.gathered), channel_id=1, source_target_pairs={{0,3},{1,2},{2,1},{3,0},{4,7},{5,6},{6,5},{7,4},{8,11},{9,10},{10,... | collective-permute-start | bytes 737288 | tf_op jit(solution)/shard_map/ppermute | solution.py:24
  18.2 13.3 %collective-permute-start.13 = (f32[240,256]{1,0:T(8,128)S(1)}, f32[240,256]{1,0:T(8,128)S(1)}, u32[]{:S(2)}, u32[]{:S(2)}) collective-permute-start(f32[240,256]{1,0:T(8,128)S(1)} %get-tuple-element.38.gathered), channel_id=1, source_target_pairs={{0,2},{1,3},{2,0},{3,1},{4,6},{5,7},{6,4},{7,5},{8,10},{9,11},{10,... | collective-permute-start | bytes 737288 | tf_op jit(solution)/shard_map/ppermute | solution.py:24
  18.5 13.0 %collective-permute-start.12 = (f32[240,256]{1,0:T(8,128)S(1)}, f32[240,256]{1,0:T(8,128)S(1)}, u32[]{:S(2)}, u32[]{:S(2)}) collective-permute-start(f32[240,256]{1,0:T(8,128)S(1)} %get-tuple-element.38.gathered), channel_id=1, source_target_pairs={{0,1},{1,0},{2,3},{3,2},{4,5},{5,4},{6,7},{7,6},{8,9},{9,8},{10,11... | collective-permute-start | bytes 737288 | tf_op jit(solution)/shard_map/ppermute | solution.py:24
  20.1 4.0 %collective-permute-start.7 = (f32[64,128]{1,0:T(8,128)S(1)}, f32[64,128]{1,0:T(8,128)S(1)}, u32[]{:S(2)}, u32[]{:S(2)}) collective-permute-start(f32[64,128]{1,0:T(8,128)S(1)} %add.20.value), channel_id=1, source_target_pairs={{0,8},{1,9},{2,10},{3,11},{4,20},{5,21},{6,22},{7,23},{8,0},{9,1},... | collective-permute-start | bytes 98312 | tf_op jit(solution)/shard_map/ppermute | solution.py:78
  20.9 3.9 %collective-permute-start.6 = (f32[64,128]{1,0:T(8,128)S(1)}, f32[64,128]{1,0:T(8,128)S(1)}, u32[]{:S(2)}, u32[]{:S(2)}) collective-permute-start(f32[64,128]{1,0:T(8,128)S(1)} %add.20.value), channel_id=1, source_target_pairs={{0,8},{1,9},{2,10},{3,11},{4,28},{5,29},{6,30},{7,31},{8,0},{9,1},... | collective-permute-start | bytes 98312 | tf_op jit(solution)/shard_map/ppermute | solution.py:77
  24.9 2.0 %collective-permute-start.8 = (f32[64,128]{1,0:T(8,128)S(1)}, f32[64,128]{1,0:T(8,128)S(1)}, u32[]{:S(2)}, u32[]{:S(2)}) collective-permute-start(f32[64,128]{1,0:T(8,128)S(1)} %share.1), channel_id=1, source_target_pairs={{0,4},{4,0},{8,12},{12,8},{16,20},{20,16},{24,28},{28,24},{1,5},{5... | collective-permute-start | bytes 98312 | tf_op jit(solution)/shard_map/ppermute | solution.py:24
  26.9 5.2 %collective-permute-start.11 = (f32[64,128]{1,0:T(8,128)S(1)}, f32[64,128]{1,0:T(8,128)S(1)}, u32[]{:S(2)}, u32[]{:S(2)}) collective-permute-start(f32[64,128]{1,0:T(8,128)S(1)} %add.13.refs_3_), channel_id=1, source_target_pairs={{0,3},{1,2},{2,1},{3,0},{4,7},{5,6},{6,5},{7,4},{8,11},{9,10},{10,... | collective-permute-start | bytes 98312 | tf_op jit(solution)/shard_map/ppermute | solution.py:24
  27.9 4.6 %collective-permute-start.10 = (f32[64,128]{1,0:T(8,128)S(1)}, f32[64,128]{1,0:T(8,128)S(1)}, u32[]{:S(2)}, u32[]{:S(2)}) collective-permute-start(f32[64,128]{1,0:T(8,128)S(1)} %add.13.refs_3_), channel_id=1, source_target_pairs={{0,2},{1,3},{2,0},{3,1},{4,6},{5,7},{6,4},{7,5},{8,10},{9,11},{10,... | collective-permute-start | bytes 98312 | tf_op jit(solution)/shard_map/ppermute | solution.py:24
  28.6 3.9 %collective-permute-start.9 = (f32[64,128]{1,0:T(8,128)S(1)}, f32[64,128]{1,0:T(8,128)S(1)}, u32[]{:S(2)}, u32[]{:S(2)}) collective-permute-start(f32[64,128]{1,0:T(8,128)S(1)} %add.13.refs_3_), channel_id=1, source_target_pairs={{0,1},{1,0},{2,3},{3,2},{4,5},{5,4},{6,7},{7,6},{8,9},{9,8},{10,11... | collective-permute-start | bytes 98312 | tf_op jit(solution)/shard_map/ppermute | solution.py:24
  31.5 1.5 %collective-permute-start.15 = (f32[240,256]{1,0:T(8,128)S(1)}, f32[240,256]{1,0:T(8,128)S(1)}, u32[]{:S(2)}, u32[]{:S(2)}) collective-permute-start(f32[240,256]{1,0:T(8,128)S(1)} %get-tuple-element.42.refs_0_), channel_id=1, source_target_pairs={{0,4},{4,0},{8,12},{12,8},{16,20},{20,16},{24,28},{28,24},{1,5},{5... | collective-permute-start | bytes 737288 | tf_op jit(solution)/shard_map/ppermute | solution.py:24
  31.5 1.9 %collective-permute-start.16 = (f32[240,256]{1,0:T(8,128)S(1)}, f32[240,256]{1,0:T(8,128)S(1)}, u32[]{:S(2)}, u32[]{:S(2)}) collective-permute-start(f32[240,256]{1,0:T(8,128)S(1)} %get-tuple-element.43.refs_1_), channel_id=1, source_target_pairs={{0,4},{4,0},{8,12},{12,8},{16,20},{20,16},{24,28},{28,24},{1,5},{5... | collective-permute-start | bytes 737288 | tf_op jit(solution)/shard_map/ppermute | solution.py:24
  32.0 1.7 %collective-permute-start.17 = (f32[240,256]{1,0:T(8,128)S(1)}, f32[240,256]{1,0:T(8,128)S(1)}, u32[]{:S(2)}, u32[]{:S(2)}) collective-permute-start(f32[240,256]{1,0:T(8,128)S(1)} %get-tuple-element.44.refs_2_), channel_id=1, source_target_pairs={{0,4},{4,0},{8,12},{12,8},{16,20},{20,16},{24,28},{28,24},{1,5},{5... | collective-permute-start | bytes 737288 | tf_op jit(solution)/shard_map/ppermute | solution.py:24
  38.1 3.6 %collective-permute-start.18 = (f32[8,128]{1,0:T(8,128)S(1)}, f32[8,128]{1,0:T(8,128)S(1)}, u32[]{:S(2)}, u32[]{:S(2)}) collective-permute-start(f32[8,128]{1,0:T(8,128)S(1)} %get-tuple-element.51), channel_id=1, source_target_pairs={{0,1},{1,0},{2,3},{3,2},{4,5},{5,4},{6,7},{7,6},{8,9},{9,8},{10,11... | collective-permute-start | bytes 12296 | tf_op jit(solution)/shard_map/ppermute | solution.py:37
  38.7 3.6 %collective-permute-start.20 = (f32[8,128]{1,0:T(8,128)S(1)}, f32[8,128]{1,0:T(8,128)S(1)}, u32[]{:S(2)}, u32[]{:S(2)}) collective-permute-start(f32[8,128]{1,0:T(8,128)S(1)} %get-tuple-element.52), channel_id=1, source_target_pairs={{3,4},{7,8},{11,12},{15,16},{19,20},{23,24},{27,28},{2,6},{10,14},... | collective-permute-start | bytes 12296 | tf_op jit(solution)/shard_map/ppermute | solution.py:43
  40.1 2.2 %collective-permute-start.19 = (f32[8,128]{1,0:T(8,128)S(1)}, f32[8,128]{1,0:T(8,128)S(1)}, u32[]{:S(2)}, u32[]{:S(2)}) collective-permute-start(f32[8,128]{1,0:T(8,128)S(1)} %get-tuple-element.52), channel_id=1, source_target_pairs={{0,4},{1,2},{2,1},{3,7},{4,0},{5,6},{6,5},{7,3},{8,12},{9,10},{10,... | collective-permute-start | bytes 12296 | tf_op jit(solution)/shard_map/ppermute | solution.py:38
